TPU v7x, 32 devices: a whole 2x2x4 slice. The times are simulated.
32 devices in a mesh: section: 2 (over core), rows: 8 (over z, y), cols: 2 (over x).
Axes of the slice: x: 2, y: 2, z: 4, core: 2. Of those that a mesh axis runs over, the one named last changes fastest.
Arguments:
- latent: bfloat16 [4, 16, 64, 384], P('section', ('rows', 'cols')), may hold values from -6 to 6
- cache_one: bfloat16 [2, 16, 64, 384], P(None, ('rows', 'cols')), may hold values from -6 to 6
- cache_two: bfloat16 [2, 16, 64, 384], P(None, ('rows', 'cols')), may hold values from -6 to 6
- cache_time: bfloat16 [2, 16, 64, 384], P(None, 'rows', 'cols'), may hold values from -6 to 6
- cache_three: bfloat16 [2, 32, 128, 192], P(None, 'rows', 'cols'), may hold values from -6 to 6
- cache_four: bfloat16 [2, 32, 128, 192], P(None, 'rows', 'cols'), may hold values from -6 to 6
- gain_one: float32 [384], replicated, may hold values from 0.25 to 1.75
- gain_two: float32 [384], replicated, may hold values from 0.25 to 1.75
- gain_three: float32 [192], replicated, may hold values from 0.25 to 1.75
- gain_four: float32 [192], replicated, may hold values from 0.25 to 1.75
- weight_one: bfloat16 [10368, 384], replicated, may hold values from -0.0625 to 0.0625
- weight_two: bfloat16 [10368, 384], replicated, may hold values from -0.0625 to 0.0625
- weight_time: bfloat16 [1152, 768], replicated, may hold values from -0.1875 to 0.1875
- weight_upsample: bfloat16 [3456, 192], replicated, may hold values from -0.109375 to 0.109375
- weight_three: bfloat16 [5184, 192], replicated, may hold values from -0.078125 to 0.078125
- weight_four: bfloat16 [5184, 192], replicated, may hold values from -0.078125 to 0.078125
Outputs:
- decoded: bfloat16 [8, 32, 128, 192], P('section', 'rows', 'cols')
All inputs are finite; a program needn't handle non-finite values.
Results may differ from a plain program's by a relative error of at most 0.0085.
Values may be sent and summed in bfloat16 or wider, within the bound.
No kernel may reach another device: no remote copies, remote signals or barrier semaphores. Data moves between devices by JAX's collectives and lax.ppermute only.
A program may use at most 128 MiB of HBM per device.

v0:
```python
import functools

import jax
import jax.numpy as jnp
from jax import lax
from jax.experimental import pallas as pl
from jax.experimental.pallas import tpu as pltpu
from jax.sharding import PartitionSpec as P

EPSILON = 1e-06
HALO = 4
LANES = 256


def swapped(value, axis):
    return lax.ppermute(value, axis, [(0, 1), (1, 0)])


def shifted(value, axis, steps):
    count = lax.axis_size(axis)
    initial, last = (max(0, -steps), min(count, count - steps))
    return lax.ppermute(value, axis, [(source, source + steps) for source in range(initial, last)])


def silu(scaled):
    half = scaled * 0.5
    return half * (1.0 + jnp.tanh(half))


def activate(values, gain, mask):
    mean = jnp.mean(values * values, axis=-1, keepdims=True)
    return silu(values * (lax.rsqrt(mean + EPSILON) * mask) * gain)


def activate_pairs(values, gain, mask):
    channels = values.shape[-1] // 2
    squares = values * values
    first = lax.broadcasted_iota(jnp.int32, (1, 2 * channels), 1) < channels
    total = jnp.sum(squares, axis=-1, keepdims=True)
    low = jnp.sum(jnp.where(first, squares, 0.0), axis=-1, keepdims=True)
    scale_low = lax.rsqrt(low / channels + EPSILON) * mask
    scale_high = lax.rsqrt((total - low) / channels + EPSILON) * mask
    return silu(values * jnp.where(first, scale_low, scale_high) * gain)


def decode_kernel(
    wide,
    low2,
    low1,
    own,
    high1,
    high2,
    time_ref,
    three_ref,
    four_ref,
    masks,
    gains,
    weight_one,
    weight_two,
    weight_time,
    weight_up,
    weight_three,
    weight_four,
    out_ref,
    w1,
    w2,
    wt,
    wu,
    w3,
    w4,
    acc,
    x1e,
    x1o,
    x2e,
    x2o,
    mixed,
    de,
    do,
    x3e,
    x3o,
    x4e,
    x4o,
    lifted_ref,
    sems,
):
    f32, bf16 = jnp.float32, jnp.bfloat16
    channels = own.shape[-1]
    frames = own.shape[0] - 4
    pieces = (low2, low1, own, high1, high2)
    copies_one = [
        pltpu.make_async_copy(
            weight_one.at[:, dx], w1.at[:, :, pl.ds(dx * channels, channels)], sems.at[dx]
        )
        for dx in range(3)
    ]
    copies_two = [
        pltpu.make_async_copy(
            weight_two.at[:, dx], w2.at[:, :, pl.ds(dx * channels, channels)], sems.at[3 + dx]
        )
        for dx in range(3)
    ]
    copy_time = pltpu.make_async_copy(weight_time, wt, sems.at[6])
    copy_up = pltpu.make_async_copy(weight_up, wu, sems.at[7])
    copy_three = pltpu.make_async_copy(weight_three, w3, sems.at[8])
    copy_four = pltpu.make_async_copy(weight_four, w4, sems.at[9])
    for copy in copies_one + copies_two + [copy_time, copy_up, copy_three, copy_four]:
        copy.start()

    def rows_of(refs, index):
        return jnp.concatenate([ref[index].astype(f32) for ref in refs], axis=0)

    def store(even, odd, slot, values, height):
        even[pl.ds(slot * (height * wide), height * wide), :] = values.astype(bf16)
        odd[pl.ds(slot * ((height - 2) * wide), (height - 2) * wide), :] = values[
            wide : (height - 1) * wide
        ].astype(bf16)

    def taps(even, odd, count, height, dt, dy):
        inner = (height - 2) * wide
        if dy == 1:
            parts = [odd[pl.ds((f + dt) * inner, inner), :] for f in range(count)]
        else:
            parts = [
                even[pl.ds((f + dt) * height * wide + dy * wide, inner), :] for f in range(count)
            ]
        return jnp.concatenate(parts, axis=0)

    def product(even, odd, count, height, weights):
        rows = count * (height - 2) * wide

        def column(n, carry):
            lanes = pl.ds(pl.multiple_of(n * LANES, LANES), LANES)
            total = None
            for first, last in ((0, 4), (4, 8), (8, 9)):
                left = jnp.concatenate(
                    [taps(even, odd, count, height, t // 3, t % 3) for t in range(first, last)],
                    axis=1,
                )
                right = weights[first:last, :, lanes].reshape((last - first) * channels, LANES)
                part = jnp.dot(left, right, preferred_element_type=f32)
                total = part if total is None else total + part
            acc[0:rows, lanes] = total
            return carry

        lax.fori_loop(0, weights.shape[-1] // LANES, column, 0)

    def gather_low(start, size):
        center = acc[pl.ds(start, size), channels : 2 * channels]
        before = acc[pl.ds(start, size), 0:channels]
        after = acc[pl.ds(start, size), 2 * channels : 3 * channels]
        return center + pltpu.roll(before, 1, 0) + pltpu.roll(after, size - 1, 0)

    def gather_pairs(start, size):
        center = acc[pl.ds(start, size), 0:channels]
        side = acc[pl.ds(start, size), channels : 2 * channels]
        first = lax.broadcasted_iota(jnp.int32, (1, channels), 1) < channels // 2
        return center + jnp.where(first, pltpu.roll(side, 1, 0), pltpu.roll(side, size - 1, 0))

    def aligned(index, size):
        return pl.multiple_of(index * size, 16)

    gain = [gains[i : i + 1, :] for i in range(4)]

    for f in range(2):
        store(x1e, x1o, f, rows_of(pieces, frames + f), 10)

    def norm_one(f, carry):
        values = activate(rows_of(pieces, f), gain[0], 1.0)
        store(x1e, x1o, f + 2, values, 10)
        return carry

    lax.fori_loop(0, frames, norm_one, 0)
    for copy in copies_one:
        copy.wait()
    product(x1e, x1o, frames, 10, w1)

    for f in range(2):
        store(x2e, x2o, f, rows_of(pieces, frames + 2 + f)[wide : 9 * wide], 8)

    def norm_two(f, carry):
        size = 8 * wide
        values = activate(gather_low(aligned(f, size), size), gain[1], masks[0:size, 0:1])
        store(x2e, x2o, f + 2, values, 8)
        return carry

    lax.fori_loop(0, frames, norm_two, 0)
    for copy in copies_two:
        copy.wait()
    product(x2e, x2o, frames, 8, w2)

    size = 6 * wide
    mixed[0 : 2 * size, :] = time_ref[...]

    def residual_one(f, carry):
        values = gather_low(aligned(f, size), size) + rows_of(pieces[1:4], f)
        mixed[pl.ds(aligned(f + 2, size), size), :] = values.astype(bf16)
        return carry

    lax.fori_loop(0, frames, residual_one, 0)
    copy_time.wait()

    def mix(n, carry):
        lanes = pl.ds(pl.multiple_of(n * LANES, LANES), LANES)
        left = jnp.concatenate(
            [mixed[pl.ds(t * size, frames * size), :] for t in range(3)], axis=1
        )
        acc[0 : frames * size, lanes] = jnp.dot(left, wt[:, lanes], preferred_element_type=f32)
        return carry

    lax.fori_loop(0, 2 * channels // LANES, mix, 0)

    def double(t, carry):
        mask = masks[wide : wide + size, 0:1]
        for half in range(2):
            values = acc[pl.ds(aligned(t, size), size), half * channels : (half + 1) * channels]
            store(de, do, 2 * t + half, values * mask, 6)
        return carry

    lax.fori_loop(0, frames, double, 0)
    copy_up.wait()

    count = 2 * frames
    for py in range(2):

        def enlarge(n, carry):
            lanes = pl.ds(pl.multiple_of(n * LANES, LANES), LANES)
            left = jnp.concatenate(
                [taps(de, do, count, 6, 0, py), taps(de, do, count, 6, 0, py + 1)], axis=1
            )
            right = wu[2 * py : 2 * py + 2, :, lanes].reshape(2 * channels, LANES)
            acc[py * count * 4 * wide : (py + 1) * count * 4 * wide, lanes] = jnp.dot(
                left, right, preferred_element_type=f32
            )
            return carry

        lax.fori_loop(0, 2 * channels // LANES, enlarge, 0)

    store(x3e, x3o, 0, three_ref[0].astype(f32), 8)
    store(x3e, x3o, 1, three_ref[1].astype(f32), 8)

    def norm_three(f, carry):
        part = 4 * wide
        values = [
            gather_pairs(pl.multiple_of(py * count * part + f * part, 16), part).astype(bf16)
            for py in range(2)
        ]
        values = [v.astype(f32) for v in values]
        rows = jnp.concatenate(
            [values[h % 2][(h // 2) * wide : (h // 2 + 1) * wide] for h in range(8)], axis=0
        )
        lifted_ref[pl.ds(aligned(f, part), part), :] = rows[2 * wide : 6 * wide]
        begin = 8 * wide
        store(x3e, x3o, f + 2, activate_pairs(rows, gain[2], masks[begin : 2 * begin, 0:1]), 8)
        return carry

    lax.fori_loop(0, count, norm_three, 0)
    copy_three.wait()
    product(x3e, x3o, count, 8, w3)

    store(x4e, x4o, 0, four_ref[0].astype(f32), 6)
    store(x4e, x4o, 1, four_ref[1].astype(f32), 6)

    def norm_four(f, carry):
        begin = 9 * wide
        values = gather_pairs(aligned(f, size), size)
        store(x4e, x4o, f + 2, activate_pairs(values, gain[3], masks[begin : begin + size, 0:1]), 6)
        return carry

    lax.fori_loop(0, count, norm_four, 0)
    copy_four.wait()
    product(x4e, x4o, count, 6, w4)

    def finish(f, carry):
        part = 4 * wide
        start = aligned(f, part)
        values = gather_pairs(start, part) + lifted_ref[pl.ds(start, part), :]
        values = pltpu.roll(values, part - HALO, 0)
        for y in range(4):
            inner = wide - 2 * HALO
            out_ref[f, y] = values[y * wide : y * wide + inner].astype(bf16)
        return carry

    lax.fori_loop(0, count, finish, 0)


def decode(pieces, time, three, four, masks, gains, weights):
    bf16, f32 = jnp.bfloat16, jnp.float32
    units, _, channels = pieces[0].shape
    frames = units - 4
    count = 2 * frames
    wide = pieces[0].shape[1] // 2
    weight_one, weight_two, weight_time, weight_up, weight_three, weight_four = weights
    padded_lanes = -(-3 * channels // LANES) * LANES
    vmem = pl.BlockSpec(memory_space=pltpu.VMEM)
    anywhere = pl.BlockSpec(memory_space=pl.ANY)

    def planes(slots, height):
        return [
            pltpu.VMEM((slots * height * wide, channels), bf16),
            pltpu.VMEM((slots * (height - 2) * wide, channels), bf16),
        ]

    return pl.pallas_call(
        functools.partial(decode_kernel, wide),
        out_shape=jax.ShapeDtypeStruct((count, 4, wide - 2 * HALO, channels), bf16),
        in_specs=[vmem] * 10 + [anywhere] * 6,
        out_specs=vmem,
        scratch_shapes=[
            pltpu.VMEM((9, channels, padded_lanes), bf16),
            pltpu.VMEM((9, channels, padded_lanes), bf16),
            pltpu.VMEM(weight_time.shape, bf16),
            pltpu.VMEM(weight_up.shape, bf16),
            pltpu.VMEM(weight_three.shape, bf16),
            pltpu.VMEM(weight_four.shape, bf16),
            pltpu.VMEM((2 * count * 4 * wide, padded_lanes), f32),
            *planes(frames + 2, 10),
            *planes(frames + 2, 8),
            pltpu.VMEM(((frames + 2) * 6 * wide, channels), bf16),
            *planes(count, 6),
            *planes(count + 2, 8),
            *planes(count + 2, 6),
            pltpu.VMEM((count * 4 * wide, channels), f32),
            pltpu.SemaphoreType.DMA((10,)),
        ],
        compiler_params=pltpu.CompilerParams(vmem_limit_bytes=60 * 1024 * 1024),
        name="decode",
    )(*pieces, time, three, four, masks, gains, *weights)


def pair_weights(weight, channels):
    taps = weight.reshape(9, 3, channels, channels)
    none = jnp.zeros_like(taps[:, 0])
    even = jnp.concatenate([taps[:, 1], taps[:, 0], none, taps[:, 2]], axis=-1)
    odd = jnp.concatenate([taps[:, 2], taps[:, 1], taps[:, 0], none], axis=-1)
    return jnp.concatenate([even, odd], axis=1)


def enlarge_weights(weight, channels):
    taps = weight.reshape(3, 3, -1, channels).astype(jnp.float32)
    rows = [taps[0], taps[1] + taps[2], taps[0] + taps[1], taps[2]]
    parts = [jnp.concatenate([r[1] + r[2], r[0] + r[1], r[0], r[2]], axis=-1) for r in rows]
    return jnp.stack(parts).astype(jnp.bfloat16)


def body(
    latent,
    cache_one,
    cache_two,
    cache_time,
    cache_three,
    cache_four,
    gain_one,
    gain_two,
    gain_three,
    gain_four,
    weight_one,
    weight_two,
    weight_time,
    weight_upsample,
    weight_three,
    weight_four,
):
    section, row, col = (lax.axis_index(name) for name in ("section", "rows", "cols"))
    sections, row_count, col_count = (lax.axis_size(name) for name in ("section", "rows", "cols"))
    width, channels = latent.shape[2:]
    tile = width // col_count
    part = tile // sections
    wide = part + 2 * HALO
    half = weight_three.shape[1]

    def windows(array, which):
        padded = jnp.pad(array[:, 0], ((0, 0), (HALO, HALO), (0, 0)))
        return jnp.stack(
            [
                lax.dynamic_slice_in_dim(padded, c * tile + which * part, wide, 1)
                for c in range(col_count)
            ]
        )

    kept = windows(latent, section)
    arrived = swapped(windows(latent, 1 - section), "section")
    low = section == 0
    units = jnp.concatenate(
        [
            jnp.where(low, kept, arrived),
            jnp.where(low, arrived, kept),
            windows(cache_one, section),
            windows(cache_two, section),
        ],
        axis=1,
    )
    mine = lax.dynamic_index_in_dim(units, col, 0, keepdims=False)
    theirs = swapped(lax.dynamic_index_in_dim(units, 1 - col, 0, keepdims=False), "cols")
    left = col == 0
    own = jnp.concatenate([jnp.where(left, mine, theirs), jnp.where(left, theirs, mine)], axis=1)
    pieces = [
        shifted(own, "rows", 2),
        shifted(own, "rows", 1),
        own,
        shifted(own, "rows", -1),
        shifted(own, "rows", -2),
    ]

    def paired(array):
        return array.reshape(array.shape[0], array.shape[1], tile, channels)

    tiles = jnp.concatenate([cache_time, paired(cache_three), paired(cache_four)], axis=1)
    edge = jnp.where(left, tiles[:, :, tile - HALO :], tiles[:, :, :HALO])
    edge = swapped(edge, "cols")
    nothing = jnp.zeros_like(edge)
    tiles = jnp.concatenate(
        [jnp.where(left, nothing, edge), tiles, jnp.where(left, edge, nothing)], axis=2
    )
    tiles = lax.dynamic_slice_in_dim(tiles, section * part, wide, 2)
    time, three, four = tiles[:, 0:2], tiles[:, 2:6], tiles[:, 6:10]
    above = shifted(jnp.concatenate([time, three[:, 2:], four[:, 3:]], axis=1), "rows", 1)
    below = shifted(jnp.concatenate([time, three[:, :2], four[:, :1]], axis=1), "rows", -1)
    time = jnp.concatenate([above[:, 0:2], time, below[:, 0:2]], axis=1)
    three = jnp.concatenate([above[:, 2:4], three, below[:, 2:4]], axis=1)
    four = jnp.concatenate([above[:, 4:], four, below[:, 4:]], axis=1)

    height = 2 * row_count
    columns = col * tile + section * part - HALO + jnp.arange(wide, dtype=jnp.int32)
    inside = (columns >= 0) & (columns < width)

    def mask(first, count, limit):
        lines = first + jnp.arange(count, dtype=jnp.int32)
        good = (lines >= 0) & (lines < limit)
        return (good[:, None] & inside[None, :]).reshape(-1)

    masks = jnp.concatenate(
        [mask(2 * row - 3, 8, height), mask(4 * row - 2, 8, 2 * height)]
    ).astype(jnp.float32)
    masks = jnp.broadcast_to(masks[:, None], (masks.shape[0], 128))
    gains = jnp.stack(
        [gain_one, gain_two, jnp.tile(gain_three, 2), jnp.tile(gain_four, 2)]
    ).astype(jnp.float32)

    frames = decode(
        pieces,
        time.reshape(-1, channels),
        three.reshape(2, -1, channels),
        four.reshape(2, -1, channels),
        masks,
        gains,
        (
            weight_one.reshape(9, 3, channels, channels),
            weight_two.reshape(9, 3, channels, channels),
            weight_time,
            enlarge_weights(weight_upsample, half),
            pair_weights(weight_three, half),
            pair_weights(weight_four, half),
        ),
    )
    count = frames.shape[0] // sections
    given = lax.dynamic_slice_in_dim(frames, (1 - section) * count, count, 0)
    kept = lax.dynamic_slice_in_dim(frames, section * count, count, 0)
    arrived = swapped(given, "section")
    joined = jnp.concatenate(
        [jnp.where(low, kept, arrived), jnp.where(low, arrived, kept)], axis=2
    )
    return joined.reshape(count, 4, 2 * tile, half)


def solution(mesh):
    placed = (
        P("section", ("rows", "cols"), None, None),
        P(None, ("rows", "cols"), None, None),
        P(None, ("rows", "cols"), None, None),
        P(None, "rows", "cols", None),
        P(None, "rows", "cols", None),
        P(None, "rows", "cols", None),
    ) + (P(),) * 10
    return jax.shard_map(
        body,
        mesh=mesh,
        in_specs=placed,
        out_specs=P("section", "rows", "cols", None),
        check_vma=False,
    )
```

profile of v0, /device:TPU:9, one launch (start us, length us, event | category | flops | bytes accessed | tf_op | source)
XLA Modules:
  0.0 130.1 jit_solution(3518980440368385174)
XLA Ops:
  0.0 0.9 constant_dynamic-update-slice_fusion.2
  0.9 1.2 reshape.113
  2.1 1.2 reshape.114
  4.1 1.2 collective-permute-start.6
  5.3 1.6 %fusion.22 = (bf16[1,2,24,384]{3,2,1,0:T(8,128)(2,1)}, bf16[1,2,24,384]{3,2,1,0:T(8,128)(2,1)}, bf16[1,2,24,384]{3,2,1,0:T(8,128)(2,1)S(1)}, bf16[1,2,24,384]{3,2,1,0:T(8,128)(2,1)S(1)}) fusion(s32[]{:T(128)S(6)} %select_n.87, bf16[2,64,384]{2,1,0:T(8,128)(2,1)} %bitcast.117, s32[]{:T(128)S(6)} %select_n.88, s32[]{:T(128)S(6)} %select_n.89, s32[]{:T(128)S(6)} %select_n.90), kind=kLoop, calls=%fused_computation.86 | loop fusion | bytes 245776 | tf_op jit(solution)/shard_map/stack | solution.py:373
  7.5 1.0 collective-permute-start
  8.5 2.5 %copy.20 = f32[3456,192]{1,0:T(8,128)S(1)} copy(bf16[3456,192]{0,1:T(8,128)(2,1)} %param.29) | data formatting | bytes 3981312 | tf_op jit(solution)/shard_map/convert_element_type | solution.py:339
  11.0 0.9 fusion.7
  12.0 1.0 fusion.14
  15.7 0.8 fusion.18
  18.8 3.8 %copy.23 = bf16[5184,192]{1,0:T(8,128)(2,1)S(1)} copy(bf16[5184,192]{0,1:T(8,128)(2,1)} %param.30) | data formatting | bytes 3981312 | tf_op args[14]
  22.7 4.4 %copy.27 = bf16[5184,192]{1,0:T(8,128)(2,1)} copy(bf16[5184,192]{0,1:T(8,128)(2,1)} %param.31) | data formatting | bytes 3981312 | tf_op args[15]
  28.0 3.8 %slice_bitcast_fusion = (bf16[9,192,192]{2,1,0:T(8,128)(2,1)S(1)}, bf16[9,192,192]{2,1,0:T(8,128)(2,1)}, bf16[9,192,192]{2,1,0:T(8,128)(2,1)}, bf16[9,192,192]{2...) fusion(bf16[9,3,192,192]{3,2,1,0:T(8,128)(2,1)} %bitcast.107, ...), kind=kLoop, calls=%fused_computation.9 | loop fusion | bytes 7962624 | tf_op jit(solution)/shard_map/squeeze | solution.py:333
  31.9 2.0 %maximum_bitcast_fusion = (bf16[1,384,768]{2,1,0:T(8,128)(2,1)S(1)}, bf16[1,384,768]{2,1,0:T(8,128)(2,1)S(1)}) fusion(bf16[384,192]{1,0:T(8,128)(2,1)} %get-tuple-element.12, bf16[384,192]{1,0:T(8,128)(2,1)} %get-tuple-element.9, bf16[384,192]{1,0:T(8,128)(2,1)} %get-tuple-element.6, bf16[384,192]{1,0:T(8,128)(2,1)} %get-tuple-element.5, ...), kind=kLoop, calls=%fused_computation.20 | loop fusion | flops 4718592 | bytes 2359296 | tf_op jit(solution)/shard_map/stack | solution.py:342
  34.6 1.8 %pad_maximum_fusion.4.weight_up = bf16[4,384,768]{2,1,0:T(8,128)(2,1)} fusion(bf16[1,384,768]{2,1,0:T(8,128)(2,1)S(1)} %get-tuple-element.65, bf16[1,384,768]{2,1,0:T(8,128)(2,1)S(1)} %get-tuple-element.67, bf16[1,384,768]{2,1,0:T(8,128)(2,1)S(1)} %get-tuple-element.66, bf16[1,384,768]{2,1,0:T(8,128)(2,1)S(1)} %get-tuple-element.64), kind=kLoop, calls=%fused_computation.8 | loop fusion | flops 3538944 | bytes 4718592 | tf_op jit(solution)/shard_map/stack | solution.py:342
  37.7 9.5 %fusion.3 = (bf16[9,384,768]{2,1,0:T(8,128)(2,1)}, bf16[9,384,768]{2,1,0:T(8,128)(2,1)}) fusion(bf16[9,192,192]{2,1,0:T(8,128)(2,1)S(1)} %broadcast.71, bf16[9,192,192]{2,1,0:T(8,128)(2,1)S(1)} %copy-done.1, bf16[9,192,192]{2,1,0:T(8,128)(2,1)S(1)} %copy-done.2, bf16[9,192,192]{2,1,0:T(8,128)(2,1)S(1)} %get-tuple-element.13, ...), kind=kLoop, calls=%fused_computation.7 | loop fusion | flops 79626240 | bytes 15261696 | tf_op jit(solution)/shard_map/concatenate | solution.py:335
  47.3 0.9 broadcast_select_fusion.4
  48.7 0.9 broadcast_select_fusion.3
  50.1 3.1 %collective-permute-start.7 = (bf16[2,5,24,384]{3,2,1,0:T(8,128)(2,1)S(1)}, bf16[2,5,24,384]{3,2,1,0:T(8,128)(2,1)S(1)}, u32[]{:S(2)}, u32[]{:S(2)}) collective-permute-start(bf16[2,5,24,384]{3,2,1,0:T(8,128)(2,1)S(1)} %pad_maximum_fusion.10), channel_id=1, source_target_pairs={{0,2},{2,4},{4,6},{6,8},{8,10},{10,12},{12,14},{1,3},{3,5},{5,7},{... | collective-permute-start | bytes 552968 | tf_op jit(solution)/shard_map/ppermute | solution.py:22
  53.3 3.0 %collective-permute-start.8 = (bf16[2,5,24,384]{3,2,1,0:T(8,128)(2,1)S(1)}, bf16[2,5,24,384]{3,2,1,0:T(8,128)(2,1)S(1)}, u32[]{:S(2)}, u32[]{:S(2)}) collective-permute-start(bf16[2,5,24,384]{3,2,1,0:T(8,128)(2,1)S(1)} %pad_maximum_fusion.11), channel_id=1, source_target_pairs={{2,0},{4,2},{6,4},{8,6},{10,8},{12,10},{14,12},{3,1},{5,3},{7,5},{... | collective-permute-start | bytes 552968 | tf_op jit(solution)/shard_map/ppermute | solution.py:22
  56.4 3.2 %collective-permute-start.2 = (bf16[8,48,384]{2,1,0:T(8,128)(2,1)S(1)}, bf16[8,48,384]{2,1,0:T(8,128)(2,1)S(1)}, u32[]{:S(2)}, u32[]{:S(2)}) collective-permute-start(bf16[8,48,384]{2,1,0:T(8,128)(2,1)S(1)} %pad_maximum_fusion.6.own), channel_id=1, source_target_pairs={{0,4},{2,6},{4,8},{6,10},{8,12},{10,14},{1,5},{3,7},{5,9},{7,11},{... | collective-permute-start | bytes 884744 | tf_op jit(solution)/shard_map/ppermute | solution.py:22
  59.6 2.2 %collective-permute-start.3 = (bf16[8,48,384]{2,1,0:T(8,128)(2,1)S(1)}, bf16[8,48,384]{2,1,0:T(8,128)(2,1)S(1)}, u32[]{:S(2)}, u32[]{:S(2)}) collective-permute-start(bf16[8,48,384]{2,1,0:T(8,128)(2,1)S(1)} %pad_maximum_fusion.6.own), channel_id=1, source_target_pairs={{0,2},{2,4},{4,6},{6,8},{8,10},{10,12},{12,14},{1,3},{3,5},{5,7},{... | collective-permute-start | bytes 884744 | tf_op jit(solution)/shard_map/ppermute | solution.py:22
  61.9 3.9 %collective-permute-start.4 = (bf16[8,48,384]{2,1,0:T(8,128)(2,1)S(1)}, bf16[8,48,384]{2,1,0:T(8,128)(2,1)S(1)}, u32[]{:S(2)}, u32[]{:S(2)}) collective-permute-start(bf16[8,48,384]{2,1,0:T(8,128)(2,1)S(1)} %pad_maximum_fusion.6.own), channel_id=1, source_target_pairs={{2,0},{4,2},{6,4},{8,6},{10,8},{12,10},{14,12},{3,1},{5,3},{7,5},{... | collective-permute-start | bytes 884744 | tf_op jit(solution)/shard_map/ppermute | solution.py:22
  65.9 2.1 %collective-permute-start.5 = (bf16[8,48,384]{2,1,0:T(8,128)(2,1)S(1)}, bf16[8,48,384]{2,1,0:T(8,128)(2,1)S(1)}, u32[]{:S(2)}, u32[]{:S(2)}) collective-permute-start(bf16[8,48,384]{2,1,0:T(8,128)(2,1)S(1)} %pad_maximum_fusion.6.own), channel_id=1, source_target_pairs={{4,0},{6,2},{8,4},{10,6},{12,8},{14,10},{5,1},{7,3},{9,5},{11,7},{... | collective-permute-start | bytes 884744 | tf_op jit(solution)/shard_map/ppermute | solution.py:22
  70.2 2.2 %collective-permute-done.3.low1 = bf16[8,48,384]{2,1,0:T(8,128)(2,1)S(1)} collective-permute-done((bf16[8,48,384]{2,1,0:T(8,128)(2,1)S(1)}, bf16[8,48,384]{2,1,0:T(8,128)(2,1)S(1)}, u32[]{:S(2)}, u32[]{:S(2)}) %collective-permute-start.3) | collective-permute-done | bytes 294944 | tf_op jit(solution)/shard_map/ppermute | solution.py:22
  72.4 6.0 %collective-permute-done.4.high1 = bf16[8,48,384]{2,1,0:T(8,128)(2,1)S(1)} collective-permute-done((bf16[8,48,384]{2,1,0:T(8,128)(2,1)S(1)}, bf16[8,48,384]{2,1,0:T(8,128)(2,1)S(1)}, u32[]{:S(2)}, u32[]{:S(2)}) %collective-permute-start.4) | collective-permute-done | bytes 294944 | tf_op jit(solution)/shard_map/ppermute | solution.py:22
  80.0 43.6 %decode.1 = bf16[8,4,16,384]{3,2,1,0:T(8,128)(2,1)} custom-call(bf16[8,48,384]{2,1,0:T(8,128)(2,1)} %copy-done.17, bf16[8,48,384]{2,1,0:T(8,128)(2,1)} %copy-done.18, bf16[8,48,384]{2,1,0:T(8,128)(2,1)} %copy-done.6, bf16[8,48,384]{2,1,0:T(8,128)(2,1)} %copy-done.19, bf16[8,48,384]{2,1,0:T(8,128)(2,1)} %copy-done.20, bf16[288,384]{1,0:T(8,128)(2,1)} %bitcast.115, ...), custom_call_target="tpu_custom_call" | custom-call | tf_op jit(solution)/shard_map/decode/pallas_call | solution.py:303
  123.6 1.0 constant_dynamic-slice_fusion
  124.5 2.3 %collective-permute-start.9 = (bf16[4,4,16,384]{3,2,1,0:T(8,128)(2,1)S(1)}, bf16[4,4,16,384]{3,2,1,0:T(8,128)(2,1)S(1)}, u32[]{:S(2)}, u32[]{:S(2)}) collective-permute-start(bf16[4,4,16,384]{3,2,1,0:T(8,128)(2,1)S(1)} %constant_dynamic-slice_fusion), channel_id=1, source_target_pairs={{0,16},{16,0},{1,17},{17,1},{2,18},{18,2},{3,19},{19,3},{4,20},{20... | collective-permute-start | bytes 589832 | tf_op jit(solution)/shard_map/ppermute | solution.py:16
  126.9 1.1 collective-permute-done.9
  127.9 1.0 broadcast_select_fusion.1
  129.0 1.1 reshape.122
  (124 shorter events, 14.0 us)
Async XLA Ops:
  3.3 5.2 %copy-start.7 = (bf16[2,10,32,384]{3,2,1,0:T(8,128)(2,1)}, bf16[2,10,32,384]{3,2,1,0:T(8,128)(2,1)S(1)}, u32[]{:S(2)}) copy-start(bf16[2,10,32,384]{3,2,1,0:T(8,128)(2,1)S(1)} %constant_dynamic-update-slice_fusion) | copy-start | bytes 1474564
  4.1 43.2 %collective-permute-start.6 = (bf16[2,10,4,384]{3,2,1,0:T(4,128)(2,1)}, bf16[2,10,4,384]{3,2,1,0:T(4,128)(2,1)}, u32[]{:S(2)}, u32[]{:S(2)}) collective-permute-start(bf16[2,10,4,384]{3,2,1,0:T(4,128)(2,1)} %slice_select_fusion), channel_id=1, source_target_pairs={{0,1},{1,0},{2,3},{3,2},{4,5},{5,4},{6,7},{7,6},{8,9},{9,8},{10,11... | collective-permute-start | bytes 184328 | tf_op jit(solution)/shard_map/ppermute | solution.py:16
  7.5 41.1 %collective-permute-start = (bf16[2,2,24,384]{3,2,1,0:T(8,128)(2,1)}, bf16[2,2,24,384]{3,2,1,0:T(8,128)(2,1)}, u32[]{:S(2)}, u32[]{:S(2)}) collective-permute-start(bf16[2,2,24,384]{3,2,1,0:T(8,128)(2,1)} %pad_maximum_fusion.13), channel_id=1, source_target_pairs={{0,16},{16,0},{1,17},{17,1},{2,18},{18,2},{3,19},{19,3},{4,20},{20... | collective-permute-start | bytes 221192 | tf_op jit(solution)/shard_map/ppermute | solution.py:16
  22.6 4.5 %copy-start.31 = (f32[192]{0:T(256)S(1)}, f32[192]{0:T(256)}, u32[]{:S(2)}) copy-start(f32[192]{0:T(256)} %param.24) | copy-start | bytes 2308
  22.6 4.5 %copy-start.32 = (f32[192]{0:T(256)S(1)}, f32[192]{0:T(256)}, u32[]{:S(2)}) copy-start(f32[192]{0:T(256)} %param.25) | copy-start | bytes 2308
  22.7 4.6 %copy-start.29 = (f32[384]{0:T(512)S(1)}, f32[384]{0:T(512)}, u32[]{:S(2)}) copy-start(f32[384]{0:T(512)} %param.22) | copy-start | bytes 4612
  22.7 4.6 %copy-start.30 = (f32[384]{0:T(512)S(1)}, f32[384]{0:T(512)}, u32[]{:S(2)}) copy-start(f32[384]{0:T(512)} %param.23) | copy-start | bytes 4612
  22.7 4.6 %copy-start.27 = (bf16[2,1,64,384]{3,2,1,0:T(8,128)(2,1)S(1)}, bf16[2,1,64,384]{3,2,1,0:T(8,128)(2,1)}, u32[]{:S(2)}) copy-start(bf16[2,1,64,384]{3,2,1,0:T(8,128)(2,1)} %param.17) | copy-start | bytes 294916
  22.7 4.6 %copy-start.28 = (bf16[2,1,64,384]{3,2,1,0:T(8,128)(2,1)S(1)}, bf16[2,1,64,384]{3,2,1,0:T(8,128)(2,1)}, u32[]{:S(2)}) copy-start(bf16[2,1,64,384]{3,2,1,0:T(8,128)(2,1)} %param.18) | copy-start | bytes 294916
  34.6 2.5 %copy-start.1 = (bf16[9,192,192]{2,1,0:T(8,128)(2,1)S(1)}, bf16[9,192,192]{2,1,0:T(8,128)(2,1)}, u32[]{:S(2)}) copy-start(bf16[9,192,192]{2,1,0:T(8,128)(2,1)} %get-tuple-element.14) | copy-start | bytes 1990660
  34.6 2.5 %copy-start.2 = (bf16[9,192,192]{2,1,0:T(8,128)(2,1)S(1)}, bf16[9,192,192]{2,1,0:T(8,128)(2,1)}, u32[]{:S(2)}) copy-start(bf16[9,192,192]{2,1,0:T(8,128)(2,1)} %get-tuple-element.15) | copy-start | bytes 1990660
  34.6 2.5 %copy-start.3 = (bf16[9,192,192]{2,1,0:T(8,128)(2,1)S(1)}, bf16[9,192,192]{2,1,0:T(8,128)(2,1)}, u32[]{:S(2)}) copy-start(bf16[9,192,192]{2,1,0:T(8,128)(2,1)} %get-tuple-element.68) | copy-start | bytes 1990660
  34.6 2.8 %copy-start.4 = (bf16[9,192,192]{2,1,0:T(8,128)(2,1)S(1)}, bf16[9,192,192]{2,1,0:T(8,128)(2,1)}, u32[]{:S(2)}) copy-start(bf16[9,192,192]{2,1,0:T(8,128)(2,1)} %get-tuple-element.69) | copy-start | bytes 1990660
  34.6 3.1 %copy-start.5 = (bf16[9,192,192]{2,1,0:T(8,128)(2,1)S(1)}, bf16[9,192,192]{2,1,0:T(8,128)(2,1)}, u32[]{:S(2)}) copy-start(bf16[9,192,192]{2,1,0:T(8,128)(2,1)} %get-tuple-element.70) | copy-start | bytes 1990660
  37.7 9.6 %copy-start.33 = (pred[192]{0:T(512)(128)(4,1)S(1)}, pred[192]{0:T(512)(128)(4,1)}, u32[]{:S(2)}) copy-start(pred[192]{0:T(512)(128)(4,1)} %and.65) | copy-start | bytes 580
  37.7 9.6 %copy-start.34 = (pred[192]{0:T(512)(128)(4,1)S(1)}, pred[192]{0:T(512)(128)(4,1)}, u32[]{:S(2)}) copy-start(pred[192]{0:T(512)(128)(4,1)} %and.69) | copy-start | bytes 580
  37.7 10.6 %copy-start.8 = (bf16[2,10,32,384]{3,2,1,0:T(8,128)(2,1)S(1)}, bf16[2,10,32,384]{3,2,1,0:T(8,128)(2,1)}, u32[]{:S(2)}) copy-start(bf16[2,10,32,384]{3,2,1,0:T(8,128)(2,1)} %copy-done.7) | copy-start | bytes 1474564
  37.7 11.0 %copy-start.21 = (bf16[1,2,24,384]{3,2,1,0:T(8,128)(2,1)S(1)}, bf16[1,2,24,384]{3,2,1,0:T(8,128)(2,1)}, u32[]{:S(2)}) copy-start(bf16[1,2,24,384]{3,2,1,0:T(8,128)(2,1)} %get-tuple-element.48) | copy-start | bytes 110596
  37.7 11.0 %copy-start.22 = (bf16[1,2,24,384]{3,2,1,0:T(8,128)(2,1)S(1)}, bf16[1,2,24,384]{3,2,1,0:T(8,128)(2,1)}, u32[]{:S(2)}) copy-start(bf16[1,2,24,384]{3,2,1,0:T(8,128)(2,1)} %get-tuple-element.49) | copy-start | bytes 110596
  47.2 2.4 %copy-start.24 = (bf16[1,2,24,384]{3,2,1,0:T(8,128)(2,1)S(1)}, bf16[1,2,24,384]{3,2,1,0:T(8,128)(2,1)}, u32[]{:S(2)}) copy-start(bf16[1,2,24,384]{3,2,1,0:T(8,128)(2,1)} %get-tuple-element.53) | copy-start | bytes 110596
  47.2 2.4 %copy-start.25 = (bf16[1,2,24,384]{3,2,1,0:T(8,128)(2,1)S(1)}, bf16[1,2,24,384]{3,2,1,0:T(8,128)(2,1)}, u32[]{:S(2)}) copy-start(bf16[1,2,24,384]{3,2,1,0:T(8,128)(2,1)} %get-tuple-element.62) | copy-start | bytes 110596
  49.7 6.6 %collective-permute-start.1 = (bf16[8,24,384]{2,1,0:T(8,128)(2,1)S(1)}, bf16[8,24,384]{2,1,0:T(8,128)(2,1)S(1)}, u32[]{:S(2)}, u32[]{:S(2)}) collective-permute-start(bf16[8,24,384]{2,1,0:T(8,128)(2,1)S(1)} %dynamic-slice_bitcast_fusion), channel_id=1, source_target_pairs={{0,1},{1,0},{2,3},{3,2},{4,5},{5,4},{6,7},{7,6},{8,9},{9,8},{10,11... | collective-permute-start | bytes 442376 | tf_op jit(solution)/shard_map/ppermute | solution.py:16
  50.1 15.7 %collective-permute-start.7 = (bf16[2,5,24,384]{3,2,1,0:T(8,128)(2,1)S(1)}, bf16[2,5,24,384]{3,2,1,0:T(8,128)(2,1)S(1)}, u32[]{:S(2)}, u32[]{:S(2)}) collective-permute-start(bf16[2,5,24,384]{3,2,1,0:T(8,128)(2,1)S(1)} %pad_maximum_fusion.10), channel_id=1, source_target_pairs={{0,2},{2,4},{4,6},{6,8},{8,10},{10,12},{12,14},{1,3},{3,5},{5,7},{... | collective-permute-start | bytes 552968 | tf_op jit(solution)/shard_map/ppermute | solution.py:22
  53.3 14.7 %collective-permute-start.8 = (bf16[2,5,24,384]{3,2,1,0:T(8,128)(2,1)S(1)}, bf16[2,5,24,384]{3,2,1,0:T(8,128)(2,1)S(1)}, u32[]{:S(2)}, u32[]{:S(2)}) collective-permute-start(bf16[2,5,24,384]{3,2,1,0:T(8,128)(2,1)S(1)} %pad_maximum_fusion.11), channel_id=1, source_target_pairs={{2,0},{4,2},{6,4},{8,6},{10,8},{12,10},{14,12},{3,1},{5,3},{7,5},{... | collective-permute-start | bytes 552968 | tf_op jit(solution)/shard_map/ppermute | solution.py:22
  56.4 23.5 %copy-start.6 = (bf16[8,48,384]{2,1,0:T(8,128)(2,1)}, bf16[8,48,384]{2,1,0:T(8,128)(2,1)S(1)}, u32[]{:S(2)}) copy-start(bf16[8,48,384]{2,1,0:T(8,128)(2,1)S(1)} %pad_maximum_fusion.6.own) | copy-start | bytes 884740
  56.4 13.8 %collective-permute-start.2 = (bf16[8,48,384]{2,1,0:T(8,128)(2,1)S(1)}, bf16[8,48,384]{2,1,0:T(8,128)(2,1)S(1)}, u32[]{:S(2)}, u32[]{:S(2)}) collective-permute-start(bf16[8,48,384]{2,1,0:T(8,128)(2,1)S(1)} %pad_maximum_fusion.6.own), channel_id=1, source_target_pairs={{0,4},{2,6},{4,8},{6,10},{8,12},{10,14},{1,5},{3,7},{5,9},{7,11},{... | collective-permute-start | bytes 884744 | tf_op jit(solution)/shard_map/ppermute | solution.py:22
  59.6 12.8 %collective-permute-start.3 = (bf16[8,48,384]{2,1,0:T(8,128)(2,1)S(1)}, bf16[8,48,384]{2,1,0:T(8,128)(2,1)S(1)}, u32[]{:S(2)}, u32[]{:S(2)}) collective-permute-start(bf16[8,48,384]{2,1,0:T(8,128)(2,1)S(1)} %pad_maximum_fusion.6.own), channel_id=1, source_target_pairs={{0,2},{2,4},{4,6},{6,8},{8,10},{10,12},{12,14},{1,3},{3,5},{5,7},{... | collective-permute-start | bytes 884744 | tf_op jit(solution)/shard_map/ppermute | solution.py:22
  61.9 16.5 %collective-permute-start.4 = (bf16[8,48,384]{2,1,0:T(8,128)(2,1)S(1)}, bf16[8,48,384]{2,1,0:T(8,128)(2,1)S(1)}, u32[]{:S(2)}, u32[]{:S(2)}) collective-permute-start(bf16[8,48,384]{2,1,0:T(8,128)(2,1)S(1)} %pad_maximum_fusion.6.own), channel_id=1, source_target_pairs={{2,0},{4,2},{6,4},{8,6},{10,8},{12,10},{14,12},{3,1},{5,3},{7,5},{... | collective-permute-start | bytes 884744 | tf_op jit(solution)/shard_map/ppermute | solution.py:22
  65.9 13.3 %collective-permute-start.5 = (bf16[8,48,384]{2,1,0:T(8,128)(2,1)S(1)}, bf16[8,48,384]{2,1,0:T(8,128)(2,1)S(1)}, u32[]{:S(2)}, u32[]{:S(2)}) collective-permute-start(bf16[8,48,384]{2,1,0:T(8,128)(2,1)S(1)} %pad_maximum_fusion.6.own), channel_id=1, source_target_pairs={{4,0},{6,2},{8,4},{10,6},{12,8},{14,10},{5,1},{7,3},{9,5},{11,7},{... | collective-permute-start | bytes 884744 | tf_op jit(solution)/shard_map/ppermute | solution.py:22
  70.2 9.7 %copy-start.17 = (bf16[8,48,384]{2,1,0:T(8,128)(2,1)}, bf16[8,48,384]{2,1,0:T(8,128)(2,1)S(1)}, u32[]{:S(2)}) copy-start(bf16[8,48,384]{2,1,0:T(8,128)(2,1)S(1)} %collective-permute-done.2.low2) | copy-start | bytes 884740
  72.4 7.5 %copy-start.18 = (bf16[8,48,384]{2,1,0:T(8,128)(2,1)}, bf16[8,48,384]{2,1,0:T(8,128)(2,1)S(1)}, u32[]{:S(2)}) copy-start(bf16[8,48,384]{2,1,0:T(8,128)(2,1)S(1)} %collective-permute-done.3.low1) | copy-start | bytes 884740
  124.5 3.4 %collective-permute-start.9 = (bf16[4,4,16,384]{3,2,1,0:T(8,128)(2,1)S(1)}, bf16[4,4,16,384]{3,2,1,0:T(8,128)(2,1)S(1)}, u32[]{:S(2)}, u32[]{:S(2)}) collective-permute-start(bf16[4,4,16,384]{3,2,1,0:T(8,128)(2,1)S(1)} %constant_dynamic-slice_fusion), channel_id=1, source_target_pairs={{0,16},{16,0},{1,17},{17,1},{2,18},{18,2},{3,19},{19,3},{4,20},{20... | collective-permute-start | bytes 589832 | tf_op jit(solution)/shard_map/ppermute | solution.py:16
  (13 other events, 26.2 us)
where the time goes:
time: 132 us; the launch traced here: 130 us
  Pallas kernels  43.6 us (33%)
  local copies, waits for them, and re-layouts  28.7 us (22%)
  other arithmetic  24.6 us (19%)
  starting transfers between devices  22.5 us (17%)
  waiting for transfers between devices  10 us (8%)
    pallas_call x1, Pallas kernels, decode(): pl.pallas_call(functools.partial(decode_kernel, wide), out_shape=jax.Shap...  43.6 us
    ppermute x6, starting transfers between devices, shifted(): lax.ppermute(value, axis, [(source, source + steps) for source in range(i...  17.7 us
    unnamed x74, local copies, waits for them, and re-layouts  9.85 us
    concatenate x1, other arithmetic, pair_weights(): return jnp.concatenate([even, odd], axis=1)  9.53 us
    ppermute x6, waiting for transfers between devices, shifted(): lax.ppermute(value, axis, [(source, source + steps) for source in range(i...  8.92 us
    ppermute x4, starting transfers between devices, swapped(): return lax.ppermute(value, axis, [(0, 1), (1, 0)])  4.84 us
    another operation x3, other arithmetic, enlarge_weights(): return jnp.stack(parts).astype(jnp.bfloat16)  4.37 us
    squeeze x1, local copies, waits for them, and re-layouts, pair_weights(): even = jnp.concatenate([taps[:, 1], taps[:, 0], none, taps[:, 2]], axis=-1)  3.82 us
  transfers between devices with their start and end apart: 10, of which 4 were waited for; matrix products, arithmetic and copies ran while one was open for 34% of the time, Pallas kernels for 0%

commit v1 on v0

v1 whole, which is shorter than its diff:
```python
import functools

import jax
import jax.numpy as jnp
from jax import lax
from jax.experimental import pallas as pl
from jax.experimental.pallas import tpu as pltpu
from jax.sharding import PartitionSpec as P

EPSILON = 1e-06
HALO = 4
LANES = 256
BF16 = jnp.bfloat16
F32 = jnp.float32


def swapped(value, axis):
    return lax.ppermute(value, axis, [(0, 1), (1, 0)])


def shifted(value, axis, steps):
    count = lax.axis_size(axis)
    initial, last = (max(0, -steps), min(count, count - steps))
    return lax.ppermute(value, axis, [(source, source + steps) for source in range(initial, last)])


def silu(scaled):
    half = scaled * 0.5
    return half * (1.0 + jnp.tanh(half))


def activate(values, gain, mask):
    mean = jnp.mean(values * values, axis=-1, keepdims=True)
    return silu(values * (lax.rsqrt(mean + EPSILON) * mask) * gain)


def activate_pairs(values, gain, mask):
    channels = values.shape[-1] // 2
    squares = values * values
    first = lax.broadcasted_iota(jnp.int32, (1, 2 * channels), 1) < channels
    total = jnp.sum(squares, axis=-1, keepdims=True)
    low = jnp.sum(jnp.where(first, squares, 0.0), axis=-1, keepdims=True)
    scale_low = lax.rsqrt(low / channels + EPSILON) * mask
    scale_high = lax.rsqrt((total - low) / channels + EPSILON) * mask
    return silu(values * jnp.where(first, scale_low, scale_high) * gain)


def merge(even, odd, channels):
    turned = pltpu.roll(odd, channels - 128, 1)
    first = lax.broadcasted_iota(jnp.int32, (1, 128), 1) < channels - 128
    middle = jnp.where(first, even[:, 128:], turned[:, :128])
    return jnp.concatenate([even[:, :128], middle, turned[:, 128:]], axis=1)


def aligned(index, size):
    return pl.multiple_of(index * size, 16)


def line_mask(place, wide, first, count, limit, width):
    columns = place[2] + lax.broadcasted_iota(jnp.int32, (wide, 1), 0)
    inside = jnp.where((columns >= 0) & (columns < width), 1.0, 0.0)
    lines = []
    for i in range(count):
        line = first + i
        lines.append(inside * jnp.where((line >= 0) & (line < limit), 1.0, 0.0))
    return jnp.concatenate(lines, axis=0)


def store(even, odd, slot, values, height, wide):
    even[pl.ds(slot * (height * wide), height * wide), :] = values.astype(BF16)
    odd[pl.ds(slot * ((height - 2) * wide), (height - 2) * wide), :] = values[
        wide : (height - 1) * wide
    ].astype(BF16)


def taps(even, odd, begin, count, height, wide, dt, dy, lanes=slice(None)):
    inner = (height - 2) * wide
    if dy == 1:
        parts = [odd[pl.ds((begin + f + dt) * inner, inner), lanes] for f in range(count)]
    else:
        parts = [
            even[pl.ds((begin + f + dt) * height * wide + dy * wide, inner), lanes]
            for f in range(count)
        ]
    return jnp.concatenate(parts, axis=0)


def low_product(acc, even, odd, count, height, wide, weights):
    rows = count * (height - 2) * wide
    channels = weights.shape[1]

    def column(n, carry):
        lanes = pl.ds(pl.multiple_of(n * LANES, LANES), LANES)
        total = None
        for first, last in ((0, 4), (4, 8), (8, 9)):
            left = jnp.concatenate(
                [
                    taps(even, odd, 0, count, height, wide, t // 3, t % 3)
                    for t in range(first, last)
                ],
                axis=1,
            )
            right = weights[first:last, :, lanes].reshape((last - first) * channels, LANES)
            part = jnp.dot(left, right, preferred_element_type=F32)
            total = part if total is None else total + part
        acc[n, 0:rows, :] = total
        return carry

    lax.fori_loop(0, weights.shape[-1] // LANES, column, 0)


def low_sum(acc, start, size):
    rows = pl.ds(start, size)
    before = jnp.concatenate([acc[0, rows, :], acc[1, rows, 0:128]], axis=1)
    center = jnp.concatenate([acc[1, rows, 128:256], acc[2, rows, :]], axis=1)
    after = jnp.concatenate([acc[3, rows, :], acc[4, rows, 0:128]], axis=1)
    return center + pltpu.roll(before, 1, 0) + pltpu.roll(after, size - 1, 0)


def high_product(acc, even, odd, count, height, wide, weights, sides):
    rows = count * (height - 2) * wide
    channels = weights.shape[-1]

    def center(o, carry):
        total = None
        for first, last in ((0, 4), (4, 8), (8, 9)):
            left = jnp.concatenate(
                [
                    taps(even, odd, 0, count, height, wide, t // 3, t % 3)
                    for t in range(first, last)
                ],
                axis=1,
            )
            begin = pl.multiple_of((1 - o) * channels, 16)
            right = weights[first:last, pl.ds(begin, 2 * channels), :]
            right = right.reshape((last - first) * 2 * channels, channels)
            part = jnp.dot(left, right, preferred_element_type=F32)
            total = part if total is None else total + part
        acc[o, 0:rows, 0:channels] = total
        return carry

    lax.fori_loop(0, 2, center, 0)

    def side(o, carry):
        lanes = pl.ds(pl.multiple_of((1 - o) * 128, 128), LANES)
        left = jnp.concatenate(
            [taps(even, odd, 0, count, height, wide, t // 3, t % 3, lanes) for t in range(9)],
            axis=1,
        )
        right = sides[o].reshape(9 * LANES, channels)
        acc[2 + o, 0:rows, 0:channels] = jnp.dot(left, right, preferred_element_type=F32)
        return carry

    lax.fori_loop(0, 2, side, 0)


def high_sum(acc, start, size, channels):
    rows = pl.ds(start, size)
    even = acc[0, rows, :] + pltpu.roll(acc[2, rows, :], 1, 0)
    odd = acc[1, rows, :] + pltpu.roll(acc[3, rows, :], size - 1, 0)
    return merge(even, odd, channels)


def pack_kernel(wide, tile, part, place, latent, arrived, one, two, mine, theirs, spread):
    section, col = place[0], place[1]
    width, channels = latent.shape[1:]
    empty = jnp.zeros((spread.shape[1] - width, channels), F32)

    def put(slot, values):
        spread[slot] = pltpu.roll(
            jnp.concatenate([values.astype(F32), empty], axis=0), HALO, 0
        )

    for i in range(2):
        put(2 * section + i, latent[i])
        put(2 * (1 - section) + i, arrived[i])
        put(4 + i, one[i])
        put(6 + i, two[i])
    for slot in range(8):
        for ref, which in ((mine, col), (theirs, 1 - col)):
            begin = pl.multiple_of(which * tile + section * part, 8)
            ref[slot] = spread[slot, pl.ds(begin, wide), :].astype(BF16)


def pack(place, latent, arrived, one, two, wide, tile, part):
    width, channels = latent.shape[1:]
    vmem = pl.BlockSpec(memory_space=pltpu.VMEM)
    return pl.pallas_call(
        functools.partial(pack_kernel, wide, tile, part),
        out_shape=[jax.ShapeDtypeStruct((8, wide, channels), BF16)] * 2,
        in_specs=[pl.BlockSpec(memory_space=pltpu.SMEM)] + [vmem] * 4,
        out_specs=[vmem] * 2,
        scratch_shapes=[pltpu.VMEM((8, width + 16, channels), F32)],
        name="pack",
    )(place, latent, arrived, one, two)


def first_kernel(
    wide,
    sizes,
    place,
    low2,
    low1,
    own,
    high1,
    high2,
    gain_one,
    gain_two,
    weight_one,
    weight_two,
    out_ref,
    w1,
    w2,
    acc,
    x1e,
    x1o,
    x2e,
    x2o,
    sems,
):
    channels = own.shape[-1]
    frames = own.shape[1] - 4
    height, width = sizes
    col, row = place[1], place[3]
    pieces = (low2, low1, own, high1, high2)

    def load(source, target, base):
        return [
            pltpu.make_async_copy(
                source.at[:, dx], target.at[:, :, pl.ds(dx * channels, channels)], sems.at[base + dx]
            )
            for dx in range(3)
        ]

    copies_one = load(weight_one, w1, 0)
    copies_two = load(weight_two, w2, 3)
    for copy in copies_one:
        copy.start()

    def rows_of(refs, index):
        return jnp.concatenate(
            [ref[lax.rem(y + col, 2), index].astype(F32) for ref in refs for y in range(2)], axis=0
        )

    for f in range(2):
        store(x1e, x1o, f, rows_of(pieces, frames + f), 10, wide)
        store(x2e, x2o, f, rows_of(pieces, frames + 2 + f)[wide : 9 * wide], 8, wide)

    def norm_one(f, carry):
        values = activate(rows_of(pieces, f), gain_one[...], 1.0)
        store(x1e, x1o, f + 2, values, 10, wide)
        return carry

    lax.fori_loop(0, frames, norm_one, 0)
    for copy in copies_one:
        copy.wait()
    for copy in copies_two:
        copy.start()
    low_product(acc, x1e, x1o, frames, 10, wide, w1)

    mask = line_mask(place, wide, 2 * row - 3, 8, height, width)

    def norm_two(f, carry):
        size = 8 * wide
        values = activate(low_sum(acc, aligned(f, size), size), gain_two[...], mask)
        store(x2e, x2o, f + 2, values, 8, wide)
        return carry

    lax.fori_loop(0, frames, norm_two, 0)
    for copy in copies_two:
        copy.wait()
    low_product(acc, x2e, x2o, frames, 8, wide, w2)

    def residual(f, carry):
        size = 6 * wide
        values = low_sum(acc, aligned(f, size), size) + rows_of(pieces[1:4], f)
        out_ref[pl.ds(aligned(f, size), size), :] = values.astype(BF16)
        return carry

    lax.fori_loop(0, frames, residual, 0)


def planes(slots, height, wide, channels):
    return [
        pltpu.VMEM((slots * height * wide, channels), BF16),
        pltpu.VMEM((slots * (height - 2) * wide, channels), BF16),
    ]


def first_block(place, pieces, gain_one, gain_two, weight_one, weight_two, sizes):
    _, units, wide, channels = pieces[0].shape
    frames = units - 4
    slots = -(-3 * channels // LANES)
    vmem = pl.BlockSpec(memory_space=pltpu.VMEM)
    anywhere = pl.BlockSpec(memory_space=pl.ANY)
    return pl.pallas_call(
        functools.partial(first_kernel, wide, sizes),
        out_shape=jax.ShapeDtypeStruct((frames * 6 * wide, channels), BF16),
        in_specs=[pl.BlockSpec(memory_space=pltpu.SMEM)] + [vmem] * 7 + [anywhere] * 2,
        out_specs=vmem,
        scratch_shapes=[
            pltpu.VMEM((9, channels, slots * LANES), BF16),
            pltpu.VMEM((9, channels, slots * LANES), BF16),
            pltpu.VMEM((slots, frames * 8 * wide, LANES), F32),
            *planes(frames + 2, 10, wide, channels),
            *planes(frames + 2, 8, wide, channels),
            pltpu.SemaphoreType.DMA((6,)),
        ],
        compiler_params=pltpu.CompilerParams(vmem_limit_bytes=48 * 1024 * 1024),
        cost_estimate=pl.CostEstimate(
            flops=2 * 27 * channels * channels * frames * 14 * wide,
            bytes_accessed=2 * 54 * channels * channels,
            transcendentals=0,
        ),
        name="first_block",
    )(place, *pieces, gain_one, gain_two, weight_one, weight_two)


def second_kernel(
    wide,
    sizes,
    place,
    blocked,
    time_ref,
    three_ref,
    four_ref,
    gain_three,
    gain_four,
    weight_time,
    weight_up,
    weight_three,
    weight_four,
    out_ref,
    wt,
    wr,
    wu,
    w3,
    s3,
    w4,
    s4,
    acc,
    mixed,
    de,
    do,
    x3e,
    x3o,
    x4e,
    x4o,
    lifted_ref,
    sems,
):
    channels = blocked.shape[-1]
    half = channels // 2
    size = 6 * wide
    frames = blocked.shape[0] // size
    count = 2 * frames
    height, width = sizes
    row = place[3]

    def load_high(source, target, sides, base):
        blank = LANES - half
        return [
            pltpu.make_async_copy(source, target, sems.at[base]),
            pltpu.make_async_copy(
                source.at[:, pl.ds(0, half), :],
                sides.at[0, :, pl.ds(blank, half), :],
                sems.at[base + 1],
            ),
            pltpu.make_async_copy(
                source.at[:, pl.ds(2 * half, half), :],
                sides.at[1, :, pl.ds(0, half), :],
                sems.at[base + 2],
            ),
        ]

    copy_time = pltpu.make_async_copy(weight_time, wt, sems.at[0])
    copy_up = pltpu.make_async_copy(weight_up, wr, sems.at[1])
    copies_three = load_high(weight_three, w3, s3, 2)
    copies_four = load_high(weight_four, w4, s4, 5)
    copy_time.start()
    copy_up.start()
    for copy in copies_three + copies_four:
        copy.start()

    blank = jnp.zeros((9, LANES - half, half), BF16)
    for sides in (s3, s4):
        sides[0, :, 0 : LANES - half, :] = blank
        sides[1, :, half:LANES, :] = blank

    mixed[0 : 2 * size, :] = time_ref[...]
    mixed[2 * size : (frames + 2) * size, :] = blocked[...]
    copy_time.wait()

    def mix(n, carry):
        lanes = pl.ds(pl.multiple_of(n * LANES, LANES), LANES)
        left = jnp.concatenate(
            [mixed[pl.ds(t * size, frames * size), :] for t in range(3)], axis=1
        )
        acc[n, 0 : frames * size, :] = jnp.dot(left, wt[:, lanes], preferred_element_type=F32)
        return carry

    lax.fori_loop(0, 2 * channels // LANES, mix, 0)
    mask_low = line_mask(place, wide, 2 * row - 2, 6, height, width)

    def double(t, carry):
        rows = pl.ds(aligned(t, size), size)
        first = jnp.concatenate([acc[0, rows, :], acc[1, rows, 0:128]], axis=1)
        second = jnp.concatenate([acc[1, rows, 128:256], acc[2, rows, :]], axis=1)
        store(de, do, 2 * t, first * mask_low, 6, wide)
        store(de, do, 2 * t + 1, second * mask_low, 6, wide)
        return carry

    lax.fori_loop(0, frames, double, 0)
    copy_up.wait()

    chunk = 16

    def combine(k, carry):
        rows = pl.ds(aligned(k, chunk), chunk)
        taken = [[wr[3 * dy + dx, rows, :].astype(F32) for dx in range(3)] for dy in range(3)]
        gap = jnp.zeros((chunk, LANES - half), F32)
        for slot, dys in enumerate(((0,), (1, 2), (0, 1), (2,))):
            line = [sum(taken[dy][dx] for dy in dys) for dx in range(3)]
            line = [jnp.concatenate([part, gap], axis=1) for part in line]
            into = pl.ds(aligned(k, chunk) + (slot % 2) * channels, chunk)
            wu[slot // 2, into, 0:channels] = merge(
                line[1] + line[2], line[0] + line[1], half
            ).astype(BF16)
            wu[slot // 2, into, channels : 2 * channels] = merge(line[0], line[2], half).astype(
                BF16
            )
        return carry

    lax.fori_loop(0, channels // chunk, combine, 0)

    for py in range(2):

        def enlarge(n, carry):
            lanes = pl.ds(pl.multiple_of(n * LANES, LANES), LANES)
            left = jnp.concatenate(
                [taps(de, do, 0, count, 6, wide, 0, py), taps(de, do, 0, count, 6, wide, 0, py + 1)],
                axis=1,
            )
            acc[n, py * count * 4 * wide : (py + 1) * count * 4 * wide, :] = jnp.dot(
                left, wu[py, :, lanes], preferred_element_type=F32
            )
            return carry

        lax.fori_loop(0, 2 * channels // LANES, enlarge, 0)

    for f in range(2):
        store(x3e, x3o, f, three_ref[f].astype(F32), 8, wide)
        store(x4e, x4o, f, four_ref[f].astype(F32), 6, wide)
    gain3 = jnp.concatenate([gain_three[...], gain_three[...]], axis=1)
    gain4 = jnp.concatenate([gain_four[...], gain_four[...]], axis=1)
    mask_three = line_mask(place, wide, 4 * row - 2, 8, 2 * height, width)
    first_half = lax.broadcasted_iota(jnp.int32, (1, channels), 1) < half
    part = 4 * wide

    def norm_three(f, carry):
        values = []
        for py in range(2):
            rows = pl.ds(pl.multiple_of(py * count * part + f * part, 16), part)
            center = jnp.concatenate([acc[0, rows, :], acc[1, rows, 0:128]], axis=1)
            side = jnp.concatenate([acc[1, rows, 128:256], acc[2, rows, :]], axis=1)
            side = jnp.where(first_half, pltpu.roll(side, 1, 0), pltpu.roll(side, part - 1, 0))
            values.append((center + side).astype(BF16).astype(F32))
        lifted = jnp.concatenate(
            [values[h % 2][(h // 2) * wide : (h // 2 + 1) * wide] for h in range(8)], axis=0
        )
        lifted_ref[pl.ds(aligned(f, part), part), :] = lifted[2 * wide : 6 * wide]
        store(x3e, x3o, f + 2, activate_pairs(lifted, gain3, mask_three), 8, wide)
        return carry

    lax.fori_loop(0, count, norm_three, 0)
    for copy in copies_three:
        copy.wait()
    high_product(acc, x3e, x3o, count, 8, wide, w3, s3)

    mask_four = mask_three[wide : 7 * wide]

    def norm_four(f, carry):
        values = high_sum(acc, aligned(f, size), size, half)
        store(x4e, x4o, f + 2, activate_pairs(values, gain4, mask_four), 6, wide)
        return carry

    lax.fori_loop(0, count, norm_four, 0)
    for copy in copies_four:
        copy.wait()
    high_product(acc, x4e, x4o, count, 6, wide, w4, s4)

    def finish(f, carry):
        start = aligned(f, part)
        values = high_sum(acc, start, part, half) + lifted_ref[pl.ds(start, part), :]
        values = pltpu.roll(values, part - HALO, 0)
        for y in range(4):
            inner = wide - 2 * HALO
            out_ref[f, y] = values[y * wide : y * wide + inner].astype(BF16)
        return carry

    lax.fori_loop(0, count, finish, 0)


def second_block(place, blocked, time, three, four, gains, weights, sizes, wide):
    channels = blocked.shape[-1]
    half = channels // 2
    frames = blocked.shape[0] // (6 * wide)
    count = 2 * frames
    weight_time, weight_up, weight_three, weight_four = weights
    vmem = pl.BlockSpec(memory_space=pltpu.VMEM)
    anywhere = pl.BlockSpec(memory_space=pl.ANY)
    return pl.pallas_call(
        functools.partial(second_kernel, wide, sizes),
        out_shape=jax.ShapeDtypeStruct((count, 4, wide - 2 * HALO, channels), BF16),
        in_specs=[pl.BlockSpec(memory_space=pltpu.SMEM)] + [vmem] * 6 + [anywhere] * 4,
        out_specs=vmem,
        scratch_shapes=[
            pltpu.VMEM(weight_time.shape, BF16),
            pltpu.VMEM(weight_up.shape, BF16),
            pltpu.VMEM((2, 2 * channels, 2 * channels), BF16),
            pltpu.VMEM(weight_three.shape, BF16),
            pltpu.VMEM((2, 9, LANES, half), BF16),
            pltpu.VMEM(weight_four.shape, BF16),
            pltpu.VMEM((2, 9, LANES, half), BF16),
            pltpu.VMEM((4, 2 * count * 4 * wide, LANES), F32),
            pltpu.VMEM(((frames + 2) * 6 * wide, channels), BF16),
            *planes(count, 6, wide, channels),
            *planes(count + 2, 8, wide, channels),
            *planes(count + 2, 6, wide, channels),
            pltpu.VMEM((count * 4 * wide, channels), F32),
            pltpu.SemaphoreType.DMA((8,)),
        ],
        compiler_params=pltpu.CompilerParams(vmem_limit_bytes=48 * 1024 * 1024),
        name="second_block",
    )(place, blocked, time, three, four, *gains, *weights)


def body(
    latent,
    cache_one,
    cache_two,
    cache_time,
    cache_three,
    cache_four,
    gain_one,
    gain_two,
    gain_three,
    gain_four,
    weight_one,
    weight_two,
    weight_time,
    weight_upsample,
    weight_three,
    weight_four,
):
    section, row, col = (lax.axis_index(name) for name in ("section", "rows", "cols"))
    sections, row_count, col_count = (lax.axis_size(name) for name in ("section", "rows", "cols"))
    width, channels = latent.shape[2:]
    tile = width // col_count
    part = tile // sections
    wide = part + 2 * HALO
    half = weight_three.shape[1]
    sizes = (2 * row_count, width)
    place = jnp.stack([section, col, col * tile + section * part - HALO, row]).astype(jnp.int32)

    latent = latent.reshape(latent.shape[0], width, channels)
    arrived = swapped(latent, "section")
    mine, theirs = pack(
        place, latent, arrived, cache_one[:, 0], cache_two[:, 0], wide, tile, part
    )
    theirs = swapped(theirs, "cols")
    own = jnp.stack([mine, theirs])
    pieces = [
        shifted(own, "rows", 2),
        shifted(own, "rows", 1),
        own,
        shifted(own, "rows", -1),
        shifted(own, "rows", -2),
    ]
    blocked = first_block(
        place,
        pieces,
        gain_one.reshape(1, -1),
        gain_two.reshape(1, -1),
        weight_one.reshape(9, 3, channels, channels),
        weight_two.reshape(9, 3, channels, channels),
        sizes,
    )

    def paired(array):
        return array.reshape(array.shape[0], array.shape[1], tile, channels)

    left = col == 0
    tiles = jnp.concatenate([cache_time, paired(cache_three), paired(cache_four)], axis=1)
    edge = jnp.where(left, tiles[:, :, tile - HALO :], tiles[:, :, :HALO])
    edge = swapped(edge, "cols")
    nothing = jnp.zeros_like(edge)
    tiles = jnp.concatenate(
        [jnp.where(left, nothing, edge), tiles, jnp.where(left, edge, nothing)], axis=2
    )
    tiles = lax.dynamic_slice_in_dim(tiles, section * part, wide, 2)
    time, three, four = tiles[:, 0:2], tiles[:, 2:6], tiles[:, 6:10]
    above = shifted(jnp.concatenate([time, three[:, 2:], four[:, 3:]], axis=1), "rows", 1)
    below = shifted(jnp.concatenate([time, three[:, :2], four[:, :1]], axis=1), "rows", -1)
    time = jnp.concatenate([above[:, 0:2], time, below[:, 0:2]], axis=1)
    three = jnp.concatenate([above[:, 2:4], three, below[:, 2:4]], axis=1)
    four = jnp.concatenate([above[:, 4:], four, below[:, 4:]], axis=1)

    frames = second_block(
        place,
        blocked,
        time.reshape(-1, channels),
        three.reshape(2, -1, channels),
        four.reshape(2, -1, channels),
        (gain_three.reshape(1, -1), gain_four.reshape(1, -1)),
        (
            weight_time,
            weight_upsample.reshape(9, channels, half),
            weight_three.reshape(9, 3 * half, half),
            weight_four.reshape(9, 3 * half, half),
        ),
        sizes,
        wide,
    )
    count = frames.shape[0] // sections
    given = lax.dynamic_slice_in_dim(frames, (1 - section) * count, count, 0)
    kept = lax.dynamic_slice_in_dim(frames, section * count, count, 0)
    arrived = swapped(given, "section")
    low = section == 0
    joined = jnp.concatenate(
        [jnp.where(low, kept, arrived), jnp.where(low, arrived, kept)], axis=2
    )
    return joined.reshape(count, 4, 2 * tile, half)


def solution(mesh):
    placed = (
        P("section", ("rows", "cols"), None, None),
        P(None, ("rows", "cols"), None, None),
        P(None, ("rows", "cols"), None, None),
        P(None, "rows", "cols", None),
        P(None, "rows", "cols", None),
        P(None, "rows", "cols", None),
    ) + (P(),) * 10
    return jax.shard_map(
        body,
        mesh=mesh,
        in_specs=placed,
        out_specs=P("section", "rows", "cols", None),
        check_vma=False,
    )
```

time: 132 us -> 104 us (0.79)
  other arithmetic: 24.6 us -> 3.26 us
  local copies, waits for them, and re-layouts: 28.7 us -> 14.8 us
  Pallas kernels: 43.6 us -> 49.7 us
  waiting for transfers between devices: 10 us -> 12 us
    concatenate x2 -> x0, other arithmetic: 9.56 us -> none  [the longest x1 9.53 us: pair_weights(): return jnp.concatenate([even, odd], axis=1)]
    another operation x8 -> x2, other arithmetic: 8.28 us -> 1.55 us  [the longest x1 0.95 us: body(): own = jnp.stack([mine, theirs])]
    pallas_call x1 -> x3, Pallas kernels: 43.6 us -> 49.7 us  [the longest x1 28.4 us: second_block(): pl.pallas_call(functools.partial(second_kernel, wide, sizes), out_shape=j...]
    another operation x12 -> x0, local copies, waits for them, and re-layouts: 5.15 us -> none
    squeeze x2 -> x0, local copies, waits for them, and re-layouts: 3.85 us -> none  [the longest x1 3.82 us: pair_weights(): even = jnp.concatenate([taps[:, 1], taps[:, 0], none, taps[:, 2]], axis=-1)]
    convert_element_type x1 -> x0, local copies, waits for them, and re-layouts: 2.52 us -> none  [enlarge_weights(): taps = weight.reshape(3, 3, -1, channels).astype(jnp.float32)]
    ppermute x6, waiting for transfers between devices: 8.92 us -> 10.9 us  [shifted(): lax.ppermute(value, axis, [(source, source + steps) for source in range(i...]
    select_n x2 -> x1, other arithmetic: 1.88 us -> 0.04 us  [body(): jnp.where(low, kept, arrived)]
  transfers between devices with their start and end apart: 10 -> 10, of which waited for: 4 -> 4; matrix products, arithmetic and copies ran while one was open for 34% -> 12% of each run, Pallas kernels for 0% -> 0%
where the time goes in v1:
time: 104 us; the launch traced here: 103 us
  Pallas kernels  49.7 us (48%)
  starting transfers between devices  22.5 us (22%)
  local copies, waits for them, and re-layouts  14.8 us (14%)
  waiting for transfers between devices  12 us (12%)
  other arithmetic  3.26 us (3%)
    pallas_call x1, Pallas kernels, second_block(): pl.pallas_call(functools.partial(second_kernel, wide, sizes), out_shape=j...  28.4 us
    pallas_call x1, Pallas kernels, first_block(): pl.pallas_call(functools.partial(first_kernel, wide, sizes), out_shape=ja...  19.5 us
    ppermute x6, starting transfers between devices, shifted(): lax.ppermute(value, axis, [(source, source + steps) for source in range(i...  17.7 us
    unnamed x25, local copies, waits for them, and re-layouts  11.2 us
    ppermute x6, waiting for transfers between devices, shifted(): lax.ppermute(value, axis, [(source, source + steps) for source in range(i...  10.9 us
    ppermute x4, starting transfers between devices, swapped(): return lax.ppermute(value, axis, [(0, 1), (1, 0)])  4.85 us
    reshape x2, local copies, waits for them, and re-layouts, paired(): return array.reshape(array.shape[0], array.shape[1], tile, channels)  2.33 us
  transfers between devices with their start and end apart: 10, of which 4 were waited for; matrix products, arithmetic and copies ran while one was open for 12% of the time, Pallas kernels for 0%

profile of v1, /device:TPU:9, one launch (start us, length us, event | category | flops | bytes accessed | tf_op | source)
XLA Modules:
  0.0 102.7 jit_solution(9504935766805084913)
XLA Ops:
  0.0 0.9 constant_dynamic-update-slice_fusion.2
  1.0 1.2 %reshape.53 = bf16[2,4,32,384]{3,2,1,0:T(8,128)(2,1)S(1)} reshape(bf16[2,4,64,192]{3,2,1,0:T(8,128)(2,1)} %param.20) | data formatting | bytes 393216 | tf_op jit(solution)/shard_map/reshape | solution.py:591
  2.1 1.2 %reshape.54 = bf16[2,4,32,384]{3,2,1,0:T(8,128)(2,1)S(1)} reshape(bf16[2,4,64,192]{3,2,1,0:T(8,128)(2,1)} %param.21) | data formatting | bytes 393216 | tf_op jit(solution)/shard_map/reshape | solution.py:591
  3.4 0.0 copy-start.5
  3.4 0.1 slice_select_fusion
  3.4 1.3 %collective-permute-start.6 = (bf16[2,10,4,384]{3,2,1,0:T(4,128)(2,1)S(1)}, bf16[2,10,4,384]{3,2,1,0:T(4,128)(2,1)S(1)}, u32[]{:S(2)}, u32[]{:S(2)}) collective-permute-start(bf16[2,10,4,384]{3,2,1,0:T(4,128)(2,1)S(1)} %slice_select_fusion), channel_id=1, source_target_pairs={{0,1},{1,0},{2,3},{3,2},{4,5},{5,4},{6,7},{7,6},{8,9},{9,8},{10,11... | collective-permute-start | bytes 184328 | tf_op jit(solution)/shard_map/ppermute | solution.py:18
  4.7 1.0 collective-permute-start
  5.7 4.3 %copy.18 = bf16[5184,192]{1,0:T(8,128)(2,1)} copy(bf16[5184,192]{0,1:T(8,128)(2,1)} %param.30) | data formatting | bytes 3981312 | tf_op args[14]
  10.0 4.4 %copy.19 = bf16[5184,192]{1,0:T(8,128)(2,1)} copy(bf16[5184,192]{0,1:T(8,128)(2,1)} %param.31) | data formatting | bytes 3981312 | tf_op args[15]
  14.4 0.9 copy.17
  15.3 0.6 pad_add_fusion.place
  15.9 0.0 collective-permute-done.6
  15.9 0.1 broadcast_select_fusion.2
  15.9 1.3 %fusion.1 = bf16[2,10,24,384]{3,2,1,0:T(8,128)(2,1)S(1)} fusion(s32[]{:T(128)S(6)} %select_n.42, bf16[2,10,4,384]{3,2,1,0:T(4,128)(2,1)S(1)} %get-tuple-element.23, bf16[2,10,32,384]{3,2,1,0:T(8,128)(2,1)} %copy-done.5, bf16[2,10,4,384]{3,2,1,0:T(4,128)(2,1)S(1)} %get-tuple-element.22), kind=kLoop, calls=%fused_computation.5 | loop fusion | flops 1105920 | bytes 983044 | tf_op jit(solution)/shard_map/concatenate | solution.py:598
  17.4 0.6 copy-done.7
  18.1 1.9 %pack.1 = (bf16[8,24,384]{2,1,0:T(8,128)(2,1)}, bf16[8,24,384]{2,1,0:T(8,128)(2,1)}) custom-call(s32[4]{0:T(128)} %pad_add_fusion.place, bf16[2,64,384]{2,1,0:T(8,128)(2,1)} %bitcast.35, bf16[2,64,384]{2,1,0:T(8,128)(2,1)} %copy-done.7, bf16[2,64,384]{2,1,0:T(8,128)(2,1)} %bitcast.37, bf16[2,64,384]{2,1,0:T(8,128)(2,1)} %bitcast.38), custom_call_target="tpu_custom_call" | custom-call | tf_op jit(solution)/shard_map/pack/pallas_call | solution.py:188
  19.9 0.3 collective-permute-start.1
  20.2 3.1 %collective-permute-start.7 = (bf16[2,5,24,384]{3,2,1,0:T(8,128)(2,1)S(1)}, bf16[2,5,24,384]{3,2,1,0:T(8,128)(2,1)S(1)}, u32[]{:S(2)}, u32[]{:S(2)}) collective-permute-start(bf16[2,5,24,384]{3,2,1,0:T(8,128)(2,1)S(1)} %pad_maximum_fusion.5), channel_id=1, source_target_pairs={{0,2},{2,4},{4,6},{6,8},{8,10},{10,12},{12,14},{1,3},{3,5},{5,7},{... | collective-permute-start | bytes 552968 | tf_op jit(solution)/shard_map/ppermute | solution.py:24
  23.4 3.0 %collective-permute-start.8 = (bf16[2,5,24,384]{3,2,1,0:T(8,128)(2,1)S(1)}, bf16[2,5,24,384]{3,2,1,0:T(8,128)(2,1)S(1)}, u32[]{:S(2)}, u32[]{:S(2)}) collective-permute-start(bf16[2,5,24,384]{3,2,1,0:T(8,128)(2,1)S(1)} %pad_maximum_fusion.6), channel_id=1, source_target_pairs={{2,0},{4,2},{6,4},{8,6},{10,8},{12,10},{14,12},{3,1},{5,3},{7,5},{... | collective-permute-start | bytes 552968 | tf_op jit(solution)/shard_map/ppermute | solution.py:24
  26.5 0.9 pad_maximum_fusion.1.own
  27.4 3.2 %collective-permute-start.2 = (bf16[2,8,24,384]{3,2,1,0:T(8,128)(2,1)S(1)}, bf16[2,8,24,384]{3,2,1,0:T(8,128)(2,1)S(1)}, u32[]{:S(2)}, u32[]{:S(2)}) collective-permute-start(bf16[2,8,24,384]{3,2,1,0:T(8,128)(2,1)S(1)} %pad_maximum_fusion.1.own), channel_id=1, source_target_pairs={{0,4},{2,6},{4,8},{6,10},{8,12},{10,14},{1,5},{3,7},{5,9},{7,11},{... | collective-permute-start | bytes 884744 | tf_op jit(solution)/shard_map/ppermute | solution.py:24
  30.6 2.3 %collective-permute-start.3 = (bf16[2,8,24,384]{3,2,1,0:T(8,128)(2,1)S(1)}, bf16[2,8,24,384]{3,2,1,0:T(8,128)(2,1)S(1)}, u32[]{:S(2)}, u32[]{:S(2)}) collective-permute-start(bf16[2,8,24,384]{3,2,1,0:T(8,128)(2,1)S(1)} %pad_maximum_fusion.1.own), channel_id=1, source_target_pairs={{0,2},{2,4},{4,6},{6,8},{8,10},{10,12},{12,14},{1,3},{3,5},{5,7},{... | collective-permute-start | bytes 884744 | tf_op jit(solution)/shard_map/ppermute | solution.py:24
  32.9 3.9 %collective-permute-start.4 = (bf16[2,8,24,384]{3,2,1,0:T(8,128)(2,1)S(1)}, bf16[2,8,24,384]{3,2,1,0:T(8,128)(2,1)S(1)}, u32[]{:S(2)}, u32[]{:S(2)}) collective-permute-start(bf16[2,8,24,384]{3,2,1,0:T(8,128)(2,1)S(1)} %pad_maximum_fusion.1.own), channel_id=1, source_target_pairs={{2,0},{4,2},{6,4},{8,6},{10,8},{12,10},{14,12},{3,1},{5,3},{7,5},{... | collective-permute-start | bytes 884744 | tf_op jit(solution)/shard_map/ppermute | solution.py:24
  36.8 2.1 %collective-permute-start.5 = (bf16[2,8,24,384]{3,2,1,0:T(8,128)(2,1)S(1)}, bf16[2,8,24,384]{3,2,1,0:T(8,128)(2,1)S(1)}, u32[]{:S(2)}, u32[]{:S(2)}) collective-permute-start(bf16[2,8,24,384]{3,2,1,0:T(8,128)(2,1)S(1)} %pad_maximum_fusion.1.own), channel_id=1, source_target_pairs={{4,0},{6,2},{8,4},{10,6},{12,8},{14,10},{5,1},{7,3},{9,5},{11,7},{... | collective-permute-start | bytes 884744 | tf_op jit(solution)/shard_map/ppermute | solution.py:24
  39.2 4.3 %collective-permute-done.3.low1 = bf16[2,8,24,384]{3,2,1,0:T(8,128)(2,1)S(1)} collective-permute-done((bf16[2,8,24,384]{3,2,1,0:T(8,128)(2,1)S(1)}, bf16[2,8,24,384]{3,2,1,0:T(8,128)(2,1)S(1)}, u32[]{:S(2)}, u32[]{:S(2)}) %collective-permute-start.3) | collective-permute-done | bytes 294944 | tf_op jit(solution)/shard_map/ppermute | solution.py:24
  43.5 5.9 %collective-permute-done.4.high1 = bf16[2,8,24,384]{3,2,1,0:T(8,128)(2,1)S(1)} collective-permute-done((bf16[2,8,24,384]{3,2,1,0:T(8,128)(2,1)S(1)}, bf16[2,8,24,384]{3,2,1,0:T(8,128)(2,1)S(1)}, u32[]{:S(2)}, u32[]{:S(2)}) %collective-permute-start.4) | collective-permute-done | bytes 294944 | tf_op jit(solution)/shard_map/ppermute | solution.py:24
  49.4 0.7 collective-permute-done.5.high2
  50.1 19.5 %first_block.1.blocked = bf16[576,384]{1,0:T(8,128)(2,1)S(1)} custom-call(s32[4]{0:T(128)S(1)} %copy-done.1, bf16[2,8,24,384]{3,2,1,0:T(8,128)(2,1)S(1)} %collective-permute-done.2.low2, bf16[2,8,24,384]{3,2,1,0:T(8,128)(2,1)S(1)} %collective-permute-done.3.low1, bf16[2,8,24,384]{3,2,1,0:T(8,128)(2,1)S(1)} %pad_maximum_fusion.1.own, ...), custom_call_target="tpu_custom_call" | custom-call | flops 10701766656 | bytes 15925248 | tf_op jit(solution)/shard_map/first_block/pallas_call | solution.py:296
  69.6 28.4 %second_block.1 = bf16[8,4,16,384]{3,2,1,0:T(8,128)(2,1)S(1)} custom-call(s32[4]{0:T(128)S(1)} %copy-done.1, bf16[576,384]{1,0:T(8,128)(2,1)S(1)} %first_block.1.blocked, bf16[288,384]{1,0:T(8,128)(2,1)S(1)} %bitcast.27, bf16[2,192,384]{2,1,0:T(8,128)(2,1)S(1)} %bitcast.26, bf16[2,144,384]{2,1,0:T(8,128)(2,1)S(1)} %bitcast.28, f32[1,192]{1,0:T(1,128)S(1)} %bitcast.29, ...), custom_call_target="tpu_custom_call" | custom-call | tf_op jit(solution)/shard_map/second_block/pallas_call | solution.py:512
  98.1 2.4 %collective-permute-start.9 = (bf16[4,4,16,384]{3,2,1,0:T(8,128)(2,1)S(1)}, bf16[4,4,16,384]{3,2,1,0:T(8,128)(2,1)S(1)}, u32[]{:S(2)}, u32[]{:S(2)}) collective-permute-start(bf16[4,4,16,384]{3,2,1,0:T(8,128)(2,1)S(1)} %constant_dynamic-slice_fusion), channel_id=1, source_target_pairs={{0,16},{16,0},{1,17},{17,1},{2,18},{18,2},{3,19},{19,3},{4,20},{20... | collective-permute-start | bytes 589832 | tf_op jit(solution)/shard_map/ppermute | solution.py:18
  100.4 1.1 %collective-permute-done.9 = bf16[4,4,16,384]{3,2,1,0:T(8,128)(2,1)S(1)} collective-permute-done((bf16[4,4,16,384]{3,2,1,0:T(8,128)(2,1)S(1)}, bf16[4,4,16,384]{3,2,1,0:T(8,128)(2,1)S(1)}, u32[]{:S(2)}, u32[]{:S(2)}) %collective-permute-start.9) | collective-permute-done | bytes 196640 | tf_op jit(solution)/shard_map/ppermute | solution.py:18
  101.6 1.1 %reshape.63 = bf16[4,4,64,192]{3,2,1,0:T(8,128)(2,1)} reshape(bf16[4,4,32,384]{3,2,1,0:T(8,128)(2,1)S(1)} %pad_maximum_fusion) | data formatting | bytes 786432 | tf_op jit(solution)/shard_map/reshape | solution.py:633
  (42 shorter events, 0.5 us)
Async XLA Ops:
  0.0 4.7 %copy-start.6 = (bf16[2,1,64,384]{3,2,1,0:T(8,128)(2,1)S(1)}, bf16[2,1,64,384]{3,2,1,0:T(8,128)(2,1)}, u32[]{:S(2)}) copy-start(bf16[2,1,64,384]{3,2,1,0:T(8,128)(2,1)} %param.16) | copy-start | bytes 294916
  0.0 5.7 %copy-start.8 = (f32[384]{0:T(512)S(1)}, f32[384]{0:T(512)}, u32[]{:S(2)}) copy-start(f32[384]{0:T(512)} %param.22) | copy-start | bytes 4612
  0.0 5.7 %copy-start.9 = (f32[384]{0:T(512)S(1)}, f32[384]{0:T(512)}, u32[]{:S(2)}) copy-start(f32[384]{0:T(512)} %param.23) | copy-start | bytes 4612
  3.4 6.6 %copy-start.5 = (bf16[2,10,32,384]{3,2,1,0:T(8,128)(2,1)}, bf16[2,10,32,384]{3,2,1,0:T(8,128)(2,1)S(1)}, u32[]{:S(2)}) copy-start(bf16[2,10,32,384]{3,2,1,0:T(8,128)(2,1)S(1)} %constant_dynamic-update-slice_fusion) | copy-start | bytes 1474564
  3.4 12.4 %collective-permute-start.6 = (bf16[2,10,4,384]{3,2,1,0:T(4,128)(2,1)S(1)}, bf16[2,10,4,384]{3,2,1,0:T(4,128)(2,1)S(1)}, u32[]{:S(2)}, u32[]{:S(2)}) collective-permute-start(bf16[2,10,4,384]{3,2,1,0:T(4,128)(2,1)S(1)} %slice_select_fusion), channel_id=1, source_target_pairs={{0,1},{1,0},{2,3},{3,2},{4,5},{5,4},{6,7},{7,6},{8,9},{9,8},{10,11... | collective-permute-start | bytes 184328 | tf_op jit(solution)/shard_map/ppermute | solution.py:18
  4.7 12.7 %collective-permute-start = (bf16[2,64,384]{2,1,0:T(8,128)(2,1)S(1)}, bf16[2,64,384]{2,1,0:T(8,128)(2,1)S(1)}, u32[]{:S(2)}, u32[]{:S(2)}) collective-permute-start(bf16[2,64,384]{2,1,0:T(8,128)(2,1)S(1)} %bitcast.36), channel_id=1, source_target_pairs={{0,16},{16,0},{1,17},{17,1},{2,18},{18,2},{3,19},{19,3},{4,20},{20... | collective-permute-start | bytes 294920 | tf_op jit(solution)/shard_map/ppermute | solution.py:18
  10.0 4.4 %copy-start.4 = (bf16[3456,192]{0,1:T(8,128)(2,1)S(1)}, bf16[3456,192]{0,1:T(8,128)(2,1)}, u32[]{:S(2)}) copy-start(bf16[3456,192]{0,1:T(8,128)(2,1)} %param.29) | copy-start | bytes 3981316
  17.4 32.7 %copy-start.1 = (s32[4]{0:T(128)S(1)}, s32[4]{0:T(128)}, u32[]{:S(2)}) copy-start(s32[4]{0:T(128)} %pad_add_fusion.place) | copy-start | bytes 52
  17.4 0.7 copy-start.7
  19.9 6.5 %collective-permute-start.1 = (bf16[8,24,384]{2,1,0:T(8,128)(2,1)}, bf16[8,24,384]{2,1,0:T(8,128)(2,1)S(1)}, u32[]{:S(2)}, u32[]{:S(2)}) collective-permute-start(bf16[8,24,384]{2,1,0:T(8,128)(2,1)} %get-tuple-element.8), channel_id=1, source_target_pairs={{0,1},{1,0},{2,3},{3,2},{4,5},{5,4},{6,7},{7,6},{8,9},{9,8},{10,11... | collective-permute-start | bytes 442376 | tf_op jit(solution)/shard_map/ppermute | solution.py:18
  20.2 16.6 %collective-permute-start.7 = (bf16[2,5,24,384]{3,2,1,0:T(8,128)(2,1)S(1)}, bf16[2,5,24,384]{3,2,1,0:T(8,128)(2,1)S(1)}, u32[]{:S(2)}, u32[]{:S(2)}) collective-permute-start(bf16[2,5,24,384]{3,2,1,0:T(8,128)(2,1)S(1)} %pad_maximum_fusion.5), channel_id=1, source_target_pairs={{0,2},{2,4},{4,6},{6,8},{8,10},{10,12},{12,14},{1,3},{3,5},{5,7},{... | collective-permute-start | bytes 552968 | tf_op jit(solution)/shard_map/ppermute | solution.py:24
  23.4 15.6 %collective-permute-start.8 = (bf16[2,5,24,384]{3,2,1,0:T(8,128)(2,1)S(1)}, bf16[2,5,24,384]{3,2,1,0:T(8,128)(2,1)S(1)}, u32[]{:S(2)}, u32[]{:S(2)}) collective-permute-start(bf16[2,5,24,384]{3,2,1,0:T(8,128)(2,1)S(1)} %pad_maximum_fusion.6), channel_id=1, source_target_pairs={{2,0},{4,2},{6,4},{8,6},{10,8},{12,10},{14,12},{3,1},{5,3},{7,5},{... | collective-permute-start | bytes 552968 | tf_op jit(solution)/shard_map/ppermute | solution.py:24
  27.4 11.8 %collective-permute-start.2 = (bf16[2,8,24,384]{3,2,1,0:T(8,128)(2,1)S(1)}, bf16[2,8,24,384]{3,2,1,0:T(8,128)(2,1)S(1)}, u32[]{:S(2)}, u32[]{:S(2)}) collective-permute-start(bf16[2,8,24,384]{3,2,1,0:T(8,128)(2,1)S(1)} %pad_maximum_fusion.1.own), channel_id=1, source_target_pairs={{0,4},{2,6},{4,8},{6,10},{8,12},{10,14},{1,5},{3,7},{5,9},{7,11},{... | collective-permute-start | bytes 884744 | tf_op jit(solution)/shard_map/ppermute | solution.py:24
  30.6 12.8 %collective-permute-start.3 = (bf16[2,8,24,384]{3,2,1,0:T(8,128)(2,1)S(1)}, bf16[2,8,24,384]{3,2,1,0:T(8,128)(2,1)S(1)}, u32[]{:S(2)}, u32[]{:S(2)}) collective-permute-start(bf16[2,8,24,384]{3,2,1,0:T(8,128)(2,1)S(1)} %pad_maximum_fusion.1.own), channel_id=1, source_target_pairs={{0,2},{2,4},{4,6},{6,8},{8,10},{10,12},{12,14},{1,3},{3,5},{5,7},{... | collective-permute-start | bytes 884744 | tf_op jit(solution)/shard_map/ppermute | solution.py:24
  32.9 16.5 %collective-permute-start.4 = (bf16[2,8,24,384]{3,2,1,0:T(8,128)(2,1)S(1)}, bf16[2,8,24,384]{3,2,1,0:T(8,128)(2,1)S(1)}, u32[]{:S(2)}, u32[]{:S(2)}) collective-permute-start(bf16[2,8,24,384]{3,2,1,0:T(8,128)(2,1)S(1)} %pad_maximum_fusion.1.own), channel_id=1, source_target_pairs={{2,0},{4,2},{6,4},{8,6},{10,8},{12,10},{14,12},{3,1},{5,3},{7,5},{... | collective-permute-start | bytes 884744 | tf_op jit(solution)/shard_map/ppermute | solution.py:24
  36.8 13.3 %collective-permute-start.5 = (bf16[2,8,24,384]{3,2,1,0:T(8,128)(2,1)S(1)}, bf16[2,8,24,384]{3,2,1,0:T(8,128)(2,1)S(1)}, u32[]{:S(2)}, u32[]{:S(2)}) collective-permute-start(bf16[2,8,24,384]{3,2,1,0:T(8,128)(2,1)S(1)} %pad_maximum_fusion.1.own), channel_id=1, source_target_pairs={{4,0},{6,2},{8,4},{10,6},{12,8},{14,10},{5,1},{7,3},{9,5},{11,7},{... | collective-permute-start | bytes 884744 | tf_op jit(solution)/shard_map/ppermute | solution.py:24
  50.1 19.5 %copy-start = (bf16[1152,768]{1,0:T(8,128)(2,1)S(1)}, bf16[1152,768]{1,0:T(8,128)(2,1)}, u32[]{:S(2)}) copy-start(bf16[1152,768]{1,0:T(8,128)(2,1)} %weight_time.1) | copy-start | bytes 5308420
  50.1 19.5 %copy-start.2 = (f32[192]{0:T(256)S(1)}, f32[192]{0:T(256)}, u32[]{:S(2)}) copy-start(f32[192]{0:T(256)} %param.24) | copy-start | bytes 2308
  50.1 19.5 %copy-start.3 = (f32[192]{0:T(256)S(1)}, f32[192]{0:T(256)}, u32[]{:S(2)}) copy-start(f32[192]{0:T(256)} %param.25) | copy-start | bytes 2308
  98.1 3.4 %collective-permute-start.9 = (bf16[4,4,16,384]{3,2,1,0:T(8,128)(2,1)S(1)}, bf16[4,4,16,384]{3,2,1,0:T(8,128)(2,1)S(1)}, u32[]{:S(2)}, u32[]{:S(2)}) collective-permute-start(bf16[4,4,16,384]{3,2,1,0:T(8,128)(2,1)S(1)} %constant_dynamic-slice_fusion), channel_id=1, source_target_pairs={{0,16},{16,0},{1,17},{17,1},{2,18},{18,2},{3,19},{19,3},{4,20},{20... | collective-permute-start | bytes 589832 | tf_op jit(solution)/shard_map/ppermute | solution.py:18

commit v2 on v1

--- a/solution.py
+++ b/solution.py
@@ -88,9 +88,9 @@
 def low_product(acc, even, odd, count, height, wide, weights):
     rows = count * (height - 2) * wide
     channels = weights.shape[1]
-
-    def column(n, carry):
-        lanes = pl.ds(pl.multiple_of(n * LANES, LANES), LANES)
+    lanes = 3 * channels
+    for n in range(-(-lanes // LANES)):
+        size = min(LANES, lanes - n * LANES)
         total = None
         for first, last in ((0, 4), (4, 8), (8, 9)):
             left = jnp.concatenate(
@@ -100,13 +100,20 @@
                 ],
                 axis=1,
             )
-            right = weights[first:last, :, lanes].reshape((last - first) * channels, LANES)
+            right = []
+            for t in range(first, last):
+                parts = []
+                for dx in range(3):
+                    begin = max(n * LANES - dx * channels, 0)
+                    end = min(n * LANES + size - dx * channels, channels)
+                    if begin < end:
+                        base = (3 * t + dx) * channels
+                        parts.append(weights[base : base + channels, begin:end])
+                right.append(jnp.concatenate(parts, axis=1))
+            right = jnp.concatenate(right, axis=0)
             part = jnp.dot(left, right, preferred_element_type=F32)
             total = part if total is None else total + part
-        acc[n, 0:rows, :] = total
-        return carry
-
-    lax.fori_loop(0, weights.shape[-1] // LANES, column, 0)
+        acc[n, 0:rows, 0:size] = total
 
 
 def low_sum(acc, start, size):
@@ -206,17 +213,14 @@
     high2,
     gain_one,
     gain_two,
-    weight_one,
-    weight_two,
-    out_ref,
     w1,
     w2,
+    out_ref,
     acc,
     x1e,
     x1o,
     x2e,
     x2o,
-    sems,
 ):
     channels = own.shape[-1]
     frames = own.shape[1] - 4
@@ -224,19 +228,6 @@
     col, row = place[1], place[3]
     pieces = (low2, low1, own, high1, high2)
 
-    def load(source, target, base):
-        return [
-            pltpu.make_async_copy(
-                source.at[:, dx], target.at[:, :, pl.ds(dx * channels, channels)], sems.at[base + dx]
-            )
-            for dx in range(3)
-        ]
-
-    copies_one = load(weight_one, w1, 0)
-    copies_two = load(weight_two, w2, 3)
-    for copy in copies_one:
-        copy.start()
-
     def rows_of(refs, index):
         return jnp.concatenate(
             [ref[lax.rem(y + col, 2), index].astype(F32) for ref in refs for y in range(2)], axis=0
@@ -252,10 +243,6 @@
         return carry
 
     lax.fori_loop(0, frames, norm_one, 0)
-    for copy in copies_one:
-        copy.wait()
-    for copy in copies_two:
-        copy.start()
     low_product(acc, x1e, x1o, frames, 10, wide, w1)
 
     mask = line_mask(place, wide, 2 * row - 3, 8, height, width)
@@ -267,8 +254,6 @@
         return carry
 
     lax.fori_loop(0, frames, norm_two, 0)
-    for copy in copies_two:
-        copy.wait()
     low_product(acc, x2e, x2o, frames, 8, wide, w2)
 
     def residual(f, carry):
@@ -292,21 +277,17 @@
     frames = units - 4
     slots = -(-3 * channels // LANES)
     vmem = pl.BlockSpec(memory_space=pltpu.VMEM)
-    anywhere = pl.BlockSpec(memory_space=pl.ANY)
     return pl.pallas_call(
         functools.partial(first_kernel, wide, sizes),
         out_shape=jax.ShapeDtypeStruct((frames * 6 * wide, channels), BF16),
-        in_specs=[pl.BlockSpec(memory_space=pltpu.SMEM)] + [vmem] * 7 + [anywhere] * 2,
+        in_specs=[pl.BlockSpec(memory_space=pltpu.SMEM)] + [vmem] * 9,
         out_specs=vmem,
         scratch_shapes=[
-            pltpu.VMEM((9, channels, slots * LANES), BF16),
-            pltpu.VMEM((9, channels, slots * LANES), BF16),
             pltpu.VMEM((slots, frames * 8 * wide, LANES), F32),
             *planes(frames + 2, 10, wide, channels),
             *planes(frames + 2, 8, wide, channels),
-            pltpu.SemaphoreType.DMA((6,)),
         ],
-        compiler_params=pltpu.CompilerParams(vmem_limit_bytes=48 * 1024 * 1024),
+        compiler_params=pltpu.CompilerParams(vmem_limit_bytes=16 * 1024 * 1024),
         cost_estimate=pl.CostEstimate(
             flops=2 * 27 * channels * channels * frames * 14 * wide,
             bytes_accessed=2 * 54 * channels * channels,
@@ -582,8 +563,8 @@
         pieces,
         gain_one.reshape(1, -1),
         gain_two.reshape(1, -1),
-        weight_one.reshape(9, 3, channels, channels),
-        weight_two.reshape(9, 3, channels, channels),
+        weight_one,
+        weight_two,
         sizes,
     )
 
@@ -591,9 +572,15 @@
         return array.reshape(array.shape[0], array.shape[1], tile, channels)
 
     left = col == 0
+    cache_time, cache_three, cache_four, _ = lax.optimization_barrier(
+        (cache_time, cache_three, cache_four, mine)
+    )
     tiles = jnp.concatenate([cache_time, paired(cache_three), paired(cache_four)], axis=1)
     edge = jnp.where(left, tiles[:, :, tile - HALO :], tiles[:, :, :HALO])
     edge = swapped(edge, "cols")
+    tiles, edge, weight_upsample, weight_three, weight_four, _ = lax.optimization_barrier(
+        (tiles, edge, weight_upsample, weight_three, weight_four, own)
+    )
     nothing = jnp.zeros_like(edge)
     tiles = jnp.concatenate(
         [jnp.where(left, nothing, edge), tiles, jnp.where(left, edge, nothing)], axis=2

time: 104 us -> 107 us (1.029)
  local copies, waits for them, and re-layouts: 14.8 us -> 27.3 us
  waiting for transfers between devices: 12 us -> 4.55 us
  Pallas kernels: 49.7 us -> 48 us
    optimization_barrier x0 -> x3, local copies, waits for them, and re-layouts: none -> 11.1 us  [body(): lax.optimization_barrier((tiles, edge, weight_upsample, weight_three, wei...]
    ppermute x6, waiting for transfers between devices: 10.9 us -> 2.7 us  [shifted(): lax.ppermute(value, axis, [(source, source + steps) for source in range(i...]
    unnamed x25 -> x20, local copies, waits for them, and re-layouts: 11.2 us -> 8.23 us
    pallas_call x1, Pallas kernels: 19.5 us -> 17.5 us  [first_block(): pl.pallas_call(functools.partial(first_kernel, wide, sizes), out_shape=ja...]
  transfers between devices with their start and end apart: 10 -> 10, of which waited for: 4 -> 3; matrix products, arithmetic and copies ran while one was open for 12% -> 21% of each run, Pallas kernels for 0% -> 0%
where the time goes in v2:
time: 107 us; the launch traced here: 105 us
  Pallas kernels  48 us (45%)
  local copies, waits for them, and re-layouts  27.3 us (26%)
  starting transfers between devices  21.8 us (20%)
  waiting for transfers between devices  4.55 us (4%)
  other arithmetic  2.8 us (3%)
    pallas_call x1, Pallas kernels, second_block(): pl.pallas_call(functools.partial(second_kernel, wide, sizes), out_shape=j...  28.6 us
    pallas_call x1, Pallas kernels, first_block(): pl.pallas_call(functools.partial(first_kernel, wide, sizes), out_shape=ja...  17.5 us
    ppermute x6, starting transfers between devices, shifted(): lax.ppermute(value, axis, [(source, source + steps) for source in range(i...  16.8 us
    optimization_barrier x3, local copies, waits for them, and re-layouts, body(): lax.optimization_barrier((tiles, edge, weight_upsample, weight_three, wei...  11.1 us
    unnamed x20, local copies, waits for them, and re-layouts  8.23 us
    ppermute x4, starting transfers between devices, swapped(): return lax.ppermute(value, axis, [(0, 1), (1, 0)])  5.05 us
    ppermute x6, waiting for transfers between devices, shifted(): lax.ppermute(value, axis, [(source, source + steps) for source in range(i...  2.7 us
    reshape x2, local copies, waits for them, and re-layouts, paired(): return array.reshape(array.shape[0], array.shape[1], tile, channels)  2.33 us
  transfers between devices with their start and end apart: 10, of which 3 were waited for; matrix products, arithmetic and copies ran while one was open for 21% of the time, Pallas kernels for 0%

profile of v2, /device:TPU:9, one launch (start us, length us, event | category | flops | bytes accessed | tf_op | source)
XLA Modules:
  0.0 104.8 jit_solution(17014212464367171349)
XLA Ops:
  0.0 0.7 collective-permute-start
  0.7 0.7 reshape.43.gain_one
  1.4 0.7 reshape.44.gain_two
  2.6 0.6 copy-done.8
  3.3 1.9 %pack.1 = (bf16[8,24,384]{2,1,0:T(8,128)(2,1)}, bf16[8,24,384]{2,1,0:T(8,128)(2,1)}) custom-call(s32[4]{0:T(128)} %pad_add_fusion.place, bf16[2,64,384]{2,1,0:T(8,128)(2,1)} %bitcast.34, bf16[2,64,384]{2,1,0:T(8,128)(2,1)} %copy-done.8, bf16[2,64,384]{2,1,0:T(8,128)(2,1)} %bitcast.35, bf16[2,64,384]{2,1,0:T(8,128)(2,1)} %bitcast.36), custom_call_target="tpu_custom_call" | custom-call | tf_op jit(solution)/shard_map/pack/pallas_call | solution.py:195
  5.1 1.2 %collective-permute-start.1 = (bf16[8,24,384]{2,1,0:T(8,128)(2,1)}, bf16[8,24,384]{2,1,0:T(8,128)(2,1)S(1)}, u32[]{:S(2)}, u32[]{:S(2)}) collective-permute-start(bf16[8,24,384]{2,1,0:T(8,128)(2,1)} %get-tuple-element.16), channel_id=1, source_target_pairs={{0,1},{1,0},{2,3},{3,2},{4,5},{5,4},{6,7},{7,6},{8,9},{9,8},{10,11... | collective-permute-start | bytes 442376 | tf_op jit(solution)/shard_map/ppermute | solution.py:18
  6.3 0.9 constant_dynamic-update-slice_fusion.2
  7.2 1.2 %reshape.45 = bf16[2,4,32,384]{3,2,1,0:T(8,128)(2,1)S(1)} reshape(bf16[2,4,64,192]{3,2,1,0:T(8,128)(2,1)} %param.20) | data formatting | bytes 393216 | tf_op jit(solution)/shard_map/reshape | solution.py:572
  8.4 1.2 %reshape.46 = bf16[2,4,32,384]{3,2,1,0:T(8,128)(2,1)S(1)} reshape(bf16[2,4,64,192]{3,2,1,0:T(8,128)(2,1)} %param.21) | data formatting | bytes 393216 | tf_op jit(solution)/shard_map/reshape | solution.py:572
  10.0 0.8 collective-permute-done.1
  10.9 3.2 %collective-permute-start.2 = (bf16[2,8,24,384]{3,2,1,0:T(8,128)(2,1)S(1)}, bf16[2,8,24,384]{3,2,1,0:T(8,128)(2,1)S(1)}, u32[]{:S(2)}, u32[]{:S(2)}) collective-permute-start(bf16[2,8,24,384]{3,2,1,0:T(8,128)(2,1)S(1)} %pad_maximum_fusion.1.own), channel_id=1, source_target_pairs={{0,4},{2,6},{4,8},{6,10},{8,12},{10,14},{1,5},{3,7},{5,9},{7,11},{... | collective-permute-start | bytes 884744 | tf_op jit(solution)/shard_map/ppermute | solution.py:24
  14.1 3.1 %collective-permute-start.3 = (bf16[2,8,24,384]{3,2,1,0:T(8,128)(2,1)S(1)}, bf16[2,8,24,384]{3,2,1,0:T(8,128)(2,1)S(1)}, u32[]{:S(2)}, u32[]{:S(2)}) collective-permute-start(bf16[2,8,24,384]{3,2,1,0:T(8,128)(2,1)S(1)} %pad_maximum_fusion.1.own), channel_id=1, source_target_pairs={{0,2},{2,4},{4,6},{6,8},{8,10},{10,12},{12,14},{1,3},{3,5},{5,7},{... | collective-permute-start | bytes 884744 | tf_op jit(solution)/shard_map/ppermute | solution.py:24
  17.2 3.0 %collective-permute-start.4 = (bf16[2,8,24,384]{3,2,1,0:T(8,128)(2,1)S(1)}, bf16[2,8,24,384]{3,2,1,0:T(8,128)(2,1)S(1)}, u32[]{:S(2)}, u32[]{:S(2)}) collective-permute-start(bf16[2,8,24,384]{3,2,1,0:T(8,128)(2,1)S(1)} %pad_maximum_fusion.1.own), channel_id=1, source_target_pairs={{2,0},{4,2},{6,4},{8,6},{10,8},{12,10},{14,12},{3,1},{5,3},{7,5},{... | collective-permute-start | bytes 884744 | tf_op jit(solution)/shard_map/ppermute | solution.py:24
  20.3 1.9 %collective-permute-start.5 = (bf16[2,8,24,384]{3,2,1,0:T(8,128)(2,1)S(1)}, bf16[2,8,24,384]{3,2,1,0:T(8,128)(2,1)S(1)}, u32[]{:S(2)}, u32[]{:S(2)}) collective-permute-start(bf16[2,8,24,384]{3,2,1,0:T(8,128)(2,1)S(1)} %pad_maximum_fusion.1.own), channel_id=1, source_target_pairs={{4,0},{6,2},{8,4},{10,6},{12,8},{14,10},{5,1},{7,3},{9,5},{11,7},{... | collective-permute-start | bytes 884744 | tf_op jit(solution)/shard_map/ppermute | solution.py:24
  23.2 0.7 fusion.2
  24.0 0.7 pad_maximum_fusion.6
  24.7 1.9 %collective-permute-start.8 = (bf16[2,5,24,384]{3,2,1,0:T(8,128)(2,1)}, bf16[2,5,24,384]{3,2,1,0:T(8,128)(2,1)}, u32[]{:S(2)}, u32[]{:S(2)}) collective-permute-start(bf16[2,5,24,384]{3,2,1,0:T(8,128)(2,1)} %pad_maximum_fusion.6), channel_id=1, source_target_pairs={{2,0},{4,2},{6,4},{8,6},{10,8},{12,10},{14,12},{3,1},{5,3},{7,5},{... | collective-permute-start | bytes 552968 | tf_op jit(solution)/shard_map/ppermute | solution.py:24
  26.6 2.5 %copy.17 = bf16[3456,192]{1,0:T(8,128)(2,1)S(1)} copy(bf16[3456,192]{0,1:T(8,128)(2,1)} %param.29) | data formatting | bytes 2654208 | tf_op jit(solution)/shard_map/optimization_barrier | solution.py:581
  29.1 4.3 %copy.18 = bf16[5184,192]{1,0:T(8,128)(2,1)} copy(bf16[5184,192]{0,1:T(8,128)(2,1)} %param.30) | data formatting | bytes 3981312 | tf_op jit(solution)/shard_map/optimization_barrier | solution.py:581
  33.4 4.3 %copy.19 = bf16[5184,192]{1,0:T(8,128)(2,1)} copy(bf16[5184,192]{0,1:T(8,128)(2,1)} %param.31) | data formatting | bytes 3981312 | tf_op jit(solution)/shard_map/optimization_barrier | solution.py:581
  37.8 0.8 pad_maximum_fusion.5
  38.6 3.5 %collective-permute-start.7 = (bf16[2,5,24,384]{3,2,1,0:T(8,128)(2,1)S(1)}, bf16[2,5,24,384]{3,2,1,0:T(8,128)(2,1)S(1)}, u32[]{:S(2)}, u32[]{:S(2)}) collective-permute-start(bf16[2,5,24,384]{3,2,1,0:T(8,128)(2,1)S(1)} %pad_maximum_fusion.5), channel_id=1, source_target_pairs={{0,2},{2,4},{4,6},{6,8},{8,10},{10,12},{12,14},{1,3},{3,5},{5,7},{... | collective-permute-start | bytes 552968 | tf_op jit(solution)/shard_map/ppermute | solution.py:24
  42.2 0.9 fusion.6
  43.1 2.7 %collective-permute-done.7 = bf16[2,5,24,384]{3,2,1,0:T(8,128)(2,1)S(1)} collective-permute-done((bf16[2,5,24,384]{3,2,1,0:T(8,128)(2,1)S(1)}, bf16[2,5,24,384]{3,2,1,0:T(8,128)(2,1)S(1)}, u32[]{:S(2)}, u32[]{:S(2)}) %collective-permute-start.7) | collective-permute-done | bytes 184352 | tf_op jit(solution)/shard_map/ppermute | solution.py:24
  45.8 0.8 slice.79
  46.8 3.4 %copy-done.4 = bf16[10368,384]{1,0:T(8,128)(2,1)S(1)} copy-done((bf16[10368,384]{1,0:T(8,128)(2,1)S(1)}, bf16[10368,384]{1,0:T(8,128)(2,1)}, u32[]{:S(2)}) %copy-start.4) | copy-done | bytes 7962648
  50.2 3.3 %copy-done.5 = bf16[10368,384]{1,0:T(8,128)(2,1)S(1)} copy-done((bf16[10368,384]{1,0:T(8,128)(2,1)S(1)}, bf16[10368,384]{1,0:T(8,128)(2,1)}, u32[]{:S(2)}) %copy-start.5) | copy-done | bytes 7962648
  53.5 17.5 %first_block.1.blocked = bf16[576,384]{1,0:T(8,128)(2,1)S(1)} custom-call(s32[4]{0:T(128)S(1)} %copy-done.1, bf16[2,8,24,384]{3,2,1,0:T(8,128)(2,1)S(1)} %collective-permute-done.2.low2, bf16[2,8,24,384]{3,2,1,0:T(8,128)(2,1)S(1)} %collective-permute-done.3.low1, bf16[2,8,24,384]{3,2,1,0:T(8,128)(2,1)S(1)} %pad_maximum_fusion.1.own, ...), custom_call_target="tpu_custom_call" | custom-call | flops 10701766656 | bytes 15925248 | tf_op jit(solution)/shard_map/first_block/pallas_call | solution.py:280
  71.0 28.6 %second_block.1 = bf16[8,4,16,384]{3,2,1,0:T(8,128)(2,1)S(1)} custom-call(s32[4]{0:T(128)S(1)} %copy-done.1, bf16[576,384]{1,0:T(8,128)(2,1)S(1)} %first_block.1.blocked, bf16[288,384]{1,0:T(8,128)(2,1)S(1)} %bitcast.25, bf16[2,192,384]{2,1,0:T(8,128)(2,1)S(1)} %bitcast.24, bf16[2,144,384]{2,1,0:T(8,128)(2,1)S(1)} %bitcast.26, f32[1,192]{1,0:T(1,128)S(1)} %bitcast.27, ...), custom_call_target="tpu_custom_call" | custom-call | tf_op jit(solution)/shard_map/second_block/pallas_call | solution.py:493
  99.7 2.8 %collective-permute-start.9 = (bf16[4,4,16,384]{3,2,1,0:T(8,128)(2,1)S(1)}, bf16[4,4,16,384]{3,2,1,0:T(8,128)(2,1)S(1)}, u32[]{:S(2)}, u32[]{:S(2)}) collective-permute-start(bf16[4,4,16,384]{3,2,1,0:T(8,128)(2,1)S(1)} %constant_dynamic-slice_fusion), channel_id=1, source_target_pairs={{0,16},{16,0},{1,17},{17,1},{2,18},{18,2},{3,19},{19,3},{4,20},{20... | collective-permute-start | bytes 589832 | tf_op jit(solution)/shard_map/ppermute | solution.py:18
  102.6 1.1 %collective-permute-done.9 = bf16[4,4,16,384]{3,2,1,0:T(8,128)(2,1)S(1)} collective-permute-done((bf16[4,4,16,384]{3,2,1,0:T(8,128)(2,1)S(1)}, bf16[4,4,16,384]{3,2,1,0:T(8,128)(2,1)S(1)}, u32[]{:S(2)}, u32[]{:S(2)}) %collective-permute-start.9) | collective-permute-done | bytes 196640 | tf_op jit(solution)/shard_map/ppermute | solution.py:18
  103.7 1.1 %reshape.55 = bf16[4,4,64,192]{3,2,1,0:T(8,128)(2,1)} reshape(bf16[4,4,32,384]{3,2,1,0:T(8,128)(2,1)S(1)} %pad_maximum_fusion) | data formatting | bytes 786432 | tf_op jit(solution)/shard_map/reshape | solution.py:620
  (40 shorter events, 2.4 us)
Async XLA Ops:
  0.0 2.6 %collective-permute-start = (bf16[2,64,384]{2,1,0:T(8,128)(2,1)}, bf16[2,64,384]{2,1,0:T(8,128)(2,1)S(1)}, u32[]{:S(2)}, u32[]{:S(2)}) collective-permute-start(bf16[2,64,384]{2,1,0:T(8,128)(2,1)} %bitcast.33), channel_id=1, source_target_pairs={{0,16},{16,0},{1,17},{17,1},{2,18},{18,2},{3,19},{19,3},{4,20},{20... | collective-permute-start | bytes 294920 | tf_op jit(solution)/shard_map/ppermute | solution.py:18
  2.6 0.6 copy-start.8
  5.1 5.7 %copy-start.7 = (bf16[8,24,384]{2,1,0:T(8,128)(2,1)S(1)}, bf16[8,24,384]{2,1,0:T(8,128)(2,1)}, u32[]{:S(2)}) copy-start(bf16[8,24,384]{2,1,0:T(8,128)(2,1)} %get-tuple-element.15) | copy-start | bytes 442372
  5.1 5.7 %collective-permute-start.1 = (bf16[8,24,384]{2,1,0:T(8,128)(2,1)}, bf16[8,24,384]{2,1,0:T(8,128)(2,1)S(1)}, u32[]{:S(2)}, u32[]{:S(2)}) collective-permute-start(bf16[8,24,384]{2,1,0:T(8,128)(2,1)} %get-tuple-element.16), channel_id=1, source_target_pairs={{0,1},{1,0},{2,3},{3,2},{4,5},{5,4},{6,7},{7,6},{8,9},{9,8},{10,11... | collective-permute-start | bytes 442376 | tf_op jit(solution)/shard_map/ppermute | solution.py:18
  9.7 12.5 %collective-permute-start.6 = (bf16[2,10,4,384]{3,2,1,0:T(4,128)(2,1)S(1)}, bf16[2,10,4,384]{3,2,1,0:T(4,128)(2,1)S(1)}, u32[]{:S(2)}, u32[]{:S(2)}) collective-permute-start(bf16[2,10,4,384]{3,2,1,0:T(4,128)(2,1)S(1)} %slice_select_fusion), channel_id=1, source_target_pairs={{0,1},{1,0},{2,3},{3,2},{4,5},{5,4},{6,7},{7,6},{8,9},{9,8},{10,11... | collective-permute-start | bytes 184328 | tf_op jit(solution)/shard_map/ppermute | solution.py:18
  10.9 35.9 %collective-permute-start.2 = (bf16[2,8,24,384]{3,2,1,0:T(8,128)(2,1)S(1)}, bf16[2,8,24,384]{3,2,1,0:T(8,128)(2,1)S(1)}, u32[]{:S(2)}, u32[]{:S(2)}) collective-permute-start(bf16[2,8,24,384]{3,2,1,0:T(8,128)(2,1)S(1)} %pad_maximum_fusion.1.own), channel_id=1, source_target_pairs={{0,4},{2,6},{4,8},{6,10},{8,12},{10,14},{1,5},{3,7},{5,9},{7,11},{... | collective-permute-start | bytes 884744 | tf_op jit(solution)/shard_map/ppermute | solution.py:24
  14.1 32.7 %collective-permute-start.3 = (bf16[2,8,24,384]{3,2,1,0:T(8,128)(2,1)S(1)}, bf16[2,8,24,384]{3,2,1,0:T(8,128)(2,1)S(1)}, u32[]{:S(2)}, u32[]{:S(2)}) collective-permute-start(bf16[2,8,24,384]{3,2,1,0:T(8,128)(2,1)S(1)} %pad_maximum_fusion.1.own), channel_id=1, source_target_pairs={{0,2},{2,4},{4,6},{6,8},{8,10},{10,12},{12,14},{1,3},{3,5},{5,7},{... | collective-permute-start | bytes 884744 | tf_op jit(solution)/shard_map/ppermute | solution.py:24
  17.2 29.6 %collective-permute-start.4 = (bf16[2,8,24,384]{3,2,1,0:T(8,128)(2,1)S(1)}, bf16[2,8,24,384]{3,2,1,0:T(8,128)(2,1)S(1)}, u32[]{:S(2)}, u32[]{:S(2)}) collective-permute-start(bf16[2,8,24,384]{3,2,1,0:T(8,128)(2,1)S(1)} %pad_maximum_fusion.1.own), channel_id=1, source_target_pairs={{2,0},{4,2},{6,4},{8,6},{10,8},{12,10},{14,12},{3,1},{5,3},{7,5},{... | collective-permute-start | bytes 884744 | tf_op jit(solution)/shard_map/ppermute | solution.py:24
  20.3 26.5 %collective-permute-start.5 = (bf16[2,8,24,384]{3,2,1,0:T(8,128)(2,1)S(1)}, bf16[2,8,24,384]{3,2,1,0:T(8,128)(2,1)S(1)}, u32[]{:S(2)}, u32[]{:S(2)}) collective-permute-start(bf16[2,8,24,384]{3,2,1,0:T(8,128)(2,1)S(1)} %pad_maximum_fusion.1.own), channel_id=1, source_target_pairs={{4,0},{6,2},{8,4},{10,6},{12,8},{14,10},{5,1},{7,3},{9,5},{11,7},{... | collective-permute-start | bytes 884744 | tf_op jit(solution)/shard_map/ppermute | solution.py:24
  24.7 13.9 %collective-permute-start.8 = (bf16[2,5,24,384]{3,2,1,0:T(8,128)(2,1)}, bf16[2,5,24,384]{3,2,1,0:T(8,128)(2,1)}, u32[]{:S(2)}, u32[]{:S(2)}) collective-permute-start(bf16[2,5,24,384]{3,2,1,0:T(8,128)(2,1)} %pad_maximum_fusion.6), channel_id=1, source_target_pairs={{2,0},{4,2},{6,4},{8,6},{10,8},{12,10},{14,12},{3,1},{5,3},{7,5},{... | collective-permute-start | bytes 552968 | tf_op jit(solution)/shard_map/ppermute | solution.py:24
  37.8 8.9 %copy-start.6 = (bf16[2,4,24,384]{3,2,1,0:T(8,128)(2,1)S(1)}, bf16[2,4,24,384]{3,2,1,0:T(8,128)(2,1)}, u32[]{:S(2)}) copy-start(bf16[2,4,24,384]{3,2,1,0:T(8,128)(2,1)} %get-tuple-element.28) | copy-start | bytes 442372
  37.8 9.1 %copy-start.1 = (s32[4]{0:T(128)S(1)}, s32[4]{0:T(128)}, u32[]{:S(2)}) copy-start(s32[4]{0:T(128)} %pad_add_fusion.place) | copy-start | bytes 52
  38.6 7.2 %collective-permute-start.7 = (bf16[2,5,24,384]{3,2,1,0:T(8,128)(2,1)S(1)}, bf16[2,5,24,384]{3,2,1,0:T(8,128)(2,1)S(1)}, u32[]{:S(2)}, u32[]{:S(2)}) collective-permute-start(bf16[2,5,24,384]{3,2,1,0:T(8,128)(2,1)S(1)} %pad_maximum_fusion.5), channel_id=1, source_target_pairs={{0,2},{2,4},{4,6},{6,8},{8,10},{10,12},{12,14},{1,3},{3,5},{5,7},{... | collective-permute-start | bytes 552968 | tf_op jit(solution)/shard_map/ppermute | solution.py:24
  46.7 24.2 %copy-start = (bf16[1152,768]{1,0:T(8,128)(2,1)S(1)}, bf16[1152,768]{1,0:T(8,128)(2,1)}, u32[]{:S(2)}) copy-start(bf16[1152,768]{1,0:T(8,128)(2,1)} %weight_time.1) | copy-start | bytes 5308420
  46.8 24.2 %copy-start.2 = (f32[192]{0:T(256)S(1)}, f32[192]{0:T(256)}, u32[]{:S(2)}) copy-start(f32[192]{0:T(256)} %param.24) | copy-start | bytes 2308
  46.8 24.2 %copy-start.3 = (f32[192]{0:T(256)S(1)}, f32[192]{0:T(256)}, u32[]{:S(2)}) copy-start(f32[192]{0:T(256)} %param.25) | copy-start | bytes 2308
  46.8 3.4 %copy-start.4 = (bf16[10368,384]{1,0:T(8,128)(2,1)S(1)}, bf16[10368,384]{1,0:T(8,128)(2,1)}, u32[]{:S(2)}) copy-start(bf16[10368,384]{1,0:T(8,128)(2,1)} %w1.1) | copy-start | bytes 23887876
  50.2 3.3 %copy-start.5 = (bf16[10368,384]{1,0:T(8,128)(2,1)S(1)}, bf16[10368,384]{1,0:T(8,128)(2,1)}, u32[]{:S(2)}) copy-start(bf16[10368,384]{1,0:T(8,128)(2,1)} %w2.1) | copy-start | bytes 23887876
  99.7 3.9 %collective-permute-start.9 = (bf16[4,4,16,384]{3,2,1,0:T(8,128)(2,1)S(1)}, bf16[4,4,16,384]{3,2,1,0:T(8,128)(2,1)S(1)}, u32[]{:S(2)}, u32[]{:S(2)}) collective-permute-start(bf16[4,4,16,384]{3,2,1,0:T(8,128)(2,1)S(1)} %constant_dynamic-slice_fusion), channel_id=1, source_target_pairs={{0,16},{16,0},{1,17},{17,1},{2,18},{18,2},{3,19},{19,3},{4,20},{20... | collective-permute-start | bytes 589832 | tf_op jit(solution)/shard_map/ppermute | solution.py:18

commit v3 on v1

--- a/solution.py
+++ b/solution.py
@@ -85,12 +85,16 @@
     return jnp.concatenate(parts, axis=0)
 
 
-def low_product(acc, even, odd, count, height, wide, weights):
+def low_product(acc, even, odd, count, height, wide, weights, copies):
     rows = count * (height - 2) * wide
     channels = weights.shape[1]
-
-    def column(n, carry):
-        lanes = pl.ds(pl.multiple_of(n * LANES, LANES), LANES)
+    lanes = 3 * channels
+    waited = 0
+    for n in range(-(-lanes // LANES)):
+        begin, end = n * LANES, min((n + 1) * LANES, lanes)
+        while waited * channels < end:
+            copies[waited].wait()
+            waited += 1
         total = None
         for first, last in ((0, 4), (4, 8), (8, 9)):
             left = jnp.concatenate(
@@ -100,13 +104,10 @@
                 ],
                 axis=1,
             )
-            right = weights[first:last, :, lanes].reshape((last - first) * channels, LANES)
+            right = weights[first:last, :, begin:end].reshape((last - first) * channels, -1)
             part = jnp.dot(left, right, preferred_element_type=F32)
             total = part if total is None else total + part
-        acc[n, 0:rows, :] = total
-        return carry
-
-    lax.fori_loop(0, weights.shape[-1] // LANES, column, 0)
+        acc[n, 0:rows, 0 : end - begin] = total
 
 
 def low_sum(acc, start, size):
@@ -199,11 +200,9 @@
     wide,
     sizes,
     place,
-    low2,
-    low1,
+    above,
     own,
-    high1,
-    high2,
+    below,
     gain_one,
     gain_two,
     weight_one,
@@ -222,7 +221,7 @@
     frames = own.shape[1] - 4
     height, width = sizes
     col, row = place[1], place[3]
-    pieces = (low2, low1, own, high1, high2)
+    pieces = (above, own, below)
 
     def load(source, target, base):
         return [
@@ -234,7 +233,7 @@
 
     copies_one = load(weight_one, w1, 0)
     copies_two = load(weight_two, w2, 3)
-    for copy in copies_one:
+    for copy in copies_one + copies_two:
         copy.start()
 
     def rows_of(refs, index):
@@ -243,38 +242,32 @@
         )
 
     for f in range(2):
-        store(x1e, x1o, f, rows_of(pieces, frames + f), 10, wide)
-        store(x2e, x2o, f, rows_of(pieces, frames + 2 + f)[wide : 9 * wide], 8, wide)
+        store(x1e, x1o, f, rows_of(pieces, frames + f), 6, wide)
+        store(x2e, x2o, f, rows_of(pieces, frames + 2 + f)[wide : 5 * wide], 4, wide)
 
     def norm_one(f, carry):
         values = activate(rows_of(pieces, f), gain_one[...], 1.0)
-        store(x1e, x1o, f + 2, values, 10, wide)
+        store(x1e, x1o, f + 2, values, 6, wide)
         return carry
 
     lax.fori_loop(0, frames, norm_one, 0)
-    for copy in copies_one:
-        copy.wait()
-    for copy in copies_two:
-        copy.start()
-    low_product(acc, x1e, x1o, frames, 10, wide, w1)
-
-    mask = line_mask(place, wide, 2 * row - 3, 8, height, width)
+    low_product(acc, x1e, x1o, frames, 6, wide, w1, copies_one)
+
+    mask = line_mask(place, wide, 2 * row - 1, 4, height, width)
 
     def norm_two(f, carry):
-        size = 8 * wide
+        size = 4 * wide
         values = activate(low_sum(acc, aligned(f, size), size), gain_two[...], mask)
-        store(x2e, x2o, f + 2, values, 8, wide)
+        store(x2e, x2o, f + 2, values, 4, wide)
         return carry
 
     lax.fori_loop(0, frames, norm_two, 0)
-    for copy in copies_two:
-        copy.wait()
-    low_product(acc, x2e, x2o, frames, 8, wide, w2)
+    low_product(acc, x2e, x2o, frames, 4, wide, w2, copies_two)
 
     def residual(f, carry):
-        size = 6 * wide
-        values = low_sum(acc, aligned(f, size), size) + rows_of(pieces[1:4], f)
-        out_ref[pl.ds(aligned(f, size), size), :] = values.astype(BF16)
+        size = 2 * wide
+        values = low_sum(acc, aligned(f, size), size) + rows_of((own,), f)
+        out_ref[f] = values.astype(BF16)
         return carry
 
     lax.fori_loop(0, frames, residual, 0)
@@ -295,20 +288,20 @@
     anywhere = pl.BlockSpec(memory_space=pl.ANY)
     return pl.pallas_call(
         functools.partial(first_kernel, wide, sizes),
-        out_shape=jax.ShapeDtypeStruct((frames * 6 * wide, channels), BF16),
-        in_specs=[pl.BlockSpec(memory_space=pltpu.SMEM)] + [vmem] * 7 + [anywhere] * 2,
+        out_shape=jax.ShapeDtypeStruct((frames, 2 * wide, channels), BF16),
+        in_specs=[pl.BlockSpec(memory_space=pltpu.SMEM)] + [vmem] * 5 + [anywhere] * 2,
         out_specs=vmem,
         scratch_shapes=[
             pltpu.VMEM((9, channels, slots * LANES), BF16),
             pltpu.VMEM((9, channels, slots * LANES), BF16),
-            pltpu.VMEM((slots, frames * 8 * wide, LANES), F32),
-            *planes(frames + 2, 10, wide, channels),
-            *planes(frames + 2, 8, wide, channels),
+            pltpu.VMEM((slots, frames * 4 * wide, LANES), F32),
+            *planes(frames + 2, 6, wide, channels),
+            *planes(frames + 2, 4, wide, channels),
             pltpu.SemaphoreType.DMA((6,)),
         ],
-        compiler_params=pltpu.CompilerParams(vmem_limit_bytes=48 * 1024 * 1024),
+        compiler_params=pltpu.CompilerParams(vmem_limit_bytes=40 * 1024 * 1024),
         cost_estimate=pl.CostEstimate(
-            flops=2 * 27 * channels * channels * frames * 14 * wide,
+            flops=2 * 27 * channels * channels * frames * 6 * wide,
             bytes_accessed=2 * 54 * channels * channels,
             transcendentals=0,
         ),
@@ -320,7 +313,9 @@
     wide,
     sizes,
     place,
+    above,
     blocked,
+    below,
     time_ref,
     three_ref,
     four_ref,
@@ -352,7 +347,7 @@
     channels = blocked.shape[-1]
     half = channels // 2
     size = 6 * wide
-    frames = blocked.shape[0] // size
+    frames = blocked.shape[0]
     count = 2 * frames
     height, width = sizes
     row = place[3]
@@ -388,7 +383,10 @@
         sides[1, :, half:LANES, :] = blank
 
     mixed[0 : 2 * size, :] = time_ref[...]
-    mixed[2 * size : (frames + 2) * size, :] = blocked[...]
+    for f in range(frames):
+        for i, ref in enumerate((above, blocked, below)):
+            begin = (f + 2) * size + i * 2 * wide
+            mixed[begin : begin + 2 * wide, :] = ref[f]
     copy_time.wait()
 
     def mix(n, carry):
@@ -501,10 +499,9 @@
     lax.fori_loop(0, count, finish, 0)
 
 
-def second_block(place, blocked, time, three, four, gains, weights, sizes, wide):
-    channels = blocked.shape[-1]
+def second_block(place, pieces, time, three, four, gains, weights, sizes, wide):
+    frames, _, channels = pieces[0].shape
     half = channels // 2
-    frames = blocked.shape[0] // (6 * wide)
     count = 2 * frames
     weight_time, weight_up, weight_three, weight_four = weights
     vmem = pl.BlockSpec(memory_space=pltpu.VMEM)
@@ -512,7 +509,7 @@
     return pl.pallas_call(
         functools.partial(second_kernel, wide, sizes),
         out_shape=jax.ShapeDtypeStruct((count, 4, wide - 2 * HALO, channels), BF16),
-        in_specs=[pl.BlockSpec(memory_space=pltpu.SMEM)] + [vmem] * 6 + [anywhere] * 4,
+        in_specs=[pl.BlockSpec(memory_space=pltpu.SMEM)] + [vmem] * 8 + [anywhere] * 4,
         out_specs=vmem,
         scratch_shapes=[
             pltpu.VMEM(weight_time.shape, BF16),
@@ -532,7 +529,7 @@
         ],
         compiler_params=pltpu.CompilerParams(vmem_limit_bytes=48 * 1024 * 1024),
         name="second_block",
-    )(place, blocked, time, three, four, *gains, *weights)
+    )(place, *pieces, time, three, four, *gains, *weights)
 
 
 def body(
@@ -570,13 +567,7 @@
     )
     theirs = swapped(theirs, "cols")
     own = jnp.stack([mine, theirs])
-    pieces = [
-        shifted(own, "rows", 2),
-        shifted(own, "rows", 1),
-        own,
-        shifted(own, "rows", -1),
-        shifted(own, "rows", -2),
-    ]
+    pieces = [shifted(own, "rows", 1), own, shifted(own, "rows", -1)]
     blocked = first_block(
         place,
         pieces,
@@ -586,29 +577,39 @@
         weight_two.reshape(9, 3, channels, channels),
         sizes,
     )
+    blocks = [shifted(blocked, "rows", 1), blocked, shifted(blocked, "rows", -1)]
 
     def paired(array):
         return array.reshape(array.shape[0], array.shape[1], tile, channels)
 
     left = col == 0
+    cache_time, cache_three, cache_four, _ = lax.optimization_barrier(
+        (cache_time, cache_three, cache_four, mine)
+    )
     tiles = jnp.concatenate([cache_time, paired(cache_three), paired(cache_four)], axis=1)
     edge = jnp.where(left, tiles[:, :, tile - HALO :], tiles[:, :, :HALO])
     edge = swapped(edge, "cols")
+    weight_upsample, weight_three, _ = lax.optimization_barrier(
+        (weight_upsample, weight_three, own)
+    )
+    weight_four, _ = lax.optimization_barrier((weight_four, blocked))
     nothing = jnp.zeros_like(edge)
     tiles = jnp.concatenate(
         [jnp.where(left, nothing, edge), tiles, jnp.where(left, edge, nothing)], axis=2
     )
     tiles = lax.dynamic_slice_in_dim(tiles, section * part, wide, 2)
     time, three, four = tiles[:, 0:2], tiles[:, 2:6], tiles[:, 6:10]
-    above = shifted(jnp.concatenate([time, three[:, 2:], four[:, 3:]], axis=1), "rows", 1)
-    below = shifted(jnp.concatenate([time, three[:, :2], four[:, :1]], axis=1), "rows", -1)
+    above = jnp.concatenate([time, three[:, 2:], four[:, 3:]], axis=1)
+    below = jnp.concatenate([time, three[:, :2], four[:, :1]], axis=1)
+    above, below, *_ = lax.optimization_barrier((above, below, *pieces))
+    above, below = shifted(above, "rows", 1), shifted(below, "rows", -1)
     time = jnp.concatenate([above[:, 0:2], time, below[:, 0:2]], axis=1)
     three = jnp.concatenate([above[:, 2:4], three, below[:, 2:4]], axis=1)
     four = jnp.concatenate([above[:, 4:], four, below[:, 4:]], axis=1)
 
     frames = second_block(
         place,
-        blocked,
+        blocks,
         time.reshape(-1, channels),
         three.reshape(2, -1, channels),
         four.reshape(2, -1, channels),

time: 104 us -> 97.6 us (0.938)
  Pallas kernels: 49.7 us -> 41.1 us
  local copies, waits for them, and re-layouts: 14.8 us -> 20.2 us
  other arithmetic: 3.26 us -> 2.08 us
  waiting for transfers between devices: 12 us -> 10.9 us
    optimization_barrier x0 -> x3, local copies, waits for them, and re-layouts: none -> 11.1 us  [the longest x2 6.81 us: body(): lax.optimization_barrier((weight_upsample, weight_three, own))]
    pallas_call x1, Pallas kernels: 19.5 us -> 10.8 us  [first_block(): pl.pallas_call(functools.partial(first_kernel, wide, sizes), out_shape=ja...]
    ppermute x6, waiting for transfers between devices: 10.9 us -> 4.97 us  [shifted(): lax.ppermute(value, axis, [(source, source + steps) for source in range(i...]
    unnamed x25 -> x22, local copies, waits for them, and re-layouts: 11.2 us -> 5.43 us
    ppermute x4, waiting for transfers between devices: 1.08 us -> 5.92 us  [swapped(): return lax.ppermute(value, axis, [(0, 1), (1, 0)])]
  transfers between devices with their start and end apart: 10 -> 10, of which waited for: 4 -> 6; matrix products, arithmetic and copies ran while one was open for 12% -> 14% of each run, Pallas kernels for 0% -> 11%
where the time goes in v3:
time: 97.6 us; the launch traced here: 96.3 us
  Pallas kernels  41.1 us (42%)
  starting transfers between devices  21.8 us (22%)
  local copies, waits for them, and re-layouts  20.2 us (21%)
  waiting for transfers between devices  10.9 us (11%)
  other arithmetic  2.08 us (2%)
    pallas_call x1, Pallas kernels, second_block(): pl.pallas_call(functools.partial(second_kernel, wide, sizes), out_shape=j...  28.4 us
    ppermute x6, starting transfers between devices, shifted(): lax.ppermute(value, axis, [(source, source + steps) for source in range(i...  17.8 us
    pallas_call x1, Pallas kernels, first_block(): pl.pallas_call(functools.partial(first_kernel, wide, sizes), out_shape=ja...  10.8 us
    optimization_barrier x2, local copies, waits for them, and re-layouts, body(): lax.optimization_barrier((weight_upsample, weight_three, own))  6.81 us
    ppermute x4, waiting for transfers between devices, swapped(): return lax.ppermute(value, axis, [(0, 1), (1, 0)])  5.92 us
    unnamed x22, local copies, waits for them, and re-layouts  5.43 us
    ppermute x6, waiting for transfers between devices, shifted(): lax.ppermute(value, axis, [(source, source + steps) for source in range(i...  4.97 us
    optimization_barrier x1, local copies, waits for them, and re-layouts, body(): weight_four, _ = lax.optimization_barrier((weight_four, blocked))  4.3 us
  transfers between devices with their start and end apart: 10, of which 6 were waited for; matrix products, arithmetic and copies ran while one was open for 14% of the time, Pallas kernels for 11%

profile of v3, /device:TPU:9, one launch (start us, length us, event | category | flops | bytes accessed | tf_op | source)
XLA Modules:
  0.0 96.3 jit_solution(13706309130121412320)
XLA Ops:
  0.0 0.7 collective-permute-start
  0.7 0.7 pad_add_fusion.place
  1.3 0.5 collective-permute-done.arrived
  1.8 0.6 copy-done.6
  2.5 1.9 %pack.1 = (bf16[8,24,384]{2,1,0:T(8,128)(2,1)}, bf16[8,24,384]{2,1,0:T(8,128)(2,1)}) custom-call(s32[4]{0:T(128)} %pad_add_fusion.place, bf16[2,64,384]{2,1,0:T(8,128)(2,1)} %bitcast.37, bf16[2,64,384]{2,1,0:T(8,128)(2,1)} %copy-done.6, bf16[2,64,384]{2,1,0:T(8,128)(2,1)} %bitcast.38, bf16[2,64,384]{2,1,0:T(8,128)(2,1)} %bitcast.39), custom_call_target="tpu_custom_call" | custom-call | tf_op jit(solution)/shard_map/pack/pallas_call | solution.py:189
  4.3 0.9 constant_dynamic-update-slice_fusion.2
  5.3 1.2 %reshape.53 = bf16[2,4,32,384]{3,2,1,0:T(8,128)(2,1)S(1)} reshape(bf16[2,4,64,192]{3,2,1,0:T(8,128)(2,1)} %param.20) | data formatting | bytes 393216 | tf_op jit(solution)/shard_map/reshape | solution.py:583
  6.5 1.2 %reshape.54 = bf16[2,4,32,384]{3,2,1,0:T(8,128)(2,1)S(1)} reshape(bf16[2,4,64,192]{3,2,1,0:T(8,128)(2,1)} %param.21) | data formatting | bytes 393216 | tf_op jit(solution)/shard_map/reshape | solution.py:583
  7.8 1.3 %collective-permute-start.6 = (bf16[2,10,4,384]{3,2,1,0:T(4,128)(2,1)S(1)}, bf16[2,10,4,384]{3,2,1,0:T(4,128)(2,1)S(1)}, u32[]{:S(2)}, u32[]{:S(2)}) collective-permute-start(bf16[2,10,4,384]{3,2,1,0:T(4,128)(2,1)S(1)} %slice_select_fusion), channel_id=1, source_target_pairs={{0,1},{1,0},{2,3},{3,2},{4,5},{5,4},{6,7},{7,6},{8,9},{9,8},{10,11... | collective-permute-start | bytes 184328 | tf_op jit(solution)/shard_map/ppermute | solution.py:18
  9.1 0.3 collective-permute-start.1
  9.4 1.5 %collective-permute-done.6 = bf16[2,10,4,384]{3,2,1,0:T(4,128)(2,1)S(1)} collective-permute-done((bf16[2,10,4,384]{3,2,1,0:T(4,128)(2,1)S(1)}, bf16[2,10,4,384]{3,2,1,0:T(4,128)(2,1)S(1)}, u32[]{:S(2)}, u32[]{:S(2)}) %collective-permute-start.6) | collective-permute-done | bytes 61472 | tf_op jit(solution)/shard_map/ppermute | solution.py:18
  11.0 0.3 fusion.1
  11.4 2.8 %collective-permute-done.1 = bf16[8,24,384]{2,1,0:T(8,128)(2,1)S(1)} collective-permute-done((bf16[8,24,384]{2,1,0:T(8,128)(2,1)S(1)}, bf16[8,24,384]{2,1,0:T(8,128)(2,1)S(1)}, u32[]{:S(2)}, u32[]{:S(2)}) %collective-permute-start.1) | collective-permute-done | bytes 147488 | tf_op jit(solution)/shard_map/ppermute | solution.py:18
  14.3 3.1 %collective-permute-start.2 = (bf16[2,8,24,384]{3,2,1,0:T(8,128)(2,1)S(1)}, bf16[2,8,24,384]{3,2,1,0:T(8,128)(2,1)S(1)}, u32[]{:S(2)}, u32[]{:S(2)}) collective-permute-start(bf16[2,8,24,384]{3,2,1,0:T(8,128)(2,1)S(1)} %pad_maximum_fusion.1.own), channel_id=1, source_target_pairs={{0,2},{2,4},{4,6},{6,8},{8,10},{10,12},{12,14},{1,3},{3,5},{5,7},{... | collective-permute-start | bytes 884744 | tf_op jit(solution)/shard_map/ppermute | solution.py:24
  17.5 3.0 %collective-permute-start.3 = (bf16[2,8,24,384]{3,2,1,0:T(8,128)(2,1)S(1)}, bf16[2,8,24,384]{3,2,1,0:T(8,128)(2,1)S(1)}, u32[]{:S(2)}, u32[]{:S(2)}) collective-permute-start(bf16[2,8,24,384]{3,2,1,0:T(8,128)(2,1)S(1)} %pad_maximum_fusion.1.own), channel_id=1, source_target_pairs={{2,0},{4,2},{6,4},{8,6},{10,8},{12,10},{14,12},{3,1},{5,3},{7,5},{... | collective-permute-start | bytes 884744 | tf_op jit(solution)/shard_map/ppermute | solution.py:24
  20.5 0.7 pad_maximum_fusion.5
  21.3 4.3 %copy.18 = bf16[5184,192]{1,0:T(8,128)(2,1)} copy(bf16[5184,192]{0,1:T(8,128)(2,1)} %param.30) | data formatting | bytes 3981312 | tf_op jit(solution)/shard_map/optimization_barrier | solution.py:592
  25.6 2.5 %copy.17 = bf16[3456,192]{1,0:T(8,128)(2,1)S(1)} copy(bf16[3456,192]{0,1:T(8,128)(2,1)} %param.29) | data formatting | bytes 2654208 | tf_op jit(solution)/shard_map/optimization_barrier | solution.py:592
  28.1 4.3 %collective-permute-done.3.below = bf16[2,8,24,384]{3,2,1,0:T(8,128)(2,1)S(1)} collective-permute-done((bf16[2,8,24,384]{3,2,1,0:T(8,128)(2,1)S(1)}, bf16[2,8,24,384]{3,2,1,0:T(8,128)(2,1)S(1)}, u32[]{:S(2)}, u32[]{:S(2)}) %collective-permute-start.3) | collective-permute-done | bytes 294944 | tf_op jit(solution)/shard_map/ppermute | solution.py:24
  32.4 1.9 %collective-permute-start.7 = (bf16[2,5,24,384]{3,2,1,0:T(8,128)(2,1)}, bf16[2,5,24,384]{3,2,1,0:T(8,128)(2,1)S(1)}, u32[]{:S(2)}, u32[]{:S(2)}) collective-permute-start(bf16[2,5,24,384]{3,2,1,0:T(8,128)(2,1)} %get-tuple-element.20), channel_id=1, source_target_pairs={{0,2},{2,4},{4,6},{6,8},{8,10},{10,12},{12,14},{1,3},{3,5},{5,7},{... | collective-permute-start | bytes 552968 | tf_op jit(solution)/shard_map/ppermute | solution.py:24
  34.3 3.3 %copy-done.4 = bf16[10368,384]{1,0:T(8,128)(2,1)S(1)} copy-done((bf16[10368,384]{1,0:T(8,128)(2,1)S(1)}, bf16[10368,384]{1,0:T(8,128)(2,1)}, u32[]{:S(2)}) %copy-start.4) | copy-done | bytes 7962648
  37.5 10.8 %first_block.1.blocked = bf16[4,48,384]{2,1,0:T(8,128)(2,1)S(1)} custom-call(s32[4]{0:T(128)S(1)} %copy-done.1, bf16[2,8,24,384]{3,2,1,0:T(8,128)(2,1)S(1)} %collective-permute-done.2.above, bf16[2,8,24,384]{3,2,1,0:T(8,128)(2,1)S(1)} %pad_maximum_fusion.1.own, bf16[2,8,24,384]{3,2,1,0:T(8,128)(2,1)S(1)} %collective-permute-done.3.below, ...), custom_call_target="tpu_custom_call" | custom-call | flops 4586471424 | bytes 15925248 | tf_op jit(solution)/shard_map/first_block/pallas_call | solution.py:289
  48.4 4.4 %collective-permute-start.4 = (bf16[4,48,384]{2,1,0:T(8,128)(2,1)S(1)}, bf16[4,48,384]{2,1,0:T(8,128)(2,1)S(1)}, u32[]{:S(2)}, u32[]{:S(2)}) collective-permute-start(bf16[4,48,384]{2,1,0:T(8,128)(2,1)S(1)} %first_block.1.blocked), channel_id=1, source_target_pairs={{0,2},{2,4},{4,6},{6,8},{8,10},{10,12},{12,14},{1,3},{3,5},{5,7},{... | collective-permute-start | bytes 442376 | tf_op jit(solution)/shard_map/ppermute | solution.py:24
  52.8 1.9 %collective-permute-start.5 = (bf16[4,48,384]{2,1,0:T(8,128)(2,1)S(1)}, bf16[4,48,384]{2,1,0:T(8,128)(2,1)S(1)}, u32[]{:S(2)}, u32[]{:S(2)}) collective-permute-start(bf16[4,48,384]{2,1,0:T(8,128)(2,1)S(1)} %first_block.1.blocked), channel_id=1, source_target_pairs={{2,0},{4,2},{6,4},{8,6},{10,8},{12,10},{14,12},{3,1},{5,3},{7,5},{... | collective-permute-start | bytes 442376 | tf_op jit(solution)/shard_map/ppermute | solution.py:24
  54.7 3.4 %collective-permute-start.8 = (bf16[2,5,24,384]{3,2,1,0:T(8,128)(2,1)S(1)}, bf16[2,5,24,384]{3,2,1,0:T(8,128)(2,1)S(1)}, u32[]{:S(2)}, u32[]{:S(2)}) collective-permute-start(bf16[2,5,24,384]{3,2,1,0:T(8,128)(2,1)S(1)} %get-tuple-element.21), channel_id=1, source_target_pairs={{2,0},{4,2},{6,4},{8,6},{10,8},{12,10},{14,12},{3,1},{5,3},{7,5},{... | collective-permute-start | bytes 552968 | tf_op jit(solution)/shard_map/ppermute | solution.py:24
  58.1 4.3 %copy.19 = bf16[5184,192]{1,0:T(8,128)(2,1)} copy(bf16[5184,192]{0,1:T(8,128)(2,1)} %param.31) | data formatting | bytes 3981312 | tf_op jit(solution)/shard_map/optimization_barrier | solution.py:595
  62.5 0.7 collective-permute-done.8
  63.4 0.5 copy-done
  63.9 28.4 %second_block.1 = bf16[8,4,16,384]{3,2,1,0:T(8,128)(2,1)S(1)} custom-call(s32[4]{0:T(128)S(1)} %copy-done.1, bf16[4,48,384]{2,1,0:T(8,128)(2,1)S(1)} %collective-permute-done.4.above, bf16[4,48,384]{2,1,0:T(8,128)(2,1)S(1)} %first_block.1.blocked, bf16[4,48,384]{2,1,0:T(8,128)(2,1)S(1)} %collective-permute-done.5.below, bf16[288,384]{1,0:T(8,128)(2,1)S(1)} %bitcast.27, ...), custom_call_target="tpu_custom_call" | custom-call | tf_op jit(solution)/shard_map/second_block/pallas_call | solution.py:509
  92.3 1.7 %collective-permute-start.9 = (bf16[4,4,16,384]{3,2,1,0:T(8,128)(2,1)S(1)}, bf16[4,4,16,384]{3,2,1,0:T(8,128)(2,1)S(1)}, u32[]{:S(2)}, u32[]{:S(2)}) collective-permute-start(bf16[4,4,16,384]{3,2,1,0:T(8,128)(2,1)S(1)} %constant_dynamic-slice_fusion), channel_id=1, source_target_pairs={{0,16},{16,0},{1,17},{17,1},{2,18},{18,2},{3,19},{19,3},{4,20},{20... | collective-permute-start | bytes 589832 | tf_op jit(solution)/shard_map/ppermute | solution.py:18
  94.0 1.1 %collective-permute-done.9 = bf16[4,4,16,384]{3,2,1,0:T(8,128)(2,1)S(1)} collective-permute-done((bf16[4,4,16,384]{3,2,1,0:T(8,128)(2,1)S(1)}, bf16[4,4,16,384]{3,2,1,0:T(8,128)(2,1)S(1)}, u32[]{:S(2)}, u32[]{:S(2)}) %collective-permute-start.9) | collective-permute-done | bytes 196640 | tf_op jit(solution)/shard_map/ppermute | solution.py:18
  95.2 1.1 %reshape.63 = bf16[4,4,64,192]{3,2,1,0:T(8,128)(2,1)} reshape(bf16[4,4,32,384]{3,2,1,0:T(8,128)(2,1)S(1)} %pad_maximum_fusion) | data formatting | bytes 786432 | tf_op jit(solution)/shard_map/reshape | solution.py:634
  (41 shorter events, 0.6 us)
Async XLA Ops:
  0.0 9.1 %copy-start.7 = (f32[384]{0:T(512)S(1)}, f32[384]{0:T(512)}, u32[]{:S(2)}) copy-start(f32[384]{0:T(512)} %param.22) | copy-start | bytes 4612
  0.0 9.1 %copy-start.8 = (f32[384]{0:T(512)S(1)}, f32[384]{0:T(512)}, u32[]{:S(2)}) copy-start(f32[384]{0:T(512)} %param.23) | copy-start | bytes 4612
  0.0 1.8 %collective-permute-start = (bf16[2,64,384]{2,1,0:T(8,128)(2,1)}, bf16[2,64,384]{2,1,0:T(8,128)(2,1)S(1)}, u32[]{:S(2)}, u32[]{:S(2)}) collective-permute-start(bf16[2,64,384]{2,1,0:T(8,128)(2,1)} %bitcast.36), channel_id=1, source_target_pairs={{0,16},{16,0},{1,17},{17,1},{2,18},{18,2},{3,19},{19,3},{4,20},{20... | collective-permute-start | bytes 294920 | tf_op jit(solution)/shard_map/ppermute | solution.py:18
  1.8 0.6 copy-start.6
  4.3 4.8 %copy-start.9 = (bf16[8,24,384]{2,1,0:T(8,128)(2,1)S(1)}, bf16[8,24,384]{2,1,0:T(8,128)(2,1)}, u32[]{:S(2)}) copy-start(bf16[8,24,384]{2,1,0:T(8,128)(2,1)} %get-tuple-element.16) | copy-start | bytes 442372
  6.5 7.8 %copy-start.5 = (bf16[8,24,384]{2,1,0:T(8,128)(2,1)S(1)}, bf16[8,24,384]{2,1,0:T(8,128)(2,1)}, u32[]{:S(2)}) copy-start(bf16[8,24,384]{2,1,0:T(8,128)(2,1)} %get-tuple-element.15) | copy-start | bytes 442372
  7.8 3.1 %collective-permute-start.6 = (bf16[2,10,4,384]{3,2,1,0:T(4,128)(2,1)S(1)}, bf16[2,10,4,384]{3,2,1,0:T(4,128)(2,1)S(1)}, u32[]{:S(2)}, u32[]{:S(2)}) collective-permute-start(bf16[2,10,4,384]{3,2,1,0:T(4,128)(2,1)S(1)} %slice_select_fusion), channel_id=1, source_target_pairs={{0,1},{1,0},{2,3},{3,2},{4,5},{5,4},{6,7},{7,6},{8,9},{9,8},{10,11... | collective-permute-start | bytes 184328 | tf_op jit(solution)/shard_map/ppermute | solution.py:18
  9.1 5.2 %collective-permute-start.1 = (bf16[8,24,384]{2,1,0:T(8,128)(2,1)S(1)}, bf16[8,24,384]{2,1,0:T(8,128)(2,1)S(1)}, u32[]{:S(2)}, u32[]{:S(2)}) collective-permute-start(bf16[8,24,384]{2,1,0:T(8,128)(2,1)S(1)} %copy-done.9), channel_id=1, source_target_pairs={{0,1},{1,0},{2,3},{3,2},{4,5},{5,4},{6,7},{7,6},{8,9},{9,8},{10,11... | collective-permute-start | bytes 442376 | tf_op jit(solution)/shard_map/ppermute | solution.py:18
  14.3 13.8 %collective-permute-start.2 = (bf16[2,8,24,384]{3,2,1,0:T(8,128)(2,1)S(1)}, bf16[2,8,24,384]{3,2,1,0:T(8,128)(2,1)S(1)}, u32[]{:S(2)}, u32[]{:S(2)}) collective-permute-start(bf16[2,8,24,384]{3,2,1,0:T(8,128)(2,1)S(1)} %pad_maximum_fusion.1.own), channel_id=1, source_target_pairs={{0,2},{2,4},{4,6},{6,8},{8,10},{10,12},{12,14},{1,3},{3,5},{5,7},{... | collective-permute-start | bytes 884744 | tf_op jit(solution)/shard_map/ppermute | solution.py:24
  17.5 14.9 %collective-permute-start.3 = (bf16[2,8,24,384]{3,2,1,0:T(8,128)(2,1)S(1)}, bf16[2,8,24,384]{3,2,1,0:T(8,128)(2,1)S(1)}, u32[]{:S(2)}, u32[]{:S(2)}) collective-permute-start(bf16[2,8,24,384]{3,2,1,0:T(8,128)(2,1)S(1)} %pad_maximum_fusion.1.own), channel_id=1, source_target_pairs={{2,0},{4,2},{6,4},{8,6},{10,8},{12,10},{14,12},{3,1},{5,3},{7,5},{... | collective-permute-start | bytes 884744 | tf_op jit(solution)/shard_map/ppermute | solution.py:24
  25.6 8.7 %copy-start.1 = (s32[4]{0:T(128)S(1)}, s32[4]{0:T(128)}, u32[]{:S(2)}) copy-start(s32[4]{0:T(128)} %pad_add_fusion.place) | copy-start | bytes 52
  32.4 30.1 %collective-permute-start.7 = (bf16[2,5,24,384]{3,2,1,0:T(8,128)(2,1)}, bf16[2,5,24,384]{3,2,1,0:T(8,128)(2,1)S(1)}, u32[]{:S(2)}, u32[]{:S(2)}) collective-permute-start(bf16[2,5,24,384]{3,2,1,0:T(8,128)(2,1)} %get-tuple-element.20), channel_id=1, source_target_pairs={{0,2},{2,4},{4,6},{6,8},{8,10},{10,12},{12,14},{1,3},{3,5},{5,7},{... | collective-permute-start | bytes 552968 | tf_op jit(solution)/shard_map/ppermute | solution.py:24
  34.3 3.3 %copy-start.4 = (bf16[10368,384]{1,0:T(8,128)(2,1)S(1)}, bf16[10368,384]{1,0:T(8,128)(2,1)}, u32[]{:S(2)}) copy-start(bf16[10368,384]{1,0:T(8,128)(2,1)} %param.26) | copy-start | bytes 23887876
  48.4 15.0 %collective-permute-start.4 = (bf16[4,48,384]{2,1,0:T(8,128)(2,1)S(1)}, bf16[4,48,384]{2,1,0:T(8,128)(2,1)S(1)}, u32[]{:S(2)}, u32[]{:S(2)}) collective-permute-start(bf16[4,48,384]{2,1,0:T(8,128)(2,1)S(1)} %first_block.1.blocked), channel_id=1, source_target_pairs={{0,2},{2,4},{4,6},{6,8},{8,10},{10,12},{12,14},{1,3},{3,5},{5,7},{... | collective-permute-start | bytes 442376 | tf_op jit(solution)/shard_map/ppermute | solution.py:24
  52.8 10.6 %collective-permute-start.5 = (bf16[4,48,384]{2,1,0:T(8,128)(2,1)S(1)}, bf16[4,48,384]{2,1,0:T(8,128)(2,1)S(1)}, u32[]{:S(2)}, u32[]{:S(2)}) collective-permute-start(bf16[4,48,384]{2,1,0:T(8,128)(2,1)S(1)} %first_block.1.blocked), channel_id=1, source_target_pairs={{2,0},{4,2},{6,4},{8,6},{10,8},{12,10},{14,12},{3,1},{5,3},{7,5},{... | collective-permute-start | bytes 442376 | tf_op jit(solution)/shard_map/ppermute | solution.py:24
  54.7 8.5 %collective-permute-start.8 = (bf16[2,5,24,384]{3,2,1,0:T(8,128)(2,1)S(1)}, bf16[2,5,24,384]{3,2,1,0:T(8,128)(2,1)S(1)}, u32[]{:S(2)}, u32[]{:S(2)}) collective-permute-start(bf16[2,5,24,384]{3,2,1,0:T(8,128)(2,1)S(1)} %get-tuple-element.21), channel_id=1, source_target_pairs={{2,0},{4,2},{6,4},{8,6},{10,8},{12,10},{14,12},{3,1},{5,3},{7,5},{... | collective-permute-start | bytes 552968 | tf_op jit(solution)/shard_map/ppermute | solution.py:24
  62.4 1.5 %copy-start = (bf16[1152,768]{1,0:T(8,128)(2,1)S(1)}, bf16[1152,768]{1,0:T(8,128)(2,1)}, u32[]{:S(2)}) copy-start(bf16[1152,768]{1,0:T(8,128)(2,1)} %weight_time.1) | copy-start | bytes 5308420
  62.4 1.5 %copy-start.2 = (f32[192]{0:T(256)S(1)}, f32[192]{0:T(256)}, u32[]{:S(2)}) copy-start(f32[192]{0:T(256)} %param.24) | copy-start | bytes 2308
  62.4 1.5 %copy-start.3 = (f32[192]{0:T(256)S(1)}, f32[192]{0:T(256)}, u32[]{:S(2)}) copy-start(f32[192]{0:T(256)} %param.25) | copy-start | bytes 2308
  92.3 2.8 %collective-permute-start.9 = (bf16[4,4,16,384]{3,2,1,0:T(8,128)(2,1)S(1)}, bf16[4,4,16,384]{3,2,1,0:T(8,128)(2,1)S(1)}, u32[]{:S(2)}, u32[]{:S(2)}) collective-permute-start(bf16[4,4,16,384]{3,2,1,0:T(8,128)(2,1)S(1)} %constant_dynamic-slice_fusion), channel_id=1, source_target_pairs={{0,16},{16,0},{1,17},{17,1},{2,18},{18,2},{3,19},{19,3},{4,20},{20... | collective-permute-start | bytes 589832 | tf_op jit(solution)/shard_map/ppermute | solution.py:18

commit v4 on v3

--- a/solution.py
+++ b/solution.py
@@ -196,6 +196,185 @@
     )(place, latent, arrived, one, two)
 
 
+def stack_kernel(place, mine, theirs, later, own, up, down):
+    del later
+    count = mine.shape[0] - 2
+    own[0], own[1] = mine[...], theirs[...]
+    for ref, y in ((up, 1), (down, 0)):
+        ref[0:count], ref[count : 2 * count] = mine[0:count], theirs[0:count]
+        here = lax.rem(y + place[1], 2) == 0
+        ref[2 * count :] = jnp.where(here, mine[count:], theirs[count:])
+
+
+def stack(place, mine, theirs, later):
+    units, wide, channels = mine.shape
+    vmem = pl.BlockSpec(memory_space=pltpu.VMEM)
+    lines = 2 * units - 2
+    return pl.pallas_call(
+        stack_kernel,
+        out_shape=[jax.ShapeDtypeStruct((2, units, wide, channels), BF16)]
+        + [jax.ShapeDtypeStruct((lines, wide, channels), BF16)] * 2,
+        in_specs=[pl.BlockSpec(memory_space=pltpu.SMEM)]
+        + [vmem] * 2
+        + [pl.BlockSpec(memory_space=pl.ANY)],
+        out_specs=[vmem] * 3,
+        name="stack",
+    )(place, mine, theirs, later)
+
+
+def tiles_kernel(time, three, four, own, up, down, low, high):
+    half = three.shape[-1]
+    slot = 0
+    for f in range(2):
+        for y in range(2):
+            line = time[f, y]
+            own[slot] = line
+            up[2 * f + y] = line
+            down[2 * f + y] = line
+            slot += 1
+    for ref, base, depth in ((three, 4, 2), (four, 8, 1)):
+        for f in range(2):
+            for y in range(4):
+                values = ref[f, y].astype(F32)
+                low[...] = values[:, :128]
+                high[:, 0 : half - 128] = values[:, 128:]
+                count = values.shape[0] // 2
+                even, odd = (
+                    jnp.concatenate(
+                        [part[pl.ds(o, count, stride=2), :] for part in (low, high)], axis=1
+                    )
+                    for o in range(2)
+                )
+                line = merge(even, odd, half).astype(BF16)
+                own[slot] = line
+                if y >= 4 - depth:
+                    up[base + depth * f + y - (4 - depth)] = line
+                if y < depth:
+                    down[base + depth * f + y] = line
+                slot += 1
+
+
+def pair_tiles(time, three, four):
+    tile, channels = time.shape[2:]
+    vmem = pl.BlockSpec(memory_space=pltpu.VMEM)
+    return pl.pallas_call(
+        tiles_kernel,
+        out_shape=[jax.ShapeDtypeStruct((n, tile, channels), BF16) for n in (20, 10, 10)],
+        in_specs=[vmem] * 3,
+        out_specs=[vmem] * 3,
+        scratch_shapes=[pltpu.VMEM((three.shape[2], 128), F32)] * 2,
+        name="pair_tiles",
+    )(time, three, four)
+
+
+def edges_kernel(place, own, above, below, edge):
+    left = place[1] == 0
+    slot = 0
+    for ref in (own, above, below):
+        for i in range(ref.shape[0]):
+            line = ref[i].astype(F32)
+            edge[slot] = jnp.where(left, line[-8:], line[:8]).astype(BF16)
+            slot += 1
+
+
+def tile_edges(place, own, above, below):
+    channels = own.shape[-1]
+    vmem = pl.BlockSpec(memory_space=pltpu.VMEM)
+    lines = own.shape[0] + above.shape[0] + below.shape[0]
+    return pl.pallas_call(
+        edges_kernel,
+        out_shape=jax.ShapeDtypeStruct((lines, 8, channels), BF16),
+        in_specs=[pl.BlockSpec(memory_space=pltpu.SMEM)] + [vmem] * 3,
+        out_specs=vmem,
+        name="tile_edges",
+    )(place, own, above, below)
+
+
+def windows_kernel(wide, place, own, above, below, edge, time, three, four):
+    first, left = place[0] == 0, place[1] == 0
+    part = wide - 2 * HALO
+    width = own.shape[1] + 16
+    empty = jnp.zeros((8, own.shape[-1]), F32)
+
+    def line(ref, index, slot):
+        side = edge[slot].astype(F32)
+        whole = jnp.concatenate(
+            [
+                jnp.where(left, empty, side),
+                ref[index].astype(F32),
+                jnp.where(left, side, empty),
+            ],
+            axis=0,
+        )
+        begin = 8 - HALO
+        low = pltpu.roll(whole, width - begin, 0)[:wide]
+        high = pltpu.roll(whole, width - begin - part, 0)[:wide]
+        return jnp.where(first, low, high)
+
+    def lines(ref, offset, begin, count):
+        return [line(ref, i, offset + i) for i in range(begin, begin + count)]
+
+    n = own.shape[0]
+    m = n + above.shape[0]
+    for f in range(2):
+        for ref, base, start, count, depth in (
+            (time, 0, 0, 2, 2),
+            (three, 4, 4, 4, 2),
+            (four, 12, 8, 4, 1),
+        ):
+            parts = lines(above, n, start + depth * f, depth)
+            parts += lines(own, 0, base + count * f, count)
+            parts += lines(below, m, start + depth * f, depth)
+            ref[f] = jnp.concatenate(parts, axis=0).astype(BF16)
+
+
+def tile_windows(place, own, above, below, edge, wide):
+    channels = own.shape[-1]
+    vmem = pl.BlockSpec(memory_space=pltpu.VMEM)
+    return pl.pallas_call(
+        functools.partial(windows_kernel, wide),
+        out_shape=[jax.ShapeDtypeStruct((2, n * wide, channels), BF16) for n in (6, 8, 6)],
+        in_specs=[pl.BlockSpec(memory_space=pltpu.SMEM)] + [vmem] * 4,
+        out_specs=[vmem] * 3,
+        name="tile_windows",
+    )(place, own, above, below, edge)
+
+
+def combine_kernel(wr, wu):
+    channels, half = wr.shape[1:]
+    chunk = 32
+
+    def combine(k, carry):
+        rows = pl.ds(aligned(k, chunk), chunk)
+        taken = [[wr[3 * dy + dx, rows, :].astype(F32) for dx in range(3)] for dy in range(3)]
+        gap = jnp.zeros((chunk, LANES - half), F32)
+        for slot, dys in enumerate(((0,), (1, 2), (0, 1), (2,))):
+            line = [sum(taken[dy][dx] for dy in dys) for dx in range(3)]
+            line = [jnp.concatenate([part, gap], axis=1) for part in line]
+            into = pl.ds(aligned(k, chunk) + (slot % 2) * channels, chunk)
+            wu[slot // 2, into, 0:channels] = merge(
+                line[1] + line[2], line[0] + line[1], half
+            ).astype(BF16)
+            wu[slot // 2, into, channels : 2 * channels] = merge(line[0], line[2], half).astype(
+                BF16
+            )
+        return carry
+
+    lax.fori_loop(0, channels // chunk, combine, 0)
+
+
+def combine_weights(weight):
+    channels = weight.shape[1]
+    vmem = pl.BlockSpec(memory_space=pltpu.VMEM)
+    return pl.pallas_call(
+        combine_kernel,
+        out_shape=jax.ShapeDtypeStruct((2, 2 * channels, 2 * channels), BF16),
+        in_specs=[vmem],
+        out_specs=vmem,
+        name="combine_weights",
+    )(weight)
+
+
 def first_kernel(
     wide,
     sizes,
@@ -207,6 +386,8 @@
     gain_two,
     weight_one,
     weight_two,
+    later_one,
+    later_two,
     out_ref,
     w1,
     w2,
@@ -221,7 +402,8 @@
     frames = own.shape[1] - 4
     height, width = sizes
     col, row = place[1], place[3]
-    pieces = (above, own, below)
+    units = frames + 2
+    del later_one, later_two
 
     def load(source, target, base):
         return [
@@ -236,17 +418,24 @@
     for copy in copies_one + copies_two:
         copy.start()
 
-    def rows_of(refs, index):
-        return jnp.concatenate(
-            [ref[lax.rem(y + col, 2), index].astype(F32) for ref in refs for y in range(2)], axis=0
-        )
+    slots = [lax.rem(y + col, 2) for y in range(2)]
+
+    def own_rows(index):
+        return [own[slot, index].astype(F32) for slot in slots]
+
+    def rows_of(index):
+        first = [above[slot * units + index].astype(F32) for slot in slots]
+        last = [below[slot * units + index].astype(F32) for slot in slots]
+        return jnp.concatenate(first + own_rows(index) + last, axis=0)
 
     for f in range(2):
-        store(x1e, x1o, f, rows_of(pieces, frames + f), 6, wide)
-        store(x2e, x2o, f, rows_of(pieces, frames + 2 + f)[wide : 5 * wide], 4, wide)
+        store(x1e, x1o, f, rows_of(frames + f), 6, wide)
+        first, last = above[2 * units + f].astype(F32), below[2 * units + f].astype(F32)
+        values = jnp.concatenate([first] + own_rows(units + f) + [last], axis=0)
+        store(x2e, x2o, f, values, 4, wide)
 
     def norm_one(f, carry):
-        values = activate(rows_of(pieces, f), gain_one[...], 1.0)
+        values = activate(rows_of(f), gain_one[...], 1.0)
         store(x1e, x1o, f + 2, values, 6, wide)
         return carry
 
@@ -266,7 +455,7 @@
 
     def residual(f, carry):
         size = 2 * wide
-        values = low_sum(acc, aligned(f, size), size) + rows_of((own,), f)
+        values = low_sum(acc, aligned(f, size), size) + jnp.concatenate(own_rows(f), axis=0)
         out_ref[f] = values.astype(BF16)
         return carry
 
@@ -280,8 +469,8 @@
     ]
 
 
-def first_block(place, pieces, gain_one, gain_two, weight_one, weight_two, sizes):
-    _, units, wide, channels = pieces[0].shape
+def first_block(place, pieces, gain_one, gain_two, weight_one, weight_two, later, sizes):
+    _, units, wide, channels = pieces[1].shape
     frames = units - 4
     slots = -(-3 * channels // LANES)
     vmem = pl.BlockSpec(memory_space=pltpu.VMEM)
@@ -289,7 +478,7 @@
     return pl.pallas_call(
         functools.partial(first_kernel, wide, sizes),
         out_shape=jax.ShapeDtypeStruct((frames, 2 * wide, channels), BF16),
-        in_specs=[pl.BlockSpec(memory_space=pltpu.SMEM)] + [vmem] * 5 + [anywhere] * 2,
+        in_specs=[pl.BlockSpec(memory_space=pltpu.SMEM)] + [vmem] * 5 + [anywhere] * 4,
         out_specs=vmem,
         scratch_shapes=[
             pltpu.VMEM((9, channels, slots * LANES), BF16),
@@ -299,14 +488,14 @@
             *planes(frames + 2, 4, wide, channels),
             pltpu.SemaphoreType.DMA((6,)),
         ],
-        compiler_params=pltpu.CompilerParams(vmem_limit_bytes=40 * 1024 * 1024),
+        compiler_params=pltpu.CompilerParams(vmem_limit_bytes=52 * 1024 * 1024),
         cost_estimate=pl.CostEstimate(
             flops=2 * 27 * channels * channels * frames * 6 * wide,
             bytes_accessed=2 * 54 * channels * channels,
             transcendentals=0,
         ),
         name="first_block",
-    )(place, *pieces, gain_one, gain_two, weight_one, weight_two)
+    )(place, *pieces, gain_one, gain_two, weight_one, weight_two, *later)
 
 
 def second_kernel(
@@ -321,14 +510,11 @@
     four_ref,
     gain_three,
     gain_four,
-    weight_time,
-    weight_up,
+    wt,
+    wu,
     weight_three,
     weight_four,
     out_ref,
-    wt,
-    wr,
-    wu,
     w3,
     s3,
     w4,
@@ -368,12 +554,8 @@
             ),
         ]
 
-    copy_time = pltpu.make_async_copy(weight_time, wt, sems.at[0])
-    copy_up = pltpu.make_async_copy(weight_up, wr, sems.at[1])
-    copies_three = load_high(weight_three, w3, s3, 2)
-    copies_four = load_high(weight_four, w4, s4, 5)
-    copy_time.start()
-    copy_up.start()
+    copies_three = load_high(weight_three, w3, s3, 0)
+    copies_four = load_high(weight_four, w4, s4, 3)
     for copy in copies_three + copies_four:
         copy.start()
 
@@ -382,12 +564,12 @@
         sides[0, :, 0 : LANES - half, :] = blank
         sides[1, :, half:LANES, :] = blank
 
-    mixed[0 : 2 * size, :] = time_ref[...]
+    for f in range(2):
+        mixed[f * size : (f + 1) * size, :] = time_ref[f]
     for f in range(frames):
         for i, ref in enumerate((above, blocked, below)):
             begin = (f + 2) * size + i * 2 * wide
             mixed[begin : begin + 2 * wide, :] = ref[f]
-    copy_time.wait()
 
     def mix(n, carry):
         lanes = pl.ds(pl.multiple_of(n * LANES, LANES), LANES)
@@ -409,27 +591,6 @@
         return carry
 
     lax.fori_loop(0, frames, double, 0)
-    copy_up.wait()
-
-    chunk = 16
-
-    def combine(k, carry):
-        rows = pl.ds(aligned(k, chunk), chunk)
-        taken = [[wr[3 * dy + dx, rows, :].astype(F32) for dx in range(3)] for dy in range(3)]
-        gap = jnp.zeros((chunk, LANES - half), F32)
-        for slot, dys in enumerate(((0,), (1, 2), (0, 1), (2,))):
-            line = [sum(taken[dy][dx] for dy in dys) for dx in range(3)]
-            line = [jnp.concatenate([part, gap], axis=1) for part in line]
-            into = pl.ds(aligned(k, chunk) + (slot % 2) * channels, chunk)
-            wu[slot // 2, into, 0:channels] = merge(
-                line[1] + line[2], line[0] + line[1], half
-            ).astype(BF16)
-            wu[slot // 2, into, channels : 2 * channels] = merge(line[0], line[2], half).astype(
-                BF16
-            )
-        return carry
-
-    lax.fori_loop(0, channels // chunk, combine, 0)
 
     for py in range(2):
 
@@ -509,12 +670,9 @@
     return pl.pallas_call(
         functools.partial(second_kernel, wide, sizes),
         out_shape=jax.ShapeDtypeStruct((count, 4, wide - 2 * HALO, channels), BF16),
-        in_specs=[pl.BlockSpec(memory_space=pltpu.SMEM)] + [vmem] * 8 + [anywhere] * 4,
+        in_specs=[pl.BlockSpec(memory_space=pltpu.SMEM)] + [vmem] * 10 + [anywhere] * 2,
         out_specs=vmem,
         scratch_shapes=[
-            pltpu.VMEM(weight_time.shape, BF16),
-            pltpu.VMEM(weight_up.shape, BF16),
-            pltpu.VMEM((2, 2 * channels, 2 * channels), BF16),
             pltpu.VMEM(weight_three.shape, BF16),
             pltpu.VMEM((2, 9, LANES, half), BF16),
             pltpu.VMEM(weight_four.shape, BF16),
@@ -525,7 +683,7 @@
             *planes(count + 2, 8, wide, channels),
             *planes(count + 2, 6, wide, channels),
             pltpu.VMEM((count * 4 * wide, channels), F32),
-            pltpu.SemaphoreType.DMA((8,)),
+            pltpu.SemaphoreType.DMA((6,)),
         ],
         compiler_params=pltpu.CompilerParams(vmem_limit_bytes=48 * 1024 * 1024),
         name="second_block",
@@ -565,9 +723,21 @@
     mine, theirs = pack(
         place, latent, arrived, cache_one[:, 0], cache_two[:, 0], wide, tile, part
     )
-    theirs = swapped(theirs, "cols")
-    own = jnp.stack([mine, theirs])
-    pieces = [shifted(own, "rows", 1), own, shifted(own, "rows", -1)]
+    weight_four, mine = lax.optimization_barrier((weight_four, mine))
+    weight_four = weight_four.reshape(9, 3 * half, half)
+    own, up, down = stack(place, mine, swapped(theirs, "cols"), weight_four)
+    pieces = [shifted(up, "rows", 1), own, shifted(down, "rows", -1)]
+
+    cache_time, cache_three, cache_four, weight_upsample, weight_three, _ = (
+        lax.optimization_barrier(
+            (cache_time, cache_three, cache_four, weight_upsample, weight_three, own)
+        )
+    )
+    weight_three = weight_three.reshape(9, 3 * half, half)
+    weight_upsample = weight_upsample.reshape(9, channels, half)
+    tiles, up, down = pair_tiles(cache_time, cache_three, cache_four)
+    above, below = shifted(up, "rows", 1), shifted(down, "rows", -1)
+
     blocked = first_block(
         place,
         pieces,
@@ -575,50 +745,29 @@
         gain_two.reshape(1, -1),
         weight_one.reshape(9, 3, channels, channels),
         weight_two.reshape(9, 3, channels, channels),
+        (weight_three, weight_upsample),
         sizes,
     )
     blocks = [shifted(blocked, "rows", 1), blocked, shifted(blocked, "rows", -1)]
 
-    def paired(array):
-        return array.reshape(array.shape[0], array.shape[1], tile, channels)
-
-    left = col == 0
-    cache_time, cache_three, cache_four, _ = lax.optimization_barrier(
-        (cache_time, cache_three, cache_four, mine)
+    above, below, weight_upsample, _ = lax.optimization_barrier(
+        (above, below, weight_upsample, blocked)
     )
-    tiles = jnp.concatenate([cache_time, paired(cache_three), paired(cache_four)], axis=1)
-    edge = jnp.where(left, tiles[:, :, tile - HALO :], tiles[:, :, :HALO])
-    edge = swapped(edge, "cols")
-    weight_upsample, weight_three, _ = lax.optimization_barrier(
-        (weight_upsample, weight_three, own)
-    )
-    weight_four, _ = lax.optimization_barrier((weight_four, blocked))
-    nothing = jnp.zeros_like(edge)
-    tiles = jnp.concatenate(
-        [jnp.where(left, nothing, edge), tiles, jnp.where(left, edge, nothing)], axis=2
-    )
-    tiles = lax.dynamic_slice_in_dim(tiles, section * part, wide, 2)
-    time, three, four = tiles[:, 0:2], tiles[:, 2:6], tiles[:, 6:10]
-    above = jnp.concatenate([time, three[:, 2:], four[:, 3:]], axis=1)
-    below = jnp.concatenate([time, three[:, :2], four[:, :1]], axis=1)
-    above, below, *_ = lax.optimization_barrier((above, below, *pieces))
-    above, below = shifted(above, "rows", 1), shifted(below, "rows", -1)
-    time = jnp.concatenate([above[:, 0:2], time, below[:, 0:2]], axis=1)
-    three = jnp.concatenate([above[:, 2:4], three, below[:, 2:4]], axis=1)
-    four = jnp.concatenate([above[:, 4:], four, below[:, 4:]], axis=1)
+    edge = swapped(tile_edges(place, tiles, above, below), "cols")
+    time, three, four = tile_windows(place, tiles, above, below, edge, wide)
 
     frames = second_block(
         place,
         blocks,
-        time.reshape(-1, channels),
-        three.reshape(2, -1, channels),
-        four.reshape(2, -1, channels),
+        time,
+        three,
+        four,
         (gain_three.reshape(1, -1), gain_four.reshape(1, -1)),
         (
             weight_time,
-            weight_upsample.reshape(9, channels, half),
-            weight_three.reshape(9, 3 * half, half),
-            weight_four.reshape(9, 3 * half, half),
+            combine_weights(weight_upsample),
+            weight_three,
+            weight_four,
         ),
         sizes,
         wide,

time: 97.6 us -> 99.3 us (1.017)
  Pallas kernels: 41.1 us -> 51.3 us
  waiting for transfers between devices: 10.9 us -> 1.69 us
  starting transfers between devices: 21.8 us -> 24.7 us
  other arithmetic: 2.08 us -> 0.69 us
    pallas_call x0 -> x5, Pallas kernels: none -> 13 us  [the longest x1 4.41 us: combine_weights(): pl.pallas_call(combine_kernel, out_shape=jax.ShapeDtypeStruct((2, 2 * cha...]
    ppermute x6, waiting for transfers between devices: 4.97 us -> 0.06 us  [shifted(): lax.ppermute(value, axis, [(source, source + steps) for source in range(i...]
    ppermute x4, waiting for transfers between devices: 5.92 us -> 1.63 us  [swapped(): return lax.ppermute(value, axis, [(0, 1), (1, 0)])]
    pallas_call x1, Pallas kernels: 28.4 us -> 25.3 us  [second_block(): pl.pallas_call(functools.partial(second_kernel, wide, sizes), out_shape=j...]
    reshape x2 -> x0, local copies, waits for them, and re-layouts: 2.36 us -> none  [paired(): return array.reshape(array.shape[0], array.shape[1], tile, channels)]
    ppermute x4, starting transfers between devices: 3.95 us -> 6.01 us  [swapped(): return lax.ppermute(value, axis, [(0, 1), (1, 0)])]
    unnamed x22 -> x36, local copies, waits for them, and re-layouts: 5.43 us -> 7.31 us
    concatenate x5 -> x0, other arithmetic: 1.19 us -> none  [the longest x1 0.73 us: body(): above = jnp.concatenate([time, three[:, 2:], four[:, 3:]], axis=1)]
  transfers between devices with their start and end apart: 10 -> 10, of which waited for: 6 -> 2; matrix products, arithmetic and copies ran while one was open for 14% -> 12% of each run, Pallas kernels for 11% -> 20%
where the time goes in v4:
time: 99.3 us; the launch traced here: 98.7 us
  Pallas kernels  51.3 us (52%)
  starting transfers between devices  24.7 us (25%)
  local copies, waits for them, and re-layouts  20 us (20%)
  waiting for transfers between devices  1.69 us (2%)
    pallas_call x1, Pallas kernels, second_block(): pl.pallas_call(functools.partial(second_kernel, wide, sizes), out_shape=j...  25.3 us
    ppermute x6, starting transfers between devices, shifted(): lax.ppermute(value, axis, [(source, source + steps) for source in range(i...  18.7 us
    pallas_call x1, Pallas kernels, first_block(): pl.pallas_call(functools.partial(first_kernel, wide, sizes), out_shape=ja...  11.1 us
    unnamed x36, local copies, waits for them, and re-layouts  7.31 us
    optimization_barrier x2, local copies, waits for them, and re-layouts, body(): lax.optimization_barrier((cache_time, cache_three, cache_four, weight_ups...  7.21 us
    ppermute x4, starting transfers between devices, swapped(): return lax.ppermute(value, axis, [(0, 1), (1, 0)])  6.01 us
    pallas_call x1, Pallas kernels, combine_weights(): pl.pallas_call(combine_kernel, out_shape=jax.ShapeDtypeStruct((2, 2 * cha...  4.41 us
    optimization_barrier x1, local copies, waits for them, and re-layouts, body(): weight_four, mine = lax.optimization_barrier((weight_four, mine))  4.3 us
  transfers between devices with their start and end apart: 10, of which 2 were waited for; matrix products, arithmetic and copies ran while one was open for 12% of the time, Pallas kernels for 20%

profile of v4, /device:TPU:9, one launch (start us, length us, event | category | flops | bytes accessed | tf_op | source)
XLA Modules:
  0.0 98.7 jit_solution(1342780856127501095)
XLA Ops:
  0.0 0.7 collective-permute-start
  0.7 0.6 pad_add_fusion.place
  1.8 0.6 copy-done.15
  2.5 1.9 %pack.1 = (bf16[8,24,384]{2,1,0:T(8,128)(2,1)}, bf16[8,24,384]{2,1,0:T(8,128)(2,1)}) custom-call(s32[4]{0:T(128)} %pad_add_fusion.place, bf16[2,64,384]{2,1,0:T(8,128)(2,1)} %bitcast.27, bf16[2,64,384]{2,1,0:T(8,128)(2,1)} %copy-done.15, bf16[2,64,384]{2,1,0:T(8,128)(2,1)} %bitcast.28, bf16[2,64,384]{2,1,0:T(8,128)(2,1)} %bitcast.29), custom_call_target="tpu_custom_call" | custom-call | tf_op jit(solution)/shard_map/pack/pallas_call | solution.py:189
  4.3 1.2 %collective-permute-start.1 = (bf16[8,24,384]{2,1,0:T(8,128)(2,1)}, bf16[8,24,384]{2,1,0:T(8,128)(2,1)S(1)}, u32[]{:S(2)}, u32[]{:S(2)}) collective-permute-start(bf16[8,24,384]{2,1,0:T(8,128)(2,1)} %get-tuple-element.28), channel_id=1, source_target_pairs={{0,1},{1,0},{2,3},{3,2},{4,5},{5,4},{6,7},{7,6},{8,9},{9,8},{10,11... | collective-permute-start | bytes 442376 | tf_op jit(solution)/shard_map/ppermute | solution.py:18
  5.5 4.3 %copy.17 = bf16[5184,192]{1,0:T(8,128)(2,1)} copy(bf16[5184,192]{0,1:T(8,128)(2,1)} %param.31) | data formatting | bytes 3981312 | tf_op jit(solution)/shard_map/optimization_barrier | solution.py:726
  9.9 0.7 copy-done.14
  10.5 2.0 %stack.21 = (bf16[2,8,24,384]{3,2,1,0:T(8,128)(2,1)}, bf16[14,24,384]{2,1,0:T(8,128)(2,1)}, bf16[14,24,384]{2,1,0:T(8,128)(2,1)}) custom-call(s32[4]{0:T(128)} %pad_add_fusion.place, bf16[8,24,384]{2,1,0:T(8,128)(2,1)} %get-tuple-element.27.mine, bf16[8,24,384]{2,1,0:T(8,128)(2,1)} %copy-done.14, bf16[9,576,192]{2,1,0:T(8,128)(2,1)} %bitcast.20), custom_call_target="tpu_custom_call" | custom-call | tf_op jit(solution)/shard_map/stack/pallas_call | solution.py:213
  12.5 3.1 %collective-permute-start.2 = (bf16[14,24,384]{2,1,0:T(8,128)(2,1)}, bf16[14,24,384]{2,1,0:T(8,128)(2,1)S(1)}, u32[]{:S(2)}, u32[]{:S(2)}) collective-permute-start(bf16[14,24,384]{2,1,0:T(8,128)(2,1)} %get-tuple-element.30), channel_id=1, source_target_pairs={{0,2},{2,4},{4,6},{6,8},{8,10},{10,12},{12,14},{1,3},{3,5},{5,7},{... | collective-permute-start | bytes 774152 | tf_op jit(solution)/shard_map/ppermute | solution.py:24
  15.7 3.0 %collective-permute-start.3 = (bf16[14,24,384]{2,1,0:T(8,128)(2,1)}, bf16[14,24,384]{2,1,0:T(8,128)(2,1)S(1)}, u32[]{:S(2)}, u32[]{:S(2)}) collective-permute-start(bf16[14,24,384]{2,1,0:T(8,128)(2,1)} %get-tuple-element.32), channel_id=1, source_target_pairs={{2,0},{4,2},{6,4},{8,6},{10,8},{12,10},{14,12},{3,1},{5,3},{7,5},{... | collective-permute-start | bytes 774152 | tf_op jit(solution)/shard_map/ppermute | solution.py:24
  18.7 2.2 %pair_tiles.1 = (bf16[20,32,384]{2,1,0:T(8,128)(2,1)}, bf16[10,32,384]{2,1,0:T(8,128)(2,1)}, bf16[10,32,384]{2,1,0:T(8,128)(2,1)}) custom-call(bf16[2,2,32,384]{3,2,1,0:T(8,128)(2,1)} %time, bf16[2,4,64,192]{3,2,1,0:T(8,128)(2,1)} %three, bf16[2,4,64,192]{3,2,1,0:T(8,128)(2,1)} %four), custom_call_target="tpu_custom_call" | custom-call | tf_op jit(solution)/shard_map/pair_tiles/pallas_call | solution.py:260
  21.0 2.2 %collective-permute-start.6 = (bf16[10,32,384]{2,1,0:T(8,128)(2,1)}, bf16[10,32,384]{2,1,0:T(8,128)(2,1)S(1)}, u32[]{:S(2)}, u32[]{:S(2)}) collective-permute-start(bf16[10,32,384]{2,1,0:T(8,128)(2,1)} %get-tuple-element.39), channel_id=1, source_target_pairs={{0,2},{2,4},{4,6},{6,8},{8,10},{10,12},{12,14},{1,3},{3,5},{5,7},{... | collective-permute-start | bytes 737288 | tf_op jit(solution)/shard_map/ppermute | solution.py:24
  23.2 3.9 %collective-permute-start.7 = (bf16[10,32,384]{2,1,0:T(8,128)(2,1)}, bf16[10,32,384]{2,1,0:T(8,128)(2,1)S(1)}, u32[]{:S(2)}, u32[]{:S(2)}) collective-permute-start(bf16[10,32,384]{2,1,0:T(8,128)(2,1)} %get-tuple-element.40), channel_id=1, source_target_pairs={{2,0},{4,2},{6,4},{8,6},{10,8},{12,10},{14,12},{3,1},{5,3},{7,5},{... | collective-permute-start | bytes 737288 | tf_op jit(solution)/shard_map/ppermute | solution.py:24
  27.2 3.5 %copy.18 = bf16[5184,192]{1,0:T(8,128)(2,1)} copy(bf16[5184,192]{0,1:T(8,128)(2,1)S(1)} %copy-done.10) | data formatting | bytes 3981312 | tf_op jit(solution)/shard_map/optimization_barrier | solution.py:732
  30.7 3.7 %copy.19 = bf16[3456,192]{1,0:T(8,128)(2,1)} copy(bf16[3456,192]{0,1:T(8,128)(2,1)} %param.29) | data formatting | bytes 2654208 | tf_op jit(solution)/shard_map/optimization_barrier | solution.py:732
  34.4 11.1 %first_block.1.blocked = bf16[4,48,384]{2,1,0:T(8,128)(2,1)S(1)} custom-call(s32[4]{0:T(128)S(1)} %copy-done.6, bf16[14,24,384]{2,1,0:T(8,128)(2,1)S(1)} %collective-permute-done.2.above, bf16[2,8,24,384]{3,2,1,0:T(8,128)(2,1)S(1)} %copy-done.3, bf16[14,24,384]{2,1,0:T(8,128)(2,1)S(1)} %collective-permute-done.3.below, f32[1,384]{1,0:T(1,128)S(1)} %reshape.35.gain_one, ...), custom_call_target="tpu_custom_call" | custom-call | flops 4586471424 | bytes 15925248 | tf_op jit(solution)/shard_map/first_block/pallas_call | solution.py:478
  45.6 0.7 copy-done.11
  46.3 2.0 %tile_edges.1 = bf16[40,8,384]{2,1,0:T(8,128)(2,1)} custom-call(s32[4]{0:T(128)} %pad_add_fusion.place, bf16[20,32,384]{2,1,0:T(8,128)(2,1)} %get-tuple-element.38.own, bf16[10,32,384]{2,1,0:T(8,128)(2,1)} %copy-done.11, bf16[10,32,384]{2,1,0:T(8,128)(2,1)} %copy-done.12), custom_call_target="tpu_custom_call" | custom-call | tf_op jit(solution)/shard_map/tile_edges/pallas_call | solution.py:284
  48.3 0.9 collective-permute-start.8
  49.3 2.0 %collective-permute-start.4 = (bf16[4,48,384]{2,1,0:T(8,128)(2,1)S(1)}, bf16[4,48,384]{2,1,0:T(8,128)(2,1)S(1)}, u32[]{:S(2)}, u32[]{:S(2)}) collective-permute-start(bf16[4,48,384]{2,1,0:T(8,128)(2,1)S(1)} %first_block.1.blocked), channel_id=1, source_target_pairs={{0,2},{2,4},{4,6},{6,8},{8,10},{10,12},{12,14},{1,3},{3,5},{5,7},{... | collective-permute-start | bytes 442376 | tf_op jit(solution)/shard_map/ppermute | solution.py:24
  51.3 4.4 %collective-permute-start.5 = (bf16[4,48,384]{2,1,0:T(8,128)(2,1)S(1)}, bf16[4,48,384]{2,1,0:T(8,128)(2,1)S(1)}, u32[]{:S(2)}, u32[]{:S(2)}) collective-permute-start(bf16[4,48,384]{2,1,0:T(8,128)(2,1)S(1)} %first_block.1.blocked), channel_id=1, source_target_pairs={{2,0},{4,2},{6,4},{8,6},{10,8},{12,10},{14,12},{3,1},{5,3},{7,5},{... | collective-permute-start | bytes 442376 | tf_op jit(solution)/shard_map/ppermute | solution.py:24
  55.7 4.4 %combine_weights.1.wu = bf16[2,768,768]{2,1,0:T(8,128)(2,1)} custom-call(bf16[9,384,192]{2,1,0:T(8,128)(2,1)} %bitcast.23), custom_call_target="tpu_custom_call" | custom-call | tf_op jit(solution)/shard_map/combine_weights/pallas_call | solution.py:369
  60.1 0.7 copy-done.13
  60.8 2.4 %tile_windows.1 = (bf16[2,144,384]{2,1,0:T(8,128)(2,1)}, bf16[2,192,384]{2,1,0:T(8,128)(2,1)}, bf16[2,144,384]{2,1,0:T(8,128)(2,1)}) custom-call(s32[4]{0:T(128)} %pad_add_fusion.place, bf16[20,32,384]{2,1,0:T(8,128)(2,1)} %get-tuple-element.38.own, bf16[10,32,384]{2,1,0:T(8,128)(2,1)} %copy-done.11, bf16[10,32,384]{2,1,0:T(8,128)(2,1)} %copy-done.12, ...), custom_call_target="tpu_custom_call" | custom-call | tf_op jit(solution)/shard_map/tile_windows/pallas_call | solution.py:334
  63.3 1.7 %copy-done = bf16[2,768,768]{2,1,0:T(8,128)(2,1)S(1)} copy-done((bf16[2,768,768]{2,1,0:T(8,128)(2,1)S(1)}, bf16[2,768,768]{2,1,0:T(8,128)(2,1)}, u32[]{:S(2)}) %copy-start) | copy-done | bytes 2359320
  65.0 1.0 copy-done.2
  65.9 0.9 copy-done.4
  66.9 0.9 copy-done.5
  67.8 25.3 %second_block.1 = bf16[8,4,16,384]{3,2,1,0:T(8,128)(2,1)S(1)} custom-call(s32[4]{0:T(128)S(1)} %copy-done.7, bf16[4,48,384]{2,1,0:T(8,128)(2,1)S(1)} %collective-permute-done.4.above, bf16[4,48,384]{2,1,0:T(8,128)(2,1)S(1)} %first_block.1.blocked, bf16[4,48,384]{2,1,0:T(8,128)(2,1)S(1)} %collective-permute-done.5.below, bf16[2,144,384]{2,1,0:T(8,128)(2,1)S(1)} %copy-done.4, ...), custom_call_target="tpu_custom_call" | custom-call | tf_op jit(solution)/shard_map/second_block/pallas_call | solution.py:670
  93.2 3.2 %collective-permute-start.9 = (bf16[4,4,16,384]{3,2,1,0:T(8,128)(2,1)S(1)}, bf16[4,4,16,384]{3,2,1,0:T(8,128)(2,1)S(1)}, u32[]{:S(2)}, u32[]{:S(2)}) collective-permute-start(bf16[4,4,16,384]{3,2,1,0:T(8,128)(2,1)S(1)} %constant_dynamic-slice_fusion), channel_id=1, source_target_pairs={{0,16},{16,0},{1,17},{17,1},{2,18},{18,2},{3,19},{19,3},{4,20},{20... | collective-permute-start | bytes 589832 | tf_op jit(solution)/shard_map/ppermute | solution.py:18
  96.4 1.1 %collective-permute-done.9 = bf16[4,4,16,384]{3,2,1,0:T(8,128)(2,1)S(1)} collective-permute-done((bf16[4,4,16,384]{3,2,1,0:T(8,128)(2,1)S(1)}, bf16[4,4,16,384]{3,2,1,0:T(8,128)(2,1)S(1)}, u32[]{:S(2)}, u32[]{:S(2)}) %collective-permute-start.9) | collective-permute-done | bytes 196640 | tf_op jit(solution)/shard_map/ppermute | solution.py:18
  97.5 1.1 %reshape.43 = bf16[4,4,64,192]{3,2,1,0:T(8,128)(2,1)} reshape(bf16[4,4,32,384]{3,2,1,0:T(8,128)(2,1)S(1)} %pad_maximum_fusion) | data formatting | bytes 786432 | tf_op jit(solution)/shard_map/reshape | solution.py:783
  (42 shorter events, 0.9 us)
Async XLA Ops:
  0.0 1.8 %collective-permute-start = (bf16[2,64,384]{2,1,0:T(8,128)(2,1)}, bf16[2,64,384]{2,1,0:T(8,128)(2,1)S(1)}, u32[]{:S(2)}, u32[]{:S(2)}) collective-permute-start(bf16[2,64,384]{2,1,0:T(8,128)(2,1)} %bitcast.26), channel_id=1, source_target_pairs={{0,16},{16,0},{1,17},{17,1},{2,18},{18,2},{3,19},{19,3},{4,20},{20... | collective-permute-start | bytes 294920 | tf_op jit(solution)/shard_map/ppermute | solution.py:18
  1.8 0.6 copy-start.15
  4.3 5.5 %collective-permute-start.1 = (bf16[8,24,384]{2,1,0:T(8,128)(2,1)}, bf16[8,24,384]{2,1,0:T(8,128)(2,1)S(1)}, u32[]{:S(2)}, u32[]{:S(2)}) collective-permute-start(bf16[8,24,384]{2,1,0:T(8,128)(2,1)} %get-tuple-element.28), channel_id=1, source_target_pairs={{0,1},{1,0},{2,3},{3,2},{4,5},{5,4},{6,7},{7,6},{8,9},{9,8},{10,11... | collective-permute-start | bytes 442376 | tf_op jit(solution)/shard_map/ppermute | solution.py:18
  9.8 8.8 %copy-start.16 = (f32[384]{0:T(512)S(1)}, f32[384]{0:T(512)}, u32[]{:S(2)}) copy-start(f32[384]{0:T(512)} %param.22) | copy-start | bytes 4612
  9.9 8.9 %copy-start.17 = (f32[384]{0:T(512)S(1)}, f32[384]{0:T(512)}, u32[]{:S(2)}) copy-start(f32[384]{0:T(512)} %param.23) | copy-start | bytes 4612
  9.9 17.3 %copy-start.10 = (bf16[5184,192]{0,1:T(8,128)(2,1)S(1)}, bf16[5184,192]{0,1:T(8,128)(2,1)}, u32[]{:S(2)}) copy-start(bf16[5184,192]{0,1:T(8,128)(2,1)} %param.30) | copy-start | bytes 5971972
  9.9 0.7 copy-start.14
  12.5 21.9 %collective-permute-start.2 = (bf16[14,24,384]{2,1,0:T(8,128)(2,1)}, bf16[14,24,384]{2,1,0:T(8,128)(2,1)S(1)}, u32[]{:S(2)}, u32[]{:S(2)}) collective-permute-start(bf16[14,24,384]{2,1,0:T(8,128)(2,1)} %get-tuple-element.30), channel_id=1, source_target_pairs={{0,2},{2,4},{4,6},{6,8},{8,10},{10,12},{12,14},{1,3},{3,5},{5,7},{... | collective-permute-start | bytes 774152 | tf_op jit(solution)/shard_map/ppermute | solution.py:24
  15.7 18.8 %collective-permute-start.3 = (bf16[14,24,384]{2,1,0:T(8,128)(2,1)}, bf16[14,24,384]{2,1,0:T(8,128)(2,1)S(1)}, u32[]{:S(2)}, u32[]{:S(2)}) collective-permute-start(bf16[14,24,384]{2,1,0:T(8,128)(2,1)} %get-tuple-element.32), channel_id=1, source_target_pairs={{2,0},{4,2},{6,4},{8,6},{10,8},{12,10},{14,12},{3,1},{5,3},{7,5},{... | collective-permute-start | bytes 774152 | tf_op jit(solution)/shard_map/ppermute | solution.py:24
  21.0 24.6 %collective-permute-start.6 = (bf16[10,32,384]{2,1,0:T(8,128)(2,1)}, bf16[10,32,384]{2,1,0:T(8,128)(2,1)S(1)}, u32[]{:S(2)}, u32[]{:S(2)}) collective-permute-start(bf16[10,32,384]{2,1,0:T(8,128)(2,1)} %get-tuple-element.39), channel_id=1, source_target_pairs={{0,2},{2,4},{4,6},{6,8},{8,10},{10,12},{12,14},{1,3},{3,5},{5,7},{... | collective-permute-start | bytes 737288 | tf_op jit(solution)/shard_map/ppermute | solution.py:24
  23.2 22.3 %collective-permute-start.7 = (bf16[10,32,384]{2,1,0:T(8,128)(2,1)}, bf16[10,32,384]{2,1,0:T(8,128)(2,1)S(1)}, u32[]{:S(2)}, u32[]{:S(2)}) collective-permute-start(bf16[10,32,384]{2,1,0:T(8,128)(2,1)} %get-tuple-element.40), channel_id=1, source_target_pairs={{2,0},{4,2},{6,4},{8,6},{10,8},{12,10},{14,12},{3,1},{5,3},{7,5},{... | collective-permute-start | bytes 737288 | tf_op jit(solution)/shard_map/ppermute | solution.py:24
  30.7 3.7 %copy-start.3 = (bf16[2,8,24,384]{3,2,1,0:T(8,128)(2,1)S(1)}, bf16[2,8,24,384]{3,2,1,0:T(8,128)(2,1)}, u32[]{:S(2)}) copy-start(bf16[2,8,24,384]{3,2,1,0:T(8,128)(2,1)} %get-tuple-element.31.own) | copy-start | bytes 884740
  30.7 3.7 %copy-start.6 = (s32[4]{0:T(128)S(1)}, s32[4]{0:T(128)}, u32[]{:S(2)}) copy-start(s32[4]{0:T(128)} %pad_add_fusion.place) | copy-start | bytes 52
  45.5 0.7 copy-start.11
  45.6 0.8 copy-start.12
  48.3 11.8 %collective-permute-start.8 = (bf16[40,8,384]{2,1,0:T(8,128)(2,1)}, bf16[40,8,384]{2,1,0:T(8,128)(2,1)S(1)}, u32[]{:S(2)}, u32[]{:S(2)}) collective-permute-start(bf16[40,8,384]{2,1,0:T(8,128)(2,1)} %tile_edges.1), channel_id=1, source_target_pairs={{0,1},{1,0},{2,3},{3,2},{4,5},{5,4},{6,7},{7,6},{8,9},{9,8},{10,11... | collective-permute-start | bytes 737288 | tf_op jit(solution)/shard_map/ppermute | solution.py:18
  49.3 14.0 %collective-permute-start.4 = (bf16[4,48,384]{2,1,0:T(8,128)(2,1)S(1)}, bf16[4,48,384]{2,1,0:T(8,128)(2,1)S(1)}, u32[]{:S(2)}, u32[]{:S(2)}) collective-permute-start(bf16[4,48,384]{2,1,0:T(8,128)(2,1)S(1)} %first_block.1.blocked), channel_id=1, source_target_pairs={{0,2},{2,4},{4,6},{6,8},{8,10},{10,12},{12,14},{1,3},{3,5},{5,7},{... | collective-permute-start | bytes 442376 | tf_op jit(solution)/shard_map/ppermute | solution.py:24
  51.3 12.0 %collective-permute-start.5 = (bf16[4,48,384]{2,1,0:T(8,128)(2,1)S(1)}, bf16[4,48,384]{2,1,0:T(8,128)(2,1)S(1)}, u32[]{:S(2)}, u32[]{:S(2)}) collective-permute-start(bf16[4,48,384]{2,1,0:T(8,128)(2,1)S(1)} %first_block.1.blocked), channel_id=1, source_target_pairs={{2,0},{4,2},{6,4},{8,6},{10,8},{12,10},{14,12},{3,1},{5,3},{7,5},{... | collective-permute-start | bytes 442376 | tf_op jit(solution)/shard_map/ppermute | solution.py:24
  55.7 7.6 %copy-start.1 = (bf16[1152,768]{1,0:T(8,128)(2,1)S(1)}, bf16[1152,768]{1,0:T(8,128)(2,1)}, u32[]{:S(2)}) copy-start(bf16[1152,768]{1,0:T(8,128)(2,1)} %wt.1) | copy-start | bytes 5308420
  55.7 7.6 %copy-start.7 = (s32[4]{0:T(128)S(1)}, s32[4]{0:T(128)}, u32[]{:S(2)}) copy-start(s32[4]{0:T(128)} %pad_add_fusion.place) | copy-start | bytes 52
  55.7 7.6 %copy-start.8 = (f32[192]{0:T(256)S(1)}, f32[192]{0:T(256)}, u32[]{:S(2)}) copy-start(f32[192]{0:T(256)} %param.24) | copy-start | bytes 2308
  55.7 7.6 %copy-start.9 = (f32[192]{0:T(256)S(1)}, f32[192]{0:T(256)}, u32[]{:S(2)}) copy-start(f32[192]{0:T(256)} %param.25) | copy-start | bytes 2308
  60.1 0.7 copy-start.13
  63.3 1.7 %copy-start = (bf16[2,768,768]{2,1,0:T(8,128)(2,1)S(1)}, bf16[2,768,768]{2,1,0:T(8,128)(2,1)}, u32[]{:S(2)}) copy-start(bf16[2,768,768]{2,1,0:T(8,128)(2,1)} %combine_weights.1.wu) | copy-start | bytes 7077892
  65.0 1.0 copy-start.2
  65.9 0.9 copy-start.4
  66.9 0.9 copy-start.5
  93.2 4.3 %collective-permute-start.9 = (bf16[4,4,16,384]{3,2,1,0:T(8,128)(2,1)S(1)}, bf16[4,4,16,384]{3,2,1,0:T(8,128)(2,1)S(1)}, u32[]{:S(2)}, u32[]{:S(2)}) collective-permute-start(bf16[4,4,16,384]{3,2,1,0:T(8,128)(2,1)S(1)} %constant_dynamic-slice_fusion), channel_id=1, source_target_pairs={{0,16},{16,0},{1,17},{17,1},{2,18},{18,2},{3,19},{19,3},{4,20},{20... | collective-permute-start | bytes 589832 | tf_op jit(solution)/shard_map/ppermute | solution.py:18

commit v5 on v3

v5 whole, which is shorter than its diff:
```python
import functools

import jax
import jax.numpy as jnp
from jax import lax
from jax.experimental import pallas as pl
from jax.experimental.pallas import tpu as pltpu
from jax.sharding import PartitionSpec as P

EPSILON = 1e-06
HALO = 4
LANES = 256
BF16 = jnp.bfloat16
F32 = jnp.float32


def swapped(value, axis):
    return lax.ppermute(value, axis, [(0, 1), (1, 0)])


def shifted(value, axis, steps):
    count = lax.axis_size(axis)
    initial, last = (max(0, -steps), min(count, count - steps))
    return lax.ppermute(value, axis, [(source, source + steps) for source in range(initial, last)])


def silu(scaled):
    half = scaled * 0.5
    return half * (1.0 + jnp.tanh(half))


def activate(values, gain, mask):
    mean = jnp.mean(values * values, axis=-1, keepdims=True)
    return silu(values * (lax.rsqrt(mean + EPSILON) * mask) * gain)


def activate_pairs(values, gain, mask):
    channels = values.shape[-1] // 2
    squares = values * values
    first = lax.broadcasted_iota(jnp.int32, (1, 2 * channels), 1) < channels
    total = jnp.sum(squares, axis=-1, keepdims=True)
    low = jnp.sum(jnp.where(first, squares, 0.0), axis=-1, keepdims=True)
    scale_low = lax.rsqrt(low / channels + EPSILON) * mask
    scale_high = lax.rsqrt((total - low) / channels + EPSILON) * mask
    return silu(values * jnp.where(first, scale_low, scale_high) * gain)


def merge(even, odd, channels):
    turned = pltpu.roll(odd, channels - 128, 1)
    first = lax.broadcasted_iota(jnp.int32, (1, 128), 1) < channels - 128
    middle = jnp.where(first, even[:, 128:], turned[:, :128])
    return jnp.concatenate([even[:, :128], middle, turned[:, 128:]], axis=1)


def aligned(index, size):
    return pl.multiple_of(index * size, 16)


def line_mask(place, wide, first, count, limit, width):
    columns = place[2] + lax.broadcasted_iota(jnp.int32, (wide, 1), 0)
    inside = jnp.where((columns >= 0) & (columns < width), 1.0, 0.0)
    lines = []
    for i in range(count):
        line = first + i
        lines.append(inside * jnp.where((line >= 0) & (line < limit), 1.0, 0.0))
    return jnp.concatenate(lines, axis=0)


def store(even, odd, slot, values, height, wide):
    even[pl.ds(slot * (height * wide), height * wide), :] = values.astype(BF16)
    odd[pl.ds(slot * ((height - 2) * wide), (height - 2) * wide), :] = values[
        wide : (height - 1) * wide
    ].astype(BF16)


def taps(even, odd, begin, count, height, wide, dt, dy, lanes=slice(None)):
    inner = (height - 2) * wide
    if dy == 1:
        parts = [odd[pl.ds((begin + f + dt) * inner, inner), lanes] for f in range(count)]
    else:
        parts = [
            even[pl.ds((begin + f + dt) * height * wide + dy * wide, inner), lanes]
            for f in range(count)
        ]
    return jnp.concatenate(parts, axis=0)


def low_product(acc, even, odd, count, height, wide, weights, copies):
    rows = count * (height - 2) * wide
    channels = weights.shape[1]
    lanes = 3 * channels
    waited = 0
    for n in range(-(-lanes // LANES)):
        begin, end = n * LANES, min((n + 1) * LANES, lanes)
        while waited * channels < end:
            copies[waited].wait()
            waited += 1
        total = None
        for first, last in ((0, 4), (4, 8), (8, 9)):
            left = jnp.concatenate(
                [
                    taps(even, odd, 0, count, height, wide, t // 3, t % 3)
                    for t in range(first, last)
                ],
                axis=1,
            )
            right = weights[first:last, :, begin:end].reshape((last - first) * channels, -1)
            part = jnp.dot(left, right, preferred_element_type=F32)
            total = part if total is None else total + part
        acc[n, 0:rows, 0 : end - begin] = total


def low_sum(acc, start, size):
    rows = pl.ds(start, size)
    before = jnp.concatenate([acc[0, rows, :], acc[1, rows, 0:128]], axis=1)
    center = jnp.concatenate([acc[1, rows, 128:256], acc[2, rows, :]], axis=1)
    after = jnp.concatenate([acc[3, rows, :], acc[4, rows, 0:128]], axis=1)
    return center + pltpu.roll(before, 1, 0) + pltpu.roll(after, size - 1, 0)


def transposed_dot(left, right):
    return lax.dot_general(left, right, (((1,), (1,)), ((), ())), preferred_element_type=F32)


def high_product(acc, even, odd, count, height, wide, weights):
    rows = count * (height - 2) * wide
    channels = weights.shape[1] // 9

    def column(n, carry):
        outputs = pl.ds(pl.multiple_of(n * LANES, LANES), LANES)
        total = None
        for first, last in ((0, 4), (4, 8), (8, 9)):
            left = jnp.concatenate(
                [
                    taps(even, odd, 0, count, height, wide, t // 3, t % 3)
                    for t in range(first, last)
                ],
                axis=1,
            )
            part = transposed_dot(left, weights[outputs, first * channels : last * channels])
            total = part if total is None else total + part
        acc[n, 0:rows, :] = total
        return carry

    lax.fori_loop(0, weights.shape[0] // LANES, column, 0)


def high_sum(acc, start, size):
    rows = pl.ds(start, size)
    center = jnp.concatenate([acc[0, rows, :], acc[1, rows, 0:128]], axis=1)
    side = jnp.concatenate([acc[1, rows, 128:256], acc[2, rows, :]], axis=1)
    channels = center.shape[1]
    first = lax.broadcasted_iota(jnp.int32, (1, channels), 1) < channels // 2
    return center + jnp.where(first, pltpu.roll(side, 1, 0), pltpu.roll(side, size - 1, 0))


def pack_kernel(
    wide,
    tile,
    part,
    place,
    latent,
    arrived,
    one,
    two,
    time,
    three,
    four,
    gain_one,
    gain_two,
    gain_three,
    gain_four,
    mine,
    theirs,
    tiles,
    gains,
    spread,
    low,
    high,
):
    section, col = place[0], place[1]
    width, channels = latent.shape[1:]
    half = three.shape[-1]
    empty = jnp.zeros((spread.shape[1] - width, channels), F32)

    def put(slot, values):
        spread[slot] = pltpu.roll(
            jnp.concatenate([values.astype(F32), empty], axis=0), HALO, 0
        )

    for i in range(2):
        put(2 * section + i, latent[i])
        put(2 * (1 - section) + i, arrived[i])
        put(4 + i, one[i])
        put(6 + i, two[i])
    for slot in range(8):
        for ref, which in ((mine, col), (theirs, 1 - col)):
            begin = pl.multiple_of(which * tile + section * part, 8)
            ref[slot] = spread[slot, pl.ds(begin, wide), :].astype(BF16)

    lines = [time[f, y].astype(F32) for f in range(2) for y in range(2)]
    for ref in (three, four):
        for f in range(2):
            for y in range(4):
                values = ref[f, y].astype(F32)
                low[...] = values[:, :128]
                high[:, 0 : half - 128] = values[:, 128:]
                count = values.shape[0] // 2
                even, odd = (
                    jnp.concatenate(
                        [lanes[pl.ds(o, count, stride=2), :] for lanes in (low, high)], axis=1
                    )
                    for o in range(2)
                )
                lines.append(merge(even, odd, half))
    for i, line in enumerate(lines):
        tiles[i] = line.astype(BF16)

    left = col == 0
    upper = lax.broadcasted_iota(jnp.int32, (8, 1), 0) < HALO
    blocks = []
    for i in range(0, len(lines), 2):
        one_line, two_line = lines[i], lines[i + 1]
        last = jnp.where(upper, pltpu.roll(one_line[-8:], HALO, 0), two_line[-8:])
        first = jnp.where(upper, one_line[:8], pltpu.roll(two_line[:8], HALO, 0))
        blocks.append(jnp.where(left, last, first))
    gap = jnp.zeros_like(blocks[0])
    count = wide // 8
    for i in range(theirs.shape[0] - 8):
        group = (blocks + [gap] * count)[i * count : (i + 1) * count]
        theirs[8 + i] = jnp.concatenate(group, axis=0).astype(BF16)

    pairs = [jnp.concatenate([g[...], g[...]], axis=1) for g in (gain_three, gain_four)]
    for i, values in enumerate([gain_one[...], gain_two[...]] + pairs):
        gains[i : i + 1, :] = values


def pack(place, latent, arrived, one, two, time, three, four, gains, wide, tile, part):
    width, channels = latent.shape[1:]
    vmem = pl.BlockSpec(memory_space=pltpu.VMEM)
    lines = 20
    extra = -(-lines * HALO // wide)
    return pl.pallas_call(
        functools.partial(pack_kernel, wide, tile, part),
        out_shape=[
            jax.ShapeDtypeStruct((8, wide, channels), BF16),
            jax.ShapeDtypeStruct((8 + extra, wide, channels), BF16),
            jax.ShapeDtypeStruct((lines, tile, channels), BF16),
            jax.ShapeDtypeStruct((8, channels), F32),
        ],
        in_specs=[pl.BlockSpec(memory_space=pltpu.SMEM)] + [vmem] * 11,
        out_specs=[vmem] * 4,
        scratch_shapes=[
            pltpu.VMEM((8, width + 16, channels), F32),
            pltpu.VMEM((three.shape[2], 128), F32),
            pltpu.VMEM((three.shape[2], 128), F32),
        ],
        name="pack",
    )(place, latent, arrived, one, two, time, three, four, *gains)


def stack_kernel(
    wide, place, mine, theirs, tiles, later, own, up, down, windows, tile_up, tile_down
):
    del later
    section, col = place[0], place[1]
    count = mine.shape[0] - 2
    own[0], own[1] = mine[...], theirs[0 : count + 2]
    for ref, y in ((up, 1), (down, 0)):
        ref[0:count], ref[count : 2 * count] = mine[0:count], theirs[0:count]
        here = lax.rem(y + col, 2) == 0
        ref[2 * count :] = jnp.where(here, mine[count:], theirs[count : count + 2])

    part = wide - 2 * HALO
    upper = lax.broadcasted_iota(jnp.int32, (8, 1), 0) < HALO
    groups = wide // 8
    for i in range(tiles.shape[0]):
        line = tiles[i].astype(F32)
        block = i // 2
        begin = block % groups * 8
        edge = theirs[count + 2 + block // groups].astype(F32)[begin : begin + 8]
        turned = pltpu.roll(edge, HALO, 0)
        before, after = (edge, turned) if i % 2 == 0 else (turned, edge)
        first = pltpu.roll(line, HALO, 0)[:wide]
        head = jnp.where(upper, jnp.where(col == 1, before, 0.0), first[:8])
        first = jnp.concatenate([head, first[8:]], axis=0)
        last = pltpu.roll(line, line.shape[0] - (part - HALO), 0)[:wide]
        tail = jnp.where(upper, last[-8:], jnp.where(col == 0, after, 0.0))
        last = jnp.concatenate([last[:-8], tail], axis=0)
        line = jnp.where(section == 0, first, last).astype(BF16)
        windows[i] = line
        if i < 4:
            tile_up[i] = line
            tile_down[i] = line
            continue
        f, y = (i - 4) % 8 // 4, (i - 4) % 4
        base, depth = (4, 2) if i < 12 else (8, 1)
        if y >= 4 - depth:
            tile_up[base + depth * f + y - (4 - depth)] = line
        if y < depth:
            tile_down[base + depth * f + y] = line


def stack(place, mine, theirs, tiles, later):
    units, wide, channels = mine.shape
    vmem = pl.BlockSpec(memory_space=pltpu.VMEM)
    lines = 2 * units - 2
    shapes = [(2, units), (lines,), (lines,), (tiles.shape[0],), (10,), (10,)]
    return pl.pallas_call(
        functools.partial(stack_kernel, wide),
        out_shape=[jax.ShapeDtypeStruct(shape + (wide, channels), BF16) for shape in shapes],
        in_specs=[pl.BlockSpec(memory_space=pltpu.SMEM)]
        + [vmem] * 3
        + [pl.BlockSpec(memory_space=pl.ANY)],
        out_specs=[vmem] * 6,
        name="stack",
    )(place, mine, theirs, tiles, later)


def align_kernel(weight, out):
    half = weight.shape[0]
    chunk = 16

    def move(k, carry):
        for t in range(9):
            base = 3 * t * half
            first = base // 128 * 128
            width = min(-(-(base + 3 * half - first) // 128) * 128, weight.shape[1] - first)
            values = weight[pl.ds(aligned(k, chunk), chunk), first : first + width].astype(F32)
            values = values[:, base - first : base - first + 3 * half]
            none = jnp.zeros((chunk, half), F32)
            blocks = (
                values[:, half:],
                values[:, : 2 * half],
                jnp.concatenate([none, values[:, :half]], axis=1),
                jnp.concatenate([values[:, 2 * half :], none], axis=1),
            )
            for n, block in enumerate(blocks):
                rows = pl.ds(aligned(k, chunk) + n * half, chunk)
                out[rows, 2 * half * t : 2 * half * (t + 1)] = block.astype(BF16)
        return carry

    lax.fori_loop(0, half // chunk, move, 0)


def align_weights(weight):
    half = weight.shape[1]
    vmem = pl.BlockSpec(memory_space=pltpu.VMEM)
    return pl.pallas_call(
        align_kernel,
        out_shape=jax.ShapeDtypeStruct((4 * half, 18 * half), BF16),
        in_specs=[vmem],
        out_specs=vmem,
        name="align_weights",
    )(weight.T)


def combine_kernel(weight, out):
    half = weight.shape[0]
    channels = weight.shape[1] // 9
    chunk = 16

    def combine(k, carry):
        rows = pl.ds(aligned(k, chunk), chunk)
        taken = [
            [
                weight[rows, (3 * dy + dx) * channels : (3 * dy + dx + 1) * channels].astype(F32)
                for dx in range(3)
            ]
            for dy in range(3)
        ]
        for slot, dys in enumerate(((0,), (1, 2), (0, 1), (2,))):
            line = [sum(taken[dy][dx] for dy in dys) for dx in range(3)]
            lanes = slice(slot % 2 * channels, (slot % 2 + 1) * channels)
            for n, block in enumerate((line[1] + line[2], line[0] + line[1], line[0], line[2])):
                into = pl.ds(aligned(k, chunk) + n * half, chunk)
                out[slot // 2, into, lanes] = block.astype(BF16)
        return carry

    lax.fori_loop(0, half // chunk, combine, 0)


def combine_weights(weight):
    channels = 2 * weight.shape[1]
    vmem = pl.BlockSpec(memory_space=pltpu.VMEM)
    return pl.pallas_call(
        combine_kernel,
        out_shape=jax.ShapeDtypeStruct((2, 2 * channels, 2 * channels), BF16),
        in_specs=[vmem],
        out_specs=vmem,
        name="combine_weights",
    )(weight.T)


def first_kernel(
    wide,
    sizes,
    place,
    above,
    own,
    below,
    gains,
    weight_one,
    weight_two,
    later_one,
    later_two,
    out_ref,
    w1,
    w2,
    acc,
    x1e,
    x1o,
    x2e,
    x2o,
    sems,
):
    channels = own.shape[-1]
    frames = own.shape[1] - 4
    height, width = sizes
    col, row = place[1], place[3]
    units = frames + 2
    del later_one, later_two

    def load(source, target, base):
        return [
            pltpu.make_async_copy(
                source.at[:, dx], target.at[:, :, pl.ds(dx * channels, channels)], sems.at[base + dx]
            )
            for dx in range(3)
        ]

    copies_one = load(weight_one, w1, 0)
    copies_two = load(weight_two, w2, 3)
    for copy in copies_one + copies_two:
        copy.start()

    slots = [lax.rem(y + col, 2) for y in range(2)]

    def own_rows(index):
        return [own[slot, index].astype(F32) for slot in slots]

    def rows_of(index):
        first = [above[slot * units + index].astype(F32) for slot in slots]
        last = [below[slot * units + index].astype(F32) for slot in slots]
        return jnp.concatenate(first + own_rows(index) + last, axis=0)

    for f in range(2):
        store(x1e, x1o, f, rows_of(frames + f), 6, wide)
        first, last = above[2 * units + f].astype(F32), below[2 * units + f].astype(F32)
        values = jnp.concatenate([first] + own_rows(units + f) + [last], axis=0)
        store(x2e, x2o, f, values, 4, wide)

    def norm_one(f, carry):
        values = activate(rows_of(f), gains[0:1, :], 1.0)
        store(x1e, x1o, f + 2, values, 6, wide)
        return carry

    lax.fori_loop(0, frames, norm_one, 0)
    low_product(acc, x1e, x1o, frames, 6, wide, w1, copies_one)

    mask = line_mask(place, wide, 2 * row - 1, 4, height, width)

    def norm_two(f, carry):
        size = 4 * wide
        values = activate(low_sum(acc, aligned(f, size), size), gains[1:2, :], mask)
        store(x2e, x2o, f + 2, values, 4, wide)
        return carry

    lax.fori_loop(0, frames, norm_two, 0)
    low_product(acc, x2e, x2o, frames, 4, wide, w2, copies_two)

    def residual(f, carry):
        size = 2 * wide
        values = low_sum(acc, aligned(f, size), size) + jnp.concatenate(own_rows(f), axis=0)
        out_ref[f] = values.astype(BF16)
        return carry

    lax.fori_loop(0, frames, residual, 0)


def planes(slots, height, wide, channels):
    return [
        pltpu.VMEM((slots * height * wide, channels), BF16),
        pltpu.VMEM((slots * (height - 2) * wide, channels), BF16),
    ]


def first_block(place, pieces, gains, weight_one, weight_two, later, sizes):
    _, units, wide, channels = pieces[1].shape
    frames = units - 4
    slots = -(-3 * channels // LANES)
    vmem = pl.BlockSpec(memory_space=pltpu.VMEM)
    anywhere = pl.BlockSpec(memory_space=pl.ANY)
    return pl.pallas_call(
        functools.partial(first_kernel, wide, sizes),
        out_shape=jax.ShapeDtypeStruct((frames, 2 * wide, channels), BF16),
        in_specs=[pl.BlockSpec(memory_space=pltpu.SMEM)] + [vmem] * 4 + [anywhere] * 4,
        out_specs=vmem,
        scratch_shapes=[
            pltpu.VMEM((9, channels, slots * LANES), BF16),
            pltpu.VMEM((9, channels, slots * LANES), BF16),
            pltpu.VMEM((slots, frames * 4 * wide, LANES), F32),
            *planes(frames + 2, 6, wide, channels),
            *planes(frames + 2, 4, wide, channels),
            pltpu.SemaphoreType.DMA((6,)),
        ],
        compiler_params=pltpu.CompilerParams(vmem_limit_bytes=46 * 1024 * 1024),
        cost_estimate=pl.CostEstimate(
            flops=2 * 27 * channels * channels * frames * 6 * wide,
            bytes_accessed=2 * 54 * channels * channels,
            transcendentals=0,
        ),
        name="first_block",
    )(place, *pieces, gains, weight_one, weight_two, *later)


def second_kernel(
    wide,
    sizes,
    place,
    above,
    blocked,
    below,
    tile_above,
    windows,
    tile_below,
    gains,
    weight_time,
    weight_up,
    weight_three,
    weight_four,
    out_ref,
    wt,
    wu,
    w3,
    w4,
    acc,
    mixed,
    de,
    do,
    x3e,
    x3o,
    x4e,
    x4o,
    lifted_ref,
    sems,
):
    channels = blocked.shape[-1]
    half = channels // 2
    size = 6 * wide
    frames = blocked.shape[0]
    count = 2 * frames
    height, width = sizes
    row = place[3]
    copies = [
        pltpu.make_async_copy(source, target, sems.at[i])
        for i, (source, target) in enumerate(
            ((weight_time, wt), (weight_up, wu), (weight_three, w3), (weight_four, w4))
        )
    ]
    for copy in copies:
        copy.start()

    def cached(start, base, lines, depth, f):
        parts = [tile_above[start + depth * f + i] for i in range(depth)]
        parts += [windows[base + lines * f + i] for i in range(lines)]
        parts += [tile_below[start + depth * f + i] for i in range(depth)]
        return jnp.concatenate([line.astype(F32) for line in parts], axis=0)

    for f in range(2):
        mixed[f * size : (f + 1) * size, :] = cached(0, 0, 2, 2, f).astype(BF16)
    for f in range(frames):
        for i, ref in enumerate((above, blocked, below)):
            begin = (f + 2) * size + i * 2 * wide
            mixed[begin : begin + 2 * wide, :] = ref[f]

    copies[0].wait()

    def mix(n, carry):
        lanes = pl.ds(pl.multiple_of(n * LANES, LANES), LANES)
        left = jnp.concatenate(
            [mixed[pl.ds(t * size, frames * size), :] for t in range(3)], axis=1
        )
        acc[n, 0 : frames * size, :] = jnp.dot(left, wt[:, lanes], preferred_element_type=F32)
        return carry

    lax.fori_loop(0, 2 * channels // LANES, mix, 0)
    mask_low = line_mask(place, wide, 2 * row - 2, 6, height, width)

    def double(t, carry):
        rows = pl.ds(aligned(t, size), size)
        first = jnp.concatenate([acc[0, rows, :], acc[1, rows, 0:128]], axis=1)
        second = jnp.concatenate([acc[1, rows, 128:256], acc[2, rows, :]], axis=1)
        store(de, do, 2 * t, first * mask_low, 6, wide)
        store(de, do, 2 * t + 1, second * mask_low, 6, wide)
        return carry

    lax.fori_loop(0, frames, double, 0)

    copies[1].wait()

    for py in range(2):

        def enlarge(n, carry):
            lanes = pl.ds(pl.multiple_of(n * LANES, LANES), LANES)
            left = jnp.concatenate(
                [taps(de, do, 0, count, 6, wide, 0, py), taps(de, do, 0, count, 6, wide, 0, py + 1)],
                axis=1,
            )
            acc[n, py * count * 4 * wide : (py + 1) * count * 4 * wide, :] = transposed_dot(
                left, wu[py, lanes, :]
            )
            return carry

        lax.fori_loop(0, 2 * channels // LANES, enlarge, 0)

    for f in range(2):
        store(x3e, x3o, f, cached(4, 4, 4, 2, f), 8, wide)
        store(x4e, x4o, f, cached(8, 12, 4, 1, f), 6, wide)
    gain3, gain4 = gains[2:3, :], gains[3:4, :]
    mask_three = line_mask(place, wide, 4 * row - 2, 8, 2 * height, width)
    part = 4 * wide

    def norm_three(f, carry):
        values = []
        for py in range(2):
            start = pl.multiple_of(py * count * part + f * part, 16)
            values.append(high_sum(acc, start, part).astype(BF16).astype(F32))
        lifted = jnp.concatenate(
            [values[h % 2][(h // 2) * wide : (h // 2 + 1) * wide] for h in range(8)], axis=0
        )
        lifted_ref[pl.ds(aligned(f, part), part), :] = lifted[2 * wide : 6 * wide]
        store(x3e, x3o, f + 2, activate_pairs(lifted, gain3, mask_three), 8, wide)
        return carry

    lax.fori_loop(0, count, norm_three, 0)
    copies[2].wait()
    high_product(acc, x3e, x3o, count, 8, wide, w3)

    mask_four = mask_three[wide : 7 * wide]

    def norm_four(f, carry):
        values = high_sum(acc, aligned(f, size), size)
        store(x4e, x4o, f + 2, activate_pairs(values, gain4, mask_four), 6, wide)
        return carry

    lax.fori_loop(0, count, norm_four, 0)
    copies[3].wait()
    high_product(acc, x4e, x4o, count, 6, wide, w4)

    def finish(f, carry):
        start = aligned(f, part)
        values = high_sum(acc, start, part) + lifted_ref[pl.ds(start, part), :]
        values = pltpu.roll(values, part - HALO, 0)
        for y in range(4):
            inner = wide - 2 * HALO
            out_ref[f, y] = values[y * wide : y * wide + inner].astype(BF16)
        return carry

    lax.fori_loop(0, count, finish, 0)


def second_block(place, pieces, tiles, gains, weights, sizes, wide):
    frames, _, channels = pieces[0].shape
    count = 2 * frames
    vmem = pl.BlockSpec(memory_space=pltpu.VMEM)
    anywhere = pl.BlockSpec(memory_space=pl.ANY)
    return pl.pallas_call(
        functools.partial(second_kernel, wide, sizes),
        out_shape=jax.ShapeDtypeStruct((count, 4, wide - 2 * HALO, channels), BF16),
        in_specs=[pl.BlockSpec(memory_space=pltpu.SMEM)] + [vmem] * 7 + [anywhere] * 4,
        out_specs=vmem,
        scratch_shapes=[
            *(pltpu.VMEM(weight.shape, BF16) for weight in weights),
            pltpu.VMEM((3, 2 * count * 4 * wide, LANES), F32),
            pltpu.VMEM(((frames + 2) * 6 * wide, channels), BF16),
            *planes(count, 6, wide, channels),
            *planes(count + 2, 8, wide, channels),
            *planes(count + 2, 6, wide, channels),
            pltpu.VMEM((count * 4 * wide, channels), F32),
            pltpu.SemaphoreType.DMA((4,)),
        ],
        compiler_params=pltpu.CompilerParams(vmem_limit_bytes=44 * 1024 * 1024),
        name="second_block",
    )(place, *pieces, *tiles, gains, *weights)


def body(
    latent,
    cache_one,
    cache_two,
    cache_time,
    cache_three,
    cache_four,
    gain_one,
    gain_two,
    gain_three,
    gain_four,
    weight_one,
    weight_two,
    weight_time,
    weight_upsample,
    weight_three,
    weight_four,
):
    section, row, col = (lax.axis_index(name) for name in ("section", "rows", "cols"))
    sections, row_count, col_count = (lax.axis_size(name) for name in ("section", "rows", "cols"))
    width, channels = latent.shape[2:]
    tile = width // col_count
    part = tile // sections
    wide = part + 2 * HALO
    half = weight_three.shape[1]
    sizes = (2 * row_count, width)
    place = jnp.stack([section, col, col * tile + section * part - HALO, row]).astype(jnp.int32)

    latent = latent.reshape(latent.shape[0], width, channels)
    arrived = swapped(latent, "section")
    mine, theirs, tiles, gains = pack(
        place,
        latent,
        arrived,
        cache_one[:, 0],
        cache_two[:, 0],
        cache_time,
        cache_three,
        cache_four,
        [gain.reshape(1, -1) for gain in (gain_one, gain_two, gain_three, gain_four)],
        wide,
        tile,
        part,
    )
    weight_three, mine = lax.optimization_barrier((weight_three, mine))
    weight_three = align_weights(weight_three)
    own, up, down, windows, tile_up, tile_down = stack(
        place, mine, swapped(theirs, "cols"), tiles, weight_three
    )
    pieces = [shifted(up, "rows", 1), own, shifted(down, "rows", -1)]
    tiles = [shifted(tile_up, "rows", 1), windows, shifted(tile_down, "rows", -1)]
    weight_upsample, weight_four, own = lax.optimization_barrier(
        (weight_upsample, weight_four, own)
    )
    weight_upsample = combine_weights(weight_upsample)
    weight_four = align_weights(weight_four)
    blocked = first_block(
        place,
        pieces,
        gains,
        weight_one.reshape(9, 3, channels, channels),
        weight_two.reshape(9, 3, channels, channels),
        (weight_upsample, weight_four),
        sizes,
    )
    blocks = [shifted(blocked, "rows", 1), blocked, shifted(blocked, "rows", -1)]
    frames = second_block(
        place,
        blocks,
        tiles,
        gains,
        (weight_time, weight_upsample, weight_three, weight_four),
        sizes,
        wide,
    )
    count = frames.shape[0] // sections
    given = lax.dynamic_slice_in_dim(frames, (1 - section) * count, count, 0)
    kept = lax.dynamic_slice_in_dim(frames, section * count, count, 0)
    arrived = swapped(given, "section")
    low = section == 0
    joined = jnp.concatenate(
        [jnp.where(low, kept, arrived), jnp.where(low, arrived, kept)], axis=2
    )
    return joined.reshape(count, 4, 2 * tile, half)


def solution(mesh):
    placed = (
        P("section", ("rows", "cols"), None, None),
        P(None, ("rows", "cols"), None, None),
        P(None, ("rows", "cols"), None, None),
        P(None, "rows", "cols", None),
        P(None, "rows", "cols", None),
        P(None, "rows", "cols", None),
    ) + (P(),) * 10
    return jax.shard_map(
        body,
        mesh=mesh,
        in_specs=placed,
        out_specs=P("section", "rows", "cols", None),
        check_vma=False,
    )
```

time: 97.6 us -> 95 us (0.973)
  Pallas kernels: 41.1 us -> 54.7 us
  local copies, waits for them, and re-layouts: 20.2 us -> 9.65 us
  waiting for transfers between devices: 10.9 us -> 6.86 us
  other arithmetic: 2.08 us -> 0.75 us
    pallas_call x0 -> x4, Pallas kernels: none -> 16.9 us  [the longest x2 11.2 us: align_weights(): pl.pallas_call(align_kernel, out_shape=jax.ShapeDtypeStruct((4 * half, 18...]
    optimization_barrier x3 -> x0, local copies, waits for them, and re-layouts: 11.1 us -> none  [the longest x2 6.81 us: body(): lax.optimization_barrier((weight_upsample, weight_three, own))]
    ppermute x4 -> x3, waiting for transfers between devices: 5.92 us -> 1.64 us  [swapped(): return lax.ppermute(value, axis, [(0, 1), (1, 0)])]
    pallas_call x1, Pallas kernels: 28.4 us -> 24.2 us  [second_block(): pl.pallas_call(functools.partial(second_kernel, wide, sizes), out_shape=j...]
    concatenate x5 -> x0, other arithmetic: 1.19 us -> none  [the longest x1 0.73 us: body(): above = jnp.concatenate([time, three[:, 2:], four[:, 3:]], axis=1)]
    ppermute x4 -> x3, starting transfers between devices: 3.95 us -> 3.19 us  [swapped(): return lax.ppermute(value, axis, [(0, 1), (1, 0)])]
    unnamed x22 -> x24, local copies, waits for them, and re-layouts: 5.43 us -> 6.02 us
    reshape x4 -> x2, local copies, waits for them, and re-layouts: 2.37 us -> 2.48 us  [body(): gain.reshape(1, -1)]
  transfers between devices with their start and end apart: 10 -> 9, of which waited for: 6 -> 4; matrix products, arithmetic and copies ran while one was open for 14% -> 3% of each run, Pallas kernels for 11% -> 27%
where the time goes in v5:
time: 95 us; the launch traced here: 93.9 us
  Pallas kernels  54.7 us (58%)
  starting transfers between devices  21.7 us (23%)
  local copies, waits for them, and re-layouts  9.65 us (10%)
  waiting for transfers between devices  6.86 us (7%)
    pallas_call x1, Pallas kernels, second_block(): pl.pallas_call(functools.partial(second_kernel, wide, sizes), out_shape=j...  24.2 us
    ppermute x6, starting transfers between devices, shifted(): lax.ppermute(value, axis, [(source, source + steps) for source in range(i...  18.5 us
    pallas_call x2, Pallas kernels, align_weights(): pl.pallas_call(align_kernel, out_shape=jax.ShapeDtypeStruct((4 * half, 18...  11.2 us
    pallas_call x1, Pallas kernels, first_block(): pl.pallas_call(functools.partial(first_kernel, wide, sizes), out_shape=ja...  11.1 us
    unnamed x24, local copies, waits for them, and re-layouts  6.02 us
    ppermute x6, waiting for transfers between devices, shifted(): lax.ppermute(value, axis, [(source, source + steps) for source in range(i...  5.22 us
    pallas_call x1, Pallas kernels, combine_weights(): pl.pallas_call(combine_kernel, out_shape=jax.ShapeDtypeStruct((2, 2 * cha...  3.26 us
    ppermute x3, starting transfers between devices, swapped(): return lax.ppermute(value, axis, [(0, 1), (1, 0)])  3.19 us
  transfers between devices with their start and end apart: 9, of which 4 were waited for; matrix products, arithmetic and copies ran while one was open for 3% of the time, Pallas kernels for 27%

profile of v5, /device:TPU:9, one launch (start us, length us, event | category | flops | bytes accessed | tf_op | source)
XLA Modules:
  0.0 93.9 jit_solution(9145238053786577406)
XLA Ops:
  0.0 0.7 collective-permute-start
  0.7 1.3 %reshape.25.gain_one = f32[1,384]{1,0:T(1,128)} reshape(f32[384]{0:T(512)} %param.22) | data formatting | bytes 3072 | tf_op jit(solution)/shard_map/reshape | solution.py:727
  1.9 1.2 %reshape.26.gain_two = f32[1,384]{1,0:T(1,128)} reshape(f32[384]{0:T(512)} %param.23) | data formatting | bytes 3072 | tf_op jit(solution)/shard_map/reshape | solution.py:727
  3.2 0.7 pad_add_fusion.place
  3.8 0.6 copy-done.11
  4.5 2.5 %pack.1 = (bf16[8,24,384]{2,1,0:T(8,128)(2,1)}, bf16[12,24,384]{2,1,0:T(8,128)(2,1)}, bf16[20,32,384]{2,1,0:T(8,128)(2,1)}, f32[8,384]{1,0:T(8,128)}) custom-call(s32[4]{0:T(128)} %pad_add_fusion.place, bf16[2,64,384]{2,1,0:T(8,128)(2,1)} %bitcast.22, bf16[2,64,384]{2,1,0:T(8,128)(2,1)} %copy-done.11, bf16[2,64,384]{2,1,0:T(8,128)(2,1)} %bitcast.23, ...), custom_call_target="tpu_custom_call" | custom-call | tf_op jit(solution)/shard_map/pack/pallas_call | solution.py:243
  7.0 1.2 %collective-permute-start.1 = (bf16[12,24,384]{2,1,0:T(8,128)(2,1)}, bf16[12,24,384]{2,1,0:T(8,128)(2,1)S(1)}, u32[]{:S(2)}, u32[]{:S(2)}) collective-permute-start(bf16[12,24,384]{2,1,0:T(8,128)(2,1)} %get-tuple-element.21), channel_id=1, source_target_pairs={{0,1},{1,0},{2,3},{3,2},{4,5},{5,4},{6,7},{7,6},{8,9},{9,8},{10,11... | collective-permute-start | bytes 663560 | tf_op jit(solution)/shard_map/ppermute | solution.py:18
  8.2 5.5 %align_weights.2.later.weight_three = bf16[768,3456]{1,0:T(8,128)(2,1)} custom-call(bf16[192,5184]{1,0:T(8,128)(2,1)} %bitcast.18), custom_call_target="tpu_custom_call" | custom-call | tf_op jit(solution)/shard_map/align_weights/pallas_call | solution.py:349
  13.7 0.6 collective-permute-done.1.theirs
  14.2 0.7 copy-done.10
  14.9 2.5 %stack.21 = (bf16[2,8,24,384]{3,2,1,0:T(8,128)(2,1)}, bf16[14,24,384]{2,1,0:T(8,128)(2,1)}, bf16[14,24,384]{2,1,0:T(8,128)(2,1)}, bf16[20,24,384]{2,1,0:T(8,128)...) custom-call(s32[4]{0:T(128)} %pad_add_fusion.place, bf16[8,24,384]{2,1,0:T(8,128)(2,1)} %get-tuple-element.20.mine, ...), custom_call_target="tpu_custom_call" | custom-call | tf_op jit(solution)/shard_map/stack/pallas_call | solution.py:309
  17.4 3.1 %collective-permute-start.2 = (bf16[14,24,384]{2,1,0:T(8,128)(2,1)}, bf16[14,24,384]{2,1,0:T(8,128)(2,1)S(1)}, u32[]{:S(2)}, u32[]{:S(2)}) collective-permute-start(bf16[14,24,384]{2,1,0:T(8,128)(2,1)} %get-tuple-element.24), channel_id=1, source_target_pairs={{0,2},{2,4},{4,6},{6,8},{8,10},{10,12},{12,14},{1,3},{3,5},{5,7},{... | collective-permute-start | bytes 774152 | tf_op jit(solution)/shard_map/ppermute | solution.py:24
  20.5 3.0 %collective-permute-start.3 = (bf16[14,24,384]{2,1,0:T(8,128)(2,1)}, bf16[14,24,384]{2,1,0:T(8,128)(2,1)S(1)}, u32[]{:S(2)}, u32[]{:S(2)}) collective-permute-start(bf16[14,24,384]{2,1,0:T(8,128)(2,1)} %get-tuple-element.26), channel_id=1, source_target_pairs={{2,0},{4,2},{6,4},{8,6},{10,8},{12,10},{14,12},{3,1},{5,3},{7,5},{... | collective-permute-start | bytes 774152 | tf_op jit(solution)/shard_map/ppermute | solution.py:24
  23.6 3.3 %combine_weights.1.later_one.weight_up = bf16[2,768,768]{2,1,0:T(8,128)(2,1)} custom-call(bf16[192,3456]{1,0:T(8,128)(2,1)} %bitcast.20), custom_call_target="tpu_custom_call" | custom-call | tf_op jit(solution)/shard_map/combine_weights/pallas_call | solution.py:386
  26.9 5.7 %align_weights.3.later_two.weight_four = bf16[768,3456]{1,0:T(8,128)(2,1)} custom-call(bf16[192,5184]{1,0:T(8,128)(2,1)} %bitcast.19), custom_call_target="tpu_custom_call" | custom-call | tf_op jit(solution)/shard_map/align_weights/pallas_call | solution.py:349
  32.5 2.2 %collective-permute-start.6 = (bf16[10,24,384]{2,1,0:T(8,128)(2,1)}, bf16[10,24,384]{2,1,0:T(8,128)(2,1)}, u32[]{:S(2)}, u32[]{:S(2)}) collective-permute-start(bf16[10,24,384]{2,1,0:T(8,128)(2,1)} %get-tuple-element.30), channel_id=1, source_target_pairs={{0,2},{2,4},{4,6},{6,8},{8,10},{10,12},{12,14},{1,3},{3,5},{5,7},{... | collective-permute-start | bytes 552968 | tf_op jit(solution)/shard_map/ppermute | solution.py:24
  34.8 3.9 %collective-permute-start.7 = (bf16[10,24,384]{2,1,0:T(8,128)(2,1)}, bf16[10,24,384]{2,1,0:T(8,128)(2,1)}, u32[]{:S(2)}, u32[]{:S(2)}) collective-permute-start(bf16[10,24,384]{2,1,0:T(8,128)(2,1)} %get-tuple-element.32), channel_id=1, source_target_pairs={{2,0},{4,2},{6,4},{8,6},{10,8},{12,10},{14,12},{3,1},{5,3},{7,5},{... | collective-permute-start | bytes 552968 | tf_op jit(solution)/shard_map/ppermute | solution.py:24
  38.7 0.0 copy-start.4
  38.8 0.7 copy-done.4
  39.5 0.9 %copy-done.5 = bf16[14,24,384]{2,1,0:T(8,128)(2,1)S(1)} copy-done((bf16[14,24,384]{2,1,0:T(8,128)(2,1)S(1)}, bf16[14,24,384]{2,1,0:T(8,128)(2,1)}, u32[]{:S(2)}) %copy-start.5) | copy-done | bytes 258072
  40.4 11.1 %first_block.1.blocked = bf16[4,48,384]{2,1,0:T(8,128)(2,1)S(1)} custom-call(s32[4]{0:T(128)S(1)} %copy-done.9, bf16[14,24,384]{2,1,0:T(8,128)(2,1)S(1)} %collective-permute-done.2.above, bf16[2,8,24,384]{3,2,1,0:T(8,128)(2,1)S(1)} %copy-done.3, bf16[14,24,384]{2,1,0:T(8,128)(2,1)S(1)} %copy-done.5, f32[8,384]{1,0:T(8,128)S(1)} %copy-done.8, ...), custom_call_target="tpu_custom_call" | custom-call | flops 4586471424 | bytes 15925248 | tf_op jit(solution)/shard_map/first_block/pallas_call | solution.py:494
  51.5 2.0 %collective-permute-start.4 = (bf16[4,48,384]{2,1,0:T(8,128)(2,1)S(1)}, bf16[4,48,384]{2,1,0:T(8,128)(2,1)S(1)}, u32[]{:S(2)}, u32[]{:S(2)}) collective-permute-start(bf16[4,48,384]{2,1,0:T(8,128)(2,1)S(1)} %first_block.1.blocked), channel_id=1, source_target_pairs={{0,2},{2,4},{4,6},{6,8},{8,10},{10,12},{12,14},{1,3},{3,5},{5,7},{... | collective-permute-start | bytes 442376 | tf_op jit(solution)/shard_map/ppermute | solution.py:24
  53.5 4.1 %collective-permute-start.5 = (bf16[4,48,384]{2,1,0:T(8,128)(2,1)S(1)}, bf16[4,48,384]{2,1,0:T(8,128)(2,1)S(1)}, u32[]{:S(2)}, u32[]{:S(2)}) collective-permute-start(bf16[4,48,384]{2,1,0:T(8,128)(2,1)S(1)} %first_block.1.blocked), channel_id=1, source_target_pairs={{2,0},{4,2},{6,4},{8,6},{10,8},{12,10},{14,12},{3,1},{5,3},{7,5},{... | collective-permute-start | bytes 442376 | tf_op jit(solution)/shard_map/ppermute | solution.py:24
  57.7 0.6 collective-permute-done.4.above
  58.3 4.6 %collective-permute-done.5.below = bf16[4,48,384]{2,1,0:T(8,128)(2,1)S(1)} collective-permute-done((bf16[4,48,384]{2,1,0:T(8,128)(2,1)S(1)}, bf16[4,48,384]{2,1,0:T(8,128)(2,1)S(1)}, u32[]{:S(2)}, u32[]{:S(2)}) %collective-permute-start.5) | collective-permute-done | bytes 147488 | tf_op jit(solution)/shard_map/ppermute | solution.py:24
  62.9 0.7 copy-done.6
  63.6 1.5 %copy-done.1 = bf16[1152,768]{1,0:T(8,128)(2,1)S(1)} copy-done((bf16[1152,768]{1,0:T(8,128)(2,1)S(1)}, bf16[1152,768]{1,0:T(8,128)(2,1)}, u32[]{:S(2)}) %copy-start.1) | copy-done | bytes 1769496
  65.1 0.9 copy-done.7
  66.0 24.2 %second_block.1 = bf16[8,4,16,384]{3,2,1,0:T(8,128)(2,1)S(1)} custom-call(s32[4]{0:T(128)S(1)} %copy-done.9, bf16[4,48,384]{2,1,0:T(8,128)(2,1)S(1)} %collective-permute-done.4.above, bf16[4,48,384]{2,1,0:T(8,128)(2,1)S(1)} %first_block.1.blocked, bf16[4,48,384]{2,1,0:T(8,128)(2,1)S(1)} %copy-done.7, bf16[10,24,384]{2,1,0:T(8,128)(2,1)} %collective-permute-done.6.tile_above, ...), custom_call_target="tpu_custom_call" | custom-call | tf_op jit(solution)/shard_map/second_block/pallas_call | solution.py:668
  90.3 1.3 %collective-permute-start.8 = (bf16[4,4,16,384]{3,2,1,0:T(8,128)(2,1)S(1)}, bf16[4,4,16,384]{3,2,1,0:T(8,128)(2,1)S(1)}, u32[]{:S(2)}, u32[]{:S(2)}) collective-permute-start(bf16[4,4,16,384]{3,2,1,0:T(8,128)(2,1)S(1)} %constant_dynamic-slice_fusion), channel_id=1, source_target_pairs={{0,16},{16,0},{1,17},{17,1},{2,18},{18,2},{3,19},{19,3},{4,20},{20... | collective-permute-start | bytes 589832 | tf_op jit(solution)/shard_map/ppermute | solution.py:18
  91.6 1.1 %collective-permute-done.8 = bf16[4,4,16,384]{3,2,1,0:T(8,128)(2,1)S(1)} collective-permute-done((bf16[4,4,16,384]{3,2,1,0:T(8,128)(2,1)S(1)}, bf16[4,4,16,384]{3,2,1,0:T(8,128)(2,1)S(1)}, u32[]{:S(2)}, u32[]{:S(2)}) %collective-permute-start.8) | collective-permute-done | bytes 196640 | tf_op jit(solution)/shard_map/ppermute | solution.py:18
  92.7 1.1 %reshape.31 = bf16[4,4,64,192]{3,2,1,0:T(8,128)(2,1)} reshape(bf16[4,4,32,384]{3,2,1,0:T(8,128)(2,1)S(1)} %pad_maximum_fusion) | data formatting | bytes 786432 | tf_op jit(solution)/shard_map/reshape | solution.py:771
  (24 shorter events, 0.2 us)
Async XLA Ops:
  0.0 3.8 %collective-permute-start = (bf16[2,64,384]{2,1,0:T(8,128)(2,1)}, bf16[2,64,384]{2,1,0:T(8,128)(2,1)S(1)}, u32[]{:S(2)}, u32[]{:S(2)}) collective-permute-start(bf16[2,64,384]{2,1,0:T(8,128)(2,1)} %bitcast.21), channel_id=1, source_target_pairs={{0,16},{16,0},{1,17},{17,1},{2,18},{18,2},{3,19},{19,3},{4,20},{20... | collective-permute-start | bytes 294920 | tf_op jit(solution)/shard_map/ppermute | solution.py:18
  3.8 0.6 copy-start.11
  7.0 7.3 %collective-permute-start.1 = (bf16[12,24,384]{2,1,0:T(8,128)(2,1)}, bf16[12,24,384]{2,1,0:T(8,128)(2,1)S(1)}, u32[]{:S(2)}, u32[]{:S(2)}) collective-permute-start(bf16[12,24,384]{2,1,0:T(8,128)(2,1)} %get-tuple-element.21), channel_id=1, source_target_pairs={{0,1},{1,0},{2,3},{3,2},{4,5},{5,4},{6,7},{7,6},{8,9},{9,8},{10,11... | collective-permute-start | bytes 663560 | tf_op jit(solution)/shard_map/ppermute | solution.py:18
  14.2 0.7 copy-start.10
  17.4 21.3 %collective-permute-start.2 = (bf16[14,24,384]{2,1,0:T(8,128)(2,1)}, bf16[14,24,384]{2,1,0:T(8,128)(2,1)S(1)}, u32[]{:S(2)}, u32[]{:S(2)}) collective-permute-start(bf16[14,24,384]{2,1,0:T(8,128)(2,1)} %get-tuple-element.24), channel_id=1, source_target_pairs={{0,2},{2,4},{4,6},{6,8},{8,10},{10,12},{12,14},{1,3},{3,5},{5,7},{... | collective-permute-start | bytes 774152 | tf_op jit(solution)/shard_map/ppermute | solution.py:24
  20.5 18.2 %collective-permute-start.3 = (bf16[14,24,384]{2,1,0:T(8,128)(2,1)}, bf16[14,24,384]{2,1,0:T(8,128)(2,1)S(1)}, u32[]{:S(2)}, u32[]{:S(2)}) collective-permute-start(bf16[14,24,384]{2,1,0:T(8,128)(2,1)} %get-tuple-element.26), channel_id=1, source_target_pairs={{2,0},{4,2},{6,4},{8,6},{10,8},{12,10},{14,12},{3,1},{5,3},{7,5},{... | collective-permute-start | bytes 774152 | tf_op jit(solution)/shard_map/ppermute | solution.py:24
  26.8 12.6 %copy-start = (bf16[2,768,768]{2,1,0:T(8,128)(2,1)S(1)}, bf16[2,768,768]{2,1,0:T(8,128)(2,1)}, u32[]{:S(2)}) copy-start(bf16[2,768,768]{2,1,0:T(8,128)(2,1)} %combine_weights.1.later_one.weight_up) | copy-start | bytes 7077892
  26.8 12.6 %copy-start.3 = (bf16[2,8,24,384]{3,2,1,0:T(8,128)(2,1)S(1)}, bf16[2,8,24,384]{3,2,1,0:T(8,128)(2,1)}, u32[]{:S(2)}) copy-start(bf16[2,8,24,384]{3,2,1,0:T(8,128)(2,1)} %get-tuple-element.25.own) | copy-start | bytes 884740
  26.8 12.6 %copy-start.8 = (f32[8,384]{1,0:T(8,128)S(1)}, f32[8,384]{1,0:T(8,128)}, u32[]{:S(2)}) copy-start(f32[8,384]{1,0:T(8,128)} %get-tuple-element.27.gains) | copy-start | bytes 36868
  26.8 12.6 %copy-start.9 = (s32[4]{0:T(128)S(1)}, s32[4]{0:T(128)}, u32[]{:S(2)}) copy-start(s32[4]{0:T(128)} %pad_add_fusion.place) | copy-start | bytes 52
  32.5 25.2 %collective-permute-start.6 = (bf16[10,24,384]{2,1,0:T(8,128)(2,1)}, bf16[10,24,384]{2,1,0:T(8,128)(2,1)}, u32[]{:S(2)}, u32[]{:S(2)}) collective-permute-start(bf16[10,24,384]{2,1,0:T(8,128)(2,1)} %get-tuple-element.30), channel_id=1, source_target_pairs={{0,2},{2,4},{4,6},{6,8},{8,10},{10,12},{12,14},{1,3},{3,5},{5,7},{... | collective-permute-start | bytes 552968 | tf_op jit(solution)/shard_map/ppermute | solution.py:24
  34.8 22.9 %collective-permute-start.7 = (bf16[10,24,384]{2,1,0:T(8,128)(2,1)}, bf16[10,24,384]{2,1,0:T(8,128)(2,1)}, u32[]{:S(2)}, u32[]{:S(2)}) collective-permute-start(bf16[10,24,384]{2,1,0:T(8,128)(2,1)} %get-tuple-element.32), channel_id=1, source_target_pairs={{2,0},{4,2},{6,4},{8,6},{10,8},{12,10},{14,12},{3,1},{5,3},{7,5},{... | collective-permute-start | bytes 552968 | tf_op jit(solution)/shard_map/ppermute | solution.py:24
  38.7 0.7 copy-start.4
  39.5 0.9 %copy-start.5 = (bf16[14,24,384]{2,1,0:T(8,128)(2,1)S(1)}, bf16[14,24,384]{2,1,0:T(8,128)(2,1)}, u32[]{:S(2)}) copy-start(bf16[14,24,384]{2,1,0:T(8,128)(2,1)} %copy-done.4) | copy-start | bytes 774148
  40.4 23.2 %copy-start.2 = (bf16[20,24,384]{2,1,0:T(8,128)(2,1)S(1)}, bf16[20,24,384]{2,1,0:T(8,128)(2,1)}, u32[]{:S(2)}) copy-start(bf16[20,24,384]{2,1,0:T(8,128)(2,1)} %get-tuple-element.31.windows) | copy-start | bytes 1105924
  51.5 6.8 %collective-permute-start.4 = (bf16[4,48,384]{2,1,0:T(8,128)(2,1)S(1)}, bf16[4,48,384]{2,1,0:T(8,128)(2,1)S(1)}, u32[]{:S(2)}, u32[]{:S(2)}) collective-permute-start(bf16[4,48,384]{2,1,0:T(8,128)(2,1)S(1)} %first_block.1.blocked), channel_id=1, source_target_pairs={{0,2},{2,4},{4,6},{6,8},{8,10},{10,12},{12,14},{1,3},{3,5},{5,7},{... | collective-permute-start | bytes 442376 | tf_op jit(solution)/shard_map/ppermute | solution.py:24
  53.5 9.4 %collective-permute-start.5 = (bf16[4,48,384]{2,1,0:T(8,128)(2,1)S(1)}, bf16[4,48,384]{2,1,0:T(8,128)(2,1)S(1)}, u32[]{:S(2)}, u32[]{:S(2)}) collective-permute-start(bf16[4,48,384]{2,1,0:T(8,128)(2,1)S(1)} %first_block.1.blocked), channel_id=1, source_target_pairs={{2,0},{4,2},{6,4},{8,6},{10,8},{12,10},{14,12},{3,1},{5,3},{7,5},{... | collective-permute-start | bytes 442376 | tf_op jit(solution)/shard_map/ppermute | solution.py:24
  62.9 0.7 copy-start.6
  63.6 1.5 %copy-start.1 = (bf16[1152,768]{1,0:T(8,128)(2,1)S(1)}, bf16[1152,768]{1,0:T(8,128)(2,1)}, u32[]{:S(2)}) copy-start(bf16[1152,768]{1,0:T(8,128)(2,1)} %weight_time.1) | copy-start | bytes 5308420
  65.1 0.9 copy-start.7
  90.3 2.4 %collective-permute-start.8 = (bf16[4,4,16,384]{3,2,1,0:T(8,128)(2,1)S(1)}, bf16[4,4,16,384]{3,2,1,0:T(8,128)(2,1)S(1)}, u32[]{:S(2)}, u32[]{:S(2)}) collective-permute-start(bf16[4,4,16,384]{3,2,1,0:T(8,128)(2,1)S(1)} %constant_dynamic-slice_fusion), channel_id=1, source_target_pairs={{0,16},{16,0},{1,17},{17,1},{2,18},{18,2},{3,19},{19,3},{4,20},{20... | collective-permute-start | bytes 589832 | tf_op jit(solution)/shard_map/ppermute | solution.py:18

commit v6 on v5

--- a/solution.py
+++ b/solution.py
@@ -166,14 +166,9 @@
     time,
     three,
     four,
-    gain_one,
-    gain_two,
-    gain_three,
-    gain_four,
     mine,
     theirs,
     tiles,
-    gains,
     spread,
     low,
     high,
@@ -230,12 +225,8 @@
         group = (blocks + [gap] * count)[i * count : (i + 1) * count]
         theirs[8 + i] = jnp.concatenate(group, axis=0).astype(BF16)
 
-    pairs = [jnp.concatenate([g[...], g[...]], axis=1) for g in (gain_three, gain_four)]
-    for i, values in enumerate([gain_one[...], gain_two[...]] + pairs):
-        gains[i : i + 1, :] = values
-
-
-def pack(place, latent, arrived, one, two, time, three, four, gains, wide, tile, part):
+
+def pack(place, latent, arrived, one, two, time, three, four, wide, tile, part):
     width, channels = latent.shape[1:]
     vmem = pl.BlockSpec(memory_space=pltpu.VMEM)
     lines = 20
@@ -246,17 +237,17 @@
             jax.ShapeDtypeStruct((8, wide, channels), BF16),
             jax.ShapeDtypeStruct((8 + extra, wide, channels), BF16),
             jax.ShapeDtypeStruct((lines, tile, channels), BF16),
-            jax.ShapeDtypeStruct((8, channels), F32),
         ],
-        in_specs=[pl.BlockSpec(memory_space=pltpu.SMEM)] + [vmem] * 11,
-        out_specs=[vmem] * 4,
+        in_specs=[pl.BlockSpec(memory_space=pltpu.SMEM)] + [vmem] * 7,
+        out_specs=[vmem] * 3,
         scratch_shapes=[
             pltpu.VMEM((8, width + 16, channels), F32),
             pltpu.VMEM((three.shape[2], 128), F32),
             pltpu.VMEM((three.shape[2], 128), F32),
         ],
+        compiler_params=pltpu.CompilerParams(vmem_limit_bytes=8 * 1024 * 1024),
         name="pack",
-    )(place, latent, arrived, one, two, time, three, four, *gains)
+    )(place, latent, arrived, one, two, time, three, four)
 
 
 def stack_kernel(
@@ -313,6 +304,7 @@
         + [vmem] * 3
         + [pl.BlockSpec(memory_space=pl.ANY)],
         out_specs=[vmem] * 6,
+        compiler_params=pltpu.CompilerParams(vmem_limit_bytes=8 * 1024 * 1024),
         name="stack",
     )(place, mine, theirs, tiles, later)
 
@@ -320,24 +312,44 @@
 def align_kernel(weight, out):
     half = weight.shape[0]
     chunk = 16
+    tail = half - 128
+    low = lax.broadcasted_iota(jnp.int32, (1, 128), 1) < tail
 
     def move(k, carry):
+        here = aligned(k, chunk)
+        none = jnp.zeros((chunk, 128), F32)
         for t in range(9):
             base = 3 * t * half
             first = base // 128 * 128
-            width = min(-(-(base + 3 * half - first) // 128) * 128, weight.shape[1] - first)
-            values = weight[pl.ds(aligned(k, chunk), chunk), first : first + width].astype(F32)
-            values = values[:, base - first : base - first + 3 * half]
-            none = jnp.zeros((chunk, half), F32)
-            blocks = (
-                values[:, half:],
-                values[:, : 2 * half],
-                jnp.concatenate([none, values[:, :half]], axis=1),
-                jnp.concatenate([values[:, 2 * half :], none], axis=1),
-            )
+            last = min(first + 640, weight.shape[1])
+            values = weight[pl.ds(here, chunk), first:last].astype(F32)
+            if last < first + 640:
+                values = jnp.concatenate(
+                    [values[:, :512], jnp.concatenate([values[:, 512:], none[:, tail:]], axis=1)],
+                    axis=1,
+                )
+            turned = pltpu.roll(values, 640 - tail, 1)
+            tiles = [values[:, 128 * i : 128 * (i + 1)] for i in range(5)]
+            moved = [turned[:, 128 * i : 128 * (i + 1)] for i in range(5)]
+            if base == first:
+                blocks = (
+                    moved[1:4],
+                    tiles[0:3],
+                    [none, jnp.where(low, 0.0, moved[4]), moved[0]],
+                    [tiles[3], jnp.where(low, tiles[4], 0.0), none],
+                )
+            else:
+                blocks = (
+                    tiles[2:5],
+                    moved[0:3],
+                    [none, jnp.where(low, 0.0, tiles[0]), tiles[1]],
+                    [moved[3], jnp.where(low, moved[4], 0.0), none],
+                )
             for n, block in enumerate(blocks):
-                rows = pl.ds(aligned(k, chunk) + n * half, chunk)
-                out[rows, 2 * half * t : 2 * half * (t + 1)] = block.astype(BF16)
+                into = pl.ds(here + n * half, chunk)
+                out[into, 2 * half * t : 2 * half * (t + 1)] = jnp.concatenate(
+                    block, axis=1
+                ).astype(BF16)
         return carry
 
     lax.fori_loop(0, half // chunk, move, 0)
@@ -351,6 +363,7 @@
         out_shape=jax.ShapeDtypeStruct((4 * half, 18 * half), BF16),
         in_specs=[vmem],
         out_specs=vmem,
+        compiler_params=pltpu.CompilerParams(vmem_limit_bytes=8 * 1024 * 1024),
         name="align_weights",
     )(weight.T)
 
@@ -388,6 +401,7 @@
         out_shape=jax.ShapeDtypeStruct((2, 2 * channels, 2 * channels), BF16),
         in_specs=[vmem],
         out_specs=vmem,
+        compiler_params=pltpu.CompilerParams(vmem_limit_bytes=8 * 1024 * 1024),
         name="combine_weights",
     )(weight.T)
 
@@ -402,8 +416,7 @@
     gains,
     weight_one,
     weight_two,
-    later_one,
-    later_two,
+    later,
     out_ref,
     w1,
     w2,
@@ -419,7 +432,7 @@
     height, width = sizes
     col, row = place[1], place[3]
     units = frames + 2
-    del later_one, later_two
+    del later
 
     def load(source, target, base):
         return [
@@ -494,7 +507,10 @@
     return pl.pallas_call(
         functools.partial(first_kernel, wide, sizes),
         out_shape=jax.ShapeDtypeStruct((frames, 2 * wide, channels), BF16),
-        in_specs=[pl.BlockSpec(memory_space=pltpu.SMEM)] + [vmem] * 4 + [anywhere] * 4,
+        in_specs=[pl.BlockSpec(memory_space=pltpu.SMEM)]
+        + [vmem] * 4
+        + [pl.BlockSpec(memory_space=pltpu.HBM)] * 2
+        + [anywhere],
         out_specs=vmem,
         scratch_shapes=[
             pltpu.VMEM((9, channels, slots * LANES), BF16),
@@ -504,14 +520,14 @@
             *planes(frames + 2, 4, wide, channels),
             pltpu.SemaphoreType.DMA((6,)),
         ],
-        compiler_params=pltpu.CompilerParams(vmem_limit_bytes=46 * 1024 * 1024),
+        compiler_params=pltpu.CompilerParams(vmem_limit_bytes=50 * 1024 * 1024),
         cost_estimate=pl.CostEstimate(
             flops=2 * 27 * channels * channels * frames * 6 * wide,
             bytes_accessed=2 * 54 * channels * channels,
             transcendentals=0,
         ),
         name="first_block",
-    )(place, *pieces, gains, weight_one, weight_two, *later)
+    )(place, *pieces, gains, weight_one, weight_two, later)
 
 
 def second_kernel(
@@ -668,7 +684,10 @@
     return pl.pallas_call(
         functools.partial(second_kernel, wide, sizes),
         out_shape=jax.ShapeDtypeStruct((count, 4, wide - 2 * HALO, channels), BF16),
-        in_specs=[pl.BlockSpec(memory_space=pltpu.SMEM)] + [vmem] * 7 + [anywhere] * 4,
+        in_specs=[pl.BlockSpec(memory_space=pltpu.SMEM)]
+        + [vmem] * 7
+        + [pl.BlockSpec(memory_space=pltpu.HBM)]
+        + [anywhere] * 3,
         out_specs=vmem,
         scratch_shapes=[
             *(pltpu.VMEM(weight.shape, BF16) for weight in weights),
@@ -680,7 +699,7 @@
             pltpu.VMEM((count * 4 * wide, channels), F32),
             pltpu.SemaphoreType.DMA((4,)),
         ],
-        compiler_params=pltpu.CompilerParams(vmem_limit_bytes=44 * 1024 * 1024),
+        compiler_params=pltpu.CompilerParams(vmem_limit_bytes=40 * 1024 * 1024),
         name="second_block",
     )(place, *pieces, *tiles, gains, *weights)
 
@@ -713,9 +732,11 @@
     sizes = (2 * row_count, width)
     place = jnp.stack([section, col, col * tile + section * part - HALO, row]).astype(jnp.int32)
 
+    gains = jnp.stack([gain_one, gain_two, jnp.tile(gain_three, 2), jnp.tile(gain_four, 2)])
+
     latent = latent.reshape(latent.shape[0], width, channels)
     arrived = swapped(latent, "section")
-    mine, theirs, tiles, gains = pack(
+    mine, theirs, tiles = pack(
         place,
         latent,
         arrived,
@@ -724,7 +745,6 @@
         cache_time,
         cache_three,
         cache_four,
-        [gain.reshape(1, -1) for gain in (gain_one, gain_two, gain_three, gain_four)],
         wide,
         tile,
         part,
@@ -736,21 +756,20 @@
     )
     pieces = [shifted(up, "rows", 1), own, shifted(down, "rows", -1)]
     tiles = [shifted(tile_up, "rows", 1), windows, shifted(tile_down, "rows", -1)]
-    weight_upsample, weight_four, own = lax.optimization_barrier(
-        (weight_upsample, weight_four, own)
-    )
+    weight_upsample, own = lax.optimization_barrier((weight_upsample, own))
     weight_upsample = combine_weights(weight_upsample)
-    weight_four = align_weights(weight_four)
     blocked = first_block(
         place,
         pieces,
         gains,
         weight_one.reshape(9, 3, channels, channels),
         weight_two.reshape(9, 3, channels, channels),
-        (weight_upsample, weight_four),
+        weight_upsample,
         sizes,
     )
     blocks = [shifted(blocked, "rows", 1), blocked, shifted(blocked, "rows", -1)]
+    weight_four, _ = lax.optimization_barrier((weight_four, blocked))
+    weight_four = align_weights(weight_four)
     frames = second_block(
         place,
         blocks,

time: 95 us -> 90.8 us (0.956)
  Pallas kernels: 54.7 us -> 42 us
  local copies, waits for them, and re-layouts: 9.65 us -> 15.3 us
  waiting for transfers between devices: 6.86 us -> 10.8 us
    pallas_call x2, Pallas kernels: 11.2 us -> 2.98 us  [align_weights(): pl.pallas_call(align_kernel, out_shape=jax.ShapeDtypeStruct((4 * half, 18...]
    unnamed x24 -> x38, local copies, waits for them, and re-layouts: 6.02 us -> 13.9 us
    ppermute x3, waiting for transfers between devices: 1.64 us -> 4.53 us  [swapped(): return lax.ppermute(value, axis, [(0, 1), (1, 0)])]
    pallas_call x1, Pallas kernels: 3.26 us -> 0.46 us  [combine_weights(): pl.pallas_call(combine_kernel, out_shape=jax.ShapeDtypeStruct((2, 2 * cha...]
    reshape x2 -> x0, local copies, waits for them, and re-layouts: 2.48 us -> none  [body(): gain.reshape(1, -1)]
    pallas_call x1, Pallas kernels: 2.5 us -> 0.86 us  [pack(): pl.pallas_call(functools.partial(pack_kernel, wide, tile, part), out_shap...]
    ppermute x6, waiting for transfers between devices: 5.22 us -> 6.3 us  [shifted(): lax.ppermute(value, axis, [(source, source + steps) for source in range(i...]
  transfers between devices with their start and end apart: 9 -> 9, of which waited for: 4 -> 4; matrix products, arithmetic and copies ran while one was open for 3% -> 0% of each run, Pallas kernels for 27% -> 17%
where the time goes in v6:
time: 90.8 us; the launch traced here: 90.2 us
  Pallas kernels  42 us (46%)
  starting transfers between devices  21.7 us (24%)
  local copies, waits for them, and re-layouts  15.3 us (17%)
  waiting for transfers between devices  10.8 us (12%)
    pallas_call x1, Pallas kernels, second_block(): pl.pallas_call(functools.partial(second_kernel, wide, sizes), out_shape=j...  24.7 us
    ppermute x6, starting transfers between devices, shifted(): lax.ppermute(value, axis, [(source, source + steps) for source in range(i...  18.5 us
    unnamed x38, local copies, waits for them, and re-layouts  13.9 us
    pallas_call x1, Pallas kernels, first_block(): pl.pallas_call(functools.partial(first_kernel, wide, sizes), out_shape=ja...  11.5 us
    ppermute x6, waiting for transfers between devices, shifted(): lax.ppermute(value, axis, [(source, source + steps) for source in range(i...  6.3 us
    ppermute x3, waiting for transfers between devices, swapped(): return lax.ppermute(value, axis, [(0, 1), (1, 0)])  4.53 us
    ppermute x3, starting transfers between devices, swapped(): return lax.ppermute(value, axis, [(0, 1), (1, 0)])  3.16 us
    pallas_call x2, Pallas kernels, align_weights(): pl.pallas_call(align_kernel, out_shape=jax.ShapeDtypeStruct((4 * half, 18...  2.98 us
  transfers between devices with their start and end apart: 9, of which 4 were waited for; matrix products, arithmetic and copies ran while one was open for 0% of the time, Pallas kernels for 17%

profile of v6, /device:TPU:9, one launch (start us, length us, event | category | flops | bytes accessed | tf_op | source)
XLA Modules:
  0.0 90.2 jit_solution(8345657234252537315)
XLA Ops:
  0.0 0.7 collective-permute-start
  0.8 1.1 %collective-permute-done.arrived = bf16[2,64,384]{2,1,0:T(8,128)(2,1)S(1)} collective-permute-done((bf16[2,64,384]{2,1,0:T(8,128)(2,1)}, bf16[2,64,384]{2,1,0:T(8,128)(2,1)S(1)}, u32[]{:S(2)}, u32[]{:S(2)}) %collective-permute-start) | collective-permute-done | bytes 98336 | tf_op jit(solution)/shard_map/ppermute | solution.py:18
  1.8 0.9 %copy-done.7 = bf16[2,4,64,192]{3,2,1,0:T(8,128)(2,1)S(1)} copy-done((bf16[2,4,64,192]{3,2,1,0:T(8,128)(2,1)S(1)}, bf16[2,4,64,192]{3,2,1,0:T(8,128)(2,1)}, u32[]{:S(2)}) %copy-start.7) | copy-done | bytes 196632
  2.8 0.9 %copy-done.8 = bf16[2,4,64,192]{3,2,1,0:T(8,128)(2,1)S(1)} copy-done((bf16[2,4,64,192]{3,2,1,0:T(8,128)(2,1)S(1)}, bf16[2,4,64,192]{3,2,1,0:T(8,128)(2,1)}, u32[]{:S(2)}) %copy-start.8) | copy-done | bytes 196632
  3.7 0.9 copy-done.11
  4.6 0.9 copy-done.12
  5.5 0.9 copy-done.13
  6.4 0.9 copy-done.14
  7.3 0.9 pack.1
  8.2 1.3 %collective-permute-start.1 = (bf16[12,24,384]{2,1,0:T(8,128)(2,1)S(1)}, bf16[12,24,384]{2,1,0:T(8,128)(2,1)S(1)}, u32[]{:S(2)}, u32[]{:S(2)}) collective-permute-start(bf16[12,24,384]{2,1,0:T(8,128)(2,1)S(1)} %get-tuple-element.20), channel_id=1, source_target_pairs={{0,1},{1,0},{2,3},{3,2},{4,5},{5,4},{6,7},{7,6},{8,9},{9,8},{10,11... | collective-permute-start | bytes 663560 | tf_op jit(solution)/shard_map/ppermute | solution.py:18
  9.5 1.6 %copy-done.3 = bf16[5184,192]{0,1:T(8,128)(2,1)S(1)} copy-done((bf16[5184,192]{0,1:T(8,128)(2,1)S(1)}, bf16[5184,192]{0,1:T(8,128)(2,1)}, u32[]{:S(2)}) %copy-start.3) | copy-done | bytes 1990680
  11.0 1.5 %align_weights.2.later.weight_three = bf16[768,3456]{1,0:T(8,128)(2,1)S(1)} custom-call(bf16[192,5184]{1,0:T(8,128)(2,1)S(1)} %bitcast.14), custom_call_target="tpu_custom_call" | custom-call | tf_op jit(solution)/shard_map/align_weights/pallas_call | solution.py:361
  12.5 2.4 %collective-permute-done.1.theirs = bf16[12,24,384]{2,1,0:T(8,128)(2,1)S(1)} collective-permute-done((bf16[12,24,384]{2,1,0:T(8,128)(2,1)S(1)}, bf16[12,24,384]{2,1,0:T(8,128)(2,1)S(1)}, u32[]{:S(2)}, u32[]{:S(2)}) %collective-permute-start.1) | collective-permute-done | bytes 221216 | tf_op jit(solution)/shard_map/ppermute | solution.py:18
  14.9 1.5 %stack.33 = (bf16[2,8,24,384]{3,2,1,0:T(8,128)(2,1)S(1)}, bf16[14,24,384]{2,1,0:T(8,128)(2,1)}, bf16[14,24,384]{2,1,0:T(8,128)(2,1)}, bf16[20,24,384]{2,1,0:T(8,...) custom-call(s32[4]{0:T(128)S(1)} %pad_add_fusion.place, ...), custom_call_target="tpu_custom_call" | custom-call | tf_op jit(solution)/shard_map/stack/pallas_call | solution.py:300
  16.4 3.1 %collective-permute-start.2 = (bf16[14,24,384]{2,1,0:T(8,128)(2,1)}, bf16[14,24,384]{2,1,0:T(8,128)(2,1)S(1)}, u32[]{:S(2)}, u32[]{:S(2)}) collective-permute-start(bf16[14,24,384]{2,1,0:T(8,128)(2,1)} %get-tuple-element.23), channel_id=1, source_target_pairs={{0,2},{2,4},{4,6},{6,8},{8,10},{10,12},{12,14},{1,3},{3,5},{5,7},{... | collective-permute-start | bytes 774152 | tf_op jit(solution)/shard_map/ppermute | solution.py:24
  19.6 3.0 %collective-permute-start.3 = (bf16[14,24,384]{2,1,0:T(8,128)(2,1)}, bf16[14,24,384]{2,1,0:T(8,128)(2,1)}, u32[]{:S(2)}, u32[]{:S(2)}) collective-permute-start(bf16[14,24,384]{2,1,0:T(8,128)(2,1)} %get-tuple-element.25), channel_id=1, source_target_pairs={{2,0},{4,2},{6,4},{8,6},{10,8},{12,10},{14,12},{3,1},{5,3},{7,5},{... | collective-permute-start | bytes 774152 | tf_op jit(solution)/shard_map/ppermute | solution.py:24
  22.9 1.3 %copy-done.6 = bf16[3456,192]{0,1:T(8,128)(2,1)S(1)} copy-done((bf16[3456,192]{0,1:T(8,128)(2,1)S(1)}, bf16[3456,192]{0,1:T(8,128)(2,1)}, u32[]{:S(2)}) %copy-start.6) | copy-done | bytes 1327128
  24.7 2.2 %collective-permute-start.6 = (bf16[10,24,384]{2,1,0:T(8,128)(2,1)}, bf16[10,24,384]{2,1,0:T(8,128)(2,1)}, u32[]{:S(2)}, u32[]{:S(2)}) collective-permute-start(bf16[10,24,384]{2,1,0:T(8,128)(2,1)} %get-tuple-element.27), channel_id=1, source_target_pairs={{0,2},{2,4},{4,6},{6,8},{8,10},{10,12},{12,14},{1,3},{3,5},{5,7},{... | collective-permute-start | bytes 552968 | tf_op jit(solution)/shard_map/ppermute | solution.py:24
  26.9 3.9 %collective-permute-start.7 = (bf16[10,24,384]{2,1,0:T(8,128)(2,1)}, bf16[10,24,384]{2,1,0:T(8,128)(2,1)}, u32[]{:S(2)}, u32[]{:S(2)}) collective-permute-start(bf16[10,24,384]{2,1,0:T(8,128)(2,1)} %get-tuple-element.29), channel_id=1, source_target_pairs={{2,0},{4,2},{6,4},{8,6},{10,8},{12,10},{14,12},{3,1},{5,3},{7,5},{... | collective-permute-start | bytes 552968 | tf_op jit(solution)/shard_map/ppermute | solution.py:24
  30.9 6.3 %collective-permute-done.3.below = bf16[14,24,384]{2,1,0:T(8,128)(2,1)} collective-permute-done((bf16[14,24,384]{2,1,0:T(8,128)(2,1)}, bf16[14,24,384]{2,1,0:T(8,128)(2,1)}, u32[]{:S(2)}, u32[]{:S(2)}) %collective-permute-start.3) | collective-permute-done | bytes 258080 | tf_op jit(solution)/shard_map/ppermute | solution.py:24
  37.2 11.5 %first_block.1.blocked = bf16[4,48,384]{2,1,0:T(8,128)(2,1)S(1)} custom-call(s32[4]{0:T(128)S(1)} %pad_add_fusion.place, bf16[14,24,384]{2,1,0:T(8,128)(2,1)S(1)} %collective-permute-done.2.above, bf16[2,8,24,384]{3,2,1,0:T(8,128)(2,1)S(1)} %get-tuple-element.24.own, bf16[14,24,384]{2,1,0:T(8,128)(2,1)} %collective-permute-done.3.below, ...), custom_call_target="tpu_custom_call" | custom-call | flops 4586471424 | bytes 15925248 | tf_op jit(solution)/shard_map/first_block/pallas_call | solution.py:507
  48.7 1.9 %collective-permute-start.4 = (bf16[4,48,384]{2,1,0:T(8,128)(2,1)S(1)}, bf16[4,48,384]{2,1,0:T(8,128)(2,1)S(1)}, u32[]{:S(2)}, u32[]{:S(2)}) collective-permute-start(bf16[4,48,384]{2,1,0:T(8,128)(2,1)S(1)} %first_block.1.blocked), channel_id=1, source_target_pairs={{0,2},{2,4},{4,6},{6,8},{8,10},{10,12},{12,14},{1,3},{3,5},{5,7},{... | collective-permute-start | bytes 442376 | tf_op jit(solution)/shard_map/ppermute | solution.py:24
  50.6 4.3 %collective-permute-start.5 = (bf16[4,48,384]{2,1,0:T(8,128)(2,1)S(1)}, bf16[4,48,384]{2,1,0:T(8,128)(2,1)S(1)}, u32[]{:S(2)}, u32[]{:S(2)}) collective-permute-start(bf16[4,48,384]{2,1,0:T(8,128)(2,1)S(1)} %first_block.1.blocked), channel_id=1, source_target_pairs={{2,0},{4,2},{6,4},{8,6},{10,8},{12,10},{14,12},{3,1},{5,3},{7,5},{... | collective-permute-start | bytes 442376 | tf_op jit(solution)/shard_map/ppermute | solution.py:24
  54.9 1.6 %copy-done.4 = bf16[5184,192]{0,1:T(8,128)(2,1)S(1)} copy-done((bf16[5184,192]{0,1:T(8,128)(2,1)S(1)}, bf16[5184,192]{0,1:T(8,128)(2,1)}, u32[]{:S(2)}) %copy-start.4) | copy-done | bytes 1990680
  56.4 1.5 %align_weights.3.weight_four = bf16[768,3456]{1,0:T(8,128)(2,1)S(1)} custom-call(bf16[192,5184]{1,0:T(8,128)(2,1)S(1)} %bitcast.15), custom_call_target="tpu_custom_call" | custom-call | tf_op jit(solution)/shard_map/align_weights/pallas_call | solution.py:361
  57.9 2.4 %copy-done.2 = bf16[768,3456]{1,0:T(8,128)(2,1)} copy-done((bf16[768,3456]{1,0:T(8,128)(2,1)}, bf16[768,3456]{1,0:T(8,128)(2,1)S(1)}, u32[]{:S(2)}) %copy-start.2) | copy-done | bytes 5308440
  60.4 0.7 copy-done.9
  61.1 0.9 %copy-done.10 = bf16[4,48,384]{2,1,0:T(8,128)(2,1)S(1)} copy-done((bf16[4,48,384]{2,1,0:T(8,128)(2,1)S(1)}, bf16[4,48,384]{2,1,0:T(8,128)(2,1)}, u32[]{:S(2)}) %copy-start.10) | copy-done | bytes 147480
  62.0 24.7 %second_block.1 = bf16[8,4,16,384]{3,2,1,0:T(8,128)(2,1)S(1)} custom-call(s32[4]{0:T(128)S(1)} %pad_add_fusion.place, bf16[4,48,384]{2,1,0:T(8,128)(2,1)S(1)} %collective-permute-done.4.above, bf16[4,48,384]{2,1,0:T(8,128)(2,1)S(1)} %first_block.1.blocked, bf16[4,48,384]{2,1,0:T(8,128)(2,1)S(1)} %copy-done.10, ...), custom_call_target="tpu_custom_call" | custom-call | tf_op jit(solution)/shard_map/second_block/pallas_call | solution.py:684
  86.7 1.2 %collective-permute-start.8 = (bf16[4,4,16,384]{3,2,1,0:T(8,128)(2,1)S(1)}, bf16[4,4,16,384]{3,2,1,0:T(8,128)(2,1)S(1)}, u32[]{:S(2)}, u32[]{:S(2)}) collective-permute-start(bf16[4,4,16,384]{3,2,1,0:T(8,128)(2,1)S(1)} %constant_dynamic-slice_fusion), channel_id=1, source_target_pairs={{0,16},{16,0},{1,17},{17,1},{2,18},{18,2},{3,19},{19,3},{4,20},{20... | collective-permute-start | bytes 589832 | tf_op jit(solution)/shard_map/ppermute | solution.py:18
  87.9 1.1 %collective-permute-done.8 = bf16[4,4,16,384]{3,2,1,0:T(8,128)(2,1)S(1)} collective-permute-done((bf16[4,4,16,384]{3,2,1,0:T(8,128)(2,1)S(1)}, bf16[4,4,16,384]{3,2,1,0:T(8,128)(2,1)S(1)}, u32[]{:S(2)}, u32[]{:S(2)}) %collective-permute-start.8) | collective-permute-done | bytes 196640 | tf_op jit(solution)/shard_map/ppermute | solution.py:18
  89.1 1.1 %reshape.17 = bf16[4,4,64,192]{3,2,1,0:T(8,128)(2,1)} reshape(bf16[4,4,32,384]{3,2,1,0:T(8,128)(2,1)S(1)} %pad_maximum_fusion) | data formatting | bytes 786432 | tf_op jit(solution)/shard_map/reshape | solution.py:790
  (43 shorter events, 0.9 us)
Async XLA Ops:
  0.0 1.8 %collective-permute-start = (bf16[2,64,384]{2,1,0:T(8,128)(2,1)}, bf16[2,64,384]{2,1,0:T(8,128)(2,1)S(1)}, u32[]{:S(2)}, u32[]{:S(2)}) collective-permute-start(bf16[2,64,384]{2,1,0:T(8,128)(2,1)} %bitcast.17), channel_id=1, source_target_pairs={{0,16},{16,0},{1,17},{17,1},{2,18},{18,2},{3,19},{19,3},{4,20},{20... | collective-permute-start | bytes 294920 | tf_op jit(solution)/shard_map/ppermute | solution.py:18
  1.8 0.9 %copy-start.7 = (bf16[2,4,64,192]{3,2,1,0:T(8,128)(2,1)S(1)}, bf16[2,4,64,192]{3,2,1,0:T(8,128)(2,1)}, u32[]{:S(2)}) copy-start(bf16[2,4,64,192]{3,2,1,0:T(8,128)(2,1)} %three.1) | copy-start | bytes 589828
  2.8 0.9 %copy-start.8 = (bf16[2,4,64,192]{3,2,1,0:T(8,128)(2,1)S(1)}, bf16[2,4,64,192]{3,2,1,0:T(8,128)(2,1)}, u32[]{:S(2)}) copy-start(bf16[2,4,64,192]{3,2,1,0:T(8,128)(2,1)} %four.1) | copy-start | bytes 589828
  3.7 0.9 copy-start.11
  4.6 0.9 copy-start.12
  5.5 0.9 copy-start.13
  6.4 0.9 copy-start.14
  8.2 6.7 %collective-permute-start.1 = (bf16[12,24,384]{2,1,0:T(8,128)(2,1)S(1)}, bf16[12,24,384]{2,1,0:T(8,128)(2,1)S(1)}, u32[]{:S(2)}, u32[]{:S(2)}) collective-permute-start(bf16[12,24,384]{2,1,0:T(8,128)(2,1)S(1)} %get-tuple-element.20), channel_id=1, source_target_pairs={{0,1},{1,0},{2,3},{3,2},{4,5},{5,4},{6,7},{7,6},{8,9},{9,8},{10,11... | collective-permute-start | bytes 663560 | tf_op jit(solution)/shard_map/ppermute | solution.py:18
  9.5 1.6 %copy-start.3 = (bf16[5184,192]{0,1:T(8,128)(2,1)S(1)}, bf16[5184,192]{0,1:T(8,128)(2,1)}, u32[]{:S(2)}) copy-start(bf16[5184,192]{0,1:T(8,128)(2,1)} %param.30) | copy-start | bytes 5971972
  12.5 3.9 %copy-start = (bf16[768,3456]{1,0:T(8,128)(2,1)}, bf16[768,3456]{1,0:T(8,128)(2,1)S(1)}, u32[]{:S(2)}) copy-start(bf16[768,3456]{1,0:T(8,128)(2,1)S(1)} %align_weights.2.later.weight_three) | copy-start | bytes 15925252
  14.9 7.7 %copy-start.17 = (f32[192]{0:T(256)S(1)}, f32[192]{0:T(256)}, u32[]{:S(2)}) copy-start(f32[192]{0:T(256)} %param.24) | copy-start | bytes 2308
  14.9 7.8 %copy-start.18 = (f32[192]{0:T(256)S(1)}, f32[192]{0:T(256)}, u32[]{:S(2)}) copy-start(f32[192]{0:T(256)} %param.25) | copy-start | bytes 2308
  14.9 7.9 %copy-start.15 = (f32[384]{0:T(512)S(1)}, f32[384]{0:T(512)}, u32[]{:S(2)}) copy-start(f32[384]{0:T(512)} %param.22) | copy-start | bytes 4612
  14.9 7.9 %copy-start.16 = (f32[384]{0:T(512)S(1)}, f32[384]{0:T(512)}, u32[]{:S(2)}) copy-start(f32[384]{0:T(512)} %param.23) | copy-start | bytes 4612
  16.4 14.4 %collective-permute-start.2 = (bf16[14,24,384]{2,1,0:T(8,128)(2,1)}, bf16[14,24,384]{2,1,0:T(8,128)(2,1)S(1)}, u32[]{:S(2)}, u32[]{:S(2)}) collective-permute-start(bf16[14,24,384]{2,1,0:T(8,128)(2,1)} %get-tuple-element.23), channel_id=1, source_target_pairs={{0,2},{2,4},{4,6},{6,8},{8,10},{10,12},{12,14},{1,3},{3,5},{5,7},{... | collective-permute-start | bytes 774152 | tf_op jit(solution)/shard_map/ppermute | solution.py:24
  19.6 17.6 %collective-permute-start.3 = (bf16[14,24,384]{2,1,0:T(8,128)(2,1)}, bf16[14,24,384]{2,1,0:T(8,128)(2,1)}, u32[]{:S(2)}, u32[]{:S(2)}) collective-permute-start(bf16[14,24,384]{2,1,0:T(8,128)(2,1)} %get-tuple-element.25), channel_id=1, source_target_pairs={{2,0},{4,2},{6,4},{8,6},{10,8},{12,10},{14,12},{3,1},{5,3},{7,5},{... | collective-permute-start | bytes 774152 | tf_op jit(solution)/shard_map/ppermute | solution.py:24
  22.9 1.3 %copy-start.6 = (bf16[3456,192]{0,1:T(8,128)(2,1)S(1)}, bf16[3456,192]{0,1:T(8,128)(2,1)}, u32[]{:S(2)}) copy-start(bf16[3456,192]{0,1:T(8,128)(2,1)} %param.29) | copy-start | bytes 3981316
  24.7 35.7 %collective-permute-start.6 = (bf16[10,24,384]{2,1,0:T(8,128)(2,1)}, bf16[10,24,384]{2,1,0:T(8,128)(2,1)}, u32[]{:S(2)}, u32[]{:S(2)}) collective-permute-start(bf16[10,24,384]{2,1,0:T(8,128)(2,1)} %get-tuple-element.27), channel_id=1, source_target_pairs={{0,2},{2,4},{4,6},{6,8},{8,10},{10,12},{12,14},{1,3},{3,5},{5,7},{... | collective-permute-start | bytes 552968 | tf_op jit(solution)/shard_map/ppermute | solution.py:24
  26.9 33.5 %collective-permute-start.7 = (bf16[10,24,384]{2,1,0:T(8,128)(2,1)}, bf16[10,24,384]{2,1,0:T(8,128)(2,1)}, u32[]{:S(2)}, u32[]{:S(2)}) collective-permute-start(bf16[10,24,384]{2,1,0:T(8,128)(2,1)} %get-tuple-element.29), channel_id=1, source_target_pairs={{2,0},{4,2},{6,4},{8,6},{10,8},{12,10},{14,12},{3,1},{5,3},{7,5},{... | collective-permute-start | bytes 552968 | tf_op jit(solution)/shard_map/ppermute | solution.py:24
  48.7 11.7 %collective-permute-start.4 = (bf16[4,48,384]{2,1,0:T(8,128)(2,1)S(1)}, bf16[4,48,384]{2,1,0:T(8,128)(2,1)S(1)}, u32[]{:S(2)}, u32[]{:S(2)}) collective-permute-start(bf16[4,48,384]{2,1,0:T(8,128)(2,1)S(1)} %first_block.1.blocked), channel_id=1, source_target_pairs={{0,2},{2,4},{4,6},{6,8},{8,10},{10,12},{12,14},{1,3},{3,5},{5,7},{... | collective-permute-start | bytes 442376 | tf_op jit(solution)/shard_map/ppermute | solution.py:24
  50.6 9.8 %collective-permute-start.5 = (bf16[4,48,384]{2,1,0:T(8,128)(2,1)S(1)}, bf16[4,48,384]{2,1,0:T(8,128)(2,1)S(1)}, u32[]{:S(2)}, u32[]{:S(2)}) collective-permute-start(bf16[4,48,384]{2,1,0:T(8,128)(2,1)S(1)} %first_block.1.blocked), channel_id=1, source_target_pairs={{2,0},{4,2},{6,4},{8,6},{10,8},{12,10},{14,12},{3,1},{5,3},{7,5},{... | collective-permute-start | bytes 442376 | tf_op jit(solution)/shard_map/ppermute | solution.py:24
  54.9 1.6 %copy-start.4 = (bf16[5184,192]{0,1:T(8,128)(2,1)S(1)}, bf16[5184,192]{0,1:T(8,128)(2,1)}, u32[]{:S(2)}) copy-start(bf16[5184,192]{0,1:T(8,128)(2,1)} %param.31) | copy-start | bytes 5971972
  56.4 4.6 %copy-start.1 = (bf16[768,3456]{1,0:T(8,128)(2,1)S(1)}, bf16[768,3456]{1,0:T(8,128)(2,1)}, u32[]{:S(2)}) copy-start(bf16[768,3456]{1,0:T(8,128)(2,1)} %copy-done) | copy-start | bytes 15925252
  56.4 4.6 %copy-start.5 = (bf16[1152,768]{1,0:T(8,128)(2,1)S(1)}, bf16[1152,768]{1,0:T(8,128)(2,1)}, u32[]{:S(2)}) copy-start(bf16[1152,768]{1,0:T(8,128)(2,1)} %weight_time.1) | copy-start | bytes 5308420
  57.9 2.4 %copy-start.2 = (bf16[768,3456]{1,0:T(8,128)(2,1)}, bf16[768,3456]{1,0:T(8,128)(2,1)S(1)}, u32[]{:S(2)}) copy-start(bf16[768,3456]{1,0:T(8,128)(2,1)S(1)} %align_weights.3.weight_four) | copy-start | bytes 15925252
  60.4 0.7 copy-start.9
  61.1 0.9 %copy-start.10 = (bf16[4,48,384]{2,1,0:T(8,128)(2,1)S(1)}, bf16[4,48,384]{2,1,0:T(8,128)(2,1)}, u32[]{:S(2)}) copy-start(bf16[4,48,384]{2,1,0:T(8,128)(2,1)} %copy-done.9) | copy-start | bytes 442372
  86.7 2.3 %collective-permute-start.8 = (bf16[4,4,16,384]{3,2,1,0:T(8,128)(2,1)S(1)}, bf16[4,4,16,384]{3,2,1,0:T(8,128)(2,1)S(1)}, u32[]{:S(2)}, u32[]{:S(2)}) collective-permute-start(bf16[4,4,16,384]{3,2,1,0:T(8,128)(2,1)S(1)} %constant_dynamic-slice_fusion), channel_id=1, source_target_pairs={{0,16},{16,0},{1,17},{17,1},{2,18},{18,2},{3,19},{19,3},{4,20},{20... | collective-permute-start | bytes 589832 | tf_op jit(solution)/shard_map/ppermute | solution.py:18

commit v7 on v6

--- a/solution.py
+++ b/solution.py
@@ -245,7 +245,7 @@
             pltpu.VMEM((three.shape[2], 128), F32),
             pltpu.VMEM((three.shape[2], 128), F32),
         ],
-        compiler_params=pltpu.CompilerParams(vmem_limit_bytes=8 * 1024 * 1024),
+        compiler_params=pltpu.CompilerParams(vmem_limit_bytes=60 * 1024 * 1024),
         name="pack",
     )(place, latent, arrived, one, two, time, three, four)
 
@@ -541,15 +541,11 @@
     windows,
     tile_below,
     gains,
-    weight_time,
-    weight_up,
-    weight_three,
-    weight_four,
-    out_ref,
     wt,
     wu,
     w3,
     w4,
+    out_ref,
     acc,
     mixed,
     de,
@@ -559,7 +555,6 @@
     x4e,
     x4o,
     lifted_ref,
-    sems,
 ):
     channels = blocked.shape[-1]
     half = channels // 2
@@ -568,14 +563,6 @@
     count = 2 * frames
     height, width = sizes
     row = place[3]
-    copies = [
-        pltpu.make_async_copy(source, target, sems.at[i])
-        for i, (source, target) in enumerate(
-            ((weight_time, wt), (weight_up, wu), (weight_three, w3), (weight_four, w4))
-        )
-    ]
-    for copy in copies:
-        copy.start()
 
     def cached(start, base, lines, depth, f):
         parts = [tile_above[start + depth * f + i] for i in range(depth)]
@@ -590,7 +577,6 @@
             begin = (f + 2) * size + i * 2 * wide
             mixed[begin : begin + 2 * wide, :] = ref[f]
 
-    copies[0].wait()
 
     def mix(n, carry):
         lanes = pl.ds(pl.multiple_of(n * LANES, LANES), LANES)
@@ -613,7 +599,6 @@
 
     lax.fori_loop(0, frames, double, 0)
 
-    copies[1].wait()
 
     for py in range(2):
 
@@ -650,7 +635,6 @@
         return carry
 
     lax.fori_loop(0, count, norm_three, 0)
-    copies[2].wait()
     high_product(acc, x3e, x3o, count, 8, wide, w3)
 
     mask_four = mask_three[wide : 7 * wide]
@@ -661,7 +645,6 @@
         return carry
 
     lax.fori_loop(0, count, norm_four, 0)
-    copies[3].wait()
     high_product(acc, x4e, x4o, count, 6, wide, w4)
 
     def finish(f, carry):
@@ -680,26 +663,21 @@
     frames, _, channels = pieces[0].shape
     count = 2 * frames
     vmem = pl.BlockSpec(memory_space=pltpu.VMEM)
-    anywhere = pl.BlockSpec(memory_space=pl.ANY)
     return pl.pallas_call(
         functools.partial(second_kernel, wide, sizes),
         out_shape=jax.ShapeDtypeStruct((count, 4, wide - 2 * HALO, channels), BF16),
         in_specs=[pl.BlockSpec(memory_space=pltpu.SMEM)]
-        + [vmem] * 7
-        + [pl.BlockSpec(memory_space=pltpu.HBM)]
-        + [anywhere] * 3,
+        + [vmem] * 11,
         out_specs=vmem,
         scratch_shapes=[
-            *(pltpu.VMEM(weight.shape, BF16) for weight in weights),
             pltpu.VMEM((3, 2 * count * 4 * wide, LANES), F32),
             pltpu.VMEM(((frames + 2) * 6 * wide, channels), BF16),
             *planes(count, 6, wide, channels),
             *planes(count + 2, 8, wide, channels),
             *planes(count + 2, 6, wide, channels),
             pltpu.VMEM((count * 4 * wide, channels), F32),
-            pltpu.SemaphoreType.DMA((4,)),
         ],
-        compiler_params=pltpu.CompilerParams(vmem_limit_bytes=40 * 1024 * 1024),
+        compiler_params=pltpu.CompilerParams(vmem_limit_bytes=34 * 1024 * 1024),
         name="second_block",
     )(place, *pieces, *tiles, gains, *weights)
 

time: 90.8 us -> 85.9 us (0.946)
  local copies, waits for them, and re-layouts: 15.3 us -> 8 us
  waiting for transfers between devices: 10.8 us -> 12.9 us
    unnamed x38 -> x32, local copies, waits for them, and re-layouts: 13.9 us -> 6.68 us
    ppermute x6, waiting for transfers between devices: 6.3 us -> 8.72 us  [shifted(): lax.ppermute(value, axis, [(source, source + steps) for source in range(i...]
    pallas_call x1, Pallas kernels: 0.86 us -> 2.46 us  [pack(): pl.pallas_call(functools.partial(pack_kernel, wide, tile, part), out_shap...]
    pallas_call x1, Pallas kernels: 24.7 us -> 23.7 us  [second_block(): pl.pallas_call(functools.partial(second_kernel, wide, sizes), out_shape=j...]
  transfers between devices with their start and end apart: 9 -> 9, of which waited for: 4 -> 5; matrix products, arithmetic and copies ran while one was open for 0% -> 1% of each run, Pallas kernels for 17% -> 17%
where the time goes in v7:
time: 85.9 us; the launch traced here: 85.5 us
  Pallas kernels  42.6 us (50%)
  starting transfers between devices  21 us (24%)
  waiting for transfers between devices  12.9 us (15%)
  local copies, waits for them, and re-layouts  8 us (9%)
    pallas_call x1, Pallas kernels, second_block(): pl.pallas_call(functools.partial(second_kernel, wide, sizes), out_shape=j...  23.7 us
    ppermute x6, starting transfers between devices, shifted(): lax.ppermute(value, axis, [(source, source + steps) for source in range(i...  18.5 us
    pallas_call x1, Pallas kernels, first_block(): pl.pallas_call(functools.partial(first_kernel, wide, sizes), out_shape=ja...  11.5 us
    ppermute x6, waiting for transfers between devices, shifted(): lax.ppermute(value, axis, [(source, source + steps) for source in range(i...  8.72 us
    unnamed x32, local copies, waits for them, and re-layouts  6.68 us
    ppermute x3, waiting for transfers between devices, swapped(): return lax.ppermute(value, axis, [(0, 1), (1, 0)])  4.22 us
    pallas_call x2, Pallas kernels, align_weights(): pl.pallas_call(align_kernel, out_shape=jax.ShapeDtypeStruct((4 * half, 18...  2.98 us
    pallas_call x1, Pallas kernels, pack(): pl.pallas_call(functools.partial(pack_kernel, wide, tile, part), out_shap...  2.46 us
  transfers between devices with their start and end apart: 9, of which 5 were waited for; matrix products, arithmetic and copies ran while one was open for 1% of the time, Pallas kernels for 17%

profile of v7, /device:TPU:9, one launch (start us, length us, event | category | flops | bytes accessed | tf_op | source)
XLA Modules:
  0.0 85.5 jit_solution(12965158214899305212)
XLA Ops:
  0.0 0.7 collective-permute-start
  0.7 0.6 pad_add_fusion.place
  1.3 0.6 collective-permute-done.arrived
  1.8 0.6 copy-done.11
  2.5 2.5 %pack.1 = (bf16[8,24,384]{2,1,0:T(8,128)(2,1)}, bf16[12,24,384]{2,1,0:T(8,128)(2,1)}, bf16[20,32,384]{2,1,0:T(8,128)(2,1)}) custom-call(s32[4]{0:T(128)} %pad_add_fusion.place, bf16[2,64,384]{2,1,0:T(8,128)(2,1)} %bitcast.20, bf16[2,64,384]{2,1,0:T(8,128)(2,1)} %copy-done.11, bf16[2,64,384]{2,1,0:T(8,128)(2,1)} %bitcast.21, bf16[2,64,384]{2,1,0:T(8,128)(2,1)} %bitcast.22, ...), custom_call_target="tpu_custom_call" | custom-call | tf_op jit(solution)/shard_map/pack/pallas_call | solution.py:234
  4.9 1.2 %collective-permute-start.1 = (bf16[12,24,384]{2,1,0:T(8,128)(2,1)}, bf16[12,24,384]{2,1,0:T(8,128)(2,1)S(1)}, u32[]{:S(2)}, u32[]{:S(2)}) collective-permute-start(bf16[12,24,384]{2,1,0:T(8,128)(2,1)} %get-tuple-element.20), channel_id=1, source_target_pairs={{0,1},{1,0},{2,3},{3,2},{4,5},{5,4},{6,7},{7,6},{8,9},{9,8},{10,11... | collective-permute-start | bytes 663560 | tf_op jit(solution)/shard_map/ppermute | solution.py:18
  6.1 1.6 %copy-done.2 = bf16[5184,192]{0,1:T(8,128)(2,1)S(1)} copy-done((bf16[5184,192]{0,1:T(8,128)(2,1)S(1)}, bf16[5184,192]{0,1:T(8,128)(2,1)}, u32[]{:S(2)}) %copy-start.2) | copy-done | bytes 1990680
  7.7 1.5 %align_weights.2.later.w3 = bf16[768,3456]{1,0:T(8,128)(2,1)S(1)} custom-call(bf16[192,5184]{1,0:T(8,128)(2,1)S(1)} %bitcast.14), custom_call_target="tpu_custom_call" | custom-call | tf_op jit(solution)/shard_map/align_weights/pallas_call | solution.py:361
  9.2 2.6 %collective-permute-done.1.theirs = bf16[12,24,384]{2,1,0:T(8,128)(2,1)S(1)} collective-permute-done((bf16[12,24,384]{2,1,0:T(8,128)(2,1)}, bf16[12,24,384]{2,1,0:T(8,128)(2,1)S(1)}, u32[]{:S(2)}, u32[]{:S(2)}) %collective-permute-start.1) | collective-permute-done | bytes 221216 | tf_op jit(solution)/shard_map/ppermute | solution.py:18
  11.8 0.0 copy-start.12
  11.8 1.5 %stack.33 = (bf16[2,8,24,384]{3,2,1,0:T(8,128)(2,1)S(1)}, bf16[14,24,384]{2,1,0:T(8,128)(2,1)}, bf16[14,24,384]{2,1,0:T(8,128)(2,1)}, bf16[20,24,384]{2,1,0:T(8,...) custom-call(s32[4]{0:T(128)S(1)} %copy-done.10, bf16[8,24,384]{2,1,0:T(8,128)(2,1)S(1)} %copy-done.7, ...), custom_call_target="tpu_custom_call" | custom-call | tf_op jit(solution)/shard_map/stack/pallas_call | solution.py:300
  13.4 3.1 %collective-permute-start.2 = (bf16[14,24,384]{2,1,0:T(8,128)(2,1)}, bf16[14,24,384]{2,1,0:T(8,128)(2,1)S(1)}, u32[]{:S(2)}, u32[]{:S(2)}) collective-permute-start(bf16[14,24,384]{2,1,0:T(8,128)(2,1)} %get-tuple-element.23), channel_id=1, source_target_pairs={{0,2},{2,4},{4,6},{6,8},{8,10},{10,12},{12,14},{1,3},{3,5},{5,7},{... | collective-permute-start | bytes 774152 | tf_op jit(solution)/shard_map/ppermute | solution.py:24
  16.5 3.0 %collective-permute-start.3 = (bf16[14,24,384]{2,1,0:T(8,128)(2,1)}, bf16[14,24,384]{2,1,0:T(8,128)(2,1)}, u32[]{:S(2)}, u32[]{:S(2)}) collective-permute-start(bf16[14,24,384]{2,1,0:T(8,128)(2,1)} %get-tuple-element.25), channel_id=1, source_target_pairs={{2,0},{4,2},{6,4},{8,6},{10,8},{12,10},{14,12},{3,1},{5,3},{7,5},{... | collective-permute-start | bytes 774152 | tf_op jit(solution)/shard_map/ppermute | solution.py:24
  19.6 0.1 stack_tile.6
  19.7 0.1 stack_tile.7
  19.8 1.3 %copy-done.5 = bf16[3456,192]{0,1:T(8,128)(2,1)S(1)} copy-done((bf16[3456,192]{0,1:T(8,128)(2,1)S(1)}, bf16[3456,192]{0,1:T(8,128)(2,1)}, u32[]{:S(2)}) %copy-start.5) | copy-done | bytes 1327128
  21.1 0.5 combine_weights.1.later.wu
  21.6 2.2 %collective-permute-start.6 = (bf16[10,24,384]{2,1,0:T(8,128)(2,1)}, bf16[10,24,384]{2,1,0:T(8,128)(2,1)}, u32[]{:S(2)}, u32[]{:S(2)}) collective-permute-start(bf16[10,24,384]{2,1,0:T(8,128)(2,1)} %get-tuple-element.27), channel_id=1, source_target_pairs={{0,2},{2,4},{4,6},{6,8},{8,10},{10,12},{12,14},{1,3},{3,5},{5,7},{... | collective-permute-start | bytes 552968 | tf_op jit(solution)/shard_map/ppermute | solution.py:24
  23.8 3.9 %collective-permute-start.7 = (bf16[10,24,384]{2,1,0:T(8,128)(2,1)}, bf16[10,24,384]{2,1,0:T(8,128)(2,1)}, u32[]{:S(2)}, u32[]{:S(2)}) collective-permute-start(bf16[10,24,384]{2,1,0:T(8,128)(2,1)} %get-tuple-element.29), channel_id=1, source_target_pairs={{2,0},{4,2},{6,4},{8,6},{10,8},{12,10},{14,12},{3,1},{5,3},{7,5},{... | collective-permute-start | bytes 552968 | tf_op jit(solution)/shard_map/ppermute | solution.py:24
  27.8 6.3 %collective-permute-done.3.below = bf16[14,24,384]{2,1,0:T(8,128)(2,1)} collective-permute-done((bf16[14,24,384]{2,1,0:T(8,128)(2,1)}, bf16[14,24,384]{2,1,0:T(8,128)(2,1)}, u32[]{:S(2)}, u32[]{:S(2)}) %collective-permute-start.3) | collective-permute-done | bytes 258080 | tf_op jit(solution)/shard_map/ppermute | solution.py:24
  34.1 11.5 %first_block.1.blocked = bf16[4,48,384]{2,1,0:T(8,128)(2,1)S(1)} custom-call(s32[4]{0:T(128)S(1)} %copy-done.10, bf16[14,24,384]{2,1,0:T(8,128)(2,1)S(1)} %collective-permute-done.2.above, bf16[2,8,24,384]{3,2,1,0:T(8,128)(2,1)S(1)} %get-tuple-element.24.own, bf16[14,24,384]{2,1,0:T(8,128)(2,1)} %collective-permute-done.3.below, ...), custom_call_target="tpu_custom_call" | custom-call | flops 4586471424 | bytes 15925248 | tf_op jit(solution)/shard_map/first_block/pallas_call | solution.py:507
  45.6 1.9 %collective-permute-start.4 = (bf16[4,48,384]{2,1,0:T(8,128)(2,1)S(1)}, bf16[4,48,384]{2,1,0:T(8,128)(2,1)S(1)}, u32[]{:S(2)}, u32[]{:S(2)}) collective-permute-start(bf16[4,48,384]{2,1,0:T(8,128)(2,1)S(1)} %first_block.1.blocked), channel_id=1, source_target_pairs={{0,2},{2,4},{4,6},{6,8},{8,10},{10,12},{12,14},{1,3},{3,5},{5,7},{... | collective-permute-start | bytes 442376 | tf_op jit(solution)/shard_map/ppermute | solution.py:24
  47.5 4.3 %collective-permute-start.5 = (bf16[4,48,384]{2,1,0:T(8,128)(2,1)S(1)}, bf16[4,48,384]{2,1,0:T(8,128)(2,1)S(1)}, u32[]{:S(2)}, u32[]{:S(2)}) collective-permute-start(bf16[4,48,384]{2,1,0:T(8,128)(2,1)S(1)} %first_block.1.blocked), channel_id=1, source_target_pairs={{2,0},{4,2},{6,4},{8,6},{10,8},{12,10},{14,12},{3,1},{5,3},{7,5},{... | collective-permute-start | bytes 442376 | tf_op jit(solution)/shard_map/ppermute | solution.py:24
  51.8 1.6 %copy-done.3 = bf16[5184,192]{0,1:T(8,128)(2,1)S(1)} copy-done((bf16[5184,192]{0,1:T(8,128)(2,1)S(1)}, bf16[5184,192]{0,1:T(8,128)(2,1)}, u32[]{:S(2)}) %copy-start.3) | copy-done | bytes 1990680
  53.4 1.5 %align_weights.3.w4 = bf16[768,3456]{1,0:T(8,128)(2,1)S(1)} custom-call(bf16[192,5184]{1,0:T(8,128)(2,1)S(1)} %bitcast.15), custom_call_target="tpu_custom_call" | custom-call | tf_op jit(solution)/shard_map/align_weights/pallas_call | solution.py:361
  54.9 2.4 %collective-permute-done.5.below = bf16[4,48,384]{2,1,0:T(8,128)(2,1)S(1)} collective-permute-done((bf16[4,48,384]{2,1,0:T(8,128)(2,1)S(1)}, bf16[4,48,384]{2,1,0:T(8,128)(2,1)S(1)}, u32[]{:S(2)}, u32[]{:S(2)}) %collective-permute-start.5) | collective-permute-done | bytes 147488 | tf_op jit(solution)/shard_map/ppermute | solution.py:24
  57.3 0.7 copy-done.8
  58.0 0.9 %copy-done.9 = bf16[4,48,384]{2,1,0:T(8,128)(2,1)S(1)} copy-done((bf16[4,48,384]{2,1,0:T(8,128)(2,1)S(1)}, bf16[4,48,384]{2,1,0:T(8,128)(2,1)}, u32[]{:S(2)}) %copy-start.9) | copy-done | bytes 147480
  58.9 23.7 %second_block.1 = bf16[8,4,16,384]{3,2,1,0:T(8,128)(2,1)S(1)} custom-call(s32[4]{0:T(128)S(1)} %copy-done.10, bf16[4,48,384]{2,1,0:T(8,128)(2,1)S(1)} %collective-permute-done.4.above, bf16[4,48,384]{2,1,0:T(8,128)(2,1)S(1)} %first_block.1.blocked, bf16[4,48,384]{2,1,0:T(8,128)(2,1)S(1)} %copy-done.9, ...), custom_call_target="tpu_custom_call" | custom-call | tf_op jit(solution)/shard_map/second_block/pallas_call | solution.py:666
  82.6 0.6 collective-permute-start.8
  83.2 1.1 %collective-permute-done.8 = bf16[4,4,16,384]{3,2,1,0:T(8,128)(2,1)S(1)} collective-permute-done((bf16[4,4,16,384]{3,2,1,0:T(8,128)(2,1)S(1)}, bf16[4,4,16,384]{3,2,1,0:T(8,128)(2,1)S(1)}, u32[]{:S(2)}, u32[]{:S(2)}) %collective-permute-start.8) | collective-permute-done | bytes 196640 | tf_op jit(solution)/shard_map/ppermute | solution.py:18
  84.4 1.1 %reshape.17 = bf16[4,4,64,192]{3,2,1,0:T(8,128)(2,1)} reshape(bf16[4,4,32,384]{3,2,1,0:T(8,128)(2,1)S(1)} %pad_maximum_fusion) | data formatting | bytes 786432 | tf_op jit(solution)/shard_map/reshape | solution.py:768
  (37 shorter events, 0.2 us)
Async XLA Ops:
  0.0 1.8 %collective-permute-start = (bf16[2,64,384]{2,1,0:T(8,128)(2,1)}, bf16[2,64,384]{2,1,0:T(8,128)(2,1)S(1)}, u32[]{:S(2)}, u32[]{:S(2)}) collective-permute-start(bf16[2,64,384]{2,1,0:T(8,128)(2,1)} %bitcast.19), channel_id=1, source_target_pairs={{0,16},{16,0},{1,17},{17,1},{2,18},{18,2},{3,19},{19,3},{4,20},{20... | collective-permute-start | bytes 294920 | tf_op jit(solution)/shard_map/ppermute | solution.py:18
  1.8 0.6 copy-start.11
  4.9 6.9 %collective-permute-start.1 = (bf16[12,24,384]{2,1,0:T(8,128)(2,1)}, bf16[12,24,384]{2,1,0:T(8,128)(2,1)S(1)}, u32[]{:S(2)}, u32[]{:S(2)}) collective-permute-start(bf16[12,24,384]{2,1,0:T(8,128)(2,1)} %get-tuple-element.20), channel_id=1, source_target_pairs={{0,1},{1,0},{2,3},{3,2},{4,5},{5,4},{6,7},{7,6},{8,9},{9,8},{10,11... | collective-permute-start | bytes 663560 | tf_op jit(solution)/shard_map/ppermute | solution.py:18
  6.1 1.6 %copy-start.2 = (bf16[5184,192]{0,1:T(8,128)(2,1)S(1)}, bf16[5184,192]{0,1:T(8,128)(2,1)}, u32[]{:S(2)}) copy-start(bf16[5184,192]{0,1:T(8,128)(2,1)} %param.30) | copy-start | bytes 5971972
  7.7 4.1 %copy-start.6 = (bf16[20,32,384]{2,1,0:T(8,128)(2,1)S(1)}, bf16[20,32,384]{2,1,0:T(8,128)(2,1)}, u32[]{:S(2)}) copy-start(bf16[20,32,384]{2,1,0:T(8,128)(2,1)} %get-tuple-element.21.tiles) | copy-start | bytes 1474564
  7.7 4.1 %copy-start.7 = (bf16[8,24,384]{2,1,0:T(8,128)(2,1)S(1)}, bf16[8,24,384]{2,1,0:T(8,128)(2,1)}, u32[]{:S(2)}) copy-start(bf16[8,24,384]{2,1,0:T(8,128)(2,1)} %get-tuple-element.19.mine) | copy-start | bytes 442372
  7.7 4.1 %copy-start.10 = (s32[4]{0:T(128)S(1)}, s32[4]{0:T(128)}, u32[]{:S(2)}) copy-start(s32[4]{0:T(128)} %pad_add_fusion.place) | copy-start | bytes 52
  9.2 4.2 %copy-start = (bf16[768,3456]{1,0:T(8,128)(2,1)}, bf16[768,3456]{1,0:T(8,128)(2,1)S(1)}, u32[]{:S(2)}) copy-start(bf16[768,3456]{1,0:T(8,128)(2,1)S(1)} %align_weights.2.later.w3) | copy-start | bytes 15925252
  11.8 7.8 %copy-start.14 = (f32[192]{0:T(256)S(1)}, f32[192]{0:T(256)}, u32[]{:S(2)}) copy-start(f32[192]{0:T(256)} %param.24) | copy-start | bytes 2308
  11.8 7.8 %copy-start.15 = (f32[192]{0:T(256)S(1)}, f32[192]{0:T(256)}, u32[]{:S(2)}) copy-start(f32[192]{0:T(256)} %param.25) | copy-start | bytes 2308
  11.8 7.9 %copy-start.12 = (f32[384]{0:T(512)S(1)}, f32[384]{0:T(512)}, u32[]{:S(2)}) copy-start(f32[384]{0:T(512)} %param.22) | copy-start | bytes 4612
  11.8 7.9 %copy-start.13 = (f32[384]{0:T(512)S(1)}, f32[384]{0:T(512)}, u32[]{:S(2)}) copy-start(f32[384]{0:T(512)} %param.23) | copy-start | bytes 4612
  13.4 14.4 %collective-permute-start.2 = (bf16[14,24,384]{2,1,0:T(8,128)(2,1)}, bf16[14,24,384]{2,1,0:T(8,128)(2,1)S(1)}, u32[]{:S(2)}, u32[]{:S(2)}) collective-permute-start(bf16[14,24,384]{2,1,0:T(8,128)(2,1)} %get-tuple-element.23), channel_id=1, source_target_pairs={{0,2},{2,4},{4,6},{6,8},{8,10},{10,12},{12,14},{1,3},{3,5},{5,7},{... | collective-permute-start | bytes 774152 | tf_op jit(solution)/shard_map/ppermute | solution.py:24
  16.5 17.6 %collective-permute-start.3 = (bf16[14,24,384]{2,1,0:T(8,128)(2,1)}, bf16[14,24,384]{2,1,0:T(8,128)(2,1)}, u32[]{:S(2)}, u32[]{:S(2)}) collective-permute-start(bf16[14,24,384]{2,1,0:T(8,128)(2,1)} %get-tuple-element.25), channel_id=1, source_target_pairs={{2,0},{4,2},{6,4},{8,6},{10,8},{12,10},{14,12},{3,1},{5,3},{7,5},{... | collective-permute-start | bytes 774152 | tf_op jit(solution)/shard_map/ppermute | solution.py:24
  19.8 1.3 %copy-start.5 = (bf16[3456,192]{0,1:T(8,128)(2,1)S(1)}, bf16[3456,192]{0,1:T(8,128)(2,1)}, u32[]{:S(2)}) copy-start(bf16[3456,192]{0,1:T(8,128)(2,1)} %param.29) | copy-start | bytes 3981316
  21.6 33.3 %collective-permute-start.6 = (bf16[10,24,384]{2,1,0:T(8,128)(2,1)}, bf16[10,24,384]{2,1,0:T(8,128)(2,1)}, u32[]{:S(2)}, u32[]{:S(2)}) collective-permute-start(bf16[10,24,384]{2,1,0:T(8,128)(2,1)} %get-tuple-element.27), channel_id=1, source_target_pairs={{0,2},{2,4},{4,6},{6,8},{8,10},{10,12},{12,14},{1,3},{3,5},{5,7},{... | collective-permute-start | bytes 552968 | tf_op jit(solution)/shard_map/ppermute | solution.py:24
  23.8 31.0 %collective-permute-start.7 = (bf16[10,24,384]{2,1,0:T(8,128)(2,1)}, bf16[10,24,384]{2,1,0:T(8,128)(2,1)}, u32[]{:S(2)}, u32[]{:S(2)}) collective-permute-start(bf16[10,24,384]{2,1,0:T(8,128)(2,1)} %get-tuple-element.29), channel_id=1, source_target_pairs={{2,0},{4,2},{6,4},{8,6},{10,8},{12,10},{14,12},{3,1},{5,3},{7,5},{... | collective-permute-start | bytes 552968 | tf_op jit(solution)/shard_map/ppermute | solution.py:24
  45.6 9.3 %collective-permute-start.4 = (bf16[4,48,384]{2,1,0:T(8,128)(2,1)S(1)}, bf16[4,48,384]{2,1,0:T(8,128)(2,1)S(1)}, u32[]{:S(2)}, u32[]{:S(2)}) collective-permute-start(bf16[4,48,384]{2,1,0:T(8,128)(2,1)S(1)} %first_block.1.blocked), channel_id=1, source_target_pairs={{0,2},{2,4},{4,6},{6,8},{8,10},{10,12},{12,14},{1,3},{3,5},{5,7},{... | collective-permute-start | bytes 442376 | tf_op jit(solution)/shard_map/ppermute | solution.py:24
  47.5 9.8 %collective-permute-start.5 = (bf16[4,48,384]{2,1,0:T(8,128)(2,1)S(1)}, bf16[4,48,384]{2,1,0:T(8,128)(2,1)S(1)}, u32[]{:S(2)}, u32[]{:S(2)}) collective-permute-start(bf16[4,48,384]{2,1,0:T(8,128)(2,1)S(1)} %first_block.1.blocked), channel_id=1, source_target_pairs={{2,0},{4,2},{6,4},{8,6},{10,8},{12,10},{14,12},{3,1},{5,3},{7,5},{... | collective-permute-start | bytes 442376 | tf_op jit(solution)/shard_map/ppermute | solution.py:24
  51.8 1.6 %copy-start.3 = (bf16[5184,192]{0,1:T(8,128)(2,1)S(1)}, bf16[5184,192]{0,1:T(8,128)(2,1)}, u32[]{:S(2)}) copy-start(bf16[5184,192]{0,1:T(8,128)(2,1)} %param.31) | copy-start | bytes 5971972
  53.4 4.6 %copy-start.1 = (bf16[768,3456]{1,0:T(8,128)(2,1)S(1)}, bf16[768,3456]{1,0:T(8,128)(2,1)}, u32[]{:S(2)}) copy-start(bf16[768,3456]{1,0:T(8,128)(2,1)} %copy-done) | copy-start | bytes 15925252
  53.4 4.6 %copy-start.4 = (bf16[1152,768]{1,0:T(8,128)(2,1)S(1)}, bf16[1152,768]{1,0:T(8,128)(2,1)}, u32[]{:S(2)}) copy-start(bf16[1152,768]{1,0:T(8,128)(2,1)} %wt.1) | copy-start | bytes 5308420
  57.3 0.7 copy-start.8
  58.0 0.9 %copy-start.9 = (bf16[4,48,384]{2,1,0:T(8,128)(2,1)S(1)}, bf16[4,48,384]{2,1,0:T(8,128)(2,1)}, u32[]{:S(2)}) copy-start(bf16[4,48,384]{2,1,0:T(8,128)(2,1)} %copy-done.8) | copy-start | bytes 442372
  82.6 1.6 %collective-permute-start.8 = (bf16[4,4,16,384]{3,2,1,0:T(8,128)(2,1)S(1)}, bf16[4,4,16,384]{3,2,1,0:T(8,128)(2,1)S(1)}, u32[]{:S(2)}, u32[]{:S(2)}) collective-permute-start(bf16[4,4,16,384]{3,2,1,0:T(8,128)(2,1)S(1)} %constant_dynamic-slice_fusion), channel_id=1, source_target_pairs={{0,16},{16,0},{1,17},{17,1},{2,18},{18,2},{3,19},{19,3},{4,20},{20... | collective-permute-start | bytes 589832 | tf_op jit(solution)/shard_map/ppermute | solution.py:18

commit v8 on v7

--- a/solution.py
+++ b/solution.py
@@ -18,10 +18,9 @@
     return lax.ppermute(value, axis, [(0, 1), (1, 0)])
 
 
-def shifted(value, axis, steps):
-    count = lax.axis_size(axis)
-    initial, last = (max(0, -steps), min(count, count - steps))
-    return lax.ppermute(value, axis, [(source, source + steps) for source in range(initial, last)])
+def paired(value, axis, first):
+    pairs = [(i, i + 1) for i in range(first, lax.axis_size(axis) - 1, 2)]
+    return lax.ppermute(value, axis, pairs + [(high, low) for low, high in pairs])
 
 
 def silu(scaled):
@@ -88,13 +87,12 @@
 def low_product(acc, even, odd, count, height, wide, weights, copies):
     rows = count * (height - 2) * wide
     channels = weights.shape[1]
-    lanes = 3 * channels
-    waited = 0
-    for n in range(-(-lanes // LANES)):
-        begin, end = n * LANES, min((n + 1) * LANES, lanes)
-        while waited * channels < end:
-            copies[waited].wait()
-            waited += 1
+    needed = [dx * channels // LANES for dx in range(3)]
+
+    def column(n, carry):
+        for copy, when in zip(copies, needed):
+            pl.when(n == when)(copy.wait)
+        lanes = pl.ds(pl.multiple_of(n * LANES, LANES), LANES)
         total = None
         for first, last in ((0, 4), (4, 8), (8, 9)):
             left = jnp.concatenate(
@@ -104,10 +102,13 @@
                 ],
                 axis=1,
             )
-            right = weights[first:last, :, begin:end].reshape((last - first) * channels, -1)
+            right = weights[first:last, :, lanes].reshape((last - first) * channels, LANES)
             part = jnp.dot(left, right, preferred_element_type=F32)
             total = part if total is None else total + part
-        acc[n, 0:rows, 0 : end - begin] = total
+        acc[n, 0:rows, :] = total
+        return carry
+
+    lax.fori_loop(0, weights.shape[-1] // LANES, column, 0)
 
 
 def low_sum(acc, start, size):
@@ -251,13 +252,14 @@
 
 
 def stack_kernel(
-    wide, place, mine, theirs, tiles, later, own, up, down, windows, tile_up, tile_down
+    wide, place, mine, theirs, tiles, later, own, near, far, windows, tile_near, tile_far
 ):
     del later
     section, col = place[0], place[1]
     count = mine.shape[0] - 2
     own[0], own[1] = mine[...], theirs[0 : count + 2]
-    for ref, y in ((up, 1), (down, 0)):
+    parity = lax.rem(place[3], 2)
+    for ref, y in ((near, 1 - parity), (far, parity)):
         ref[0:count], ref[count : 2 * count] = mine[0:count], theirs[0:count]
         here = lax.rem(y + col, 2) == 0
         ref[2 * count :] = jnp.where(here, mine[count:], theirs[count : count + 2])
@@ -280,16 +282,15 @@
         last = jnp.concatenate([last[:-8], tail], axis=0)
         line = jnp.where(section == 0, first, last).astype(BF16)
         windows[i] = line
-        if i < 4:
-            tile_up[i] = line
-            tile_down[i] = line
-            continue
-        f, y = (i - 4) % 8 // 4, (i - 4) % 4
-        base, depth = (4, 2) if i < 12 else (8, 1)
-        if y >= 4 - depth:
-            tile_up[base + depth * f + y - (4 - depth)] = line
-        if y < depth:
-            tile_down[base + depth * f + y] = line
+    is_even = parity == 0
+    for base, start, count, depth in ((0, 0, 2, 2), (4, 4, 4, 2), (12, 8, 4, 1)):
+        for f in range(2):
+            for j in range(depth):
+                slot = start + depth * f + j
+                high = windows[base + count * f + j]
+                low = windows[base + count * f + count - depth + j]
+                tile_near[slot] = jnp.where(is_even, low, high)
+                tile_far[slot] = jnp.where(is_even, high, low)
 
 
 def stack(place, mine, theirs, tiles, later):
@@ -410,9 +411,9 @@
     wide,
     sizes,
     place,
-    above,
+    near,
     own,
-    below,
+    far,
     gains,
     weight_one,
     weight_two,
@@ -449,17 +450,25 @@
 
     slots = [lax.rem(y + col, 2) for y in range(2)]
 
+    is_even = lax.rem(row, 2) == 0
+
     def own_rows(index):
         return [own[slot, index].astype(F32) for slot in slots]
 
+    def above(line):
+        return jnp.where(is_even, far[line].astype(F32), near[line].astype(F32))
+
+    def below(line):
+        return jnp.where(is_even, near[line].astype(F32), far[line].astype(F32))
+
     def rows_of(index):
-        first = [above[slot * units + index].astype(F32) for slot in slots]
-        last = [below[slot * units + index].astype(F32) for slot in slots]
+        first = [above(slot * units + index) for slot in slots]
+        last = [below(slot * units + index) for slot in slots]
         return jnp.concatenate(first + own_rows(index) + last, axis=0)
 
     for f in range(2):
         store(x1e, x1o, f, rows_of(frames + f), 6, wide)
-        first, last = above[2 * units + f].astype(F32), below[2 * units + f].astype(F32)
+        first, last = above(2 * units + f), below(2 * units + f)
         values = jnp.concatenate([first] + own_rows(units + f) + [last], axis=0)
         store(x2e, x2o, f, values, 4, wide)
 
@@ -534,12 +543,12 @@
     wide,
     sizes,
     place,
-    above,
+    near,
     blocked,
-    below,
-    tile_above,
+    far,
+    tile_near,
     windows,
-    tile_below,
+    tile_far,
     gains,
     wt,
     wu,
@@ -564,18 +573,25 @@
     height, width = sizes
     row = place[3]
 
+    is_even = lax.rem(row, 2) == 0
+
+    def chosen(when, one, other, index):
+        return jnp.where(when, one[index].astype(F32), other[index].astype(F32))
+
     def cached(start, base, lines, depth, f):
-        parts = [tile_above[start + depth * f + i] for i in range(depth)]
-        parts += [windows[base + lines * f + i] for i in range(lines)]
-        parts += [tile_below[start + depth * f + i] for i in range(depth)]
-        return jnp.concatenate([line.astype(F32) for line in parts], axis=0)
+        slots = [start + depth * f + i for i in range(depth)]
+        parts = [chosen(is_even, tile_far, tile_near, slot) for slot in slots]
+        parts += [windows[base + lines * f + i].astype(F32) for i in range(lines)]
+        parts += [chosen(is_even, tile_near, tile_far, slot) for slot in slots]
+        return jnp.concatenate(parts, axis=0)
 
     for f in range(2):
         mixed[f * size : (f + 1) * size, :] = cached(0, 0, 2, 2, f).astype(BF16)
     for f in range(frames):
-        for i, ref in enumerate((above, blocked, below)):
+        first, last = chosen(is_even, far, near, f), chosen(is_even, near, far, f)
+        for i, values in enumerate((first.astype(BF16), blocked[f], last.astype(BF16))):
             begin = (f + 2) * size + i * 2 * wide
-            mixed[begin : begin + 2 * wide, :] = ref[f]
+            mixed[begin : begin + 2 * wide, :] = values
 
 
     def mix(n, carry):
@@ -729,11 +745,11 @@
     )
     weight_three, mine = lax.optimization_barrier((weight_three, mine))
     weight_three = align_weights(weight_three)
-    own, up, down, windows, tile_up, tile_down = stack(
+    own, near, far, windows, tile_near, tile_far = stack(
         place, mine, swapped(theirs, "cols"), tiles, weight_three
     )
-    pieces = [shifted(up, "rows", 1), own, shifted(down, "rows", -1)]
-    tiles = [shifted(tile_up, "rows", 1), windows, shifted(tile_down, "rows", -1)]
+    pieces = [paired(near, "rows", 0), own, paired(far, "rows", 1)]
+    tiles = [paired(tile_near, "rows", 0), windows, paired(tile_far, "rows", 1)]
     weight_upsample, own = lax.optimization_barrier((weight_upsample, own))
     weight_upsample = combine_weights(weight_upsample)
     blocked = first_block(
@@ -745,7 +761,7 @@
         weight_upsample,
         sizes,
     )
-    blocks = [shifted(blocked, "rows", 1), blocked, shifted(blocked, "rows", -1)]
+    blocks = [paired(blocked, "rows", 0), blocked, paired(blocked, "rows", 1)]
     weight_four, _ = lax.optimization_barrier((weight_four, blocked))
     weight_four = align_weights(weight_four)
     frames = second_block(

time: 85.9 us -> 81.9 us (0.953)
  waiting for transfers between devices: 12.9 us -> 7.61 us
  starting transfers between devices: 21 us -> 23 us
    ppermute x3, starting transfers between devices: 2.44 us -> 11.1 us  [swapped(): return lax.ppermute(value, axis, [(0, 1), (1, 0)])]
    ppermute x6, starting transfers between devices: 18.5 us -> 11.8 us  [paired(): lax.ppermute(value, axis, pairs + [(high, low) for low, high in pairs])]
    ppermute x6, waiting for transfers between devices: 8.72 us -> 3.4 us  [paired(): lax.ppermute(value, axis, pairs + [(high, low) for low, high in pairs])]
  transfers between devices with their start and end apart: 9 -> 9, of which waited for: 5 -> 5; matrix products, arithmetic and copies ran while one was open for 1% -> 1% of each run, Pallas kernels for 17% -> 18%
where the time goes in v8:
time: 81.9 us; the launch traced here: 81.6 us
  Pallas kernels  42.1 us (51%)
  starting transfers between devices  23 us (28%)
  local copies, waits for them, and re-layouts  8 us (10%)
  waiting for transfers between devices  7.61 us (9%)
    pallas_call x1, Pallas kernels, second_block(): pl.pallas_call(functools.partial(second_kernel, wide, sizes), out_shape=j...  23.7 us
    ppermute x6, starting transfers between devices, paired(): lax.ppermute(value, axis, pairs + [(high, low) for low, high in pairs])  11.8 us
    ppermute x3, starting transfers between devices, swapped(): return lax.ppermute(value, axis, [(0, 1), (1, 0)])  11.1 us
    pallas_call x1, Pallas kernels, first_block(): pl.pallas_call(functools.partial(first_kernel, wide, sizes), out_shape=ja...  11 us
    unnamed x32, local copies, waits for them, and re-layouts  6.68 us
    ppermute x3, waiting for transfers between devices, swapped(): return lax.ppermute(value, axis, [(0, 1), (1, 0)])  4.22 us
    ppermute x6, waiting for transfers between devices, paired(): lax.ppermute(value, axis, pairs + [(high, low) for low, high in pairs])  3.4 us
    pallas_call x2, Pallas kernels, align_weights(): pl.pallas_call(align_kernel, out_shape=jax.ShapeDtypeStruct((4 * half, 18...  2.98 us
  transfers between devices with their start and end apart: 9, of which 5 were waited for; matrix products, arithmetic and copies ran while one was open for 1% of the time, Pallas kernels for 18%

profile of v8, /device:TPU:9, one launch (start us, length us, event | category | flops | bytes accessed | tf_op | source)
XLA Modules:
  0.0 81.6 jit_solution(6125682057356803918)
XLA Ops:
  0.0 0.7 collective-permute-start
  0.7 0.6 pad_add_fusion.place
  1.3 0.6 collective-permute-done.arrived
  1.8 0.6 copy-done.11
  2.5 2.5 %pack.1 = (bf16[8,24,384]{2,1,0:T(8,128)(2,1)}, bf16[12,24,384]{2,1,0:T(8,128)(2,1)}, bf16[20,32,384]{2,1,0:T(8,128)(2,1)}) custom-call(s32[4]{0:T(128)} %pad_add_fusion.place, bf16[2,64,384]{2,1,0:T(8,128)(2,1)} %bitcast.20, bf16[2,64,384]{2,1,0:T(8,128)(2,1)} %copy-done.11, bf16[2,64,384]{2,1,0:T(8,128)(2,1)} %bitcast.21, bf16[2,64,384]{2,1,0:T(8,128)(2,1)} %bitcast.22, ...), custom_call_target="tpu_custom_call" | custom-call | tf_op jit(solution)/shard_map/pack/pallas_call | solution.py:235
  4.9 1.2 %collective-permute-start.1 = (bf16[12,24,384]{2,1,0:T(8,128)(2,1)}, bf16[12,24,384]{2,1,0:T(8,128)(2,1)S(1)}, u32[]{:S(2)}, u32[]{:S(2)}) collective-permute-start(bf16[12,24,384]{2,1,0:T(8,128)(2,1)} %get-tuple-element.20), channel_id=1, source_target_pairs={{0,1},{1,0},{2,3},{3,2},{4,5},{5,4},{6,7},{7,6},{8,9},{9,8},{10,11... | collective-permute-start | bytes 663560 | tf_op jit(solution)/shard_map/ppermute | solution.py:18
  6.1 1.6 %copy-done.2 = bf16[5184,192]{0,1:T(8,128)(2,1)S(1)} copy-done((bf16[5184,192]{0,1:T(8,128)(2,1)S(1)}, bf16[5184,192]{0,1:T(8,128)(2,1)}, u32[]{:S(2)}) %copy-start.2) | copy-done | bytes 1990680
  7.7 1.5 %align_weights.2.later.w3 = bf16[768,3456]{1,0:T(8,128)(2,1)S(1)} custom-call(bf16[192,5184]{1,0:T(8,128)(2,1)S(1)} %bitcast.14), custom_call_target="tpu_custom_call" | custom-call | tf_op jit(solution)/shard_map/align_weights/pallas_call | solution.py:362
  9.2 2.6 %collective-permute-done.1.theirs = bf16[12,24,384]{2,1,0:T(8,128)(2,1)S(1)} collective-permute-done((bf16[12,24,384]{2,1,0:T(8,128)(2,1)}, bf16[12,24,384]{2,1,0:T(8,128)(2,1)S(1)}, u32[]{:S(2)}, u32[]{:S(2)}) %collective-permute-start.1) | collective-permute-done | bytes 221216 | tf_op jit(solution)/shard_map/ppermute | solution.py:18
  11.8 0.0 copy-start.14
  11.8 1.5 %stack.33 = (bf16[2,8,24,384]{3,2,1,0:T(8,128)(2,1)S(1)}, bf16[14,24,384]{2,1,0:T(8,128)(2,1)}, bf16[14,24,384]{2,1,0:T(8,128)(2,1)}, bf16[20,24,384]{2,1,0:T(8,...) custom-call(s32[4]{0:T(128)S(1)} %copy-done.10, bf16[8,24,384]{2,1,0:T(8,128)(2,1)S(1)} %copy-done.7, ...), custom_call_target="tpu_custom_call" | custom-call | tf_op jit(solution)/shard_map/stack/pallas_call | solution.py:301
  13.4 1.2 %collective-permute-start.2 = (bf16[14,24,384]{2,1,0:T(8,128)(2,1)}, bf16[14,24,384]{2,1,0:T(8,128)(2,1)S(1)}, u32[]{:S(2)}, u32[]{:S(2)}) collective-permute-start(bf16[14,24,384]{2,1,0:T(8,128)(2,1)} %get-tuple-element.23), channel_id=1, source_target_pairs={{0,2},{4,6},{8,10},{12,14},{2,0},{6,4},{10,8},{14,12},{1,3},{5,7},... | collective-permute-start | bytes 774152 | tf_op jit(solution)/shard_map/ppermute | solution.py:23
  14.6 2.1 %collective-permute-start.3 = (bf16[14,24,384]{2,1,0:T(8,128)(2,1)}, bf16[14,24,384]{2,1,0:T(8,128)(2,1)}, u32[]{:S(2)}, u32[]{:S(2)}) collective-permute-start(bf16[14,24,384]{2,1,0:T(8,128)(2,1)} %get-tuple-element.25), channel_id=1, source_target_pairs={{2,4},{6,8},{10,12},{4,2},{8,6},{12,10},{3,5},{7,9},{11,13},{5,3},... | collective-permute-start | bytes 774152 | tf_op jit(solution)/shard_map/ppermute | solution.py:23
  16.7 0.1 stack_tile.6
  16.8 0.1 stack_tile.7
  16.9 1.3 %copy-done.5 = bf16[3456,192]{0,1:T(8,128)(2,1)S(1)} copy-done((bf16[3456,192]{0,1:T(8,128)(2,1)S(1)}, bf16[3456,192]{0,1:T(8,128)(2,1)}, u32[]{:S(2)}) %copy-start.5) | copy-done | bytes 1327128
  18.3 0.5 combine_weights.1.later.wu
  18.7 2.4 %collective-permute-start.6 = (bf16[10,24,384]{2,1,0:T(8,128)(2,1)}, bf16[10,24,384]{2,1,0:T(8,128)(2,1)}, u32[]{:S(2)}, u32[]{:S(2)}) collective-permute-start(bf16[10,24,384]{2,1,0:T(8,128)(2,1)} %get-tuple-element.27), channel_id=1, source_target_pairs={{0,2},{4,6},{8,10},{12,14},{2,0},{6,4},{10,8},{14,12},{1,3},{5,7},... | collective-permute-start | bytes 552968 | tf_op jit(solution)/shard_map/ppermute | solution.py:23
  21.1 1.9 %collective-permute-start.7 = (bf16[10,24,384]{2,1,0:T(8,128)(2,1)}, bf16[10,24,384]{2,1,0:T(8,128)(2,1)}, u32[]{:S(2)}, u32[]{:S(2)}) collective-permute-start(bf16[10,24,384]{2,1,0:T(8,128)(2,1)} %get-tuple-element.29), channel_id=1, source_target_pairs={{2,4},{6,8},{10,12},{4,2},{8,6},{12,10},{3,5},{7,9},{11,13},{5,3},... | collective-permute-start | bytes 552968 | tf_op jit(solution)/shard_map/ppermute | solution.py:23
  23.0 1.6 %collective-permute-done.2.near = bf16[14,24,384]{2,1,0:T(8,128)(2,1)S(1)} collective-permute-done((bf16[14,24,384]{2,1,0:T(8,128)(2,1)}, bf16[14,24,384]{2,1,0:T(8,128)(2,1)S(1)}, u32[]{:S(2)}, u32[]{:S(2)}) %collective-permute-start.2) | collective-permute-done | bytes 258080 | tf_op jit(solution)/shard_map/ppermute | solution.py:23
  24.6 11.0 %first_block.1.blocked = bf16[4,48,384]{2,1,0:T(8,128)(2,1)S(1)} custom-call(s32[4]{0:T(128)S(1)} %copy-done.10, bf16[14,24,384]{2,1,0:T(8,128)(2,1)S(1)} %collective-permute-done.2.near, bf16[2,8,24,384]{3,2,1,0:T(8,128)(2,1)S(1)} %get-tuple-element.24.own, bf16[14,24,384]{2,1,0:T(8,128)(2,1)} %collective-permute-done.3.far, ...), custom_call_target="tpu_custom_call" | custom-call | flops 4586471424 | bytes 15925248 | tf_op jit(solution)/shard_map/first_block/pallas_call | solution.py:516
  35.6 2.3 %collective-permute-start.4 = (bf16[4,48,384]{2,1,0:T(8,128)(2,1)S(1)}, bf16[4,48,384]{2,1,0:T(8,128)(2,1)S(1)}, u32[]{:S(2)}, u32[]{:S(2)}) collective-permute-start(bf16[4,48,384]{2,1,0:T(8,128)(2,1)S(1)} %first_block.1.blocked), channel_id=1, source_target_pairs={{0,2},{4,6},{8,10},{12,14},{2,0},{6,4},{10,8},{14,12},{1,3},{5,7},... | collective-permute-start | bytes 442376 | tf_op jit(solution)/shard_map/ppermute | solution.py:23
  37.9 1.9 %collective-permute-start.5 = (bf16[4,48,384]{2,1,0:T(8,128)(2,1)S(1)}, bf16[4,48,384]{2,1,0:T(8,128)(2,1)S(1)}, u32[]{:S(2)}, u32[]{:S(2)}) collective-permute-start(bf16[4,48,384]{2,1,0:T(8,128)(2,1)S(1)} %first_block.1.blocked), channel_id=1, source_target_pairs={{2,4},{6,8},{10,12},{4,2},{8,6},{12,10},{3,5},{7,9},{11,13},{5,3},... | collective-permute-start | bytes 442376 | tf_op jit(solution)/shard_map/ppermute | solution.py:23
  39.9 1.6 %copy-done.3 = bf16[5184,192]{0,1:T(8,128)(2,1)S(1)} copy-done((bf16[5184,192]{0,1:T(8,128)(2,1)S(1)}, bf16[5184,192]{0,1:T(8,128)(2,1)}, u32[]{:S(2)}) %copy-start.3) | copy-done | bytes 1990680
  41.4 1.5 %align_weights.3.w4 = bf16[768,3456]{1,0:T(8,128)(2,1)S(1)} custom-call(bf16[192,5184]{1,0:T(8,128)(2,1)S(1)} %bitcast.15), custom_call_target="tpu_custom_call" | custom-call | tf_op jit(solution)/shard_map/align_weights/pallas_call | solution.py:362
  42.9 1.8 %collective-permute-done.5.far = bf16[4,48,384]{2,1,0:T(8,128)(2,1)S(1)} collective-permute-done((bf16[4,48,384]{2,1,0:T(8,128)(2,1)S(1)}, bf16[4,48,384]{2,1,0:T(8,128)(2,1)S(1)}, u32[]{:S(2)}, u32[]{:S(2)}) %collective-permute-start.5) | collective-permute-done | bytes 147488 | tf_op jit(solution)/shard_map/ppermute | solution.py:23
  44.7 0.7 copy-done.8
  45.4 0.9 %copy-done.9 = bf16[4,48,384]{2,1,0:T(8,128)(2,1)S(1)} copy-done((bf16[4,48,384]{2,1,0:T(8,128)(2,1)S(1)}, bf16[4,48,384]{2,1,0:T(8,128)(2,1)}, u32[]{:S(2)}) %copy-start.9) | copy-done | bytes 147480
  46.3 23.7 %second_block.1 = bf16[8,4,16,384]{3,2,1,0:T(8,128)(2,1)S(1)} custom-call(s32[4]{0:T(128)S(1)} %copy-done.10, bf16[4,48,384]{2,1,0:T(8,128)(2,1)S(1)} %collective-permute-done.4.near, bf16[4,48,384]{2,1,0:T(8,128)(2,1)S(1)} %first_block.1.blocked, bf16[4,48,384]{2,1,0:T(8,128)(2,1)S(1)} %copy-done.9, bf16[10,24,384]{2,1,0:T(8,128)(2,1)} %collective-permute-done.6.tile_near, ...), custom_call_target="tpu_custom_call" | custom-call | tf_op jit(solution)/shard_map/second_block/pallas_call | solution.py:682
  70.1 9.3 %collective-permute-start.8 = (bf16[4,4,16,384]{3,2,1,0:T(8,128)(2,1)S(1)}, bf16[4,4,16,384]{3,2,1,0:T(8,128)(2,1)S(1)}, u32[]{:S(2)}, u32[]{:S(2)}) collective-permute-start(bf16[4,4,16,384]{3,2,1,0:T(8,128)(2,1)S(1)} %constant_dynamic-slice_fusion), channel_id=1, source_target_pairs={{0,16},{16,0},{1,17},{17,1},{2,18},{18,2},{3,19},{19,3},{4,20},{20... | collective-permute-start | bytes 589832 | tf_op jit(solution)/shard_map/ppermute | solution.py:18
  79.3 1.1 %collective-permute-done.8 = bf16[4,4,16,384]{3,2,1,0:T(8,128)(2,1)S(1)} collective-permute-done((bf16[4,4,16,384]{3,2,1,0:T(8,128)(2,1)S(1)}, bf16[4,4,16,384]{3,2,1,0:T(8,128)(2,1)S(1)}, u32[]{:S(2)}, u32[]{:S(2)}) %collective-permute-start.8) | collective-permute-done | bytes 196640 | tf_op jit(solution)/shard_map/ppermute | solution.py:18
  80.5 1.1 %reshape.17 = bf16[4,4,64,192]{3,2,1,0:T(8,128)(2,1)} reshape(bf16[4,4,32,384]{3,2,1,0:T(8,128)(2,1)S(1)} %pad_maximum_fusion) | data formatting | bytes 786432 | tf_op jit(solution)/shard_map/reshape | solution.py:784
  (37 shorter events, 0.2 us)
Async XLA Ops:
  0.0 1.8 %collective-permute-start = (bf16[2,64,384]{2,1,0:T(8,128)(2,1)}, bf16[2,64,384]{2,1,0:T(8,128)(2,1)S(1)}, u32[]{:S(2)}, u32[]{:S(2)}) collective-permute-start(bf16[2,64,384]{2,1,0:T(8,128)(2,1)} %bitcast.19), channel_id=1, source_target_pairs={{0,16},{16,0},{1,17},{17,1},{2,18},{18,2},{3,19},{19,3},{4,20},{20... | collective-permute-start | bytes 294920 | tf_op jit(solution)/shard_map/ppermute | solution.py:18
  1.8 0.6 copy-start.11
  4.9 6.9 %collective-permute-start.1 = (bf16[12,24,384]{2,1,0:T(8,128)(2,1)}, bf16[12,24,384]{2,1,0:T(8,128)(2,1)S(1)}, u32[]{:S(2)}, u32[]{:S(2)}) collective-permute-start(bf16[12,24,384]{2,1,0:T(8,128)(2,1)} %get-tuple-element.20), channel_id=1, source_target_pairs={{0,1},{1,0},{2,3},{3,2},{4,5},{5,4},{6,7},{7,6},{8,9},{9,8},{10,11... | collective-permute-start | bytes 663560 | tf_op jit(solution)/shard_map/ppermute | solution.py:18
  6.1 1.6 %copy-start.2 = (bf16[5184,192]{0,1:T(8,128)(2,1)S(1)}, bf16[5184,192]{0,1:T(8,128)(2,1)}, u32[]{:S(2)}) copy-start(bf16[5184,192]{0,1:T(8,128)(2,1)} %param.30) | copy-start | bytes 5971972
  7.7 4.1 %copy-start.6 = (bf16[20,32,384]{2,1,0:T(8,128)(2,1)S(1)}, bf16[20,32,384]{2,1,0:T(8,128)(2,1)}, u32[]{:S(2)}) copy-start(bf16[20,32,384]{2,1,0:T(8,128)(2,1)} %get-tuple-element.21.tiles) | copy-start | bytes 1474564
  7.7 4.1 %copy-start.7 = (bf16[8,24,384]{2,1,0:T(8,128)(2,1)S(1)}, bf16[8,24,384]{2,1,0:T(8,128)(2,1)}, u32[]{:S(2)}) copy-start(bf16[8,24,384]{2,1,0:T(8,128)(2,1)} %get-tuple-element.19.mine) | copy-start | bytes 442372
  7.7 4.1 %copy-start.10 = (s32[4]{0:T(128)S(1)}, s32[4]{0:T(128)}, u32[]{:S(2)}) copy-start(s32[4]{0:T(128)} %pad_add_fusion.place) | copy-start | bytes 52
  9.2 4.2 %copy-start = (bf16[768,3456]{1,0:T(8,128)(2,1)}, bf16[768,3456]{1,0:T(8,128)(2,1)S(1)}, u32[]{:S(2)}) copy-start(bf16[768,3456]{1,0:T(8,128)(2,1)S(1)} %align_weights.2.later.w3) | copy-start | bytes 15925252
  11.8 4.9 %copy-start.14 = (f32[192]{0:T(256)S(1)}, f32[192]{0:T(256)}, u32[]{:S(2)}) copy-start(f32[192]{0:T(256)} %param.24) | copy-start | bytes 2308
  11.8 5.0 %copy-start.15 = (f32[192]{0:T(256)S(1)}, f32[192]{0:T(256)}, u32[]{:S(2)}) copy-start(f32[192]{0:T(256)} %param.25) | copy-start | bytes 2308
  11.8 5.1 %copy-start.12 = (f32[384]{0:T(512)S(1)}, f32[384]{0:T(512)}, u32[]{:S(2)}) copy-start(f32[384]{0:T(512)} %param.22) | copy-start | bytes 4612
  11.8 5.1 %copy-start.13 = (f32[384]{0:T(512)S(1)}, f32[384]{0:T(512)}, u32[]{:S(2)}) copy-start(f32[384]{0:T(512)} %param.23) | copy-start | bytes 4612
  13.4 11.3 %collective-permute-start.2 = (bf16[14,24,384]{2,1,0:T(8,128)(2,1)}, bf16[14,24,384]{2,1,0:T(8,128)(2,1)S(1)}, u32[]{:S(2)}, u32[]{:S(2)}) collective-permute-start(bf16[14,24,384]{2,1,0:T(8,128)(2,1)} %get-tuple-element.23), channel_id=1, source_target_pairs={{0,2},{4,6},{8,10},{12,14},{2,0},{6,4},{10,8},{14,12},{1,3},{5,7},... | collective-permute-start | bytes 774152 | tf_op jit(solution)/shard_map/ppermute | solution.py:23
  14.6 10.0 %collective-permute-start.3 = (bf16[14,24,384]{2,1,0:T(8,128)(2,1)}, bf16[14,24,384]{2,1,0:T(8,128)(2,1)}, u32[]{:S(2)}, u32[]{:S(2)}) collective-permute-start(bf16[14,24,384]{2,1,0:T(8,128)(2,1)} %get-tuple-element.25), channel_id=1, source_target_pairs={{2,4},{6,8},{10,12},{4,2},{8,6},{12,10},{3,5},{7,9},{11,13},{5,3},... | collective-permute-start | bytes 774152 | tf_op jit(solution)/shard_map/ppermute | solution.py:23
  16.9 1.3 %copy-start.5 = (bf16[3456,192]{0,1:T(8,128)(2,1)S(1)}, bf16[3456,192]{0,1:T(8,128)(2,1)}, u32[]{:S(2)}) copy-start(bf16[3456,192]{0,1:T(8,128)(2,1)} %param.29) | copy-start | bytes 3981316
  18.7 24.2 %collective-permute-start.6 = (bf16[10,24,384]{2,1,0:T(8,128)(2,1)}, bf16[10,24,384]{2,1,0:T(8,128)(2,1)}, u32[]{:S(2)}, u32[]{:S(2)}) collective-permute-start(bf16[10,24,384]{2,1,0:T(8,128)(2,1)} %get-tuple-element.27), channel_id=1, source_target_pairs={{0,2},{4,6},{8,10},{12,14},{2,0},{6,4},{10,8},{14,12},{1,3},{5,7},... | collective-permute-start | bytes 552968 | tf_op jit(solution)/shard_map/ppermute | solution.py:23
  21.1 21.8 %collective-permute-start.7 = (bf16[10,24,384]{2,1,0:T(8,128)(2,1)}, bf16[10,24,384]{2,1,0:T(8,128)(2,1)}, u32[]{:S(2)}, u32[]{:S(2)}) collective-permute-start(bf16[10,24,384]{2,1,0:T(8,128)(2,1)} %get-tuple-element.29), channel_id=1, source_target_pairs={{2,4},{6,8},{10,12},{4,2},{8,6},{12,10},{3,5},{7,9},{11,13},{5,3},... | collective-permute-start | bytes 552968 | tf_op jit(solution)/shard_map/ppermute | solution.py:23
  35.6 7.3 %collective-permute-start.4 = (bf16[4,48,384]{2,1,0:T(8,128)(2,1)S(1)}, bf16[4,48,384]{2,1,0:T(8,128)(2,1)S(1)}, u32[]{:S(2)}, u32[]{:S(2)}) collective-permute-start(bf16[4,48,384]{2,1,0:T(8,128)(2,1)S(1)} %first_block.1.blocked), channel_id=1, source_target_pairs={{0,2},{4,6},{8,10},{12,14},{2,0},{6,4},{10,8},{14,12},{1,3},{5,7},... | collective-permute-start | bytes 442376 | tf_op jit(solution)/shard_map/ppermute | solution.py:23
  37.9 6.8 %collective-permute-start.5 = (bf16[4,48,384]{2,1,0:T(8,128)(2,1)S(1)}, bf16[4,48,384]{2,1,0:T(8,128)(2,1)S(1)}, u32[]{:S(2)}, u32[]{:S(2)}) collective-permute-start(bf16[4,48,384]{2,1,0:T(8,128)(2,1)S(1)} %first_block.1.blocked), channel_id=1, source_target_pairs={{2,4},{6,8},{10,12},{4,2},{8,6},{12,10},{3,5},{7,9},{11,13},{5,3},... | collective-permute-start | bytes 442376 | tf_op jit(solution)/shard_map/ppermute | solution.py:23
  39.8 1.6 %copy-start.3 = (bf16[5184,192]{0,1:T(8,128)(2,1)S(1)}, bf16[5184,192]{0,1:T(8,128)(2,1)}, u32[]{:S(2)}) copy-start(bf16[5184,192]{0,1:T(8,128)(2,1)} %param.31) | copy-start | bytes 5971972
  41.4 4.0 %copy-start.1 = (bf16[768,3456]{1,0:T(8,128)(2,1)S(1)}, bf16[768,3456]{1,0:T(8,128)(2,1)}, u32[]{:S(2)}) copy-start(bf16[768,3456]{1,0:T(8,128)(2,1)} %copy-done) | copy-start | bytes 15925252
  41.4 4.0 %copy-start.4 = (bf16[1152,768]{1,0:T(8,128)(2,1)S(1)}, bf16[1152,768]{1,0:T(8,128)(2,1)}, u32[]{:S(2)}) copy-start(bf16[1152,768]{1,0:T(8,128)(2,1)} %wt.1) | copy-start | bytes 5308420
  44.7 0.7 copy-start.8
  45.4 0.9 %copy-start.9 = (bf16[4,48,384]{2,1,0:T(8,128)(2,1)S(1)}, bf16[4,48,384]{2,1,0:T(8,128)(2,1)}, u32[]{:S(2)}) copy-start(bf16[4,48,384]{2,1,0:T(8,128)(2,1)} %copy-done.8) | copy-start | bytes 442372
  70.1 10.3 %collective-permute-start.8 = (bf16[4,4,16,384]{3,2,1,0:T(8,128)(2,1)S(1)}, bf16[4,4,16,384]{3,2,1,0:T(8,128)(2,1)S(1)}, u32[]{:S(2)}, u32[]{:S(2)}) collective-permute-start(bf16[4,4,16,384]{3,2,1,0:T(8,128)(2,1)S(1)} %constant_dynamic-slice_fusion), channel_id=1, source_target_pairs={{0,16},{16,0},{1,17},{17,1},{2,18},{18,2},{3,19},{19,3},{4,20},{20... | collective-permute-start | bytes 589832 | tf_op jit(solution)/shard_map/ppermute | solution.py:18

commit v9 on v8

--- a/solution.py
+++ b/solution.py
@@ -417,7 +417,8 @@
     gains,
     weight_one,
     weight_two,
-    later,
+    later_one,
+    later_two,
     out_ref,
     w1,
     w2,
@@ -433,7 +434,7 @@
     height, width = sizes
     col, row = place[1], place[3]
     units = frames + 2
-    del later
+    del later_one, later_two
 
     def load(source, target, base):
         return [
@@ -519,7 +520,7 @@
         in_specs=[pl.BlockSpec(memory_space=pltpu.SMEM)]
         + [vmem] * 4
         + [pl.BlockSpec(memory_space=pltpu.HBM)] * 2
-        + [anywhere],
+        + [anywhere] * 2,
         out_specs=vmem,
         scratch_shapes=[
             pltpu.VMEM((9, channels, slots * LANES), BF16),
@@ -529,14 +530,14 @@
             *planes(frames + 2, 4, wide, channels),
             pltpu.SemaphoreType.DMA((6,)),
         ],
-        compiler_params=pltpu.CompilerParams(vmem_limit_bytes=50 * 1024 * 1024),
+        compiler_params=pltpu.CompilerParams(vmem_limit_bytes=44 * 1024 * 1024),
         cost_estimate=pl.CostEstimate(
             flops=2 * 27 * channels * channels * frames * 6 * wide,
             bytes_accessed=2 * 54 * channels * channels,
             transcendentals=0,
         ),
         name="first_block",
-    )(place, *pieces, gains, weight_one, weight_two, later)
+    )(place, *pieces, gains, weight_one, weight_two, *later)
 
 
 def second_kernel(
@@ -749,21 +750,21 @@
         place, mine, swapped(theirs, "cols"), tiles, weight_three
     )
     pieces = [paired(near, "rows", 0), own, paired(far, "rows", 1)]
+    weight_upsample, weight_four, _ = lax.optimization_barrier((weight_upsample, weight_four, own))
+    weight_upsample = combine_weights(weight_upsample)
+    weight_four = align_weights(weight_four)
+    tile_near, tile_far, *_ = lax.optimization_barrier((tile_near, tile_far, *pieces))
     tiles = [paired(tile_near, "rows", 0), windows, paired(tile_far, "rows", 1)]
-    weight_upsample, own = lax.optimization_barrier((weight_upsample, own))
-    weight_upsample = combine_weights(weight_upsample)
     blocked = first_block(
         place,
         pieces,
         gains,
         weight_one.reshape(9, 3, channels, channels),
         weight_two.reshape(9, 3, channels, channels),
-        weight_upsample,
+        (weight_upsample, weight_four),
         sizes,
     )
     blocks = [paired(blocked, "rows", 0), blocked, paired(blocked, "rows", 1)]
-    weight_four, _ = lax.optimization_barrier((weight_four, blocked))
-    weight_four = align_weights(weight_four)
     frames = second_block(
         place,
         blocks,

time: 81.9 us -> 87.8 us (1.072)
  waiting for transfers between devices: 7.61 us -> 14.9 us
  starting transfers between devices: 23 us -> 17.9 us
  local copies, waits for them, and re-layouts: 8 us -> 11.6 us
    ppermute x6, waiting for transfers between devices: 3.4 us -> 10.7 us  [paired(): lax.ppermute(value, axis, pairs + [(high, low) for low, high in pairs])]
    ppermute x3, starting transfers between devices: 11.1 us -> 5.95 us  [swapped(): return lax.ppermute(value, axis, [(0, 1), (1, 0)])]
    unnamed x32 -> x36, local copies, waits for them, and re-layouts: 6.68 us -> 10.3 us
  transfers between devices with their start and end apart: 9 -> 9, of which waited for: 5 -> 6; matrix products, arithmetic and copies ran while one was open for 1% -> 1% of each run, Pallas kernels for 18% -> 16%
where the time goes in v9:
time: 87.8 us; the launch traced here: 87.5 us
  Pallas kernels  42.2 us (48%)
  starting transfers between devices  17.9 us (20%)
  waiting for transfers between devices  14.9 us (17%)
  local copies, waits for them, and re-layouts  11.6 us (13%)
    pallas_call x1, Pallas kernels, second_block(): pl.pallas_call(functools.partial(second_kernel, wide, sizes), out_shape=j...  23.7 us
    ppermute x6, starting transfers between devices, paired(): lax.ppermute(value, axis, pairs + [(high, low) for low, high in pairs])  11.9 us
    pallas_call x1, Pallas kernels, first_block(): pl.pallas_call(functools.partial(first_kernel, wide, sizes), out_shape=ja...  11 us
    ppermute x6, waiting for transfers between devices, paired(): lax.ppermute(value, axis, pairs + [(high, low) for low, high in pairs])  10.7 us
    unnamed x36, local copies, waits for them, and re-layouts  10.3 us
    ppermute x3, starting transfers between devices, swapped(): return lax.ppermute(value, axis, [(0, 1), (1, 0)])  5.95 us
    ppermute x3, waiting for transfers between devices, swapped(): return lax.ppermute(value, axis, [(0, 1), (1, 0)])  4.23 us
    pallas_call x2, Pallas kernels, align_weights(): pl.pallas_call(align_kernel, out_shape=jax.ShapeDtypeStruct((4 * half, 18...  2.98 us
  transfers between devices with their start and end apart: 9, of which 6 were waited for; matrix products, arithmetic and copies ran while one was open for 1% of the time, Pallas kernels for 16%

profile of v9, /device:TPU:9, one launch (start us, length us, event | category | flops | bytes accessed | tf_op | source)
XLA Modules:
  0.0 87.5 jit_solution(310775794286364579)
XLA Ops:
  0.0 0.7 collective-permute-start
  0.7 0.6 pad_add_fusion.place
  1.3 0.6 collective-permute-done.arrived
  1.8 0.6 copy-done.13
  2.5 2.5 %pack.1 = (bf16[8,24,384]{2,1,0:T(8,128)(2,1)}, bf16[12,24,384]{2,1,0:T(8,128)(2,1)}, bf16[20,32,384]{2,1,0:T(8,128)(2,1)}) custom-call(s32[4]{0:T(128)} %pad_add_fusion.place, bf16[2,64,384]{2,1,0:T(8,128)(2,1)} %bitcast.20, bf16[2,64,384]{2,1,0:T(8,128)(2,1)} %copy-done.13, bf16[2,64,384]{2,1,0:T(8,128)(2,1)} %bitcast.21, bf16[2,64,384]{2,1,0:T(8,128)(2,1)} %bitcast.22, ...), custom_call_target="tpu_custom_call" | custom-call | tf_op jit(solution)/shard_map/pack/pallas_call | solution.py:235
  5.0 1.2 %collective-permute-start.1 = (bf16[12,24,384]{2,1,0:T(8,128)(2,1)}, bf16[12,24,384]{2,1,0:T(8,128)(2,1)S(1)}, u32[]{:S(2)}, u32[]{:S(2)}) collective-permute-start(bf16[12,24,384]{2,1,0:T(8,128)(2,1)} %get-tuple-element.22), channel_id=1, source_target_pairs={{0,1},{1,0},{2,3},{3,2},{4,5},{5,4},{6,7},{7,6},{8,9},{9,8},{10,11... | collective-permute-start | bytes 663560 | tf_op jit(solution)/shard_map/ppermute | solution.py:18
  6.2 1.6 %copy-done.4 = bf16[5184,192]{0,1:T(8,128)(2,1)S(1)} copy-done((bf16[5184,192]{0,1:T(8,128)(2,1)S(1)}, bf16[5184,192]{0,1:T(8,128)(2,1)}, u32[]{:S(2)}) %copy-start.4) | copy-done | bytes 1990680
  7.7 1.5 %align_weights.2.later.w3 = bf16[768,3456]{1,0:T(8,128)(2,1)S(1)} custom-call(bf16[192,5184]{1,0:T(8,128)(2,1)S(1)} %bitcast.14), custom_call_target="tpu_custom_call" | custom-call | tf_op jit(solution)/shard_map/align_weights/pallas_call | solution.py:362
  9.2 2.6 %collective-permute-done.1.theirs = bf16[12,24,384]{2,1,0:T(8,128)(2,1)S(1)} collective-permute-done((bf16[12,24,384]{2,1,0:T(8,128)(2,1)}, bf16[12,24,384]{2,1,0:T(8,128)(2,1)S(1)}, u32[]{:S(2)}, u32[]{:S(2)}) %collective-permute-start.1) | collective-permute-done | bytes 221216 | tf_op jit(solution)/shard_map/ppermute | solution.py:18
  11.9 1.5 %stack.33 = (bf16[2,8,24,384]{3,2,1,0:T(8,128)(2,1)S(1)}, bf16[14,24,384]{2,1,0:T(8,128)(2,1)}, bf16[14,24,384]{2,1,0:T(8,128)(2,1)}, bf16[20,24,384]{2,1,0:T(8,...) custom-call(s32[4]{0:T(128)S(1)} %copy-done.12, bf16[8,24,384]{2,1,0:T(8,128)(2,1)S(1)} %copy-done.9, ...), custom_call_target="tpu_custom_call" | custom-call | tf_op jit(solution)/shard_map/stack/pallas_call | solution.py:301
  13.4 1.2 %collective-permute-start.2 = (bf16[14,24,384]{2,1,0:T(8,128)(2,1)}, bf16[14,24,384]{2,1,0:T(8,128)(2,1)S(1)}, u32[]{:S(2)}, u32[]{:S(2)}) collective-permute-start(bf16[14,24,384]{2,1,0:T(8,128)(2,1)} %get-tuple-element.25), channel_id=1, source_target_pairs={{0,2},{4,6},{8,10},{12,14},{2,0},{6,4},{10,8},{14,12},{1,3},{5,7},... | collective-permute-start | bytes 774152 | tf_op jit(solution)/shard_map/ppermute | solution.py:23
  14.7 2.1 %collective-permute-start.3 = (bf16[14,24,384]{2,1,0:T(8,128)(2,1)}, bf16[14,24,384]{2,1,0:T(8,128)(2,1)}, u32[]{:S(2)}, u32[]{:S(2)}) collective-permute-start(bf16[14,24,384]{2,1,0:T(8,128)(2,1)} %get-tuple-element.27), channel_id=1, source_target_pairs={{2,4},{6,8},{10,12},{4,2},{8,6},{12,10},{3,5},{7,9},{11,13},{5,3},... | collective-permute-start | bytes 774152 | tf_op jit(solution)/shard_map/ppermute | solution.py:23
  16.9 0.1 stack_tile.7
  17.0 1.5 %align_weights.3.later_two.w4 = bf16[768,3456]{1,0:T(8,128)(2,1)S(1)} custom-call(bf16[192,5184]{1,0:T(8,128)(2,1)S(1)} %bitcast.15), custom_call_target="tpu_custom_call" | custom-call | tf_op jit(solution)/shard_map/align_weights/pallas_call | solution.py:362
  18.5 0.5 combine_weights.1.later_one.wu
  19.0 5.7 %collective-permute-done.2.near = bf16[14,24,384]{2,1,0:T(8,128)(2,1)S(1)} collective-permute-done((bf16[14,24,384]{2,1,0:T(8,128)(2,1)}, bf16[14,24,384]{2,1,0:T(8,128)(2,1)S(1)}, u32[]{:S(2)}, u32[]{:S(2)}) %collective-permute-start.2) | collective-permute-done | bytes 258080 | tf_op jit(solution)/shard_map/ppermute | solution.py:23
  24.7 2.2 %collective-permute-start.6 = (bf16[10,24,384]{2,1,0:T(8,128)(2,1)}, bf16[10,24,384]{2,1,0:T(8,128)(2,1)}, u32[]{:S(2)}, u32[]{:S(2)}) collective-permute-start(bf16[10,24,384]{2,1,0:T(8,128)(2,1)} %get-tuple-element.32), channel_id=1, source_target_pairs={{0,2},{4,6},{8,10},{12,14},{2,0},{6,4},{10,8},{14,12},{1,3},{5,7},... | collective-permute-start | bytes 552968 | tf_op jit(solution)/shard_map/ppermute | solution.py:23
  26.9 1.9 %collective-permute-start.7 = (bf16[10,24,384]{2,1,0:T(8,128)(2,1)}, bf16[10,24,384]{2,1,0:T(8,128)(2,1)}, u32[]{:S(2)}, u32[]{:S(2)}) collective-permute-start(bf16[10,24,384]{2,1,0:T(8,128)(2,1)} %get-tuple-element.34), channel_id=1, source_target_pairs={{2,4},{6,8},{10,12},{4,2},{8,6},{12,10},{3,5},{7,9},{11,13},{5,3},... | collective-permute-start | bytes 552968 | tf_op jit(solution)/shard_map/ppermute | solution.py:23
  28.9 11.0 %first_block.1.blocked = bf16[4,48,384]{2,1,0:T(8,128)(2,1)S(1)} custom-call(s32[4]{0:T(128)S(1)} %copy-done.12, bf16[14,24,384]{2,1,0:T(8,128)(2,1)S(1)} %collective-permute-done.2.near, bf16[2,8,24,384]{3,2,1,0:T(8,128)(2,1)S(1)} %get-tuple-element.26.own, bf16[14,24,384]{2,1,0:T(8,128)(2,1)} %collective-permute-done.3.far, ...), custom_call_target="tpu_custom_call" | custom-call | flops 4586471424 | bytes 15925248 | tf_op jit(solution)/shard_map/first_block/pallas_call | solution.py:517
  39.9 2.5 %collective-permute-start.4 = (bf16[4,48,384]{2,1,0:T(8,128)(2,1)S(1)}, bf16[4,48,384]{2,1,0:T(8,128)(2,1)S(1)}, u32[]{:S(2)}, u32[]{:S(2)}) collective-permute-start(bf16[4,48,384]{2,1,0:T(8,128)(2,1)S(1)} %first_block.1.blocked), channel_id=1, source_target_pairs={{0,2},{4,6},{8,10},{12,14},{2,0},{6,4},{10,8},{14,12},{1,3},{5,7},... | collective-permute-start | bytes 442376 | tf_op jit(solution)/shard_map/ppermute | solution.py:23
  42.4 1.9 %collective-permute-start.5 = (bf16[4,48,384]{2,1,0:T(8,128)(2,1)S(1)}, bf16[4,48,384]{2,1,0:T(8,128)(2,1)S(1)}, u32[]{:S(2)}, u32[]{:S(2)}) collective-permute-start(bf16[4,48,384]{2,1,0:T(8,128)(2,1)S(1)} %first_block.1.blocked), channel_id=1, source_target_pairs={{2,4},{6,8},{10,12},{4,2},{8,6},{12,10},{3,5},{7,9},{11,13},{5,3},... | collective-permute-start | bytes 442376 | tf_op jit(solution)/shard_map/ppermute | solution.py:23
  44.3 0.6 collective-permute-done.4.near
  44.9 4.3 %collective-permute-done.5.far = bf16[4,48,384]{2,1,0:T(8,128)(2,1)S(1)} collective-permute-done((bf16[4,48,384]{2,1,0:T(8,128)(2,1)S(1)}, bf16[4,48,384]{2,1,0:T(8,128)(2,1)S(1)}, u32[]{:S(2)}, u32[]{:S(2)}) %collective-permute-start.5) | collective-permute-done | bytes 147488 | tf_op jit(solution)/shard_map/ppermute | solution.py:23
  49.3 0.7 copy-done.10
  49.9 2.5 %copy-done.1 = bf16[768,3456]{1,0:T(8,128)(2,1)S(1)} copy-done((bf16[768,3456]{1,0:T(8,128)(2,1)S(1)}, bf16[768,3456]{1,0:T(8,128)(2,1)}, u32[]{:S(2)}) %copy-start.1) | copy-done | bytes 5308440
  52.4 2.5 %copy-done.3 = bf16[768,3456]{1,0:T(8,128)(2,1)S(1)} copy-done((bf16[768,3456]{1,0:T(8,128)(2,1)S(1)}, bf16[768,3456]{1,0:T(8,128)(2,1)}, u32[]{:S(2)}) %copy-start.3) | copy-done | bytes 5308440
  55.0 1.5 %copy-done.6 = bf16[1152,768]{1,0:T(8,128)(2,1)S(1)} copy-done((bf16[1152,768]{1,0:T(8,128)(2,1)S(1)}, bf16[1152,768]{1,0:T(8,128)(2,1)}, u32[]{:S(2)}) %copy-start.6) | copy-done | bytes 1769496
  56.4 0.9 %copy-done.11 = bf16[4,48,384]{2,1,0:T(8,128)(2,1)S(1)} copy-done((bf16[4,48,384]{2,1,0:T(8,128)(2,1)S(1)}, bf16[4,48,384]{2,1,0:T(8,128)(2,1)}, u32[]{:S(2)}) %copy-start.11) | copy-done | bytes 147480
  57.3 23.7 %second_block.1 = bf16[8,4,16,384]{3,2,1,0:T(8,128)(2,1)S(1)} custom-call(s32[4]{0:T(128)S(1)} %copy-done.12, bf16[4,48,384]{2,1,0:T(8,128)(2,1)S(1)} %collective-permute-done.4.near, bf16[4,48,384]{2,1,0:T(8,128)(2,1)S(1)} %first_block.1.blocked, bf16[4,48,384]{2,1,0:T(8,128)(2,1)S(1)} %copy-done.11, bf16[10,24,384]{2,1,0:T(8,128)(2,1)} %collective-permute-done.6.tile_near, ...), custom_call_target="tpu_custom_call" | custom-call | tf_op jit(solution)/shard_map/second_block/pallas_call | solution.py:683
  81.1 4.1 %collective-permute-start.8 = (bf16[4,4,16,384]{3,2,1,0:T(8,128)(2,1)S(1)}, bf16[4,4,16,384]{3,2,1,0:T(8,128)(2,1)S(1)}, u32[]{:S(2)}, u32[]{:S(2)}) collective-permute-start(bf16[4,4,16,384]{3,2,1,0:T(8,128)(2,1)S(1)} %constant_dynamic-slice_fusion), channel_id=1, source_target_pairs={{0,16},{16,0},{1,17},{17,1},{2,18},{18,2},{3,19},{19,3},{4,20},{20... | collective-permute-start | bytes 589832 | tf_op jit(solution)/shard_map/ppermute | solution.py:18
  85.2 1.1 %collective-permute-done.8 = bf16[4,4,16,384]{3,2,1,0:T(8,128)(2,1)S(1)} collective-permute-done((bf16[4,4,16,384]{3,2,1,0:T(8,128)(2,1)S(1)}, bf16[4,4,16,384]{3,2,1,0:T(8,128)(2,1)S(1)}, u32[]{:S(2)}, u32[]{:S(2)}) %collective-permute-start.8) | collective-permute-done | bytes 196640 | tf_op jit(solution)/shard_map/ppermute | solution.py:18
  86.3 1.1 %reshape.17 = bf16[4,4,64,192]{3,2,1,0:T(8,128)(2,1)} reshape(bf16[4,4,32,384]{3,2,1,0:T(8,128)(2,1)S(1)} %pad_maximum_fusion) | data formatting | bytes 786432 | tf_op jit(solution)/shard_map/reshape | solution.py:785
  (41 shorter events, 0.3 us)
Async XLA Ops:
  0.0 1.8 %collective-permute-start = (bf16[2,64,384]{2,1,0:T(8,128)(2,1)}, bf16[2,64,384]{2,1,0:T(8,128)(2,1)S(1)}, u32[]{:S(2)}, u32[]{:S(2)}) collective-permute-start(bf16[2,64,384]{2,1,0:T(8,128)(2,1)} %bitcast.19), channel_id=1, source_target_pairs={{0,16},{16,0},{1,17},{17,1},{2,18},{18,2},{3,19},{19,3},{4,20},{20... | collective-permute-start | bytes 294920 | tf_op jit(solution)/shard_map/ppermute | solution.py:18
  1.8 0.6 copy-start.13
  5.0 6.9 %collective-permute-start.1 = (bf16[12,24,384]{2,1,0:T(8,128)(2,1)}, bf16[12,24,384]{2,1,0:T(8,128)(2,1)S(1)}, u32[]{:S(2)}, u32[]{:S(2)}) collective-permute-start(bf16[12,24,384]{2,1,0:T(8,128)(2,1)} %get-tuple-element.22), channel_id=1, source_target_pairs={{0,1},{1,0},{2,3},{3,2},{4,5},{5,4},{6,7},{7,6},{8,9},{9,8},{10,11... | collective-permute-start | bytes 663560 | tf_op jit(solution)/shard_map/ppermute | solution.py:18
  6.2 1.6 %copy-start.4 = (bf16[5184,192]{0,1:T(8,128)(2,1)S(1)}, bf16[5184,192]{0,1:T(8,128)(2,1)}, u32[]{:S(2)}) copy-start(bf16[5184,192]{0,1:T(8,128)(2,1)} %param.30) | copy-start | bytes 5971972
  7.7 4.1 %copy-start.8 = (bf16[20,32,384]{2,1,0:T(8,128)(2,1)S(1)}, bf16[20,32,384]{2,1,0:T(8,128)(2,1)}, u32[]{:S(2)}) copy-start(bf16[20,32,384]{2,1,0:T(8,128)(2,1)} %get-tuple-element.23.tiles) | copy-start | bytes 1474564
  7.7 4.1 %copy-start.9 = (bf16[8,24,384]{2,1,0:T(8,128)(2,1)S(1)}, bf16[8,24,384]{2,1,0:T(8,128)(2,1)}, u32[]{:S(2)}) copy-start(bf16[8,24,384]{2,1,0:T(8,128)(2,1)} %get-tuple-element.21.mine) | copy-start | bytes 442372
  7.7 4.1 %copy-start.12 = (s32[4]{0:T(128)S(1)}, s32[4]{0:T(128)}, u32[]{:S(2)}) copy-start(s32[4]{0:T(128)} %pad_add_fusion.place) | copy-start | bytes 52
  9.2 4.2 %copy-start = (bf16[768,3456]{1,0:T(8,128)(2,1)}, bf16[768,3456]{1,0:T(8,128)(2,1)S(1)}, u32[]{:S(2)}) copy-start(bf16[768,3456]{1,0:T(8,128)(2,1)S(1)} %align_weights.2.later.w3) | copy-start | bytes 15925252
  11.8 4.9 %copy-start.16 = (f32[192]{0:T(256)S(1)}, f32[192]{0:T(256)}, u32[]{:S(2)}) copy-start(f32[192]{0:T(256)} %param.24) | copy-start | bytes 2308
  11.8 5.0 %copy-start.17 = (f32[192]{0:T(256)S(1)}, f32[192]{0:T(256)}, u32[]{:S(2)}) copy-start(f32[192]{0:T(256)} %param.25) | copy-start | bytes 2308
  11.9 5.1 %copy-start.14 = (f32[384]{0:T(512)S(1)}, f32[384]{0:T(512)}, u32[]{:S(2)}) copy-start(f32[384]{0:T(512)} %param.22) | copy-start | bytes 4612
  11.9 5.1 %copy-start.15 = (f32[384]{0:T(512)S(1)}, f32[384]{0:T(512)}, u32[]{:S(2)}) copy-start(f32[384]{0:T(512)} %param.23) | copy-start | bytes 4612
  11.9 5.1 %copy-start.5 = (bf16[5184,192]{0,1:T(8,128)(2,1)S(1)}, bf16[5184,192]{0,1:T(8,128)(2,1)}, u32[]{:S(2)}) copy-start(bf16[5184,192]{0,1:T(8,128)(2,1)} %param.31) | copy-start | bytes 5971972
  13.4 11.3 %collective-permute-start.2 = (bf16[14,24,384]{2,1,0:T(8,128)(2,1)}, bf16[14,24,384]{2,1,0:T(8,128)(2,1)S(1)}, u32[]{:S(2)}, u32[]{:S(2)}) collective-permute-start(bf16[14,24,384]{2,1,0:T(8,128)(2,1)} %get-tuple-element.25), channel_id=1, source_target_pairs={{0,2},{4,6},{8,10},{12,14},{2,0},{6,4},{10,8},{14,12},{1,3},{5,7},... | collective-permute-start | bytes 774152 | tf_op jit(solution)/shard_map/ppermute | solution.py:23
  14.7 10.0 %collective-permute-start.3 = (bf16[14,24,384]{2,1,0:T(8,128)(2,1)}, bf16[14,24,384]{2,1,0:T(8,128)(2,1)}, u32[]{:S(2)}, u32[]{:S(2)}) collective-permute-start(bf16[14,24,384]{2,1,0:T(8,128)(2,1)} %get-tuple-element.27), channel_id=1, source_target_pairs={{2,4},{6,8},{10,12},{4,2},{8,6},{12,10},{3,5},{7,9},{11,13},{5,3},... | collective-permute-start | bytes 774152 | tf_op jit(solution)/shard_map/ppermute | solution.py:23
  17.0 1.5 %copy-start.7 = (bf16[3456,192]{0,1:T(8,128)(2,1)S(1)}, bf16[3456,192]{0,1:T(8,128)(2,1)}, u32[]{:S(2)}) copy-start(bf16[3456,192]{0,1:T(8,128)(2,1)} %param.29) | copy-start | bytes 3981316
  18.5 21.3 %copy-start.2 = (bf16[768,3456]{1,0:T(8,128)(2,1)}, bf16[768,3456]{1,0:T(8,128)(2,1)S(1)}, u32[]{:S(2)}) copy-start(bf16[768,3456]{1,0:T(8,128)(2,1)S(1)} %align_weights.3.later_two.w4) | copy-start | bytes 15925252
  24.7 25.2 %collective-permute-start.6 = (bf16[10,24,384]{2,1,0:T(8,128)(2,1)}, bf16[10,24,384]{2,1,0:T(8,128)(2,1)}, u32[]{:S(2)}, u32[]{:S(2)}) collective-permute-start(bf16[10,24,384]{2,1,0:T(8,128)(2,1)} %get-tuple-element.32), channel_id=1, source_target_pairs={{0,2},{4,6},{8,10},{12,14},{2,0},{6,4},{10,8},{14,12},{1,3},{5,7},... | collective-permute-start | bytes 552968 | tf_op jit(solution)/shard_map/ppermute | solution.py:23
  26.9 23.0 %collective-permute-start.7 = (bf16[10,24,384]{2,1,0:T(8,128)(2,1)}, bf16[10,24,384]{2,1,0:T(8,128)(2,1)}, u32[]{:S(2)}, u32[]{:S(2)}) collective-permute-start(bf16[10,24,384]{2,1,0:T(8,128)(2,1)} %get-tuple-element.34), channel_id=1, source_target_pairs={{2,4},{6,8},{10,12},{4,2},{8,6},{12,10},{3,5},{7,9},{11,13},{5,3},... | collective-permute-start | bytes 552968 | tf_op jit(solution)/shard_map/ppermute | solution.py:23
  39.9 5.1 %collective-permute-start.4 = (bf16[4,48,384]{2,1,0:T(8,128)(2,1)S(1)}, bf16[4,48,384]{2,1,0:T(8,128)(2,1)S(1)}, u32[]{:S(2)}, u32[]{:S(2)}) collective-permute-start(bf16[4,48,384]{2,1,0:T(8,128)(2,1)S(1)} %first_block.1.blocked), channel_id=1, source_target_pairs={{0,2},{4,6},{8,10},{12,14},{2,0},{6,4},{10,8},{14,12},{1,3},{5,7},... | collective-permute-start | bytes 442376 | tf_op jit(solution)/shard_map/ppermute | solution.py:23
  42.4 6.9 %collective-permute-start.5 = (bf16[4,48,384]{2,1,0:T(8,128)(2,1)S(1)}, bf16[4,48,384]{2,1,0:T(8,128)(2,1)S(1)}, u32[]{:S(2)}, u32[]{:S(2)}) collective-permute-start(bf16[4,48,384]{2,1,0:T(8,128)(2,1)S(1)} %first_block.1.blocked), channel_id=1, source_target_pairs={{2,4},{6,8},{10,12},{4,2},{8,6},{12,10},{3,5},{7,9},{11,13},{5,3},... | collective-permute-start | bytes 442376 | tf_op jit(solution)/shard_map/ppermute | solution.py:23
  49.3 0.7 copy-start.10
  49.9 2.5 %copy-start.1 = (bf16[768,3456]{1,0:T(8,128)(2,1)S(1)}, bf16[768,3456]{1,0:T(8,128)(2,1)}, u32[]{:S(2)}) copy-start(bf16[768,3456]{1,0:T(8,128)(2,1)} %copy-done) | copy-start | bytes 15925252
  52.4 2.5 %copy-start.3 = (bf16[768,3456]{1,0:T(8,128)(2,1)S(1)}, bf16[768,3456]{1,0:T(8,128)(2,1)}, u32[]{:S(2)}) copy-start(bf16[768,3456]{1,0:T(8,128)(2,1)} %copy-done.2) | copy-start | bytes 15925252
  54.9 1.5 %copy-start.6 = (bf16[1152,768]{1,0:T(8,128)(2,1)S(1)}, bf16[1152,768]{1,0:T(8,128)(2,1)}, u32[]{:S(2)}) copy-start(bf16[1152,768]{1,0:T(8,128)(2,1)} %wt.1) | copy-start | bytes 5308420
  56.4 0.9 %copy-start.11 = (bf16[4,48,384]{2,1,0:T(8,128)(2,1)S(1)}, bf16[4,48,384]{2,1,0:T(8,128)(2,1)}, u32[]{:S(2)}) copy-start(bf16[4,48,384]{2,1,0:T(8,128)(2,1)} %copy-done.10) | copy-start | bytes 442372
  81.1 5.1 %collective-permute-start.8 = (bf16[4,4,16,384]{3,2,1,0:T(8,128)(2,1)S(1)}, bf16[4,4,16,384]{3,2,1,0:T(8,128)(2,1)S(1)}, u32[]{:S(2)}, u32[]{:S(2)}) collective-permute-start(bf16[4,4,16,384]{3,2,1,0:T(8,128)(2,1)S(1)} %constant_dynamic-slice_fusion), channel_id=1, source_target_pairs={{0,16},{16,0},{1,17},{17,1},{2,18},{18,2},{3,19},{19,3},{4,20},{20... | collective-permute-start | bytes 589832 | tf_op jit(solution)/shard_map/ppermute | solution.py:18

commit v10 on v8

--- a/solution.py
+++ b/solution.py
@@ -123,27 +123,48 @@
     return lax.dot_general(left, right, (((1,), (1,)), ((), ())), preferred_element_type=F32)
 
 
-def high_product(acc, even, odd, count, height, wide, weights):
-    rows = count * (height - 2) * wide
+def split_frames(count):
+    first = count // 4
+    second = first + (count - first) // 2
+    return (0, first), (first, second), (second, count)
+
+
+def group_slots(group, groups):
+    first, last = groups[group]
+    return (0 if group == 0 else first + 2), last + 2
+
+
+def grouped_taps(planes, groups, frames, height, wide, dt, dy):
+    inner = (height - 2) * wide
+    parts = []
+    for f in frames:
+        for group, (even, odd) in enumerate(planes):
+            first, last = group_slots(group, groups)
+            if first <= f + dt < last:
+                slot = f + dt - first
+                if dy == 1:
+                    parts.append(odd[slot * inner : (slot + 1) * inner, :])
+                else:
+                    begin = slot * height * wide + dy * wide
+                    parts.append(even[begin : begin + inner, :])
+    return jnp.concatenate(parts, axis=0)
+
+
+def high_column(n, acc, planes, groups, group, height, wide, weights):
     channels = weights.shape[1] // 9
-
-    def column(n, carry):
-        outputs = pl.ds(pl.multiple_of(n * LANES, LANES), LANES)
-        total = None
-        for first, last in ((0, 4), (4, 8), (8, 9)):
-            left = jnp.concatenate(
-                [
-                    taps(even, odd, 0, count, height, wide, t // 3, t % 3)
-                    for t in range(first, last)
-                ],
-                axis=1,
-            )
-            part = transposed_dot(left, weights[outputs, first * channels : last * channels])
-            total = part if total is None else total + part
-        acc[n, 0:rows, :] = total
-        return carry
-
-    lax.fori_loop(0, weights.shape[0] // LANES, column, 0)
+    outputs = pl.ds(pl.multiple_of(n * LANES, LANES), LANES)
+    total = None
+    for first, last in ((0, 4), (4, 8), (8, 9)):
+        left = jnp.concatenate(
+            [
+                grouped_taps(planes, groups, range(*groups[group]), height, wide, t // 3, t % 3)
+                for t in range(first, last)
+            ],
+            axis=1,
+        )
+        part = transposed_dot(left, weights[outputs, first * channels : last * channels])
+        total = part if total is None else total + part
+    acc[n] = total
 
 
 def high_sum(acc, start, size):
@@ -559,17 +580,18 @@
     mixed,
     de,
     do,
-    x3e,
-    x3o,
-    x4e,
-    x4o,
     lifted_ref,
+    *buffers,
 ):
+    ups, threes, fours = buffers[0:3], buffers[3:6], buffers[6:9]
+    planes_three = [buffers[9 + 2 * g : 11 + 2 * g] for g in range(3)]
+    planes_four = [buffers[15 + 2 * g : 17 + 2 * g] for g in range(3)]
     channels = blocked.shape[-1]
     half = channels // 2
     size = 6 * wide
     frames = blocked.shape[0]
     count = 2 * frames
+    groups = split_frames(count)
     height, width = sizes
     row = place[3]
 
@@ -616,68 +638,98 @@
     lax.fori_loop(0, frames, double, 0)
 
 
-    for py in range(2):
-
-        def enlarge(n, carry):
-            lanes = pl.ds(pl.multiple_of(n * LANES, LANES), LANES)
+    for f in range(2):
+        store(*planes_three[0], f, cached(4, 4, 4, 2, f), 8, wide)
+        store(*planes_four[0], f, cached(8, 12, 4, 1, f), 6, wide)
+    gain3, gain4 = gains[2:3, :], gains[3:4, :]
+    mask_three = line_mask(place, wide, 4 * row - 2, 8, 2 * height, width)
+    mask_four = mask_three[wide : 7 * wide]
+    part = 4 * wide
+
+    def enlarge(group, n):
+        first, last = groups[group]
+        lanes = pl.ds(pl.multiple_of(n * LANES, LANES), LANES)
+        rows = (last - first) * part
+        for py in range(2):
             left = jnp.concatenate(
-                [taps(de, do, 0, count, 6, wide, 0, py), taps(de, do, 0, count, 6, wide, 0, py + 1)],
+                [
+                    taps(de, do, first, last - first, 6, wide, 0, py),
+                    taps(de, do, first, last - first, 6, wide, 0, py + 1),
+                ],
                 axis=1,
             )
-            acc[n, py * count * 4 * wide : (py + 1) * count * 4 * wide, :] = transposed_dot(
-                left, wu[py, lanes, :]
-            )
-            return carry
-
-        lax.fori_loop(0, 2 * channels // LANES, enlarge, 0)
-
-    for f in range(2):
-        store(x3e, x3o, f, cached(4, 4, 4, 2, f), 8, wide)
-        store(x4e, x4o, f, cached(8, 12, 4, 1, f), 6, wide)
-    gain3, gain4 = gains[2:3, :], gains[3:4, :]
-    mask_three = line_mask(place, wide, 4 * row - 2, 8, 2 * height, width)
-    part = 4 * wide
-
-    def norm_three(f, carry):
-        values = []
-        for py in range(2):
-            start = pl.multiple_of(py * count * part + f * part, 16)
-            values.append(high_sum(acc, start, part).astype(BF16).astype(F32))
+            ups[group][n, py * rows : (py + 1) * rows, :] = transposed_dot(left, wu[py, lanes, :])
+
+    def local(group, f):
+        return jnp.minimum(f, groups[group][1] - groups[group][0] - 1)
+
+    def norm_three(group, f):
+        first, last = groups[group]
+        f = local(group, f)
+        values = [
+            high_sum(ups[group], aligned(f + py * (last - first), part), part)
+            .astype(BF16)
+            .astype(F32)
+            for py in range(2)
+        ]
         lifted = jnp.concatenate(
             [values[h % 2][(h // 2) * wide : (h // 2 + 1) * wide] for h in range(8)], axis=0
         )
-        lifted_ref[pl.ds(aligned(f, part), part), :] = lifted[2 * wide : 6 * wide]
-        store(x3e, x3o, f + 2, activate_pairs(lifted, gain3, mask_three), 8, wide)
-        return carry
-
-    lax.fori_loop(0, count, norm_three, 0)
-    high_product(acc, x3e, x3o, count, 8, wide, w3)
-
-    mask_four = mask_three[wide : 7 * wide]
-
-    def norm_four(f, carry):
-        values = high_sum(acc, aligned(f, size), size)
-        store(x4e, x4o, f + 2, activate_pairs(values, gain4, mask_four), 6, wide)
-        return carry
-
-    lax.fori_loop(0, count, norm_four, 0)
-    high_product(acc, x4e, x4o, count, 6, wide, w4)
-
-    def finish(f, carry):
-        start = aligned(f, part)
-        values = high_sum(acc, start, part) + lifted_ref[pl.ds(start, part), :]
+        lifted_ref[pl.ds(aligned(f + first, part), part), :] = lifted[2 * wide : 6 * wide]
+        slot = f + (2 if group == 0 else 0)
+        store(*planes_three[group], slot, activate_pairs(lifted, gain3, mask_three), 8, wide)
+
+    def norm_four(group, f):
+        f = local(group, f)
+        values = high_sum(threes[group], aligned(f, size), size)
+        slot = f + (2 if group == 0 else 0)
+        store(*planes_four[group], slot, activate_pairs(values, gain4, mask_four), 6, wide)
+
+    def finish(group, f):
+        first = groups[group][0]
+        f = local(group, f)
+        rows = pl.ds(aligned(f + first, part), part)
+        values = high_sum(fours[group], aligned(f, part), part) + lifted_ref[rows, :]
         values = pltpu.roll(values, part - HALO, 0)
         for y in range(4):
             inner = wide - 2 * HALO
-            out_ref[f, y] = values[y * wide : y * wide + inner].astype(BF16)
-        return carry
-
-    lax.fori_loop(0, count, finish, 0)
+            out_ref[f + first, y] = values[y * wide : y * wide + inner].astype(BF16)
+
+    def third(group, n):
+        high_column(n, threes[group], planes_three, groups, group, 8, wide, w3)
+
+    def fourth(group, n):
+        high_column(n, fours[group], planes_four, groups, group, 6, wide, w4)
+
+    for product, vector in (
+        ((enlarge, 0), None),
+        ((enlarge, 1), (norm_three, 0)),
+        ((enlarge, 2), (norm_three, 1)),
+        ((third, 0), (norm_three, 2)),
+        ((third, 1), (norm_four, 0)),
+        ((third, 2), (norm_four, 1)),
+        ((fourth, 0), (norm_four, 2)),
+        ((fourth, 1), (finish, 0)),
+        ((fourth, 2), (finish, 1)),
+        (None, (finish, 2)),
+    ):
+
+        def step(n, carry, product=product, vector=vector):
+            for work in (product, vector):
+                if work is not None:
+                    work[0](work[1], n)
+            return carry
+
+        steps = max(2 * channels // LANES, *(last - first for first, last in groups))
+        lax.fori_loop(0, steps, step, 0)
 
 
 def second_block(place, pieces, tiles, gains, weights, sizes, wide):
     frames, _, channels = pieces[0].shape
     count = 2 * frames
+    groups = split_frames(count)
+    sizes_of = [last - first for first, last in groups]
+    slots = [last - first for first, last in (group_slots(g, groups) for g in range(3))]
     vmem = pl.BlockSpec(memory_space=pltpu.VMEM)
     return pl.pallas_call(
         functools.partial(second_kernel, wide, sizes),
@@ -686,12 +738,15 @@
         + [vmem] * 11,
         out_specs=vmem,
         scratch_shapes=[
-            pltpu.VMEM((3, 2 * count * 4 * wide, LANES), F32),
+            pltpu.VMEM((3, frames * 6 * wide, LANES), F32),
             pltpu.VMEM(((frames + 2) * 6 * wide, channels), BF16),
             *planes(count, 6, wide, channels),
-            *planes(count + 2, 8, wide, channels),
-            *planes(count + 2, 6, wide, channels),
             pltpu.VMEM((count * 4 * wide, channels), F32),
+            *(pltpu.VMEM((3, n * 8 * wide, LANES), F32) for n in sizes_of),
+            *(pltpu.VMEM((3, n * 6 * wide, LANES), F32) for n in sizes_of),
+            *(pltpu.VMEM((3, n * 4 * wide, LANES), F32) for n in sizes_of),
+            *(ref for n in slots for ref in planes(n, 8, wide, channels)),
+            *(ref for n in slots for ref in planes(n, 6, wide, channels)),
         ],
         compiler_params=pltpu.CompilerParams(vmem_limit_bytes=34 * 1024 * 1024),
         name="second_block",

time: 81.9 us -> 81.1 us (level)
  Pallas kernels: 42.1 us -> 41.2 us
    pallas_call x1, Pallas kernels: 23.7 us -> 22.9 us  [second_block(): pl.pallas_call(functools.partial(second_kernel, wide, sizes), out_shape=j...]
where the time goes in v10:
time: 81.1 us; the launch traced here: 80.7 us
  Pallas kernels  41.2 us (51%)
  starting transfers between devices  23 us (28%)
  local copies, waits for them, and re-layouts  8 us (10%)
  waiting for transfers between devices  7.61 us (9%)
    pallas_call x1, Pallas kernels, second_block(): pl.pallas_call(functools.partial(second_kernel, wide, sizes), out_shape=j...  22.9 us
    ppermute x6, starting transfers between devices, paired(): lax.ppermute(value, axis, pairs + [(high, low) for low, high in pairs])  11.8 us
    ppermute x3, starting transfers between devices, swapped(): return lax.ppermute(value, axis, [(0, 1), (1, 0)])  11.1 us
    pallas_call x1, Pallas kernels, first_block(): pl.pallas_call(functools.partial(first_kernel, wide, sizes), out_shape=ja...  11 us
    unnamed x32, local copies, waits for them, and re-layouts  6.68 us
    ppermute x3, waiting for transfers between devices, swapped(): return lax.ppermute(value, axis, [(0, 1), (1, 0)])  4.22 us
    ppermute x6, waiting for transfers between devices, paired(): lax.ppermute(value, axis, pairs + [(high, low) for low, high in pairs])  3.4 us
    pallas_call x2, Pallas kernels, align_weights(): pl.pallas_call(align_kernel, out_shape=jax.ShapeDtypeStruct((4 * half, 18...  2.98 us
  transfers between devices with their start and end apart: 9, of which 5 were waited for; matrix products, arithmetic and copies ran while one was open for 1% of the time, Pallas kernels for 18%

profile of v10, /device:TPU:9, one launch (start us, length us, event | category | flops | bytes accessed | tf_op | source)
XLA Modules:
  0.0 80.7 jit_solution(2645184034292494876)
XLA Ops:
  0.0 0.7 collective-permute-start
  0.7 0.6 pad_add_fusion.place
  1.3 0.6 collective-permute-done.arrived
  1.8 0.6 copy-done.11
  2.5 2.5 %pack.1 = (bf16[8,24,384]{2,1,0:T(8,128)(2,1)}, bf16[12,24,384]{2,1,0:T(8,128)(2,1)}, bf16[20,32,384]{2,1,0:T(8,128)(2,1)}) custom-call(s32[4]{0:T(128)} %pad_add_fusion.place, bf16[2,64,384]{2,1,0:T(8,128)(2,1)} %bitcast.20, bf16[2,64,384]{2,1,0:T(8,128)(2,1)} %copy-done.11, bf16[2,64,384]{2,1,0:T(8,128)(2,1)} %bitcast.21, bf16[2,64,384]{2,1,0:T(8,128)(2,1)} %bitcast.22, ...), custom_call_target="tpu_custom_call" | custom-call | tf_op jit(solution)/shard_map/pack/pallas_call | solution.py:256
  4.9 1.2 %collective-permute-start.1 = (bf16[12,24,384]{2,1,0:T(8,128)(2,1)}, bf16[12,24,384]{2,1,0:T(8,128)(2,1)S(1)}, u32[]{:S(2)}, u32[]{:S(2)}) collective-permute-start(bf16[12,24,384]{2,1,0:T(8,128)(2,1)} %get-tuple-element.20), channel_id=1, source_target_pairs={{0,1},{1,0},{2,3},{3,2},{4,5},{5,4},{6,7},{7,6},{8,9},{9,8},{10,11... | collective-permute-start | bytes 663560 | tf_op jit(solution)/shard_map/ppermute | solution.py:18
  6.1 1.6 %copy-done.2 = bf16[5184,192]{0,1:T(8,128)(2,1)S(1)} copy-done((bf16[5184,192]{0,1:T(8,128)(2,1)S(1)}, bf16[5184,192]{0,1:T(8,128)(2,1)}, u32[]{:S(2)}) %copy-start.2) | copy-done | bytes 1990680
  7.7 1.5 %align_weights.2.later.w3 = bf16[768,3456]{1,0:T(8,128)(2,1)S(1)} custom-call(bf16[192,5184]{1,0:T(8,128)(2,1)S(1)} %bitcast.14), custom_call_target="tpu_custom_call" | custom-call | tf_op jit(solution)/shard_map/align_weights/pallas_call | solution.py:383
  9.2 2.6 %collective-permute-done.1.theirs = bf16[12,24,384]{2,1,0:T(8,128)(2,1)S(1)} collective-permute-done((bf16[12,24,384]{2,1,0:T(8,128)(2,1)}, bf16[12,24,384]{2,1,0:T(8,128)(2,1)S(1)}, u32[]{:S(2)}, u32[]{:S(2)}) %collective-permute-start.1) | collective-permute-done | bytes 221216 | tf_op jit(solution)/shard_map/ppermute | solution.py:18
  11.8 0.0 copy-start.14
  11.8 1.5 %stack.33 = (bf16[2,8,24,384]{3,2,1,0:T(8,128)(2,1)S(1)}, bf16[14,24,384]{2,1,0:T(8,128)(2,1)}, bf16[14,24,384]{2,1,0:T(8,128)(2,1)}, bf16[20,24,384]{2,1,0:T(8,...) custom-call(s32[4]{0:T(128)S(1)} %copy-done.10, bf16[8,24,384]{2,1,0:T(8,128)(2,1)S(1)} %copy-done.7, ...), custom_call_target="tpu_custom_call" | custom-call | tf_op jit(solution)/shard_map/stack/pallas_call | solution.py:322
  13.4 1.2 %collective-permute-start.2 = (bf16[14,24,384]{2,1,0:T(8,128)(2,1)}, bf16[14,24,384]{2,1,0:T(8,128)(2,1)S(1)}, u32[]{:S(2)}, u32[]{:S(2)}) collective-permute-start(bf16[14,24,384]{2,1,0:T(8,128)(2,1)} %get-tuple-element.23), channel_id=1, source_target_pairs={{0,2},{4,6},{8,10},{12,14},{2,0},{6,4},{10,8},{14,12},{1,3},{5,7},... | collective-permute-start | bytes 774152 | tf_op jit(solution)/shard_map/ppermute | solution.py:23
  14.6 2.1 %collective-permute-start.3 = (bf16[14,24,384]{2,1,0:T(8,128)(2,1)}, bf16[14,24,384]{2,1,0:T(8,128)(2,1)}, u32[]{:S(2)}, u32[]{:S(2)}) collective-permute-start(bf16[14,24,384]{2,1,0:T(8,128)(2,1)} %get-tuple-element.25), channel_id=1, source_target_pairs={{2,4},{6,8},{10,12},{4,2},{8,6},{12,10},{3,5},{7,9},{11,13},{5,3},... | collective-permute-start | bytes 774152 | tf_op jit(solution)/shard_map/ppermute | solution.py:23
  16.7 0.1 stack_tile.6
  16.8 0.1 stack_tile.7
  16.9 1.3 %copy-done.5 = bf16[3456,192]{0,1:T(8,128)(2,1)S(1)} copy-done((bf16[3456,192]{0,1:T(8,128)(2,1)S(1)}, bf16[3456,192]{0,1:T(8,128)(2,1)}, u32[]{:S(2)}) %copy-start.5) | copy-done | bytes 1327128
  18.3 0.5 combine_weights.1.later.wu
  18.7 2.4 %collective-permute-start.6 = (bf16[10,24,384]{2,1,0:T(8,128)(2,1)}, bf16[10,24,384]{2,1,0:T(8,128)(2,1)}, u32[]{:S(2)}, u32[]{:S(2)}) collective-permute-start(bf16[10,24,384]{2,1,0:T(8,128)(2,1)} %get-tuple-element.27), channel_id=1, source_target_pairs={{0,2},{4,6},{8,10},{12,14},{2,0},{6,4},{10,8},{14,12},{1,3},{5,7},... | collective-permute-start | bytes 552968 | tf_op jit(solution)/shard_map/ppermute | solution.py:23
  21.1 1.9 %collective-permute-start.7 = (bf16[10,24,384]{2,1,0:T(8,128)(2,1)}, bf16[10,24,384]{2,1,0:T(8,128)(2,1)}, u32[]{:S(2)}, u32[]{:S(2)}) collective-permute-start(bf16[10,24,384]{2,1,0:T(8,128)(2,1)} %get-tuple-element.29), channel_id=1, source_target_pairs={{2,4},{6,8},{10,12},{4,2},{8,6},{12,10},{3,5},{7,9},{11,13},{5,3},... | collective-permute-start | bytes 552968 | tf_op jit(solution)/shard_map/ppermute | solution.py:23
  23.0 1.6 %collective-permute-done.2.near = bf16[14,24,384]{2,1,0:T(8,128)(2,1)S(1)} collective-permute-done((bf16[14,24,384]{2,1,0:T(8,128)(2,1)}, bf16[14,24,384]{2,1,0:T(8,128)(2,1)S(1)}, u32[]{:S(2)}, u32[]{:S(2)}) %collective-permute-start.2) | collective-permute-done | bytes 258080 | tf_op jit(solution)/shard_map/ppermute | solution.py:23
  24.6 11.0 %first_block.1.blocked = bf16[4,48,384]{2,1,0:T(8,128)(2,1)S(1)} custom-call(s32[4]{0:T(128)S(1)} %copy-done.10, bf16[14,24,384]{2,1,0:T(8,128)(2,1)S(1)} %collective-permute-done.2.near, bf16[2,8,24,384]{3,2,1,0:T(8,128)(2,1)S(1)} %get-tuple-element.24.own, bf16[14,24,384]{2,1,0:T(8,128)(2,1)} %collective-permute-done.3.far, ...), custom_call_target="tpu_custom_call" | custom-call | flops 4586471424 | bytes 15925248 | tf_op jit(solution)/shard_map/first_block/pallas_call | solution.py:537
  35.6 2.3 %collective-permute-start.4 = (bf16[4,48,384]{2,1,0:T(8,128)(2,1)S(1)}, bf16[4,48,384]{2,1,0:T(8,128)(2,1)S(1)}, u32[]{:S(2)}, u32[]{:S(2)}) collective-permute-start(bf16[4,48,384]{2,1,0:T(8,128)(2,1)S(1)} %first_block.1.blocked), channel_id=1, source_target_pairs={{0,2},{4,6},{8,10},{12,14},{2,0},{6,4},{10,8},{14,12},{1,3},{5,7},... | collective-permute-start | bytes 442376 | tf_op jit(solution)/shard_map/ppermute | solution.py:23
  37.9 1.9 %collective-permute-start.5 = (bf16[4,48,384]{2,1,0:T(8,128)(2,1)S(1)}, bf16[4,48,384]{2,1,0:T(8,128)(2,1)S(1)}, u32[]{:S(2)}, u32[]{:S(2)}) collective-permute-start(bf16[4,48,384]{2,1,0:T(8,128)(2,1)S(1)} %first_block.1.blocked), channel_id=1, source_target_pairs={{2,4},{6,8},{10,12},{4,2},{8,6},{12,10},{3,5},{7,9},{11,13},{5,3},... | collective-permute-start | bytes 442376 | tf_op jit(solution)/shard_map/ppermute | solution.py:23
  39.9 1.6 %copy-done.3 = bf16[5184,192]{0,1:T(8,128)(2,1)S(1)} copy-done((bf16[5184,192]{0,1:T(8,128)(2,1)S(1)}, bf16[5184,192]{0,1:T(8,128)(2,1)}, u32[]{:S(2)}) %copy-start.3) | copy-done | bytes 1990680
  41.4 1.5 %align_weights.3.w4 = bf16[768,3456]{1,0:T(8,128)(2,1)S(1)} custom-call(bf16[192,5184]{1,0:T(8,128)(2,1)S(1)} %bitcast.15), custom_call_target="tpu_custom_call" | custom-call | tf_op jit(solution)/shard_map/align_weights/pallas_call | solution.py:383
  42.9 1.8 %collective-permute-done.5.far = bf16[4,48,384]{2,1,0:T(8,128)(2,1)S(1)} collective-permute-done((bf16[4,48,384]{2,1,0:T(8,128)(2,1)S(1)}, bf16[4,48,384]{2,1,0:T(8,128)(2,1)S(1)}, u32[]{:S(2)}, u32[]{:S(2)}) %collective-permute-start.5) | collective-permute-done | bytes 147488 | tf_op jit(solution)/shard_map/ppermute | solution.py:23
  44.7 0.7 copy-done.8
  45.4 0.9 %copy-done.9 = bf16[4,48,384]{2,1,0:T(8,128)(2,1)S(1)} copy-done((bf16[4,48,384]{2,1,0:T(8,128)(2,1)S(1)}, bf16[4,48,384]{2,1,0:T(8,128)(2,1)}, u32[]{:S(2)}) %copy-start.9) | copy-done | bytes 147480
  46.3 22.9 %second_block.1 = bf16[8,4,16,384]{3,2,1,0:T(8,128)(2,1)S(1)} custom-call(s32[4]{0:T(128)S(1)} %copy-done.10, bf16[4,48,384]{2,1,0:T(8,128)(2,1)S(1)} %collective-permute-done.4.near, bf16[4,48,384]{2,1,0:T(8,128)(2,1)S(1)} %first_block.1.blocked, bf16[4,48,384]{2,1,0:T(8,128)(2,1)S(1)} %copy-done.9, bf16[10,24,384]{2,1,0:T(8,128)(2,1)} %collective-permute-done.6.tile_near, ...), custom_call_target="tpu_custom_call" | custom-call | tf_op jit(solution)/shard_map/second_block/pallas_call | solution.py:734
  69.2 9.3 %collective-permute-start.8 = (bf16[4,4,16,384]{3,2,1,0:T(8,128)(2,1)S(1)}, bf16[4,4,16,384]{3,2,1,0:T(8,128)(2,1)S(1)}, u32[]{:S(2)}, u32[]{:S(2)}) collective-permute-start(bf16[4,4,16,384]{3,2,1,0:T(8,128)(2,1)S(1)} %constant_dynamic-slice_fusion), channel_id=1, source_target_pairs={{0,16},{16,0},{1,17},{17,1},{2,18},{18,2},{3,19},{19,3},{4,20},{20... | collective-permute-start | bytes 589832 | tf_op jit(solution)/shard_map/ppermute | solution.py:18
  78.4 1.1 %collective-permute-done.8 = bf16[4,4,16,384]{3,2,1,0:T(8,128)(2,1)S(1)} collective-permute-done((bf16[4,4,16,384]{3,2,1,0:T(8,128)(2,1)S(1)}, bf16[4,4,16,384]{3,2,1,0:T(8,128)(2,1)S(1)}, u32[]{:S(2)}, u32[]{:S(2)}) %collective-permute-start.8) | collective-permute-done | bytes 196640 | tf_op jit(solution)/shard_map/ppermute | solution.py:18
  79.6 1.1 %reshape.17 = bf16[4,4,64,192]{3,2,1,0:T(8,128)(2,1)} reshape(bf16[4,4,32,384]{3,2,1,0:T(8,128)(2,1)S(1)} %pad_maximum_fusion) | data formatting | bytes 786432 | tf_op jit(solution)/shard_map/reshape | solution.py:839
  (37 shorter events, 0.2 us)
Async XLA Ops:
  0.0 1.8 %collective-permute-start = (bf16[2,64,384]{2,1,0:T(8,128)(2,1)}, bf16[2,64,384]{2,1,0:T(8,128)(2,1)S(1)}, u32[]{:S(2)}, u32[]{:S(2)}) collective-permute-start(bf16[2,64,384]{2,1,0:T(8,128)(2,1)} %bitcast.19), channel_id=1, source_target_pairs={{0,16},{16,0},{1,17},{17,1},{2,18},{18,2},{3,19},{19,3},{4,20},{20... | collective-permute-start | bytes 294920 | tf_op jit(solution)/shard_map/ppermute | solution.py:18
  1.8 0.6 copy-start.11
  4.9 6.9 %collective-permute-start.1 = (bf16[12,24,384]{2,1,0:T(8,128)(2,1)}, bf16[12,24,384]{2,1,0:T(8,128)(2,1)S(1)}, u32[]{:S(2)}, u32[]{:S(2)}) collective-permute-start(bf16[12,24,384]{2,1,0:T(8,128)(2,1)} %get-tuple-element.20), channel_id=1, source_target_pairs={{0,1},{1,0},{2,3},{3,2},{4,5},{5,4},{6,7},{7,6},{8,9},{9,8},{10,11... | collective-permute-start | bytes 663560 | tf_op jit(solution)/shard_map/ppermute | solution.py:18
  6.1 1.6 %copy-start.2 = (bf16[5184,192]{0,1:T(8,128)(2,1)S(1)}, bf16[5184,192]{0,1:T(8,128)(2,1)}, u32[]{:S(2)}) copy-start(bf16[5184,192]{0,1:T(8,128)(2,1)} %param.30) | copy-start | bytes 5971972
  7.7 4.1 %copy-start.6 = (bf16[20,32,384]{2,1,0:T(8,128)(2,1)S(1)}, bf16[20,32,384]{2,1,0:T(8,128)(2,1)}, u32[]{:S(2)}) copy-start(bf16[20,32,384]{2,1,0:T(8,128)(2,1)} %get-tuple-element.21.tiles) | copy-start | bytes 1474564
  7.7 4.1 %copy-start.7 = (bf16[8,24,384]{2,1,0:T(8,128)(2,1)S(1)}, bf16[8,24,384]{2,1,0:T(8,128)(2,1)}, u32[]{:S(2)}) copy-start(bf16[8,24,384]{2,1,0:T(8,128)(2,1)} %get-tuple-element.19.mine) | copy-start | bytes 442372
  7.7 4.1 %copy-start.10 = (s32[4]{0:T(128)S(1)}, s32[4]{0:T(128)}, u32[]{:S(2)}) copy-start(s32[4]{0:T(128)} %pad_add_fusion.place) | copy-start | bytes 52
  9.2 4.2 %copy-start = (bf16[768,3456]{1,0:T(8,128)(2,1)}, bf16[768,3456]{1,0:T(8,128)(2,1)S(1)}, u32[]{:S(2)}) copy-start(bf16[768,3456]{1,0:T(8,128)(2,1)S(1)} %align_weights.2.later.w3) | copy-start | bytes 15925252
  11.8 4.9 %copy-start.14 = (f32[192]{0:T(256)S(1)}, f32[192]{0:T(256)}, u32[]{:S(2)}) copy-start(f32[192]{0:T(256)} %param.24) | copy-start | bytes 2308
  11.8 5.0 %copy-start.15 = (f32[192]{0:T(256)S(1)}, f32[192]{0:T(256)}, u32[]{:S(2)}) copy-start(f32[192]{0:T(256)} %param.25) | copy-start | bytes 2308
  11.8 5.1 %copy-start.12 = (f32[384]{0:T(512)S(1)}, f32[384]{0:T(512)}, u32[]{:S(2)}) copy-start(f32[384]{0:T(512)} %param.22) | copy-start | bytes 4612
  11.8 5.1 %copy-start.13 = (f32[384]{0:T(512)S(1)}, f32[384]{0:T(512)}, u32[]{:S(2)}) copy-start(f32[384]{0:T(512)} %param.23) | copy-start | bytes 4612
  13.4 11.3 %collective-permute-start.2 = (bf16[14,24,384]{2,1,0:T(8,128)(2,1)}, bf16[14,24,384]{2,1,0:T(8,128)(2,1)S(1)}, u32[]{:S(2)}, u32[]{:S(2)}) collective-permute-start(bf16[14,24,384]{2,1,0:T(8,128)(2,1)} %get-tuple-element.23), channel_id=1, source_target_pairs={{0,2},{4,6},{8,10},{12,14},{2,0},{6,4},{10,8},{14,12},{1,3},{5,7},... | collective-permute-start | bytes 774152 | tf_op jit(solution)/shard_map/ppermute | solution.py:23
  14.6 10.0 %collective-permute-start.3 = (bf16[14,24,384]{2,1,0:T(8,128)(2,1)}, bf16[14,24,384]{2,1,0:T(8,128)(2,1)}, u32[]{:S(2)}, u32[]{:S(2)}) collective-permute-start(bf16[14,24,384]{2,1,0:T(8,128)(2,1)} %get-tuple-element.25), channel_id=1, source_target_pairs={{2,4},{6,8},{10,12},{4,2},{8,6},{12,10},{3,5},{7,9},{11,13},{5,3},... | collective-permute-start | bytes 774152 | tf_op jit(solution)/shard_map/ppermute | solution.py:23
  16.9 1.3 %copy-start.5 = (bf16[3456,192]{0,1:T(8,128)(2,1)S(1)}, bf16[3456,192]{0,1:T(8,128)(2,1)}, u32[]{:S(2)}) copy-start(bf16[3456,192]{0,1:T(8,128)(2,1)} %param.29) | copy-start | bytes 3981316
  18.7 24.2 %collective-permute-start.6 = (bf16[10,24,384]{2,1,0:T(8,128)(2,1)}, bf16[10,24,384]{2,1,0:T(8,128)(2,1)}, u32[]{:S(2)}, u32[]{:S(2)}) collective-permute-start(bf16[10,24,384]{2,1,0:T(8,128)(2,1)} %get-tuple-element.27), channel_id=1, source_target_pairs={{0,2},{4,6},{8,10},{12,14},{2,0},{6,4},{10,8},{14,12},{1,3},{5,7},... | collective-permute-start | bytes 552968 | tf_op jit(solution)/shard_map/ppermute | solution.py:23
  21.1 21.8 %collective-permute-start.7 = (bf16[10,24,384]{2,1,0:T(8,128)(2,1)}, bf16[10,24,384]{2,1,0:T(8,128)(2,1)}, u32[]{:S(2)}, u32[]{:S(2)}) collective-permute-start(bf16[10,24,384]{2,1,0:T(8,128)(2,1)} %get-tuple-element.29), channel_id=1, source_target_pairs={{2,4},{6,8},{10,12},{4,2},{8,6},{12,10},{3,5},{7,9},{11,13},{5,3},... | collective-permute-start | bytes 552968 | tf_op jit(solution)/shard_map/ppermute | solution.py:23
  35.6 7.3 %collective-permute-start.4 = (bf16[4,48,384]{2,1,0:T(8,128)(2,1)S(1)}, bf16[4,48,384]{2,1,0:T(8,128)(2,1)S(1)}, u32[]{:S(2)}, u32[]{:S(2)}) collective-permute-start(bf16[4,48,384]{2,1,0:T(8,128)(2,1)S(1)} %first_block.1.blocked), channel_id=1, source_target_pairs={{0,2},{4,6},{8,10},{12,14},{2,0},{6,4},{10,8},{14,12},{1,3},{5,7},... | collective-permute-start | bytes 442376 | tf_op jit(solution)/shard_map/ppermute | solution.py:23
  37.9 6.8 %collective-permute-start.5 = (bf16[4,48,384]{2,1,0:T(8,128)(2,1)S(1)}, bf16[4,48,384]{2,1,0:T(8,128)(2,1)S(1)}, u32[]{:S(2)}, u32[]{:S(2)}) collective-permute-start(bf16[4,48,384]{2,1,0:T(8,128)(2,1)S(1)} %first_block.1.blocked), channel_id=1, source_target_pairs={{2,4},{6,8},{10,12},{4,2},{8,6},{12,10},{3,5},{7,9},{11,13},{5,3},... | collective-permute-start | bytes 442376 | tf_op jit(solution)/shard_map/ppermute | solution.py:23
  39.8 1.6 %copy-start.3 = (bf16[5184,192]{0,1:T(8,128)(2,1)S(1)}, bf16[5184,192]{0,1:T(8,128)(2,1)}, u32[]{:S(2)}) copy-start(bf16[5184,192]{0,1:T(8,128)(2,1)} %param.31) | copy-start | bytes 5971972
  41.4 4.0 %copy-start.1 = (bf16[768,3456]{1,0:T(8,128)(2,1)S(1)}, bf16[768,3456]{1,0:T(8,128)(2,1)}, u32[]{:S(2)}) copy-start(bf16[768,3456]{1,0:T(8,128)(2,1)} %copy-done) | copy-start | bytes 15925252
  41.4 4.0 %copy-start.4 = (bf16[1152,768]{1,0:T(8,128)(2,1)S(1)}, bf16[1152,768]{1,0:T(8,128)(2,1)}, u32[]{:S(2)}) copy-start(bf16[1152,768]{1,0:T(8,128)(2,1)} %wt.1) | copy-start | bytes 5308420
  44.7 0.7 copy-start.8
  45.4 0.9 %copy-start.9 = (bf16[4,48,384]{2,1,0:T(8,128)(2,1)S(1)}, bf16[4,48,384]{2,1,0:T(8,128)(2,1)}, u32[]{:S(2)}) copy-start(bf16[4,48,384]{2,1,0:T(8,128)(2,1)} %copy-done.8) | copy-start | bytes 442372
  69.2 10.3 %collective-permute-start.8 = (bf16[4,4,16,384]{3,2,1,0:T(8,128)(2,1)S(1)}, bf16[4,4,16,384]{3,2,1,0:T(8,128)(2,1)S(1)}, u32[]{:S(2)}, u32[]{:S(2)}) collective-permute-start(bf16[4,4,16,384]{3,2,1,0:T(8,128)(2,1)S(1)} %constant_dynamic-slice_fusion), channel_id=1, source_target_pairs={{0,16},{16,0},{1,17},{17,1},{2,18},{18,2},{3,19},{19,3},{4,20},{20... | collective-permute-start | bytes 589832 | tf_op jit(solution)/shard_map/ppermute | solution.py:18

commit v11 on v10

--- a/solution.py
+++ b/solution.py
@@ -52,7 +52,7 @@
 
 
 def aligned(index, size):
-    return pl.multiple_of(index * size, 16)
+    return index * size if isinstance(index, int) else pl.multiple_of(index * size, 16)
 
 
 def line_mask(place, wide, first, count, limit, width):
@@ -93,19 +93,11 @@
         for copy, when in zip(copies, needed):
             pl.when(n == when)(copy.wait)
         lanes = pl.ds(pl.multiple_of(n * LANES, LANES), LANES)
-        total = None
-        for first, last in ((0, 4), (4, 8), (8, 9)):
-            left = jnp.concatenate(
-                [
-                    taps(even, odd, 0, count, height, wide, t // 3, t % 3)
-                    for t in range(first, last)
-                ],
-                axis=1,
-            )
-            right = weights[first:last, :, lanes].reshape((last - first) * channels, LANES)
-            part = jnp.dot(left, right, preferred_element_type=F32)
-            total = part if total is None else total + part
-        acc[n, 0:rows, :] = total
+        left = jnp.concatenate(
+            [taps(even, odd, 0, count, height, wide, t // 3, t % 3) for t in range(9)], axis=1
+        )
+        right = weights[:, :, lanes].reshape(9 * channels, LANES)
+        acc[n, 0:rows, :] = jnp.dot(left, right, preferred_element_type=F32)
         return carry
 
     lax.fori_loop(0, weights.shape[-1] // LANES, column, 0)
@@ -151,20 +143,14 @@
 
 
 def high_column(n, acc, planes, groups, group, height, wide, weights):
-    channels = weights.shape[1] // 9
-    outputs = pl.ds(pl.multiple_of(n * LANES, LANES), LANES)
-    total = None
-    for first, last in ((0, 4), (4, 8), (8, 9)):
-        left = jnp.concatenate(
-            [
-                grouped_taps(planes, groups, range(*groups[group]), height, wide, t // 3, t % 3)
-                for t in range(first, last)
-            ],
-            axis=1,
-        )
-        part = transposed_dot(left, weights[outputs, first * channels : last * channels])
-        total = part if total is None else total + part
-    acc[n] = total
+    left = jnp.concatenate(
+        [
+            grouped_taps(planes, groups, range(*groups[group]), height, wide, t // 3, t % 3)
+            for t in range(9)
+        ],
+        axis=1,
+    )
+    acc[n] = transposed_dot(left, weights[n * LANES : (n + 1) * LANES, :])
 
 
 def high_sum(acc, start, size):
@@ -428,6 +414,16 @@
     )(weight.T)
 
 
+def weight_copies(source, target, sems, base):
+    channels = source.shape[-1]
+    return [
+        pltpu.make_async_copy(
+            source.at[:, dx], target.at[:, :, pl.ds(dx * channels, channels)], sems.at[base + dx]
+        )
+        for dx in range(3)
+    ]
+
+
 def first_kernel(
     wide,
     sizes,
@@ -456,18 +452,10 @@
     units = frames + 2
     del later
 
-    def load(source, target, base):
-        return [
-            pltpu.make_async_copy(
-                source.at[:, dx], target.at[:, :, pl.ds(dx * channels, channels)], sems.at[base + dx]
-            )
-            for dx in range(3)
-        ]
-
-    copies_one = load(weight_one, w1, 0)
-    copies_two = load(weight_two, w2, 3)
-    for copy in copies_one + copies_two:
-        copy.start()
+    copies_one = weight_copies(weight_one, w1, sems, 0)
+    copies_two = weight_copies(weight_two, w2, sems, 3)
+    copies_one[0].start()
+    copies_one[1].start()
 
     slots = [lax.rem(y + col, 2) for y in range(2)]
 
@@ -499,6 +487,8 @@
         return carry
 
     lax.fori_loop(0, frames, norm_one, 0)
+    for copy in [copies_one[2]] + copies_two:
+        copy.start()
     low_product(acc, x1e, x1o, frames, 6, wide, w1, copies_one)
 
     mask = line_mask(place, wide, 2 * row - 1, 4, height, width)
@@ -648,7 +638,7 @@
 
     def enlarge(group, n):
         first, last = groups[group]
-        lanes = pl.ds(pl.multiple_of(n * LANES, LANES), LANES)
+        lanes = slice(n * LANES, (n + 1) * LANES)
         rows = (last - first) * part
         for py in range(2):
             left = jnp.concatenate(
@@ -660,12 +650,8 @@
             )
             ups[group][n, py * rows : (py + 1) * rows, :] = transposed_dot(left, wu[py, lanes, :])
 
-    def local(group, f):
-        return jnp.minimum(f, groups[group][1] - groups[group][0] - 1)
-
     def norm_three(group, f):
         first, last = groups[group]
-        f = local(group, f)
         values = [
             high_sum(ups[group], aligned(f + py * (last - first), part), part)
             .astype(BF16)
@@ -680,14 +666,12 @@
         store(*planes_three[group], slot, activate_pairs(lifted, gain3, mask_three), 8, wide)
 
     def norm_four(group, f):
-        f = local(group, f)
         values = high_sum(threes[group], aligned(f, size), size)
         slot = f + (2 if group == 0 else 0)
         store(*planes_four[group], slot, activate_pairs(values, gain4, mask_four), 6, wide)
 
     def finish(group, f):
         first = groups[group][0]
-        f = local(group, f)
         rows = pl.ds(aligned(f + first, part), part)
         values = high_sum(fours[group], aligned(f, part), part) + lifted_ref[rows, :]
         values = pltpu.roll(values, part - HALO, 0)
@@ -713,15 +697,11 @@
         ((fourth, 2), (finish, 1)),
         (None, (finish, 2)),
     ):
-
-        def step(n, carry, product=product, vector=vector):
-            for work in (product, vector):
-                if work is not None:
-                    work[0](work[1], n)
-            return carry
-
-        steps = max(2 * channels // LANES, *(last - first for first, last in groups))
-        lax.fori_loop(0, steps, step, 0)
+        for n in range(max(2 * channels // LANES, *(last - first for first, last in groups))):
+            if product is not None and n < 2 * channels // LANES:
+                product[0](product[1], n)
+            if vector is not None and n < groups[vector[1]][1] - groups[vector[1]][0]:
+                vector[0](vector[1], n)
 
 
 def second_block(place, pieces, tiles, gains, weights, sizes, wide):

time: 81.1 us -> 75.6 us (0.932)
  Pallas kernels: 41.2 us -> 35.8 us
    pallas_call x1, Pallas kernels: 22.9 us -> 17.4 us  [second_block(): pl.pallas_call(functools.partial(second_kernel, wide, sizes), out_shape=j...]
  transfers between devices with their start and end apart: 9 -> 9, of which waited for: 5 -> 5; matrix products, arithmetic and copies ran while one was open for 1% -> 1% of each run, Pallas kernels for 18% -> 19%
where the time goes in v11:
time: 75.6 us; the launch traced here: 75.3 us
  Pallas kernels  35.8 us (47%)
  starting transfers between devices  22.9 us (30%)
  local copies, waits for them, and re-layouts  8 us (11%)
  waiting for transfers between devices  7.61 us (10%)
    pallas_call x1, Pallas kernels, second_block(): pl.pallas_call(functools.partial(second_kernel, wide, sizes), out_shape=j...  17.4 us
    ppermute x6, starting transfers between devices, paired(): lax.ppermute(value, axis, pairs + [(high, low) for low, high in pairs])  11.8 us
    ppermute x3, starting transfers between devices, swapped(): return lax.ppermute(value, axis, [(0, 1), (1, 0)])  11.1 us
    pallas_call x1, Pallas kernels, first_block(): pl.pallas_call(functools.partial(first_kernel, wide, sizes), out_shape=ja...  11 us
    unnamed x32, local copies, waits for them, and re-layouts  6.68 us
    ppermute x3, waiting for transfers between devices, swapped(): return lax.ppermute(value, axis, [(0, 1), (1, 0)])  4.22 us
    ppermute x6, waiting for transfers between devices, paired(): lax.ppermute(value, axis, pairs + [(high, low) for low, high in pairs])  3.4 us
    pallas_call x2, Pallas kernels, align_weights(): pl.pallas_call(align_kernel, out_shape=jax.ShapeDtypeStruct((4 * half, 18...  2.98 us
  transfers between devices with their start and end apart: 9, of which 5 were waited for; matrix products, arithmetic and copies ran while one was open for 1% of the time, Pallas kernels for 19%

profile of v11, /device:TPU:9, one launch (start us, length us, event | category | flops | bytes accessed | tf_op | source)
XLA Modules:
  0.0 75.3 jit_solution(7945958537748425347)
XLA Ops:
  0.0 0.7 collective-permute-start
  0.7 0.6 pad_add_fusion.place
  1.3 0.6 collective-permute-done.arrived
  1.8 0.6 copy-done.11
  2.5 2.5 %pack.1 = (bf16[8,24,384]{2,1,0:T(8,128)(2,1)}, bf16[12,24,384]{2,1,0:T(8,128)(2,1)}, bf16[20,32,384]{2,1,0:T(8,128)(2,1)}) custom-call(s32[4]{0:T(128)} %pad_add_fusion.place, bf16[2,64,384]{2,1,0:T(8,128)(2,1)} %bitcast.20, bf16[2,64,384]{2,1,0:T(8,128)(2,1)} %copy-done.11, bf16[2,64,384]{2,1,0:T(8,128)(2,1)} %bitcast.21, bf16[2,64,384]{2,1,0:T(8,128)(2,1)} %bitcast.22, ...), custom_call_target="tpu_custom_call" | custom-call | tf_op jit(solution)/shard_map/pack/pallas_call | solution.py:242
  4.9 1.2 %collective-permute-start.1 = (bf16[12,24,384]{2,1,0:T(8,128)(2,1)}, bf16[12,24,384]{2,1,0:T(8,128)(2,1)S(1)}, u32[]{:S(2)}, u32[]{:S(2)}) collective-permute-start(bf16[12,24,384]{2,1,0:T(8,128)(2,1)} %get-tuple-element.20), channel_id=1, source_target_pairs={{0,1},{1,0},{2,3},{3,2},{4,5},{5,4},{6,7},{7,6},{8,9},{9,8},{10,11... | collective-permute-start | bytes 663560 | tf_op jit(solution)/shard_map/ppermute | solution.py:18
  6.1 1.6 %copy-done.2 = bf16[5184,192]{0,1:T(8,128)(2,1)S(1)} copy-done((bf16[5184,192]{0,1:T(8,128)(2,1)S(1)}, bf16[5184,192]{0,1:T(8,128)(2,1)}, u32[]{:S(2)}) %copy-start.2) | copy-done | bytes 1990680
  7.7 1.5 %align_weights.2.later.w3 = bf16[768,3456]{1,0:T(8,128)(2,1)S(1)} custom-call(bf16[192,5184]{1,0:T(8,128)(2,1)S(1)} %bitcast.14), custom_call_target="tpu_custom_call" | custom-call | tf_op jit(solution)/shard_map/align_weights/pallas_call | solution.py:369
  9.2 2.6 %collective-permute-done.1.theirs = bf16[12,24,384]{2,1,0:T(8,128)(2,1)S(1)} collective-permute-done((bf16[12,24,384]{2,1,0:T(8,128)(2,1)}, bf16[12,24,384]{2,1,0:T(8,128)(2,1)S(1)}, u32[]{:S(2)}, u32[]{:S(2)}) %collective-permute-start.1) | collective-permute-done | bytes 221216 | tf_op jit(solution)/shard_map/ppermute | solution.py:18
  11.8 0.0 copy-start.15
  11.8 1.5 %stack.33 = (bf16[2,8,24,384]{3,2,1,0:T(8,128)(2,1)S(1)}, bf16[14,24,384]{2,1,0:T(8,128)(2,1)}, bf16[14,24,384]{2,1,0:T(8,128)(2,1)}, bf16[20,24,384]{2,1,0:T(8,...) custom-call(s32[4]{0:T(128)S(1)} %copy-done.10, bf16[8,24,384]{2,1,0:T(8,128)(2,1)S(1)} %copy-done.7, ...), custom_call_target="tpu_custom_call" | custom-call | tf_op jit(solution)/shard_map/stack/pallas_call | solution.py:308
  13.4 1.2 %collective-permute-start.2 = (bf16[14,24,384]{2,1,0:T(8,128)(2,1)}, bf16[14,24,384]{2,1,0:T(8,128)(2,1)S(1)}, u32[]{:S(2)}, u32[]{:S(2)}) collective-permute-start(bf16[14,24,384]{2,1,0:T(8,128)(2,1)} %get-tuple-element.23), channel_id=1, source_target_pairs={{0,2},{4,6},{8,10},{12,14},{2,0},{6,4},{10,8},{14,12},{1,3},{5,7},... | collective-permute-start | bytes 774152 | tf_op jit(solution)/shard_map/ppermute | solution.py:23
  14.6 2.1 %collective-permute-start.3 = (bf16[14,24,384]{2,1,0:T(8,128)(2,1)}, bf16[14,24,384]{2,1,0:T(8,128)(2,1)}, u32[]{:S(2)}, u32[]{:S(2)}) collective-permute-start(bf16[14,24,384]{2,1,0:T(8,128)(2,1)} %get-tuple-element.25), channel_id=1, source_target_pairs={{2,4},{6,8},{10,12},{4,2},{8,6},{12,10},{3,5},{7,9},{11,13},{5,3},... | collective-permute-start | bytes 774152 | tf_op jit(solution)/shard_map/ppermute | solution.py:23
  16.7 0.1 stack_tile.6
  16.8 0.1 stack_tile.7
  16.9 1.3 %copy-done.5 = bf16[3456,192]{0,1:T(8,128)(2,1)S(1)} copy-done((bf16[3456,192]{0,1:T(8,128)(2,1)S(1)}, bf16[3456,192]{0,1:T(8,128)(2,1)}, u32[]{:S(2)}) %copy-start.5) | copy-done | bytes 1327128
  18.3 0.5 combine_weights.1.later.wu
  18.7 2.4 %collective-permute-start.6 = (bf16[10,24,384]{2,1,0:T(8,128)(2,1)}, bf16[10,24,384]{2,1,0:T(8,128)(2,1)}, u32[]{:S(2)}, u32[]{:S(2)}) collective-permute-start(bf16[10,24,384]{2,1,0:T(8,128)(2,1)} %get-tuple-element.27), channel_id=1, source_target_pairs={{0,2},{4,6},{8,10},{12,14},{2,0},{6,4},{10,8},{14,12},{1,3},{5,7},... | collective-permute-start | bytes 552968 | tf_op jit(solution)/shard_map/ppermute | solution.py:23
  21.1 1.9 %collective-permute-start.7 = (bf16[10,24,384]{2,1,0:T(8,128)(2,1)}, bf16[10,24,384]{2,1,0:T(8,128)(2,1)}, u32[]{:S(2)}, u32[]{:S(2)}) collective-permute-start(bf16[10,24,384]{2,1,0:T(8,128)(2,1)} %get-tuple-element.29), channel_id=1, source_target_pairs={{2,4},{6,8},{10,12},{4,2},{8,6},{12,10},{3,5},{7,9},{11,13},{5,3},... | collective-permute-start | bytes 552968 | tf_op jit(solution)/shard_map/ppermute | solution.py:23
  23.0 1.6 %collective-permute-done.2.near = bf16[14,24,384]{2,1,0:T(8,128)(2,1)S(1)} collective-permute-done((bf16[14,24,384]{2,1,0:T(8,128)(2,1)}, bf16[14,24,384]{2,1,0:T(8,128)(2,1)S(1)}, u32[]{:S(2)}, u32[]{:S(2)}) %collective-permute-start.2) | collective-permute-done | bytes 258080 | tf_op jit(solution)/shard_map/ppermute | solution.py:23
  24.6 11.0 %first_block.1.blocked = bf16[4,48,384]{2,1,0:T(8,128)(2,1)S(1)} custom-call(s32[4]{0:T(128)S(1)} %copy-done.10, bf16[14,24,384]{2,1,0:T(8,128)(2,1)S(1)} %collective-permute-done.2.near, bf16[2,8,24,384]{3,2,1,0:T(8,128)(2,1)S(1)} %get-tuple-element.24.own, bf16[14,24,384]{2,1,0:T(8,128)(2,1)} %collective-permute-done.3.far, ...), custom_call_target="tpu_custom_call" | custom-call | flops 4586471424 | bytes 15925248 | tf_op jit(solution)/shard_map/first_block/pallas_call | solution.py:527
  35.6 2.3 %collective-permute-start.4 = (bf16[4,48,384]{2,1,0:T(8,128)(2,1)S(1)}, bf16[4,48,384]{2,1,0:T(8,128)(2,1)S(1)}, u32[]{:S(2)}, u32[]{:S(2)}) collective-permute-start(bf16[4,48,384]{2,1,0:T(8,128)(2,1)S(1)} %first_block.1.blocked), channel_id=1, source_target_pairs={{0,2},{4,6},{8,10},{12,14},{2,0},{6,4},{10,8},{14,12},{1,3},{5,7},... | collective-permute-start | bytes 442376 | tf_op jit(solution)/shard_map/ppermute | solution.py:23
  37.9 1.9 %collective-permute-start.5 = (bf16[4,48,384]{2,1,0:T(8,128)(2,1)S(1)}, bf16[4,48,384]{2,1,0:T(8,128)(2,1)S(1)}, u32[]{:S(2)}, u32[]{:S(2)}) collective-permute-start(bf16[4,48,384]{2,1,0:T(8,128)(2,1)S(1)} %first_block.1.blocked), channel_id=1, source_target_pairs={{2,4},{6,8},{10,12},{4,2},{8,6},{12,10},{3,5},{7,9},{11,13},{5,3},... | collective-permute-start | bytes 442376 | tf_op jit(solution)/shard_map/ppermute | solution.py:23
  39.8 1.6 %copy-done.3 = bf16[5184,192]{0,1:T(8,128)(2,1)S(1)} copy-done((bf16[5184,192]{0,1:T(8,128)(2,1)S(1)}, bf16[5184,192]{0,1:T(8,128)(2,1)}, u32[]{:S(2)}) %copy-start.3) | copy-done | bytes 1990680
  41.4 1.5 %align_weights.3.w4 = bf16[768,3456]{1,0:T(8,128)(2,1)S(1)} custom-call(bf16[192,5184]{1,0:T(8,128)(2,1)S(1)} %bitcast.15), custom_call_target="tpu_custom_call" | custom-call | tf_op jit(solution)/shard_map/align_weights/pallas_call | solution.py:369
  42.9 1.8 %collective-permute-done.5.far = bf16[4,48,384]{2,1,0:T(8,128)(2,1)S(1)} collective-permute-done((bf16[4,48,384]{2,1,0:T(8,128)(2,1)S(1)}, bf16[4,48,384]{2,1,0:T(8,128)(2,1)S(1)}, u32[]{:S(2)}, u32[]{:S(2)}) %collective-permute-start.5) | collective-permute-done | bytes 147488 | tf_op jit(solution)/shard_map/ppermute | solution.py:23
  44.7 0.7 copy-done.8
  45.4 0.9 %copy-done.9 = bf16[4,48,384]{2,1,0:T(8,128)(2,1)S(1)} copy-done((bf16[4,48,384]{2,1,0:T(8,128)(2,1)S(1)}, bf16[4,48,384]{2,1,0:T(8,128)(2,1)}, u32[]{:S(2)}) %copy-start.9) | copy-done | bytes 147480
  46.3 17.4 %second_block.1 = bf16[8,4,16,384]{3,2,1,0:T(8,128)(2,1)S(1)} custom-call(s32[4]{0:T(128)S(1)} %copy-done.10, bf16[4,48,384]{2,1,0:T(8,128)(2,1)S(1)} %collective-permute-done.4.near, bf16[4,48,384]{2,1,0:T(8,128)(2,1)S(1)} %first_block.1.blocked, bf16[4,48,384]{2,1,0:T(8,128)(2,1)S(1)} %copy-done.9, bf16[10,24,384]{2,1,0:T(8,128)(2,1)} %collective-permute-done.6.tile_near, ...), custom_call_target="tpu_custom_call" | custom-call | tf_op jit(solution)/shard_map/second_block/pallas_call | solution.py:714
  63.7 9.3 %collective-permute-start.8 = (bf16[4,4,16,384]{3,2,1,0:T(8,128)(2,1)S(1)}, bf16[4,4,16,384]{3,2,1,0:T(8,128)(2,1)S(1)}, u32[]{:S(2)}, u32[]{:S(2)}) collective-permute-start(bf16[4,4,16,384]{3,2,1,0:T(8,128)(2,1)S(1)} %constant_dynamic-slice_fusion), channel_id=1, source_target_pairs={{0,16},{16,0},{1,17},{17,1},{2,18},{18,2},{3,19},{19,3},{4,20},{20... | collective-permute-start | bytes 589832 | tf_op jit(solution)/shard_map/ppermute | solution.py:18
  73.0 1.1 %collective-permute-done.8 = bf16[4,4,16,384]{3,2,1,0:T(8,128)(2,1)S(1)} collective-permute-done((bf16[4,4,16,384]{3,2,1,0:T(8,128)(2,1)S(1)}, bf16[4,4,16,384]{3,2,1,0:T(8,128)(2,1)S(1)}, u32[]{:S(2)}, u32[]{:S(2)}) %collective-permute-start.8) | collective-permute-done | bytes 196640 | tf_op jit(solution)/shard_map/ppermute | solution.py:18
  74.2 1.1 %reshape.17 = bf16[4,4,64,192]{3,2,1,0:T(8,128)(2,1)} reshape(bf16[4,4,32,384]{3,2,1,0:T(8,128)(2,1)S(1)} %pad_maximum_fusion) | data formatting | bytes 786432 | tf_op jit(solution)/shard_map/reshape | solution.py:819
  (37 shorter events, 0.2 us)
Async XLA Ops:
  0.0 1.8 %collective-permute-start = (bf16[2,64,384]{2,1,0:T(8,128)(2,1)}, bf16[2,64,384]{2,1,0:T(8,128)(2,1)S(1)}, u32[]{:S(2)}, u32[]{:S(2)}) collective-permute-start(bf16[2,64,384]{2,1,0:T(8,128)(2,1)} %bitcast.19), channel_id=1, source_target_pairs={{0,16},{16,0},{1,17},{17,1},{2,18},{18,2},{3,19},{19,3},{4,20},{20... | collective-permute-start | bytes 294920 | tf_op jit(solution)/shard_map/ppermute | solution.py:18
  1.8 0.6 copy-start.11
  4.9 6.9 %collective-permute-start.1 = (bf16[12,24,384]{2,1,0:T(8,128)(2,1)}, bf16[12,24,384]{2,1,0:T(8,128)(2,1)S(1)}, u32[]{:S(2)}, u32[]{:S(2)}) collective-permute-start(bf16[12,24,384]{2,1,0:T(8,128)(2,1)} %get-tuple-element.20), channel_id=1, source_target_pairs={{0,1},{1,0},{2,3},{3,2},{4,5},{5,4},{6,7},{7,6},{8,9},{9,8},{10,11... | collective-permute-start | bytes 663560 | tf_op jit(solution)/shard_map/ppermute | solution.py:18
  6.1 1.6 %copy-start.2 = (bf16[5184,192]{0,1:T(8,128)(2,1)S(1)}, bf16[5184,192]{0,1:T(8,128)(2,1)}, u32[]{:S(2)}) copy-start(bf16[5184,192]{0,1:T(8,128)(2,1)} %param.30) | copy-start | bytes 5971972
  7.7 4.1 %copy-start.6 = (bf16[20,32,384]{2,1,0:T(8,128)(2,1)S(1)}, bf16[20,32,384]{2,1,0:T(8,128)(2,1)}, u32[]{:S(2)}) copy-start(bf16[20,32,384]{2,1,0:T(8,128)(2,1)} %get-tuple-element.21.tiles) | copy-start | bytes 1474564
  7.7 4.1 %copy-start.7 = (bf16[8,24,384]{2,1,0:T(8,128)(2,1)S(1)}, bf16[8,24,384]{2,1,0:T(8,128)(2,1)}, u32[]{:S(2)}) copy-start(bf16[8,24,384]{2,1,0:T(8,128)(2,1)} %get-tuple-element.19.mine) | copy-start | bytes 442372
  7.7 4.1 %copy-start.10 = (s32[4]{0:T(128)S(1)}, s32[4]{0:T(128)}, u32[]{:S(2)}) copy-start(s32[4]{0:T(128)} %pad_add_fusion.place) | copy-start | bytes 52
  9.2 4.2 %copy-start = (bf16[768,3456]{1,0:T(8,128)(2,1)}, bf16[768,3456]{1,0:T(8,128)(2,1)S(1)}, u32[]{:S(2)}) copy-start(bf16[768,3456]{1,0:T(8,128)(2,1)S(1)} %align_weights.2.later.w3) | copy-start | bytes 15925252
  11.8 4.9 %copy-start.14 = (f32[192]{0:T(256)S(1)}, f32[192]{0:T(256)}, u32[]{:S(2)}) copy-start(f32[192]{0:T(256)} %param.24) | copy-start | bytes 2308
  11.8 5.0 %copy-start.15 = (f32[192]{0:T(256)S(1)}, f32[192]{0:T(256)}, u32[]{:S(2)}) copy-start(f32[192]{0:T(256)} %param.25) | copy-start | bytes 2308
  11.8 5.1 %copy-start.12 = (f32[384]{0:T(512)S(1)}, f32[384]{0:T(512)}, u32[]{:S(2)}) copy-start(f32[384]{0:T(512)} %param.22) | copy-start | bytes 4612
  11.8 5.1 %copy-start.13 = (f32[384]{0:T(512)S(1)}, f32[384]{0:T(512)}, u32[]{:S(2)}) copy-start(f32[384]{0:T(512)} %param.23) | copy-start | bytes 4612
  13.4 11.3 %collective-permute-start.2 = (bf16[14,24,384]{2,1,0:T(8,128)(2,1)}, bf16[14,24,384]{2,1,0:T(8,128)(2,1)S(1)}, u32[]{:S(2)}, u32[]{:S(2)}) collective-permute-start(bf16[14,24,384]{2,1,0:T(8,128)(2,1)} %get-tuple-element.23), channel_id=1, source_target_pairs={{0,2},{4,6},{8,10},{12,14},{2,0},{6,4},{10,8},{14,12},{1,3},{5,7},... | collective-permute-start | bytes 774152 | tf_op jit(solution)/shard_map/ppermute | solution.py:23
  14.6 10.0 %collective-permute-start.3 = (bf16[14,24,384]{2,1,0:T(8,128)(2,1)}, bf16[14,24,384]{2,1,0:T(8,128)(2,1)}, u32[]{:S(2)}, u32[]{:S(2)}) collective-permute-start(bf16[14,24,384]{2,1,0:T(8,128)(2,1)} %get-tuple-element.25), channel_id=1, source_target_pairs={{2,4},{6,8},{10,12},{4,2},{8,6},{12,10},{3,5},{7,9},{11,13},{5,3},... | collective-permute-start | bytes 774152 | tf_op jit(solution)/shard_map/ppermute | solution.py:23
  16.9 1.3 %copy-start.5 = (bf16[3456,192]{0,1:T(8,128)(2,1)S(1)}, bf16[3456,192]{0,1:T(8,128)(2,1)}, u32[]{:S(2)}) copy-start(bf16[3456,192]{0,1:T(8,128)(2,1)} %param.29) | copy-start | bytes 3981316
  18.7 24.2 %collective-permute-start.6 = (bf16[10,24,384]{2,1,0:T(8,128)(2,1)}, bf16[10,24,384]{2,1,0:T(8,128)(2,1)}, u32[]{:S(2)}, u32[]{:S(2)}) collective-permute-start(bf16[10,24,384]{2,1,0:T(8,128)(2,1)} %get-tuple-element.27), channel_id=1, source_target_pairs={{0,2},{4,6},{8,10},{12,14},{2,0},{6,4},{10,8},{14,12},{1,3},{5,7},... | collective-permute-start | bytes 552968 | tf_op jit(solution)/shard_map/ppermute | solution.py:23
  21.1 21.8 %collective-permute-start.7 = (bf16[10,24,384]{2,1,0:T(8,128)(2,1)}, bf16[10,24,384]{2,1,0:T(8,128)(2,1)}, u32[]{:S(2)}, u32[]{:S(2)}) collective-permute-start(bf16[10,24,384]{2,1,0:T(8,128)(2,1)} %get-tuple-element.29), channel_id=1, source_target_pairs={{2,4},{6,8},{10,12},{4,2},{8,6},{12,10},{3,5},{7,9},{11,13},{5,3},... | collective-permute-start | bytes 552968 | tf_op jit(solution)/shard_map/ppermute | solution.py:23
  35.6 7.3 %collective-permute-start.4 = (bf16[4,48,384]{2,1,0:T(8,128)(2,1)S(1)}, bf16[4,48,384]{2,1,0:T(8,128)(2,1)S(1)}, u32[]{:S(2)}, u32[]{:S(2)}) collective-permute-start(bf16[4,48,384]{2,1,0:T(8,128)(2,1)S(1)} %first_block.1.blocked), channel_id=1, source_target_pairs={{0,2},{4,6},{8,10},{12,14},{2,0},{6,4},{10,8},{14,12},{1,3},{5,7},... | collective-permute-start | bytes 442376 | tf_op jit(solution)/shard_map/ppermute | solution.py:23
  37.9 6.8 %collective-permute-start.5 = (bf16[4,48,384]{2,1,0:T(8,128)(2,1)S(1)}, bf16[4,48,384]{2,1,0:T(8,128)(2,1)S(1)}, u32[]{:S(2)}, u32[]{:S(2)}) collective-permute-start(bf16[4,48,384]{2,1,0:T(8,128)(2,1)S(1)} %first_block.1.blocked), channel_id=1, source_target_pairs={{2,4},{6,8},{10,12},{4,2},{8,6},{12,10},{3,5},{7,9},{11,13},{5,3},... | collective-permute-start | bytes 442376 | tf_op jit(solution)/shard_map/ppermute | solution.py:23
  39.8 1.6 %copy-start.3 = (bf16[5184,192]{0,1:T(8,128)(2,1)S(1)}, bf16[5184,192]{0,1:T(8,128)(2,1)}, u32[]{:S(2)}) copy-start(bf16[5184,192]{0,1:T(8,128)(2,1)} %param.31) | copy-start | bytes 5971972
  41.4 4.0 %copy-start.1 = (bf16[768,3456]{1,0:T(8,128)(2,1)S(1)}, bf16[768,3456]{1,0:T(8,128)(2,1)}, u32[]{:S(2)}) copy-start(bf16[768,3456]{1,0:T(8,128)(2,1)} %copy-done) | copy-start | bytes 15925252
  41.4 4.0 %copy-start.4 = (bf16[1152,768]{1,0:T(8,128)(2,1)S(1)}, bf16[1152,768]{1,0:T(8,128)(2,1)}, u32[]{:S(2)}) copy-start(bf16[1152,768]{1,0:T(8,128)(2,1)} %wt.1) | copy-start | bytes 5308420
  44.7 0.7 copy-start.8
  45.4 0.9 %copy-start.9 = (bf16[4,48,384]{2,1,0:T(8,128)(2,1)S(1)}, bf16[4,48,384]{2,1,0:T(8,128)(2,1)}, u32[]{:S(2)}) copy-start(bf16[4,48,384]{2,1,0:T(8,128)(2,1)} %copy-done.8) | copy-start | bytes 442372
  63.7 10.3 %collective-permute-start.8 = (bf16[4,4,16,384]{3,2,1,0:T(8,128)(2,1)S(1)}, bf16[4,4,16,384]{3,2,1,0:T(8,128)(2,1)S(1)}, u32[]{:S(2)}, u32[]{:S(2)}) collective-permute-start(bf16[4,4,16,384]{3,2,1,0:T(8,128)(2,1)S(1)} %constant_dynamic-slice_fusion), channel_id=1, source_target_pairs={{0,16},{16,0},{1,17},{17,1},{2,18},{18,2},{3,19},{19,3},{4,20},{20... | collective-permute-start | bytes 589832 | tf_op jit(solution)/shard_map/ppermute | solution.py:18

commit v12 on v11

--- a/solution.py
+++ b/solution.py
@@ -84,23 +84,27 @@
     return jnp.concatenate(parts, axis=0)
 
 
-def low_product(acc, even, odd, count, height, wide, weights, copies):
+def low_product(acc, even, odd, count, height, wide, weights):
     rows = count * (height - 2) * wide
     channels = weights.shape[1]
-    needed = [dx * channels // LANES for dx in range(3)]
-
-    def column(n, carry):
-        for copy, when in zip(copies, needed):
-            pl.when(n == when)(copy.wait)
-        lanes = pl.ds(pl.multiple_of(n * LANES, LANES), LANES)
+    lanes = 3 * channels
+    for n in range(-(-lanes // LANES)):
+        begin, end = n * LANES, min((n + 1) * LANES, lanes)
         left = jnp.concatenate(
             [taps(even, odd, 0, count, height, wide, t // 3, t % 3) for t in range(9)], axis=1
         )
-        right = weights[:, :, lanes].reshape(9 * channels, LANES)
-        acc[n, 0:rows, :] = jnp.dot(left, right, preferred_element_type=F32)
-        return carry
-
-    lax.fori_loop(0, weights.shape[-1] // LANES, column, 0)
+        right = []
+        for t in range(9):
+            parts = []
+            for dx in range(3):
+                low = max(begin - dx * channels, 0)
+                high = min(end - dx * channels, channels)
+                if low < high:
+                    base = (3 * t + dx) * channels
+                    parts.append(weights[base : base + channels, low:high])
+            right.append(jnp.concatenate(parts, axis=1))
+        right = jnp.concatenate(right, axis=0)
+        acc[n, 0:rows, 0 : end - begin] = jnp.dot(left, right, preferred_element_type=F32)
 
 
 def low_sum(acc, start, size):
@@ -414,16 +418,6 @@
     )(weight.T)
 
 
-def weight_copies(source, target, sems, base):
-    channels = source.shape[-1]
-    return [
-        pltpu.make_async_copy(
-            source.at[:, dx], target.at[:, :, pl.ds(dx * channels, channels)], sems.at[base + dx]
-        )
-        for dx in range(3)
-    ]
-
-
 def first_kernel(
     wide,
     sizes,
@@ -432,30 +426,24 @@
     own,
     far,
     gains,
-    weight_one,
-    weight_two,
-    later,
-    out_ref,
     w1,
     w2,
+    later_one,
+    later_two,
+    out_ref,
     acc,
+    acc_two,
     x1e,
     x1o,
     x2e,
     x2o,
-    sems,
 ):
     channels = own.shape[-1]
     frames = own.shape[1] - 4
     height, width = sizes
     col, row = place[1], place[3]
     units = frames + 2
-    del later
-
-    copies_one = weight_copies(weight_one, w1, sems, 0)
-    copies_two = weight_copies(weight_two, w2, sems, 3)
-    copies_one[0].start()
-    copies_one[1].start()
+    del later_one, later_two
 
     slots = [lax.rem(y + col, 2) for y in range(2)]
 
@@ -481,34 +469,20 @@
         values = jnp.concatenate([first] + own_rows(units + f) + [last], axis=0)
         store(x2e, x2o, f, values, 4, wide)
 
-    def norm_one(f, carry):
-        values = activate(rows_of(f), gains[0:1, :], 1.0)
-        store(x1e, x1o, f + 2, values, 6, wide)
-        return carry
-
-    lax.fori_loop(0, frames, norm_one, 0)
-    for copy in [copies_one[2]] + copies_two:
-        copy.start()
-    low_product(acc, x1e, x1o, frames, 6, wide, w1, copies_one)
+    for f in range(frames):
+        store(x1e, x1o, f + 2, activate(rows_of(f), gains[0:1, :], 1.0), 6, wide)
+    low_product(acc, x1e, x1o, frames, 6, wide, w1)
 
     mask = line_mask(place, wide, 2 * row - 1, 4, height, width)
-
-    def norm_two(f, carry):
+    for f in range(frames):
         size = 4 * wide
-        values = activate(low_sum(acc, aligned(f, size), size), gains[1:2, :], mask)
+        values = activate(low_sum(acc, f * size, size), gains[1:2, :], mask)
         store(x2e, x2o, f + 2, values, 4, wide)
-        return carry
-
-    lax.fori_loop(0, frames, norm_two, 0)
-    low_product(acc, x2e, x2o, frames, 4, wide, w2, copies_two)
-
-    def residual(f, carry):
+    low_product(acc_two, x2e, x2o, frames, 4, wide, w2)
+    for f in range(frames):
         size = 2 * wide
-        values = low_sum(acc, aligned(f, size), size) + jnp.concatenate(own_rows(f), axis=0)
+        values = low_sum(acc_two, f * size, size) + jnp.concatenate(own_rows(f), axis=0)
         out_ref[f] = values.astype(BF16)
-        return carry
-
-    lax.fori_loop(0, frames, residual, 0)
 
 
 def planes(slots, height, wide, channels):
@@ -528,26 +502,23 @@
         functools.partial(first_kernel, wide, sizes),
         out_shape=jax.ShapeDtypeStruct((frames, 2 * wide, channels), BF16),
         in_specs=[pl.BlockSpec(memory_space=pltpu.SMEM)]
-        + [vmem] * 4
-        + [pl.BlockSpec(memory_space=pltpu.HBM)] * 2
-        + [anywhere],
+        + [vmem] * 6
+        + [anywhere] * 2,
         out_specs=vmem,
         scratch_shapes=[
-            pltpu.VMEM((9, channels, slots * LANES), BF16),
-            pltpu.VMEM((9, channels, slots * LANES), BF16),
             pltpu.VMEM((slots, frames * 4 * wide, LANES), F32),
+            pltpu.VMEM((slots, frames * 2 * wide, LANES), F32),
             *planes(frames + 2, 6, wide, channels),
             *planes(frames + 2, 4, wide, channels),
-            pltpu.SemaphoreType.DMA((6,)),
         ],
-        compiler_params=pltpu.CompilerParams(vmem_limit_bytes=50 * 1024 * 1024),
+        compiler_params=pltpu.CompilerParams(vmem_limit_bytes=12 * 1024 * 1024),
         cost_estimate=pl.CostEstimate(
             flops=2 * 27 * channels * channels * frames * 6 * wide,
-            bytes_accessed=2 * 54 * channels * channels,
+            bytes_accessed=0,
             transcendentals=0,
         ),
         name="first_block",
-    )(place, *pieces, gains, weight_one, weight_two, later)
+    )(place, *pieces, gains, weight_one, weight_two, *later)
 
 
 def second_kernel(
@@ -728,7 +699,7 @@
             *(ref for n in slots for ref in planes(n, 8, wide, channels)),
             *(ref for n in slots for ref in planes(n, 6, wide, channels)),
         ],
-        compiler_params=pltpu.CompilerParams(vmem_limit_bytes=34 * 1024 * 1024),
+        compiler_params=pltpu.CompilerParams(vmem_limit_bytes=24 * 1024 * 1024),
         name="second_block",
     )(place, *pieces, *tiles, gains, *weights)
 
@@ -783,22 +754,28 @@
     own, near, far, windows, tile_near, tile_far = stack(
         place, mine, swapped(theirs, "cols"), tiles, weight_three
     )
-    pieces = [paired(near, "rows", 0), own, paired(far, "rows", 1)]
-    tiles = [paired(tile_near, "rows", 0), windows, paired(tile_far, "rows", 1)]
-    weight_upsample, own = lax.optimization_barrier((weight_upsample, own))
+    far = paired(far, "rows", 1)
+    near = paired(near, "rows", 0)
+    tile_far = paired(tile_far, "rows", 1)
+    tile_near = paired(tile_near, "rows", 0)
+    weight_upsample, weight_four, own = lax.optimization_barrier(
+        (weight_upsample, weight_four, own)
+    )
     weight_upsample = combine_weights(weight_upsample)
+    weight_four = align_weights(weight_four)
     blocked = first_block(
         place,
-        pieces,
+        [near, own, far],
         gains,
-        weight_one.reshape(9, 3, channels, channels),
-        weight_two.reshape(9, 3, channels, channels),
-        weight_upsample,
+        weight_one,
+        weight_two,
+        (weight_upsample, weight_four),
         sizes,
     )
-    blocks = [paired(blocked, "rows", 0), blocked, paired(blocked, "rows", 1)]
-    weight_four, _ = lax.optimization_barrier((weight_four, blocked))
-    weight_four = align_weights(weight_four)
+    far = paired(blocked, "rows", 1)
+    near = paired(blocked, "rows", 0)
+    blocks = [near, blocked, far]
+    tiles = [tile_near, windows, tile_far]
     frames = second_block(
         place,
         blocks,

time: 75.6 us -> 84.5 us (1.12)
  the two profiles are of different devices: /device:TPU:9 before, /device:TPU:27 now
where the time goes in v12:
time: 84.5 us; the launch traced here: 83.9 us
  Pallas kernels  33.3 us (39%)
  local copies, waits for them, and re-layouts  21 us (25%)
  starting transfers between devices  20.3 us (24%)
  waiting for transfers between devices  8.36 us (10%)
    unnamed x40, local copies, waits for them, and re-layouts  19.7 us
    pallas_call x1, Pallas kernels, second_block(): pl.pallas_call(functools.partial(second_kernel, wide, sizes), out_shape=j...  17.2 us
    ppermute x6, starting transfers between devices, paired(): lax.ppermute(value, axis, pairs + [(high, low) for low, high in pairs])  11.1 us
    ppermute x3, starting transfers between devices, swapped(): return lax.ppermute(value, axis, [(0, 1), (1, 0)])  9.2 us
    pallas_call x1, Pallas kernels, first_block(): pl.pallas_call(functools.partial(first_kernel, wide, sizes), out_shape=ja...  8.6 us
    ppermute x3, waiting for transfers between devices, swapped(): return lax.ppermute(value, axis, [(0, 1), (1, 0)])  5.11 us
    ppermute x6, waiting for transfers between devices, paired(): lax.ppermute(value, axis, pairs + [(high, low) for low, high in pairs])  3.25 us
    pallas_call x2, Pallas kernels, align_weights(): pl.pallas_call(align_kernel, out_shape=jax.ShapeDtypeStruct((4 * half, 18...  2.98 us
  transfers between devices with their start and end apart: 9, of which 5 were waited for; matrix products, arithmetic and copies ran while one was open for 1% of the time, Pallas kernels for 14%

profile of v12, /device:TPU:27, one launch (start us, length us, event | category | flops | bytes accessed | tf_op | source)
XLA Modules:
  0.0 83.9 jit_solution(6176602105040008266)
XLA Ops:
  0.0 0.7 collective-permute-start
  0.7 0.7 pad_add_fusion.place
  1.3 0.5 collective-permute-done.arrived
  1.8 0.6 copy-done.15
  2.5 2.5 %pack.1 = (bf16[8,24,384]{2,1,0:T(8,128)(2,1)}, bf16[12,24,384]{2,1,0:T(8,128)(2,1)}, bf16[20,32,384]{2,1,0:T(8,128)(2,1)}) custom-call(s32[4]{0:T(128)} %pad_add_fusion.place, bf16[2,64,384]{2,1,0:T(8,128)(2,1)} %bitcast.16, bf16[2,64,384]{2,1,0:T(8,128)(2,1)} %copy-done.15, bf16[2,64,384]{2,1,0:T(8,128)(2,1)} %bitcast.17, bf16[2,64,384]{2,1,0:T(8,128)(2,1)} %bitcast.18, ...), custom_call_target="tpu_custom_call" | custom-call | tf_op jit(solution)/shard_map/pack/pallas_call | solution.py:246
  4.9 0.3 collective-permute-start.1
  5.2 1.6 %copy-done.6 = bf16[5184,192]{0,1:T(8,128)(2,1)S(1)} copy-done((bf16[5184,192]{0,1:T(8,128)(2,1)S(1)}, bf16[5184,192]{0,1:T(8,128)(2,1)}, u32[]{:S(2)}) %copy-start.6) | copy-done | bytes 1990680
  6.8 1.5 %align_weights.2.later.w3 = bf16[768,3456]{1,0:T(8,128)(2,1)S(1)} custom-call(bf16[192,5184]{1,0:T(8,128)(2,1)S(1)} %bitcast.12), custom_call_target="tpu_custom_call" | custom-call | tf_op jit(solution)/shard_map/align_weights/pallas_call | solution.py:373
  8.3 3.5 %collective-permute-done.1.theirs = bf16[12,24,384]{2,1,0:T(8,128)(2,1)S(1)} collective-permute-done((bf16[12,24,384]{2,1,0:T(8,128)(2,1)}, bf16[12,24,384]{2,1,0:T(8,128)(2,1)S(1)}, u32[]{:S(2)}, u32[]{:S(2)}) %collective-permute-start.1) | collective-permute-done | bytes 221216 | tf_op jit(solution)/shard_map/ppermute | solution.py:18
  11.9 1.5 %stack.33 = (bf16[2,8,24,384]{3,2,1,0:T(8,128)(2,1)S(1)}, bf16[14,24,384]{2,1,0:T(8,128)(2,1)}, bf16[14,24,384]{2,1,0:T(8,128)(2,1)}, bf16[20,24,384]{2,1,0:T(8,...) custom-call(s32[4]{0:T(128)S(1)} %copy-done.14, bf16[8,24,384]{2,1,0:T(8,128)(2,1)S(1)} %copy-done.11, ...), custom_call_target="tpu_custom_call" | custom-call | tf_op jit(solution)/shard_map/stack/pallas_call | solution.py:312
  13.4 1.2 %collective-permute-start.2 = (bf16[14,24,384]{2,1,0:T(8,128)(2,1)}, bf16[14,24,384]{2,1,0:T(8,128)(2,1)S(1)}, u32[]{:S(2)}, u32[]{:S(2)}) collective-permute-start(bf16[14,24,384]{2,1,0:T(8,128)(2,1)} %get-tuple-element.24), channel_id=1, source_target_pairs={{0,2},{4,6},{8,10},{12,14},{2,0},{6,4},{10,8},{14,12},{1,3},{5,7},... | collective-permute-start | bytes 774152 | tf_op jit(solution)/shard_map/ppermute | solution.py:23
  14.7 2.0 %collective-permute-start.3 = (bf16[14,24,384]{2,1,0:T(8,128)(2,1)}, bf16[14,24,384]{2,1,0:T(8,128)(2,1)}, u32[]{:S(2)}, u32[]{:S(2)}) collective-permute-start(bf16[14,24,384]{2,1,0:T(8,128)(2,1)} %get-tuple-element.27), channel_id=1, source_target_pairs={{2,4},{6,8},{10,12},{4,2},{8,6},{12,10},{3,5},{7,9},{11,13},{5,3},... | collective-permute-start | bytes 774152 | tf_op jit(solution)/shard_map/ppermute | solution.py:23
  16.9 1.3 %copy-done.9 = bf16[3456,192]{0,1:T(8,128)(2,1)S(1)} copy-done((bf16[3456,192]{0,1:T(8,128)(2,1)S(1)}, bf16[3456,192]{0,1:T(8,128)(2,1)}, u32[]{:S(2)}) %copy-start.9) | copy-done | bytes 1327128
  18.2 0.5 combine_weights.1.later_one.wu
  18.7 1.6 %copy-done.7 = bf16[5184,192]{0,1:T(8,128)(2,1)S(1)} copy-done((bf16[5184,192]{0,1:T(8,128)(2,1)S(1)}, bf16[5184,192]{0,1:T(8,128)(2,1)}, u32[]{:S(2)}) %copy-start.7) | copy-done | bytes 1990680
  20.3 1.5 %align_weights.3.later_two.w4 = bf16[768,3456]{1,0:T(8,128)(2,1)S(1)} custom-call(bf16[192,5184]{1,0:T(8,128)(2,1)S(1)} %bitcast.13), custom_call_target="tpu_custom_call" | custom-call | tf_op jit(solution)/shard_map/align_weights/pallas_call | solution.py:373
  21.8 4.2 %collective-permute-start.7 = (bf16[10,24,384]{2,1,0:T(8,128)(2,1)}, bf16[10,24,384]{2,1,0:T(8,128)(2,1)}, u32[]{:S(2)}, u32[]{:S(2)}) collective-permute-start(bf16[10,24,384]{2,1,0:T(8,128)(2,1)} %get-tuple-element.32), channel_id=1, source_target_pairs={{2,4},{6,8},{10,12},{4,2},{8,6},{12,10},{3,5},{7,9},{11,13},{5,3},... | collective-permute-start | bytes 552968 | tf_op jit(solution)/shard_map/ppermute | solution.py:23
  26.1 3.3 %copy-done.4 = bf16[10368,384]{1,0:T(8,128)(2,1)S(1)} copy-done((bf16[10368,384]{1,0:T(8,128)(2,1)S(1)}, bf16[10368,384]{1,0:T(8,128)(2,1)}, u32[]{:S(2)}) %copy-start.4) | copy-done | bytes 7962648
  29.3 3.3 %copy-done.5 = bf16[10368,384]{1,0:T(8,128)(2,1)S(1)} copy-done((bf16[10368,384]{1,0:T(8,128)(2,1)S(1)}, bf16[10368,384]{1,0:T(8,128)(2,1)}, u32[]{:S(2)}) %copy-start.5) | copy-done | bytes 7962648
  32.6 8.6 %first_block.1.blocked = bf16[4,48,384]{2,1,0:T(8,128)(2,1)S(1)} custom-call(s32[4]{0:T(128)S(1)} %copy-done.14, bf16[14,24,384]{2,1,0:T(8,128)(2,1)S(1)} %collective-permute-done.2.near, bf16[2,8,24,384]{3,2,1,0:T(8,128)(2,1)S(1)} %get-tuple-element.26.own, bf16[14,24,384]{2,1,0:T(8,128)(2,1)} %collective-permute-done.3.far, ...), custom_call_target="tpu_custom_call" | custom-call | flops 4586471424 | tf_op jit(solution)/shard_map/first_block/pallas_call | solution.py:501
  41.3 3.5 %collective-permute-start.5 = (bf16[4,48,384]{2,1,0:T(8,128)(2,1)S(1)}, bf16[4,48,384]{2,1,0:T(8,128)(2,1)S(1)}, u32[]{:S(2)}, u32[]{:S(2)}) collective-permute-start(bf16[4,48,384]{2,1,0:T(8,128)(2,1)S(1)} %first_block.1.blocked), channel_id=1, source_target_pairs={{2,4},{6,8},{10,12},{4,2},{8,6},{12,10},{3,5},{7,9},{11,13},{5,3},... | collective-permute-start | bytes 442376 | tf_op jit(solution)/shard_map/ppermute | solution.py:23
  44.8 0.4 collective-permute-done.4.near
  45.2 2.8 %collective-permute-done.5.far = bf16[4,48,384]{2,1,0:T(8,128)(2,1)S(1)} collective-permute-done((bf16[4,48,384]{2,1,0:T(8,128)(2,1)S(1)}, bf16[4,48,384]{2,1,0:T(8,128)(2,1)S(1)}, u32[]{:S(2)}, u32[]{:S(2)}) %collective-permute-start.5) | collective-permute-done | bytes 147488 | tf_op jit(solution)/shard_map/ppermute | solution.py:23
  48.0 0.7 copy-done.12
  48.7 2.5 %copy-done.1 = bf16[768,3456]{1,0:T(8,128)(2,1)S(1)} copy-done((bf16[768,3456]{1,0:T(8,128)(2,1)S(1)}, bf16[768,3456]{1,0:T(8,128)(2,1)}, u32[]{:S(2)}) %copy-start.1) | copy-done | bytes 5308440
  51.2 2.5 %copy-done.3 = bf16[768,3456]{1,0:T(8,128)(2,1)S(1)} copy-done((bf16[768,3456]{1,0:T(8,128)(2,1)S(1)}, bf16[768,3456]{1,0:T(8,128)(2,1)}, u32[]{:S(2)}) %copy-start.3) | copy-done | bytes 5308440
  53.7 1.5 %copy-done.8 = bf16[1152,768]{1,0:T(8,128)(2,1)S(1)} copy-done((bf16[1152,768]{1,0:T(8,128)(2,1)S(1)}, bf16[1152,768]{1,0:T(8,128)(2,1)}, u32[]{:S(2)}) %copy-start.8) | copy-done | bytes 1769496
  55.2 0.9 %copy-done.13 = bf16[4,48,384]{2,1,0:T(8,128)(2,1)S(1)} copy-done((bf16[4,48,384]{2,1,0:T(8,128)(2,1)S(1)}, bf16[4,48,384]{2,1,0:T(8,128)(2,1)}, u32[]{:S(2)}) %copy-start.13) | copy-done | bytes 147480
  56.1 17.2 %second_block.1 = bf16[8,4,16,384]{3,2,1,0:T(8,128)(2,1)S(1)} custom-call(s32[4]{0:T(128)S(1)} %copy-done.14, bf16[4,48,384]{2,1,0:T(8,128)(2,1)S(1)} %collective-permute-done.4.near, bf16[4,48,384]{2,1,0:T(8,128)(2,1)S(1)} %first_block.1.blocked, bf16[4,48,384]{2,1,0:T(8,128)(2,1)S(1)} %copy-done.13, bf16[10,24,384]{2,1,0:T(8,128)(2,1)} %collective-permute-done.6.tile_near, ...), custom_call_target="tpu_custom_call" | custom-call | tf_op jit(solution)/shard_map/second_block/pallas_call | solution.py:685
  73.4 8.3 %collective-permute-start.8 = (bf16[4,4,16,384]{3,2,1,0:T(8,128)(2,1)S(1)}, bf16[4,4,16,384]{3,2,1,0:T(8,128)(2,1)S(1)}, u32[]{:S(2)}, u32[]{:S(2)}) collective-permute-start(bf16[4,4,16,384]{3,2,1,0:T(8,128)(2,1)S(1)} %constant_dynamic-slice_fusion), channel_id=1, source_target_pairs={{0,16},{16,0},{1,17},{17,1},{2,18},{18,2},{3,19},{19,3},{4,20},{20... | collective-permute-start | bytes 589832 | tf_op jit(solution)/shard_map/ppermute | solution.py:18
  81.7 1.1 %collective-permute-done.8 = bf16[4,4,16,384]{3,2,1,0:T(8,128)(2,1)S(1)} collective-permute-done((bf16[4,4,16,384]{3,2,1,0:T(8,128)(2,1)S(1)}, bf16[4,4,16,384]{3,2,1,0:T(8,128)(2,1)S(1)}, u32[]{:S(2)}, u32[]{:S(2)}) %collective-permute-start.8) | collective-permute-done | bytes 196640 | tf_op jit(solution)/shard_map/ppermute | solution.py:18
  82.8 1.1 %reshape.9 = bf16[4,4,64,192]{3,2,1,0:T(8,128)(2,1)} reshape(bf16[4,4,32,384]{3,2,1,0:T(8,128)(2,1)S(1)} %pad_maximum_fusion) | data formatting | bytes 786432 | tf_op jit(solution)/shard_map/reshape | solution.py:796
  (45 shorter events, 0.5 us)
Async XLA Ops:
  0.0 1.8 %collective-permute-start = (bf16[2,64,384]{2,1,0:T(8,128)(2,1)}, bf16[2,64,384]{2,1,0:T(8,128)(2,1)S(1)}, u32[]{:S(2)}, u32[]{:S(2)}) collective-permute-start(bf16[2,64,384]{2,1,0:T(8,128)(2,1)} %bitcast.15), channel_id=1, source_target_pairs={{0,16},{16,0},{1,17},{17,1},{2,18},{18,2},{3,19},{19,3},{4,20},{20... | collective-permute-start | bytes 294920 | tf_op jit(solution)/shard_map/ppermute | solution.py:18
  1.8 0.6 copy-start.15
  4.9 6.9 %collective-permute-start.1 = (bf16[12,24,384]{2,1,0:T(8,128)(2,1)}, bf16[12,24,384]{2,1,0:T(8,128)(2,1)S(1)}, u32[]{:S(2)}, u32[]{:S(2)}) collective-permute-start(bf16[12,24,384]{2,1,0:T(8,128)(2,1)} %get-tuple-element.21), channel_id=1, source_target_pairs={{0,1},{1,0},{2,3},{3,2},{4,5},{5,4},{6,7},{7,6},{8,9},{9,8},{10,11... | collective-permute-start | bytes 663560 | tf_op jit(solution)/shard_map/ppermute | solution.py:18
  5.2 1.6 %copy-start.6 = (bf16[5184,192]{0,1:T(8,128)(2,1)S(1)}, bf16[5184,192]{0,1:T(8,128)(2,1)}, u32[]{:S(2)}) copy-start(bf16[5184,192]{0,1:T(8,128)(2,1)} %param.30) | copy-start | bytes 5971972
  6.8 5.1 %copy-start.10 = (bf16[20,32,384]{2,1,0:T(8,128)(2,1)S(1)}, bf16[20,32,384]{2,1,0:T(8,128)(2,1)}, u32[]{:S(2)}) copy-start(bf16[20,32,384]{2,1,0:T(8,128)(2,1)} %get-tuple-element.22.tiles) | copy-start | bytes 1474564
  6.8 5.1 %copy-start.11 = (bf16[8,24,384]{2,1,0:T(8,128)(2,1)S(1)}, bf16[8,24,384]{2,1,0:T(8,128)(2,1)}, u32[]{:S(2)}) copy-start(bf16[8,24,384]{2,1,0:T(8,128)(2,1)} %get-tuple-element.20.mine) | copy-start | bytes 442372
  6.8 5.1 %copy-start.14 = (s32[4]{0:T(128)S(1)}, s32[4]{0:T(128)}, u32[]{:S(2)}) copy-start(s32[4]{0:T(128)} %pad_add_fusion.place) | copy-start | bytes 52
  8.3 5.1 %copy-start = (bf16[768,3456]{1,0:T(8,128)(2,1)}, bf16[768,3456]{1,0:T(8,128)(2,1)S(1)}, u32[]{:S(2)}) copy-start(bf16[768,3456]{1,0:T(8,128)(2,1)S(1)} %align_weights.2.later.w3) | copy-start | bytes 15925252
  11.8 4.8 %copy-start.18 = (f32[192]{0:T(256)S(1)}, f32[192]{0:T(256)}, u32[]{:S(2)}) copy-start(f32[192]{0:T(256)} %param.25) | copy-start | bytes 2308
  11.8 4.9 %copy-start.19 = (f32[192]{0:T(256)S(1)}, f32[192]{0:T(256)}, u32[]{:S(2)}) copy-start(f32[192]{0:T(256)} %param.24) | copy-start | bytes 2308
  11.8 5.0 %copy-start.16 = (f32[384]{0:T(512)S(1)}, f32[384]{0:T(512)}, u32[]{:S(2)}) copy-start(f32[384]{0:T(512)} %param.23) | copy-start | bytes 4612
  11.9 5.0 %copy-start.17 = (f32[384]{0:T(512)S(1)}, f32[384]{0:T(512)}, u32[]{:S(2)}) copy-start(f32[384]{0:T(512)} %param.22) | copy-start | bytes 4612
  13.4 12.6 %collective-permute-start.2 = (bf16[14,24,384]{2,1,0:T(8,128)(2,1)}, bf16[14,24,384]{2,1,0:T(8,128)(2,1)S(1)}, u32[]{:S(2)}, u32[]{:S(2)}) collective-permute-start(bf16[14,24,384]{2,1,0:T(8,128)(2,1)} %get-tuple-element.24), channel_id=1, source_target_pairs={{0,2},{4,6},{8,10},{12,14},{2,0},{6,4},{10,8},{14,12},{1,3},{5,7},... | collective-permute-start | bytes 774152 | tf_op jit(solution)/shard_map/ppermute | solution.py:23
  14.7 11.4 %collective-permute-start.3 = (bf16[14,24,384]{2,1,0:T(8,128)(2,1)}, bf16[14,24,384]{2,1,0:T(8,128)(2,1)}, u32[]{:S(2)}, u32[]{:S(2)}) collective-permute-start(bf16[14,24,384]{2,1,0:T(8,128)(2,1)} %get-tuple-element.27), channel_id=1, source_target_pairs={{2,4},{6,8},{10,12},{4,2},{8,6},{12,10},{3,5},{7,9},{11,13},{5,3},... | collective-permute-start | bytes 774152 | tf_op jit(solution)/shard_map/ppermute | solution.py:23
  16.9 1.3 %copy-start.9 = (bf16[3456,192]{0,1:T(8,128)(2,1)S(1)}, bf16[3456,192]{0,1:T(8,128)(2,1)}, u32[]{:S(2)}) copy-start(bf16[3456,192]{0,1:T(8,128)(2,1)} %param.29) | copy-start | bytes 3981316
  18.7 1.6 %copy-start.7 = (bf16[5184,192]{0,1:T(8,128)(2,1)S(1)}, bf16[5184,192]{0,1:T(8,128)(2,1)}, u32[]{:S(2)}) copy-start(bf16[5184,192]{0,1:T(8,128)(2,1)} %param.31) | copy-start | bytes 5971972
  21.8 19.4 %copy-start.2 = (bf16[768,3456]{1,0:T(8,128)(2,1)}, bf16[768,3456]{1,0:T(8,128)(2,1)S(1)}, u32[]{:S(2)}) copy-start(bf16[768,3456]{1,0:T(8,128)(2,1)S(1)} %align_weights.3.later_two.w4) | copy-start | bytes 15925252
  21.8 23.0 %collective-permute-start.6 = (bf16[10,24,384]{2,1,0:T(8,128)(2,1)}, bf16[10,24,384]{2,1,0:T(8,128)(2,1)}, u32[]{:S(2)}, u32[]{:S(2)}) collective-permute-start(bf16[10,24,384]{2,1,0:T(8,128)(2,1)} %get-tuple-element.30), channel_id=1, source_target_pairs={{0,2},{4,6},{8,10},{12,14},{2,0},{6,4},{10,8},{14,12},{1,3},{5,7},... | collective-permute-start | bytes 552968 | tf_op jit(solution)/shard_map/ppermute | solution.py:23
  21.8 23.0 %collective-permute-start.7 = (bf16[10,24,384]{2,1,0:T(8,128)(2,1)}, bf16[10,24,384]{2,1,0:T(8,128)(2,1)}, u32[]{:S(2)}, u32[]{:S(2)}) collective-permute-start(bf16[10,24,384]{2,1,0:T(8,128)(2,1)} %get-tuple-element.32), channel_id=1, source_target_pairs={{2,4},{6,8},{10,12},{4,2},{8,6},{12,10},{3,5},{7,9},{11,13},{5,3},... | collective-permute-start | bytes 552968 | tf_op jit(solution)/shard_map/ppermute | solution.py:23
  26.0 3.3 %copy-start.4 = (bf16[10368,384]{1,0:T(8,128)(2,1)S(1)}, bf16[10368,384]{1,0:T(8,128)(2,1)}, u32[]{:S(2)}) copy-start(bf16[10368,384]{1,0:T(8,128)(2,1)} %w1.1) | copy-start | bytes 23887876
  29.3 3.3 %copy-start.5 = (bf16[10368,384]{1,0:T(8,128)(2,1)S(1)}, bf16[10368,384]{1,0:T(8,128)(2,1)}, u32[]{:S(2)}) copy-start(bf16[10368,384]{1,0:T(8,128)(2,1)} %w2.1) | copy-start | bytes 23887876
  41.2 4.1 %collective-permute-start.4 = (bf16[4,48,384]{2,1,0:T(8,128)(2,1)S(1)}, bf16[4,48,384]{2,1,0:T(8,128)(2,1)S(1)}, u32[]{:S(2)}, u32[]{:S(2)}) collective-permute-start(bf16[4,48,384]{2,1,0:T(8,128)(2,1)S(1)} %first_block.1.blocked), channel_id=1, source_target_pairs={{0,2},{4,6},{8,10},{12,14},{2,0},{6,4},{10,8},{14,12},{1,3},{5,7},... | collective-permute-start | bytes 442376 | tf_op jit(solution)/shard_map/ppermute | solution.py:23
  41.3 6.8 %collective-permute-start.5 = (bf16[4,48,384]{2,1,0:T(8,128)(2,1)S(1)}, bf16[4,48,384]{2,1,0:T(8,128)(2,1)S(1)}, u32[]{:S(2)}, u32[]{:S(2)}) collective-permute-start(bf16[4,48,384]{2,1,0:T(8,128)(2,1)S(1)} %first_block.1.blocked), channel_id=1, source_target_pairs={{2,4},{6,8},{10,12},{4,2},{8,6},{12,10},{3,5},{7,9},{11,13},{5,3},... | collective-permute-start | bytes 442376 | tf_op jit(solution)/shard_map/ppermute | solution.py:23
  48.0 0.7 copy-start.12
  48.7 2.5 %copy-start.1 = (bf16[768,3456]{1,0:T(8,128)(2,1)S(1)}, bf16[768,3456]{1,0:T(8,128)(2,1)}, u32[]{:S(2)}) copy-start(bf16[768,3456]{1,0:T(8,128)(2,1)} %copy-done) | copy-start | bytes 15925252
  51.2 2.5 %copy-start.3 = (bf16[768,3456]{1,0:T(8,128)(2,1)S(1)}, bf16[768,3456]{1,0:T(8,128)(2,1)}, u32[]{:S(2)}) copy-start(bf16[768,3456]{1,0:T(8,128)(2,1)} %copy-done.2) | copy-start | bytes 15925252
  53.7 1.5 %copy-start.8 = (bf16[1152,768]{1,0:T(8,128)(2,1)S(1)}, bf16[1152,768]{1,0:T(8,128)(2,1)}, u32[]{:S(2)}) copy-start(bf16[1152,768]{1,0:T(8,128)(2,1)} %wt.1) | copy-start | bytes 5308420
  55.2 0.9 %copy-start.13 = (bf16[4,48,384]{2,1,0:T(8,128)(2,1)S(1)}, bf16[4,48,384]{2,1,0:T(8,128)(2,1)}, u32[]{:S(2)}) copy-start(bf16[4,48,384]{2,1,0:T(8,128)(2,1)} %copy-done.12) | copy-start | bytes 442372
  73.4 9.3 %collective-permute-start.8 = (bf16[4,4,16,384]{3,2,1,0:T(8,128)(2,1)S(1)}, bf16[4,4,16,384]{3,2,1,0:T(8,128)(2,1)S(1)}, u32[]{:S(2)}, u32[]{:S(2)}) collective-permute-start(bf16[4,4,16,384]{3,2,1,0:T(8,128)(2,1)S(1)} %constant_dynamic-slice_fusion), channel_id=1, source_target_pairs={{0,16},{16,0},{1,17},{17,1},{2,18},{18,2},{3,19},{19,3},{4,20},{20... | collective-permute-start | bytes 589832 | tf_op jit(solution)/shard_map/ppermute | solution.py:18

commit v13 on v12

--- a/solution.py
+++ b/solution.py
@@ -84,26 +84,20 @@
     return jnp.concatenate(parts, axis=0)
 
 
-def low_product(acc, even, odd, count, height, wide, weights):
+def low_product(acc, even, odd, count, height, wide, weights, copies):
     rows = count * (height - 2) * wide
     channels = weights.shape[1]
     lanes = 3 * channels
+    waited = 0
     for n in range(-(-lanes // LANES)):
         begin, end = n * LANES, min((n + 1) * LANES, lanes)
+        while waited * channels < end:
+            copies[waited].wait()
+            waited += 1
         left = jnp.concatenate(
             [taps(even, odd, 0, count, height, wide, t // 3, t % 3) for t in range(9)], axis=1
         )
-        right = []
-        for t in range(9):
-            parts = []
-            for dx in range(3):
-                low = max(begin - dx * channels, 0)
-                high = min(end - dx * channels, channels)
-                if low < high:
-                    base = (3 * t + dx) * channels
-                    parts.append(weights[base : base + channels, low:high])
-            right.append(jnp.concatenate(parts, axis=1))
-        right = jnp.concatenate(right, axis=0)
+        right = weights[:, :, begin:end].reshape(9 * channels, end - begin)
         acc[n, 0:rows, 0 : end - begin] = jnp.dot(left, right, preferred_element_type=F32)
 
 
@@ -418,6 +412,16 @@
     )(weight.T)
 
 
+def weight_copies(source, target, sems, base):
+    channels = source.shape[-1]
+    return [
+        pltpu.make_async_copy(
+            source.at[:, dx], target.at[:, :, pl.ds(dx * channels, channels)], sems.at[base + dx]
+        )
+        for dx in range(3)
+    ]
+
+
 def first_kernel(
     wide,
     sizes,
@@ -426,17 +430,20 @@
     own,
     far,
     gains,
-    w1,
-    w2,
+    weight_one,
+    weight_two,
     later_one,
     later_two,
     out_ref,
+    w1,
+    w2,
     acc,
     acc_two,
     x1e,
     x1o,
     x2e,
     x2o,
+    sems,
 ):
     channels = own.shape[-1]
     frames = own.shape[1] - 4
@@ -445,6 +452,10 @@
     units = frames + 2
     del later_one, later_two
 
+    copies_one = weight_copies(weight_one, w1, sems, 0)
+    copies_two = weight_copies(weight_two, w2, sems, 3)
+    copies_one[0].start()
+
     slots = [lax.rem(y + col, 2) for y in range(2)]
 
     is_even = lax.rem(row, 2) == 0
@@ -469,16 +480,19 @@
         values = jnp.concatenate([first] + own_rows(units + f) + [last], axis=0)
         store(x2e, x2o, f, values, 4, wide)
 
+    copies_one[1].start()
     for f in range(frames):
         store(x1e, x1o, f + 2, activate(rows_of(f), gains[0:1, :], 1.0), 6, wide)
-    low_product(acc, x1e, x1o, frames, 6, wide, w1)
+    for copy in [copies_one[2]] + copies_two:
+        copy.start()
+    low_product(acc, x1e, x1o, frames, 6, wide, w1, copies_one)
 
     mask = line_mask(place, wide, 2 * row - 1, 4, height, width)
     for f in range(frames):
         size = 4 * wide
         values = activate(low_sum(acc, f * size, size), gains[1:2, :], mask)
         store(x2e, x2o, f + 2, values, 4, wide)
-    low_product(acc_two, x2e, x2o, frames, 4, wide, w2)
+    low_product(acc_two, x2e, x2o, frames, 4, wide, w2, copies_two)
     for f in range(frames):
         size = 2 * wide
         values = low_sum(acc_two, f * size, size) + jnp.concatenate(own_rows(f), axis=0)
@@ -502,19 +516,23 @@
         functools.partial(first_kernel, wide, sizes),
         out_shape=jax.ShapeDtypeStruct((frames, 2 * wide, channels), BF16),
         in_specs=[pl.BlockSpec(memory_space=pltpu.SMEM)]
-        + [vmem] * 6
+        + [vmem] * 4
+        + [pl.BlockSpec(memory_space=pltpu.HBM)] * 2
         + [anywhere] * 2,
         out_specs=vmem,
         scratch_shapes=[
+            pltpu.VMEM((9, channels, slots * LANES), BF16),
+            pltpu.VMEM((9, channels, slots * LANES), BF16),
             pltpu.VMEM((slots, frames * 4 * wide, LANES), F32),
             pltpu.VMEM((slots, frames * 2 * wide, LANES), F32),
             *planes(frames + 2, 6, wide, channels),
             *planes(frames + 2, 4, wide, channels),
+            pltpu.SemaphoreType.DMA((6,)),
         ],
-        compiler_params=pltpu.CompilerParams(vmem_limit_bytes=12 * 1024 * 1024),
+        compiler_params=pltpu.CompilerParams(vmem_limit_bytes=50 * 1024 * 1024),
         cost_estimate=pl.CostEstimate(
             flops=2 * 27 * channels * channels * frames * 6 * wide,
-            bytes_accessed=0,
+            bytes_accessed=2 * 54 * channels * channels,
             transcendentals=0,
         ),
         name="first_block",
@@ -534,9 +552,12 @@
     gains,
     wt,
     wu,
+    weight_three,
+    weight_four,
+    out_ref,
     w3,
     w4,
-    out_ref,
+    sems,
     acc,
     mixed,
     de,
@@ -547,6 +568,12 @@
     ups, threes, fours = buffers[0:3], buffers[3:6], buffers[6:9]
     planes_three = [buffers[9 + 2 * g : 11 + 2 * g] for g in range(3)]
     planes_four = [buffers[15 + 2 * g : 17 + 2 * g] for g in range(3)]
+    copies = [
+        pltpu.make_async_copy(source, target, sems.at[i])
+        for i, (source, target) in enumerate(((weight_three, w3), (weight_four, w4)))
+    ]
+    for copy in copies:
+        copy.start()
     channels = blocked.shape[-1]
     half = channels // 2
     size = 6 * wide
@@ -668,6 +695,8 @@
         ((fourth, 2), (finish, 1)),
         (None, (finish, 2)),
     ):
+        if product in ((third, 0), (fourth, 0)):
+            copies[0 if product[0] is third else 1].wait()
         for n in range(max(2 * channels // LANES, *(last - first for first, last in groups))):
             if product is not None and n < 2 * channels // LANES:
                 product[0](product[1], n)
@@ -686,9 +715,13 @@
         functools.partial(second_kernel, wide, sizes),
         out_shape=jax.ShapeDtypeStruct((count, 4, wide - 2 * HALO, channels), BF16),
         in_specs=[pl.BlockSpec(memory_space=pltpu.SMEM)]
-        + [vmem] * 11,
+        + [vmem] * 9
+        + [pl.BlockSpec(memory_space=pl.ANY)] * 2,
         out_specs=vmem,
         scratch_shapes=[
+            pltpu.VMEM(weights[2].shape, BF16),
+            pltpu.VMEM(weights[3].shape, BF16),
+            pltpu.SemaphoreType.DMA((2,)),
             pltpu.VMEM((3, frames * 6 * wide, LANES), F32),
             pltpu.VMEM(((frames + 2) * 6 * wide, channels), BF16),
             *planes(count, 6, wide, channels),
@@ -699,7 +732,7 @@
             *(ref for n in slots for ref in planes(n, 8, wide, channels)),
             *(ref for n in slots for ref in planes(n, 6, wide, channels)),
         ],
-        compiler_params=pltpu.CompilerParams(vmem_limit_bytes=24 * 1024 * 1024),
+        compiler_params=pltpu.CompilerParams(vmem_limit_bytes=50 * 1024 * 1024),
         name="second_block",
     )(place, *pieces, *tiles, gains, *weights)
 
@@ -767,8 +800,8 @@
         place,
         [near, own, far],
         gains,
-        weight_one,
-        weight_two,
+        weight_one.reshape(9, 3, channels, channels),
+        weight_two.reshape(9, 3, channels, channels),
         (weight_upsample, weight_four),
         sizes,
     )

time: 84.5 us -> 76.6 us (0.907)
  the two profiles are of different devices: /device:TPU:27 before, /device:TPU:9 now
where the time goes in v13:
time: 76.6 us; the launch traced here: 76.3 us
  Pallas kernels  37.4 us (49%)
  starting transfers between devices  17.8 us (23%)
  local copies, waits for them, and re-layouts  11.1 us (14%)
  waiting for transfers between devices  8.8 us (11%)
  other arithmetic  0.77 us (1%)
    pallas_call x1, Pallas kernels, second_block(): pl.pallas_call(functools.partial(second_kernel, wide, sizes), out_shape=j...  19.3 us
    ppermute x6, starting transfers between devices, paired(): lax.ppermute(value, axis, pairs + [(high, low) for low, high in pairs])  12.1 us
    pallas_call x1, Pallas kernels, first_block(): pl.pallas_call(functools.partial(first_kernel, wide, sizes), out_shape=ja...  10.7 us
    unnamed x30, local copies, waits for them, and re-layouts  9.83 us
    ppermute x3, starting transfers between devices, swapped(): return lax.ppermute(value, axis, [(0, 1), (1, 0)])  5.7 us
    ppermute x6, waiting for transfers between devices, paired(): lax.ppermute(value, axis, pairs + [(high, low) for low, high in pairs])  4.66 us
    ppermute x3, waiting for transfers between devices, swapped(): return lax.ppermute(value, axis, [(0, 1), (1, 0)])  4.14 us
    pallas_call x2, Pallas kernels, align_weights(): pl.pallas_call(align_kernel, out_shape=jax.ShapeDtypeStruct((4 * half, 18...  2.98 us
  transfers between devices with their start and end apart: 9, of which 5 were waited for; matrix products, arithmetic and copies ran while one was open for 1% of the time, Pallas kernels for 19%

profile of v13, /device:TPU:9, one launch (start us, length us, event | category | flops | bytes accessed | tf_op | source)
XLA Modules:
  0.0 76.3 jit_solution(18071213733576505350)
XLA Ops:
  0.0 0.7 collective-permute-start
  0.7 0.7 pad_add_fusion.place
  1.3 0.5 collective-permute-done.arrived
  1.8 0.6 copy-done.10
  2.5 2.4 %pack.1 = (bf16[8,24,384]{2,1,0:T(8,128)(2,1)}, bf16[12,24,384]{2,1,0:T(8,128)(2,1)}, bf16[20,32,384]{2,1,0:T(8,128)(2,1)}) custom-call(s32[4]{0:T(128)} %pad_add_fusion.place, bf16[2,64,384]{2,1,0:T(8,128)(2,1)} %bitcast.20, bf16[2,64,384]{2,1,0:T(8,128)(2,1)} %copy-done.10, bf16[2,64,384]{2,1,0:T(8,128)(2,1)} %bitcast.21, bf16[2,64,384]{2,1,0:T(8,128)(2,1)} %bitcast.22, ...), custom_call_target="tpu_custom_call" | custom-call | tf_op jit(solution)/shard_map/pack/pallas_call | solution.py:240
  4.9 1.2 %collective-permute-start.1 = (bf16[12,24,384]{2,1,0:T(8,128)(2,1)}, bf16[12,24,384]{2,1,0:T(8,128)(2,1)S(1)}, u32[]{:S(2)}, u32[]{:S(2)}) collective-permute-start(bf16[12,24,384]{2,1,0:T(8,128)(2,1)} %get-tuple-element.21), channel_id=1, source_target_pairs={{0,1},{1,0},{2,3},{3,2},{4,5},{5,4},{6,7},{7,6},{8,9},{9,8},{10,11... | collective-permute-start | bytes 663560 | tf_op jit(solution)/shard_map/ppermute | solution.py:18
  6.1 1.6 %copy-done.3 = bf16[5184,192]{0,1:T(8,128)(2,1)S(1)} copy-done((bf16[5184,192]{0,1:T(8,128)(2,1)S(1)}, bf16[5184,192]{0,1:T(8,128)(2,1)}, u32[]{:S(2)}) %copy-start.3) | copy-done | bytes 1990680
  7.7 1.5 %align_weights.2.later.weight_three = bf16[768,3456]{1,0:T(8,128)(2,1)S(1)} custom-call(bf16[192,5184]{1,0:T(8,128)(2,1)S(1)} %bitcast.14), custom_call_target="tpu_custom_call" | custom-call | tf_op jit(solution)/shard_map/align_weights/pallas_call | solution.py:367
  9.2 2.6 %collective-permute-done.1.theirs = bf16[12,24,384]{2,1,0:T(8,128)(2,1)S(1)} collective-permute-done((bf16[12,24,384]{2,1,0:T(8,128)(2,1)}, bf16[12,24,384]{2,1,0:T(8,128)(2,1)S(1)}, u32[]{:S(2)}, u32[]{:S(2)}) %collective-permute-start.1) | collective-permute-done | bytes 221216 | tf_op jit(solution)/shard_map/ppermute | solution.py:18
  11.8 0.0 copy-start.14
  11.8 1.5 %stack.33 = (bf16[2,8,24,384]{3,2,1,0:T(8,128)(2,1)S(1)}, bf16[14,24,384]{2,1,0:T(8,128)(2,1)}, bf16[14,24,384]{2,1,0:T(8,128)(2,1)}, bf16[20,24,384]{2,1,0:T(8,...) custom-call(s32[4]{0:T(128)S(1)} %copy-done.9, bf16[8,24,384]{2,1,0:T(8,128)(2,1)S(1)} %copy-done.8, ...), custom_call_target="tpu_custom_call" | custom-call | tf_op jit(solution)/shard_map/stack/pallas_call | solution.py:306
  13.4 1.2 %collective-permute-start.2 = (bf16[14,24,384]{2,1,0:T(8,128)(2,1)}, bf16[14,24,384]{2,1,0:T(8,128)(2,1)S(1)}, u32[]{:S(2)}, u32[]{:S(2)}) collective-permute-start(bf16[14,24,384]{2,1,0:T(8,128)(2,1)} %get-tuple-element.24), channel_id=1, source_target_pairs={{0,2},{4,6},{8,10},{12,14},{2,0},{6,4},{10,8},{14,12},{1,3},{5,7},... | collective-permute-start | bytes 774152 | tf_op jit(solution)/shard_map/ppermute | solution.py:23
  14.6 2.1 %collective-permute-start.3 = (bf16[14,24,384]{2,1,0:T(8,128)(2,1)}, bf16[14,24,384]{2,1,0:T(8,128)(2,1)}, u32[]{:S(2)}, u32[]{:S(2)}) collective-permute-start(bf16[14,24,384]{2,1,0:T(8,128)(2,1)} %get-tuple-element.27), channel_id=1, source_target_pairs={{2,4},{6,8},{10,12},{4,2},{8,6},{12,10},{3,5},{7,9},{11,13},{5,3},... | collective-permute-start | bytes 774152 | tf_op jit(solution)/shard_map/ppermute | solution.py:23
  16.7 0.1 stack_tile.7
  16.8 0.1 stack_tile.6
  17.0 1.3 %copy-done.6 = bf16[3456,192]{0,1:T(8,128)(2,1)S(1)} copy-done((bf16[3456,192]{0,1:T(8,128)(2,1)S(1)}, bf16[3456,192]{0,1:T(8,128)(2,1)}, u32[]{:S(2)}) %copy-start.6) | copy-done | bytes 1327128
  18.3 0.5 combine_weights.1.later_one.wu
  18.8 2.4 %copy-done.4 = bf16[5184,192]{0,1:T(8,128)(2,1)S(1)} copy-done((bf16[5184,192]{0,1:T(8,128)(2,1)S(1)}, bf16[5184,192]{0,1:T(8,128)(2,1)}, u32[]{:S(2)}) %copy-start.4) | copy-done | bytes 1990680
  21.2 1.5 %align_weights.3.later_two.weight_four = bf16[768,3456]{1,0:T(8,128)(2,1)S(1)} custom-call(bf16[192,5184]{1,0:T(8,128)(2,1)S(1)} %bitcast.15), custom_call_target="tpu_custom_call" | custom-call | tf_op jit(solution)/shard_map/align_weights/pallas_call | solution.py:367
  22.7 2.4 %copy-done.1 = bf16[768,3456]{1,0:T(8,128)(2,1)} copy-done((bf16[768,3456]{1,0:T(8,128)(2,1)}, bf16[768,3456]{1,0:T(8,128)(2,1)S(1)}, u32[]{:S(2)}) %copy-start.1) | copy-done | bytes 5308440
  25.1 2.3 %collective-permute-start.6 = (bf16[10,24,384]{2,1,0:T(8,128)(2,1)}, bf16[10,24,384]{2,1,0:T(8,128)(2,1)}, u32[]{:S(2)}, u32[]{:S(2)}) collective-permute-start(bf16[10,24,384]{2,1,0:T(8,128)(2,1)} %get-tuple-element.30), channel_id=1, source_target_pairs={{0,2},{4,6},{8,10},{12,14},{2,0},{6,4},{10,8},{14,12},{1,3},{5,7},... | collective-permute-start | bytes 552968 | tf_op jit(solution)/shard_map/ppermute | solution.py:23
  27.4 1.9 %collective-permute-start.7 = (bf16[10,24,384]{2,1,0:T(8,128)(2,1)}, bf16[10,24,384]{2,1,0:T(8,128)(2,1)}, u32[]{:S(2)}, u32[]{:S(2)}) collective-permute-start(bf16[10,24,384]{2,1,0:T(8,128)(2,1)} %get-tuple-element.32), channel_id=1, source_target_pairs={{2,4},{6,8},{10,12},{4,2},{8,6},{12,10},{3,5},{7,9},{11,13},{5,3},... | collective-permute-start | bytes 552968 | tf_op jit(solution)/shard_map/ppermute | solution.py:23
  29.3 10.7 %first_block.1.blocked = bf16[4,48,384]{2,1,0:T(8,128)(2,1)S(1)} custom-call(s32[4]{0:T(128)S(1)} %copy-done.9, bf16[14,24,384]{2,1,0:T(8,128)(2,1)S(1)} %collective-permute-done.2.near, bf16[2,8,24,384]{3,2,1,0:T(8,128)(2,1)S(1)} %get-tuple-element.26.own, bf16[14,24,384]{2,1,0:T(8,128)(2,1)} %collective-permute-done.3.far, ...), custom_call_target="tpu_custom_call" | custom-call | flops 4586471424 | bytes 15925248 | tf_op jit(solution)/shard_map/first_block/pallas_call | solution.py:515
  40.0 2.5 %collective-permute-start.4 = (bf16[4,48,384]{2,1,0:T(8,128)(2,1)S(1)}, bf16[4,48,384]{2,1,0:T(8,128)(2,1)S(1)}, u32[]{:S(2)}, u32[]{:S(2)}) collective-permute-start(bf16[4,48,384]{2,1,0:T(8,128)(2,1)S(1)} %first_block.1.blocked), channel_id=1, source_target_pairs={{0,2},{4,6},{8,10},{12,14},{2,0},{6,4},{10,8},{14,12},{1,3},{5,7},... | collective-permute-start | bytes 442376 | tf_op jit(solution)/shard_map/ppermute | solution.py:23
  42.5 2.1 %collective-permute-start.5 = (bf16[4,48,384]{2,1,0:T(8,128)(2,1)S(1)}, bf16[4,48,384]{2,1,0:T(8,128)(2,1)S(1)}, u32[]{:S(2)}, u32[]{:S(2)}) collective-permute-start(bf16[4,48,384]{2,1,0:T(8,128)(2,1)S(1)} %first_block.1.blocked), channel_id=1, source_target_pairs={{2,4},{6,8},{10,12},{4,2},{8,6},{12,10},{3,5},{7,9},{11,13},{5,3},... | collective-permute-start | bytes 442376 | tf_op jit(solution)/shard_map/ppermute | solution.py:23
  44.7 0.4 collective-permute-done.4.near
  45.1 4.2 %collective-permute-done.5.far = bf16[4,48,384]{2,1,0:T(8,128)(2,1)S(1)} collective-permute-done((bf16[4,48,384]{2,1,0:T(8,128)(2,1)S(1)}, bf16[4,48,384]{2,1,0:T(8,128)(2,1)S(1)}, u32[]{:S(2)}, u32[]{:S(2)}) %collective-permute-start.5) | collective-permute-done | bytes 147488 | tf_op jit(solution)/shard_map/ppermute | solution.py:23
  49.3 1.5 %copy-done.5 = bf16[1152,768]{1,0:T(8,128)(2,1)S(1)} copy-done((bf16[1152,768]{1,0:T(8,128)(2,1)S(1)}, bf16[1152,768]{1,0:T(8,128)(2,1)}, u32[]{:S(2)}) %copy-start.5) | copy-done | bytes 1769496
  50.8 19.3 %second_block.1 = bf16[8,4,16,384]{3,2,1,0:T(8,128)(2,1)S(1)} custom-call(s32[4]{0:T(128)S(1)} %copy-done.9, bf16[4,48,384]{2,1,0:T(8,128)(2,1)S(1)} %collective-permute-done.4.near, bf16[4,48,384]{2,1,0:T(8,128)(2,1)S(1)} %first_block.1.blocked, bf16[4,48,384]{2,1,0:T(8,128)(2,1)S(1)} %collective-permute-done.5.far, ...), custom_call_target="tpu_custom_call" | custom-call | tf_op jit(solution)/shard_map/second_block/pallas_call | solution.py:714
  70.2 3.8 %collective-permute-start.8 = (bf16[4,4,16,384]{3,2,1,0:T(8,128)(2,1)S(1)}, bf16[4,4,16,384]{3,2,1,0:T(8,128)(2,1)S(1)}, u32[]{:S(2)}, u32[]{:S(2)}) collective-permute-start(bf16[4,4,16,384]{3,2,1,0:T(8,128)(2,1)S(1)} %constant_dynamic-slice_fusion), channel_id=1, source_target_pairs={{0,16},{16,0},{1,17},{17,1},{2,18},{18,2},{3,19},{19,3},{4,20},{20... | collective-permute-start | bytes 589832 | tf_op jit(solution)/shard_map/ppermute | solution.py:18
  74.0 1.1 %collective-permute-done.8 = bf16[4,4,16,384]{3,2,1,0:T(8,128)(2,1)S(1)} collective-permute-done((bf16[4,4,16,384]{3,2,1,0:T(8,128)(2,1)S(1)}, bf16[4,4,16,384]{3,2,1,0:T(8,128)(2,1)S(1)}, u32[]{:S(2)}, u32[]{:S(2)}) %collective-permute-start.8) | collective-permute-done | bytes 196640 | tf_op jit(solution)/shard_map/ppermute | solution.py:18
  75.1 1.1 %reshape.17 = bf16[4,4,64,192]{3,2,1,0:T(8,128)(2,1)} reshape(bf16[4,4,32,384]{3,2,1,0:T(8,128)(2,1)S(1)} %pad_maximum_fusion) | data formatting | bytes 786432 | tf_op jit(solution)/shard_map/reshape | solution.py:829
  (35 shorter events, 0.2 us)
Async XLA Ops:
  0.0 1.8 %collective-permute-start = (bf16[2,64,384]{2,1,0:T(8,128)(2,1)}, bf16[2,64,384]{2,1,0:T(8,128)(2,1)S(1)}, u32[]{:S(2)}, u32[]{:S(2)}) collective-permute-start(bf16[2,64,384]{2,1,0:T(8,128)(2,1)} %bitcast.19), channel_id=1, source_target_pairs={{0,16},{16,0},{1,17},{17,1},{2,18},{18,2},{3,19},{19,3},{4,20},{20... | collective-permute-start | bytes 294920 | tf_op jit(solution)/shard_map/ppermute | solution.py:18
  1.8 0.6 copy-start.10
  4.9 6.9 %collective-permute-start.1 = (bf16[12,24,384]{2,1,0:T(8,128)(2,1)}, bf16[12,24,384]{2,1,0:T(8,128)(2,1)S(1)}, u32[]{:S(2)}, u32[]{:S(2)}) collective-permute-start(bf16[12,24,384]{2,1,0:T(8,128)(2,1)} %get-tuple-element.21), channel_id=1, source_target_pairs={{0,1},{1,0},{2,3},{3,2},{4,5},{5,4},{6,7},{7,6},{8,9},{9,8},{10,11... | collective-permute-start | bytes 663560 | tf_op jit(solution)/shard_map/ppermute | solution.py:18
  6.1 1.6 %copy-start.3 = (bf16[5184,192]{0,1:T(8,128)(2,1)S(1)}, bf16[5184,192]{0,1:T(8,128)(2,1)}, u32[]{:S(2)}) copy-start(bf16[5184,192]{0,1:T(8,128)(2,1)} %param.30) | copy-start | bytes 5971972
  7.7 4.1 %copy-start.7 = (bf16[20,32,384]{2,1,0:T(8,128)(2,1)S(1)}, bf16[20,32,384]{2,1,0:T(8,128)(2,1)}, u32[]{:S(2)}) copy-start(bf16[20,32,384]{2,1,0:T(8,128)(2,1)} %get-tuple-element.22.tiles) | copy-start | bytes 1474564
  7.7 4.1 %copy-start.8 = (bf16[8,24,384]{2,1,0:T(8,128)(2,1)S(1)}, bf16[8,24,384]{2,1,0:T(8,128)(2,1)}, u32[]{:S(2)}) copy-start(bf16[8,24,384]{2,1,0:T(8,128)(2,1)} %get-tuple-element.20.mine) | copy-start | bytes 442372
  7.7 4.1 %copy-start.9 = (s32[4]{0:T(128)S(1)}, s32[4]{0:T(128)}, u32[]{:S(2)}) copy-start(s32[4]{0:T(128)} %pad_add_fusion.place) | copy-start | bytes 52
  9.2 4.2 %copy-start = (bf16[768,3456]{1,0:T(8,128)(2,1)}, bf16[768,3456]{1,0:T(8,128)(2,1)S(1)}, u32[]{:S(2)}) copy-start(bf16[768,3456]{1,0:T(8,128)(2,1)S(1)} %align_weights.2.later.weight_three) | copy-start | bytes 15925252
  11.8 4.9 %copy-start.13 = (f32[192]{0:T(256)S(1)}, f32[192]{0:T(256)}, u32[]{:S(2)}) copy-start(f32[192]{0:T(256)} %param.25) | copy-start | bytes 2308
  11.8 5.0 %copy-start.14 = (f32[192]{0:T(256)S(1)}, f32[192]{0:T(256)}, u32[]{:S(2)}) copy-start(f32[192]{0:T(256)} %param.24) | copy-start | bytes 2308
  11.8 5.1 %copy-start.11 = (f32[384]{0:T(512)S(1)}, f32[384]{0:T(512)}, u32[]{:S(2)}) copy-start(f32[384]{0:T(512)} %param.23) | copy-start | bytes 4612
  11.8 5.1 %copy-start.12 = (f32[384]{0:T(512)S(1)}, f32[384]{0:T(512)}, u32[]{:S(2)}) copy-start(f32[384]{0:T(512)} %param.22) | copy-start | bytes 4612
  13.4 15.9 %collective-permute-start.2 = (bf16[14,24,384]{2,1,0:T(8,128)(2,1)}, bf16[14,24,384]{2,1,0:T(8,128)(2,1)S(1)}, u32[]{:S(2)}, u32[]{:S(2)}) collective-permute-start(bf16[14,24,384]{2,1,0:T(8,128)(2,1)} %get-tuple-element.24), channel_id=1, source_target_pairs={{0,2},{4,6},{8,10},{12,14},{2,0},{6,4},{10,8},{14,12},{1,3},{5,7},... | collective-permute-start | bytes 774152 | tf_op jit(solution)/shard_map/ppermute | solution.py:23
  14.6 14.7 %collective-permute-start.3 = (bf16[14,24,384]{2,1,0:T(8,128)(2,1)}, bf16[14,24,384]{2,1,0:T(8,128)(2,1)}, u32[]{:S(2)}, u32[]{:S(2)}) collective-permute-start(bf16[14,24,384]{2,1,0:T(8,128)(2,1)} %get-tuple-element.27), channel_id=1, source_target_pairs={{2,4},{6,8},{10,12},{4,2},{8,6},{12,10},{3,5},{7,9},{11,13},{5,3},... | collective-permute-start | bytes 774152 | tf_op jit(solution)/shard_map/ppermute | solution.py:23
  16.9 1.3 %copy-start.6 = (bf16[3456,192]{0,1:T(8,128)(2,1)S(1)}, bf16[3456,192]{0,1:T(8,128)(2,1)}, u32[]{:S(2)}) copy-start(bf16[3456,192]{0,1:T(8,128)(2,1)} %param.29) | copy-start | bytes 3981316
  18.7 10.6 %copy-start.2 = (bf16[2,768,768]{2,1,0:T(8,128)(2,1)}, bf16[2,768,768]{2,1,0:T(8,128)(2,1)S(1)}, u32[]{:S(2)}) copy-start(bf16[2,768,768]{2,1,0:T(8,128)(2,1)S(1)} %combine_weights.1.later_one.wu) | copy-start | bytes 7077892
  18.7 2.4 %copy-start.4 = (bf16[5184,192]{0,1:T(8,128)(2,1)S(1)}, bf16[5184,192]{0,1:T(8,128)(2,1)}, u32[]{:S(2)}) copy-start(bf16[5184,192]{0,1:T(8,128)(2,1)} %param.31) | copy-start | bytes 5971972
  22.7 2.4 %copy-start.1 = (bf16[768,3456]{1,0:T(8,128)(2,1)}, bf16[768,3456]{1,0:T(8,128)(2,1)S(1)}, u32[]{:S(2)}) copy-start(bf16[768,3456]{1,0:T(8,128)(2,1)S(1)} %align_weights.3.later_two.weight_four) | copy-start | bytes 15925252
  25.1 19.6 %collective-permute-start.6 = (bf16[10,24,384]{2,1,0:T(8,128)(2,1)}, bf16[10,24,384]{2,1,0:T(8,128)(2,1)}, u32[]{:S(2)}, u32[]{:S(2)}) collective-permute-start(bf16[10,24,384]{2,1,0:T(8,128)(2,1)} %get-tuple-element.30), channel_id=1, source_target_pairs={{0,2},{4,6},{8,10},{12,14},{2,0},{6,4},{10,8},{14,12},{1,3},{5,7},... | collective-permute-start | bytes 552968 | tf_op jit(solution)/shard_map/ppermute | solution.py:23
  27.4 17.3 %collective-permute-start.7 = (bf16[10,24,384]{2,1,0:T(8,128)(2,1)}, bf16[10,24,384]{2,1,0:T(8,128)(2,1)}, u32[]{:S(2)}, u32[]{:S(2)}) collective-permute-start(bf16[10,24,384]{2,1,0:T(8,128)(2,1)} %get-tuple-element.32), channel_id=1, source_target_pairs={{2,4},{6,8},{10,12},{4,2},{8,6},{12,10},{3,5},{7,9},{11,13},{5,3},... | collective-permute-start | bytes 552968 | tf_op jit(solution)/shard_map/ppermute | solution.py:23
  40.0 5.1 %collective-permute-start.4 = (bf16[4,48,384]{2,1,0:T(8,128)(2,1)S(1)}, bf16[4,48,384]{2,1,0:T(8,128)(2,1)S(1)}, u32[]{:S(2)}, u32[]{:S(2)}) collective-permute-start(bf16[4,48,384]{2,1,0:T(8,128)(2,1)S(1)} %first_block.1.blocked), channel_id=1, source_target_pairs={{0,2},{4,6},{8,10},{12,14},{2,0},{6,4},{10,8},{14,12},{1,3},{5,7},... | collective-permute-start | bytes 442376 | tf_op jit(solution)/shard_map/ppermute | solution.py:23
  42.5 6.8 %collective-permute-start.5 = (bf16[4,48,384]{2,1,0:T(8,128)(2,1)S(1)}, bf16[4,48,384]{2,1,0:T(8,128)(2,1)S(1)}, u32[]{:S(2)}, u32[]{:S(2)}) collective-permute-start(bf16[4,48,384]{2,1,0:T(8,128)(2,1)S(1)} %first_block.1.blocked), channel_id=1, source_target_pairs={{2,4},{6,8},{10,12},{4,2},{8,6},{12,10},{3,5},{7,9},{11,13},{5,3},... | collective-permute-start | bytes 442376 | tf_op jit(solution)/shard_map/ppermute | solution.py:23
  49.3 1.5 %copy-start.5 = (bf16[1152,768]{1,0:T(8,128)(2,1)S(1)}, bf16[1152,768]{1,0:T(8,128)(2,1)}, u32[]{:S(2)}) copy-start(bf16[1152,768]{1,0:T(8,128)(2,1)} %wt.1) | copy-start | bytes 5308420
  70.2 4.9 %collective-permute-start.8 = (bf16[4,4,16,384]{3,2,1,0:T(8,128)(2,1)S(1)}, bf16[4,4,16,384]{3,2,1,0:T(8,128)(2,1)S(1)}, u32[]{:S(2)}, u32[]{:S(2)}) collective-permute-start(bf16[4,4,16,384]{3,2,1,0:T(8,128)(2,1)S(1)} %constant_dynamic-slice_fusion), channel_id=1, source_target_pairs={{0,16},{16,0},{1,17},{17,1},{2,18},{18,2},{3,19},{19,3},{4,20},{20... | collective-permute-start | bytes 589832 | tf_op jit(solution)/shard_map/ppermute | solution.py:18

commit v14 on v13

--- a/solution.py
+++ b/solution.py
@@ -84,7 +84,7 @@
     return jnp.concatenate(parts, axis=0)
 
 
-def low_product(acc, even, odd, count, height, wide, weights, copies):
+def low_product(acc, even, odd, count, height, wide, weights, copies, following):
     rows = count * (height - 2) * wide
     channels = weights.shape[1]
     lanes = 3 * channels
@@ -93,6 +93,8 @@
         begin, end = n * LANES, min((n + 1) * LANES, lanes)
         while waited * channels < end:
             copies[waited].wait()
+            if waited < len(following):
+                following[waited].start()
             waited += 1
         left = jnp.concatenate(
             [taps(even, odd, 0, count, height, wide, t // 3, t % 3) for t in range(9)], axis=1
@@ -483,16 +485,17 @@
     copies_one[1].start()
     for f in range(frames):
         store(x1e, x1o, f + 2, activate(rows_of(f), gains[0:1, :], 1.0), 6, wide)
-    for copy in [copies_one[2]] + copies_two:
-        copy.start()
-    low_product(acc, x1e, x1o, frames, 6, wide, w1, copies_one)
+    low_product(
+        acc, x1e, x1o, frames, 6, wide, w1, copies_one, [copies_one[2]] + copies_two[:2]
+    )
+    copies_two[2].start()
 
     mask = line_mask(place, wide, 2 * row - 1, 4, height, width)
     for f in range(frames):
         size = 4 * wide
         values = activate(low_sum(acc, f * size, size), gains[1:2, :], mask)
         store(x2e, x2o, f + 2, values, 4, wide)
-    low_product(acc_two, x2e, x2o, frames, 4, wide, w2, copies_two)
+    low_product(acc_two, x2e, x2o, frames, 4, wide, w2, copies_two, [])
     for f in range(frames):
         size = 2 * wide
         values = low_sum(acc_two, f * size, size) + jnp.concatenate(own_rows(f), axis=0)
@@ -572,8 +575,7 @@
         pltpu.make_async_copy(source, target, sems.at[i])
         for i, (source, target) in enumerate(((weight_three, w3), (weight_four, w4)))
     ]
-    for copy in copies:
-        copy.start()
+    copies[0].start()
     channels = blocked.shape[-1]
     half = channels // 2
     size = 6 * wide
@@ -695,8 +697,11 @@
         ((fourth, 2), (finish, 1)),
         (None, (finish, 2)),
     ):
-        if product in ((third, 0), (fourth, 0)):
-            copies[0 if product[0] is third else 1].wait()
+        if product == (third, 0):
+            copies[0].wait()
+            copies[1].start()
+        if product == (fourth, 0):
+            copies[1].wait()
         for n in range(max(2 * channels // LANES, *(last - first for first, last in groups))):
             if product is not None and n < 2 * channels // LANES:
                 product[0](product[1], n)

time: 76.6 us -> 76.6 us (level)
  no operation moved by 1% of the time
where the time goes in v14:
time: 76.6 us; the launch traced here: 76.2 us
  Pallas kernels  37.5 us (49%)
  starting transfers between devices  17.8 us (23%)
  local copies, waits for them, and re-layouts  11.1 us (14%)
  waiting for transfers between devices  8.8 us (11%)
  other arithmetic  0.77 us (1%)
    pallas_call x1, Pallas kernels, second_block(): pl.pallas_call(functools.partial(second_kernel, wide, sizes), out_shape=j...  19.3 us
    ppermute x6, starting transfers between devices, paired(): lax.ppermute(value, axis, pairs + [(high, low) for low, high in pairs])  12.1 us
    pallas_call x1, Pallas kernels, first_block(): pl.pallas_call(functools.partial(first_kernel, wide, sizes), out_shape=ja...  10.7 us
    unnamed x30, local copies, waits for them, and re-layouts  9.83 us
    ppermute x3, starting transfers between devices, swapped(): return lax.ppermute(value, axis, [(0, 1), (1, 0)])  5.68 us
    ppermute x6, waiting for transfers between devices, paired(): lax.ppermute(value, axis, pairs + [(high, low) for low, high in pairs])  4.66 us
    ppermute x3, waiting for transfers between devices, swapped(): return lax.ppermute(value, axis, [(0, 1), (1, 0)])  4.14 us
    pallas_call x2, Pallas kernels, align_weights(): pl.pallas_call(align_kernel, out_shape=jax.ShapeDtypeStruct((4 * half, 18...  2.98 us
  transfers between devices with their start and end apart: 9, of which 5 were waited for; matrix products, arithmetic and copies ran while one was open for 1% of the time, Pallas kernels for 19%

profile of v14, /device:TPU:9, one launch (start us, length us, event | category | flops | bytes accessed | tf_op | source)
XLA Modules:
  0.0 76.2 jit_solution(10340521195127584446)
XLA Ops:
  0.0 0.7 collective-permute-start
  0.7 0.7 pad_add_fusion.place
  1.3 0.5 collective-permute-done.arrived
  1.8 0.6 copy-done.10
  2.5 2.4 %pack.1 = (bf16[8,24,384]{2,1,0:T(8,128)(2,1)}, bf16[12,24,384]{2,1,0:T(8,128)(2,1)}, bf16[20,32,384]{2,1,0:T(8,128)(2,1)}) custom-call(s32[4]{0:T(128)} %pad_add_fusion.place, bf16[2,64,384]{2,1,0:T(8,128)(2,1)} %bitcast.20, bf16[2,64,384]{2,1,0:T(8,128)(2,1)} %copy-done.10, bf16[2,64,384]{2,1,0:T(8,128)(2,1)} %bitcast.21, bf16[2,64,384]{2,1,0:T(8,128)(2,1)} %bitcast.22, ...), custom_call_target="tpu_custom_call" | custom-call | tf_op jit(solution)/shard_map/pack/pallas_call | solution.py:242
  4.9 1.2 %collective-permute-start.1 = (bf16[12,24,384]{2,1,0:T(8,128)(2,1)}, bf16[12,24,384]{2,1,0:T(8,128)(2,1)S(1)}, u32[]{:S(2)}, u32[]{:S(2)}) collective-permute-start(bf16[12,24,384]{2,1,0:T(8,128)(2,1)} %get-tuple-element.21), channel_id=1, source_target_pairs={{0,1},{1,0},{2,3},{3,2},{4,5},{5,4},{6,7},{7,6},{8,9},{9,8},{10,11... | collective-permute-start | bytes 663560 | tf_op jit(solution)/shard_map/ppermute | solution.py:18
  6.1 1.6 %copy-done.3 = bf16[5184,192]{0,1:T(8,128)(2,1)S(1)} copy-done((bf16[5184,192]{0,1:T(8,128)(2,1)S(1)}, bf16[5184,192]{0,1:T(8,128)(2,1)}, u32[]{:S(2)}) %copy-start.3) | copy-done | bytes 1990680
  7.7 1.5 %align_weights.2.later.weight_three = bf16[768,3456]{1,0:T(8,128)(2,1)S(1)} custom-call(bf16[192,5184]{1,0:T(8,128)(2,1)S(1)} %bitcast.14), custom_call_target="tpu_custom_call" | custom-call | tf_op jit(solution)/shard_map/align_weights/pallas_call | solution.py:369
  9.2 2.6 %collective-permute-done.1.theirs = bf16[12,24,384]{2,1,0:T(8,128)(2,1)S(1)} collective-permute-done((bf16[12,24,384]{2,1,0:T(8,128)(2,1)}, bf16[12,24,384]{2,1,0:T(8,128)(2,1)S(1)}, u32[]{:S(2)}, u32[]{:S(2)}) %collective-permute-start.1) | collective-permute-done | bytes 221216 | tf_op jit(solution)/shard_map/ppermute | solution.py:18
  11.8 0.0 copy-start.14
  11.8 1.5 %stack.33 = (bf16[2,8,24,384]{3,2,1,0:T(8,128)(2,1)S(1)}, bf16[14,24,384]{2,1,0:T(8,128)(2,1)}, bf16[14,24,384]{2,1,0:T(8,128)(2,1)}, bf16[20,24,384]{2,1,0:T(8,...) custom-call(s32[4]{0:T(128)S(1)} %copy-done.9, bf16[8,24,384]{2,1,0:T(8,128)(2,1)S(1)} %copy-done.8, ...), custom_call_target="tpu_custom_call" | custom-call | tf_op jit(solution)/shard_map/stack/pallas_call | solution.py:308
  13.4 1.2 %collective-permute-start.2 = (bf16[14,24,384]{2,1,0:T(8,128)(2,1)}, bf16[14,24,384]{2,1,0:T(8,128)(2,1)S(1)}, u32[]{:S(2)}, u32[]{:S(2)}) collective-permute-start(bf16[14,24,384]{2,1,0:T(8,128)(2,1)} %get-tuple-element.24), channel_id=1, source_target_pairs={{0,2},{4,6},{8,10},{12,14},{2,0},{6,4},{10,8},{14,12},{1,3},{5,7},... | collective-permute-start | bytes 774152 | tf_op jit(solution)/shard_map/ppermute | solution.py:23
  14.6 2.1 %collective-permute-start.3 = (bf16[14,24,384]{2,1,0:T(8,128)(2,1)}, bf16[14,24,384]{2,1,0:T(8,128)(2,1)}, u32[]{:S(2)}, u32[]{:S(2)}) collective-permute-start(bf16[14,24,384]{2,1,0:T(8,128)(2,1)} %get-tuple-element.27), channel_id=1, source_target_pairs={{2,4},{6,8},{10,12},{4,2},{8,6},{12,10},{3,5},{7,9},{11,13},{5,3},... | collective-permute-start | bytes 774152 | tf_op jit(solution)/shard_map/ppermute | solution.py:23
  16.7 0.1 stack_tile.7
  16.8 0.1 stack_tile.6
  17.0 1.3 %copy-done.6 = bf16[3456,192]{0,1:T(8,128)(2,1)S(1)} copy-done((bf16[3456,192]{0,1:T(8,128)(2,1)S(1)}, bf16[3456,192]{0,1:T(8,128)(2,1)}, u32[]{:S(2)}) %copy-start.6) | copy-done | bytes 1327128
  18.3 0.5 combine_weights.1.later_one.wu
  18.8 2.4 %copy-done.4 = bf16[5184,192]{0,1:T(8,128)(2,1)S(1)} copy-done((bf16[5184,192]{0,1:T(8,128)(2,1)S(1)}, bf16[5184,192]{0,1:T(8,128)(2,1)}, u32[]{:S(2)}) %copy-start.4) | copy-done | bytes 1990680
  21.2 1.5 %align_weights.3.later_two.weight_four = bf16[768,3456]{1,0:T(8,128)(2,1)S(1)} custom-call(bf16[192,5184]{1,0:T(8,128)(2,1)S(1)} %bitcast.15), custom_call_target="tpu_custom_call" | custom-call | tf_op jit(solution)/shard_map/align_weights/pallas_call | solution.py:369
  22.7 2.4 %copy-done.1 = bf16[768,3456]{1,0:T(8,128)(2,1)} copy-done((bf16[768,3456]{1,0:T(8,128)(2,1)}, bf16[768,3456]{1,0:T(8,128)(2,1)S(1)}, u32[]{:S(2)}) %copy-start.1) | copy-done | bytes 5308440
  25.1 2.3 %collective-permute-start.6 = (bf16[10,24,384]{2,1,0:T(8,128)(2,1)}, bf16[10,24,384]{2,1,0:T(8,128)(2,1)}, u32[]{:S(2)}, u32[]{:S(2)}) collective-permute-start(bf16[10,24,384]{2,1,0:T(8,128)(2,1)} %get-tuple-element.30), channel_id=1, source_target_pairs={{0,2},{4,6},{8,10},{12,14},{2,0},{6,4},{10,8},{14,12},{1,3},{5,7},... | collective-permute-start | bytes 552968 | tf_op jit(solution)/shard_map/ppermute | solution.py:23
  27.4 1.9 %collective-permute-start.7 = (bf16[10,24,384]{2,1,0:T(8,128)(2,1)}, bf16[10,24,384]{2,1,0:T(8,128)(2,1)}, u32[]{:S(2)}, u32[]{:S(2)}) collective-permute-start(bf16[10,24,384]{2,1,0:T(8,128)(2,1)} %get-tuple-element.32), channel_id=1, source_target_pairs={{2,4},{6,8},{10,12},{4,2},{8,6},{12,10},{3,5},{7,9},{11,13},{5,3},... | collective-permute-start | bytes 552968 | tf_op jit(solution)/shard_map/ppermute | solution.py:23
  29.3 10.7 %first_block.1.blocked = bf16[4,48,384]{2,1,0:T(8,128)(2,1)S(1)} custom-call(s32[4]{0:T(128)S(1)} %copy-done.9, bf16[14,24,384]{2,1,0:T(8,128)(2,1)S(1)} %collective-permute-done.2.near, bf16[2,8,24,384]{3,2,1,0:T(8,128)(2,1)S(1)} %get-tuple-element.26.own, bf16[14,24,384]{2,1,0:T(8,128)(2,1)} %collective-permute-done.3.far, ...), custom_call_target="tpu_custom_call" | custom-call | flops 4586471424 | bytes 15925248 | tf_op jit(solution)/shard_map/first_block/pallas_call | solution.py:518
  40.0 2.5 %collective-permute-start.4 = (bf16[4,48,384]{2,1,0:T(8,128)(2,1)S(1)}, bf16[4,48,384]{2,1,0:T(8,128)(2,1)S(1)}, u32[]{:S(2)}, u32[]{:S(2)}) collective-permute-start(bf16[4,48,384]{2,1,0:T(8,128)(2,1)S(1)} %first_block.1.blocked), channel_id=1, source_target_pairs={{0,2},{4,6},{8,10},{12,14},{2,0},{6,4},{10,8},{14,12},{1,3},{5,7},... | collective-permute-start | bytes 442376 | tf_op jit(solution)/shard_map/ppermute | solution.py:23
  42.5 2.1 %collective-permute-start.5 = (bf16[4,48,384]{2,1,0:T(8,128)(2,1)S(1)}, bf16[4,48,384]{2,1,0:T(8,128)(2,1)S(1)}, u32[]{:S(2)}, u32[]{:S(2)}) collective-permute-start(bf16[4,48,384]{2,1,0:T(8,128)(2,1)S(1)} %first_block.1.blocked), channel_id=1, source_target_pairs={{2,4},{6,8},{10,12},{4,2},{8,6},{12,10},{3,5},{7,9},{11,13},{5,3},... | collective-permute-start | bytes 442376 | tf_op jit(solution)/shard_map/ppermute | solution.py:23
  44.7 0.4 collective-permute-done.4.near
  45.1 4.2 %collective-permute-done.5.far = bf16[4,48,384]{2,1,0:T(8,128)(2,1)S(1)} collective-permute-done((bf16[4,48,384]{2,1,0:T(8,128)(2,1)S(1)}, bf16[4,48,384]{2,1,0:T(8,128)(2,1)S(1)}, u32[]{:S(2)}, u32[]{:S(2)}) %collective-permute-start.5) | collective-permute-done | bytes 147488 | tf_op jit(solution)/shard_map/ppermute | solution.py:23
  49.3 1.5 %copy-done.5 = bf16[1152,768]{1,0:T(8,128)(2,1)S(1)} copy-done((bf16[1152,768]{1,0:T(8,128)(2,1)S(1)}, bf16[1152,768]{1,0:T(8,128)(2,1)}, u32[]{:S(2)}) %copy-start.5) | copy-done | bytes 1769496
  50.8 19.3 %second_block.1 = bf16[8,4,16,384]{3,2,1,0:T(8,128)(2,1)S(1)} custom-call(s32[4]{0:T(128)S(1)} %copy-done.9, bf16[4,48,384]{2,1,0:T(8,128)(2,1)S(1)} %collective-permute-done.4.near, bf16[4,48,384]{2,1,0:T(8,128)(2,1)S(1)} %first_block.1.blocked, bf16[4,48,384]{2,1,0:T(8,128)(2,1)S(1)} %collective-permute-done.5.far, ...), custom_call_target="tpu_custom_call" | custom-call | tf_op jit(solution)/shard_map/second_block/pallas_call | solution.py:719
  70.2 3.8 %collective-permute-start.8 = (bf16[4,4,16,384]{3,2,1,0:T(8,128)(2,1)S(1)}, bf16[4,4,16,384]{3,2,1,0:T(8,128)(2,1)S(1)}, u32[]{:S(2)}, u32[]{:S(2)}) collective-permute-start(bf16[4,4,16,384]{3,2,1,0:T(8,128)(2,1)S(1)} %constant_dynamic-slice_fusion), channel_id=1, source_target_pairs={{0,16},{16,0},{1,17},{17,1},{2,18},{18,2},{3,19},{19,3},{4,20},{20... | collective-permute-start | bytes 589832 | tf_op jit(solution)/shard_map/ppermute | solution.py:18
  74.0 1.1 %collective-permute-done.8 = bf16[4,4,16,384]{3,2,1,0:T(8,128)(2,1)S(1)} collective-permute-done((bf16[4,4,16,384]{3,2,1,0:T(8,128)(2,1)S(1)}, bf16[4,4,16,384]{3,2,1,0:T(8,128)(2,1)S(1)}, u32[]{:S(2)}, u32[]{:S(2)}) %collective-permute-start.8) | collective-permute-done | bytes 196640 | tf_op jit(solution)/shard_map/ppermute | solution.py:18
  75.1 1.1 %reshape.17 = bf16[4,4,64,192]{3,2,1,0:T(8,128)(2,1)} reshape(bf16[4,4,32,384]{3,2,1,0:T(8,128)(2,1)S(1)} %pad_maximum_fusion) | data formatting | bytes 786432 | tf_op jit(solution)/shard_map/reshape | solution.py:834
  (35 shorter events, 0.2 us)
Async XLA Ops:
  0.0 1.8 %collective-permute-start = (bf16[2,64,384]{2,1,0:T(8,128)(2,1)}, bf16[2,64,384]{2,1,0:T(8,128)(2,1)S(1)}, u32[]{:S(2)}, u32[]{:S(2)}) collective-permute-start(bf16[2,64,384]{2,1,0:T(8,128)(2,1)} %bitcast.19), channel_id=1, source_target_pairs={{0,16},{16,0},{1,17},{17,1},{2,18},{18,2},{3,19},{19,3},{4,20},{20... | collective-permute-start | bytes 294920 | tf_op jit(solution)/shard_map/ppermute | solution.py:18
  1.8 0.6 copy-start.10
  4.9 6.9 %collective-permute-start.1 = (bf16[12,24,384]{2,1,0:T(8,128)(2,1)}, bf16[12,24,384]{2,1,0:T(8,128)(2,1)S(1)}, u32[]{:S(2)}, u32[]{:S(2)}) collective-permute-start(bf16[12,24,384]{2,1,0:T(8,128)(2,1)} %get-tuple-element.21), channel_id=1, source_target_pairs={{0,1},{1,0},{2,3},{3,2},{4,5},{5,4},{6,7},{7,6},{8,9},{9,8},{10,11... | collective-permute-start | bytes 663560 | tf_op jit(solution)/shard_map/ppermute | solution.py:18
  6.1 1.6 %copy-start.3 = (bf16[5184,192]{0,1:T(8,128)(2,1)S(1)}, bf16[5184,192]{0,1:T(8,128)(2,1)}, u32[]{:S(2)}) copy-start(bf16[5184,192]{0,1:T(8,128)(2,1)} %param.30) | copy-start | bytes 5971972
  7.7 4.1 %copy-start.7 = (bf16[20,32,384]{2,1,0:T(8,128)(2,1)S(1)}, bf16[20,32,384]{2,1,0:T(8,128)(2,1)}, u32[]{:S(2)}) copy-start(bf16[20,32,384]{2,1,0:T(8,128)(2,1)} %get-tuple-element.22.tiles) | copy-start | bytes 1474564
  7.7 4.1 %copy-start.8 = (bf16[8,24,384]{2,1,0:T(8,128)(2,1)S(1)}, bf16[8,24,384]{2,1,0:T(8,128)(2,1)}, u32[]{:S(2)}) copy-start(bf16[8,24,384]{2,1,0:T(8,128)(2,1)} %get-tuple-element.20.mine) | copy-start | bytes 442372
  7.7 4.1 %copy-start.9 = (s32[4]{0:T(128)S(1)}, s32[4]{0:T(128)}, u32[]{:S(2)}) copy-start(s32[4]{0:T(128)} %pad_add_fusion.place) | copy-start | bytes 52
  9.2 4.2 %copy-start = (bf16[768,3456]{1,0:T(8,128)(2,1)}, bf16[768,3456]{1,0:T(8,128)(2,1)S(1)}, u32[]{:S(2)}) copy-start(bf16[768,3456]{1,0:T(8,128)(2,1)S(1)} %align_weights.2.later.weight_three) | copy-start | bytes 15925252
  11.8 4.9 %copy-start.13 = (f32[192]{0:T(256)S(1)}, f32[192]{0:T(256)}, u32[]{:S(2)}) copy-start(f32[192]{0:T(256)} %param.25) | copy-start | bytes 2308
  11.8 5.0 %copy-start.14 = (f32[192]{0:T(256)S(1)}, f32[192]{0:T(256)}, u32[]{:S(2)}) copy-start(f32[192]{0:T(256)} %param.24) | copy-start | bytes 2308
  11.8 5.1 %copy-start.11 = (f32[384]{0:T(512)S(1)}, f32[384]{0:T(512)}, u32[]{:S(2)}) copy-start(f32[384]{0:T(512)} %param.23) | copy-start | bytes 4612
  11.8 5.1 %copy-start.12 = (f32[384]{0:T(512)S(1)}, f32[384]{0:T(512)}, u32[]{:S(2)}) copy-start(f32[384]{0:T(512)} %param.22) | copy-start | bytes 4612
  13.4 15.9 %collective-permute-start.2 = (bf16[14,24,384]{2,1,0:T(8,128)(2,1)}, bf16[14,24,384]{2,1,0:T(8,128)(2,1)S(1)}, u32[]{:S(2)}, u32[]{:S(2)}) collective-permute-start(bf16[14,24,384]{2,1,0:T(8,128)(2,1)} %get-tuple-element.24), channel_id=1, source_target_pairs={{0,2},{4,6},{8,10},{12,14},{2,0},{6,4},{10,8},{14,12},{1,3},{5,7},... | collective-permute-start | bytes 774152 | tf_op jit(solution)/shard_map/ppermute | solution.py:23
  14.6 14.7 %collective-permute-start.3 = (bf16[14,24,384]{2,1,0:T(8,128)(2,1)}, bf16[14,24,384]{2,1,0:T(8,128)(2,1)}, u32[]{:S(2)}, u32[]{:S(2)}) collective-permute-start(bf16[14,24,384]{2,1,0:T(8,128)(2,1)} %get-tuple-element.27), channel_id=1, source_target_pairs={{2,4},{6,8},{10,12},{4,2},{8,6},{12,10},{3,5},{7,9},{11,13},{5,3},... | collective-permute-start | bytes 774152 | tf_op jit(solution)/shard_map/ppermute | solution.py:23
  16.9 1.3 %copy-start.6 = (bf16[3456,192]{0,1:T(8,128)(2,1)S(1)}, bf16[3456,192]{0,1:T(8,128)(2,1)}, u32[]{:S(2)}) copy-start(bf16[3456,192]{0,1:T(8,128)(2,1)} %param.29) | copy-start | bytes 3981316
  18.7 10.6 %copy-start.2 = (bf16[2,768,768]{2,1,0:T(8,128)(2,1)}, bf16[2,768,768]{2,1,0:T(8,128)(2,1)S(1)}, u32[]{:S(2)}) copy-start(bf16[2,768,768]{2,1,0:T(8,128)(2,1)S(1)} %combine_weights.1.later_one.wu) | copy-start | bytes 7077892
  18.7 2.4 %copy-start.4 = (bf16[5184,192]{0,1:T(8,128)(2,1)S(1)}, bf16[5184,192]{0,1:T(8,128)(2,1)}, u32[]{:S(2)}) copy-start(bf16[5184,192]{0,1:T(8,128)(2,1)} %param.31) | copy-start | bytes 5971972
  22.7 2.4 %copy-start.1 = (bf16[768,3456]{1,0:T(8,128)(2,1)}, bf16[768,3456]{1,0:T(8,128)(2,1)S(1)}, u32[]{:S(2)}) copy-start(bf16[768,3456]{1,0:T(8,128)(2,1)S(1)} %align_weights.3.later_two.weight_four) | copy-start | bytes 15925252
  25.1 19.6 %collective-permute-start.6 = (bf16[10,24,384]{2,1,0:T(8,128)(2,1)}, bf16[10,24,384]{2,1,0:T(8,128)(2,1)}, u32[]{:S(2)}, u32[]{:S(2)}) collective-permute-start(bf16[10,24,384]{2,1,0:T(8,128)(2,1)} %get-tuple-element.30), channel_id=1, source_target_pairs={{0,2},{4,6},{8,10},{12,14},{2,0},{6,4},{10,8},{14,12},{1,3},{5,7},... | collective-permute-start | bytes 552968 | tf_op jit(solution)/shard_map/ppermute | solution.py:23
  27.4 17.3 %collective-permute-start.7 = (bf16[10,24,384]{2,1,0:T(8,128)(2,1)}, bf16[10,24,384]{2,1,0:T(8,128)(2,1)}, u32[]{:S(2)}, u32[]{:S(2)}) collective-permute-start(bf16[10,24,384]{2,1,0:T(8,128)(2,1)} %get-tuple-element.32), channel_id=1, source_target_pairs={{2,4},{6,8},{10,12},{4,2},{8,6},{12,10},{3,5},{7,9},{11,13},{5,3},... | collective-permute-start | bytes 552968 | tf_op jit(solution)/shard_map/ppermute | solution.py:23
  40.0 5.1 %collective-permute-start.4 = (bf16[4,48,384]{2,1,0:T(8,128)(2,1)S(1)}, bf16[4,48,384]{2,1,0:T(8,128)(2,1)S(1)}, u32[]{:S(2)}, u32[]{:S(2)}) collective-permute-start(bf16[4,48,384]{2,1,0:T(8,128)(2,1)S(1)} %first_block.1.blocked), channel_id=1, source_target_pairs={{0,2},{4,6},{8,10},{12,14},{2,0},{6,4},{10,8},{14,12},{1,3},{5,7},... | collective-permute-start | bytes 442376 | tf_op jit(solution)/shard_map/ppermute | solution.py:23
  42.5 6.8 %collective-permute-start.5 = (bf16[4,48,384]{2,1,0:T(8,128)(2,1)S(1)}, bf16[4,48,384]{2,1,0:T(8,128)(2,1)S(1)}, u32[]{:S(2)}, u32[]{:S(2)}) collective-permute-start(bf16[4,48,384]{2,1,0:T(8,128)(2,1)S(1)} %first_block.1.blocked), channel_id=1, source_target_pairs={{2,4},{6,8},{10,12},{4,2},{8,6},{12,10},{3,5},{7,9},{11,13},{5,3},... | collective-permute-start | bytes 442376 | tf_op jit(solution)/shard_map/ppermute | solution.py:23
  49.3 1.5 %copy-start.5 = (bf16[1152,768]{1,0:T(8,128)(2,1)S(1)}, bf16[1152,768]{1,0:T(8,128)(2,1)}, u32[]{:S(2)}) copy-start(bf16[1152,768]{1,0:T(8,128)(2,1)} %wt.1) | copy-start | bytes 5308420
  70.2 4.9 %collective-permute-start.8 = (bf16[4,4,16,384]{3,2,1,0:T(8,128)(2,1)S(1)}, bf16[4,4,16,384]{3,2,1,0:T(8,128)(2,1)S(1)}, u32[]{:S(2)}, u32[]{:S(2)}) collective-permute-start(bf16[4,4,16,384]{3,2,1,0:T(8,128)(2,1)S(1)} %constant_dynamic-slice_fusion), channel_id=1, source_target_pairs={{0,16},{16,0},{1,17},{17,1},{2,18},{18,2},{3,19},{19,3},{4,20},{20... | collective-permute-start | bytes 589832 | tf_op jit(solution)/shard_map/ppermute | solution.py:18

commit v15 on v14

--- a/solution.py
+++ b/solution.py
@@ -168,7 +168,7 @@
     part,
     place,
     latent,
-    arrived,
+    arrived_ref,
     one,
     two,
     time,
@@ -180,7 +180,11 @@
     spread,
     low,
     high,
+    arrived,
+    sem,
 ):
+    copy = pltpu.make_async_copy(arrived_ref, arrived, sem)
+    copy.start()
     section, col = place[0], place[1]
     width, channels = latent.shape[1:]
     half = three.shape[-1]
@@ -190,16 +194,6 @@
         spread[slot] = pltpu.roll(
             jnp.concatenate([values.astype(F32), empty], axis=0), HALO, 0
         )
-
-    for i in range(2):
-        put(2 * section + i, latent[i])
-        put(2 * (1 - section) + i, arrived[i])
-        put(4 + i, one[i])
-        put(6 + i, two[i])
-    for slot in range(8):
-        for ref, which in ((mine, col), (theirs, 1 - col)):
-            begin = pl.multiple_of(which * tile + section * part, 8)
-            ref[slot] = spread[slot, pl.ds(begin, wide), :].astype(BF16)
 
     lines = [time[f, y].astype(F32) for f in range(2) for y in range(2)]
     for ref in (three, four):
@@ -233,6 +227,17 @@
         group = (blocks + [gap] * count)[i * count : (i + 1) * count]
         theirs[8 + i] = jnp.concatenate(group, axis=0).astype(BF16)
 
+    copy.wait()
+    for i in range(2):
+        put(2 * section + i, latent[i])
+        put(2 * (1 - section) + i, arrived[i])
+        put(4 + i, one[i])
+        put(6 + i, two[i])
+    for slot in range(8):
+        for ref, which in ((mine, col), (theirs, 1 - col)):
+            begin = pl.multiple_of(which * tile + section * part, 8)
+            ref[slot] = spread[slot, pl.ds(begin, wide), :].astype(BF16)
+
 
 def pack(place, latent, arrived, one, two, time, three, four, wide, tile, part):
     width, channels = latent.shape[1:]
@@ -246,12 +251,19 @@
             jax.ShapeDtypeStruct((8 + extra, wide, channels), BF16),
             jax.ShapeDtypeStruct((lines, tile, channels), BF16),
         ],
-        in_specs=[pl.BlockSpec(memory_space=pltpu.SMEM)] + [vmem] * 7,
+        in_specs=[
+            pl.BlockSpec(memory_space=pltpu.SMEM),
+            vmem,
+            pl.BlockSpec(memory_space=pl.ANY),
+        ]
+        + [vmem] * 5,
         out_specs=[vmem] * 3,
         scratch_shapes=[
             pltpu.VMEM((8, width + 16, channels), F32),
             pltpu.VMEM((three.shape[2], 128), F32),
             pltpu.VMEM((three.shape[2], 128), F32),
+            pltpu.VMEM(arrived.shape, BF16),
+            pltpu.SemaphoreType.DMA,
         ],
         compiler_params=pltpu.CompilerParams(vmem_limit_bytes=60 * 1024 * 1024),
         name="pack",
@@ -434,8 +446,7 @@
     gains,
     weight_one,
     weight_two,
-    later_one,
-    later_two,
+    later,
     out_ref,
     w1,
     w2,
@@ -452,7 +463,7 @@
     height, width = sizes
     col, row = place[1], place[3]
     units = frames + 2
-    del later_one, later_two
+    del later
 
     copies_one = weight_copies(weight_one, w1, sems, 0)
     copies_two = weight_copies(weight_two, w2, sems, 3)
@@ -521,7 +532,7 @@
         in_specs=[pl.BlockSpec(memory_space=pltpu.SMEM)]
         + [vmem] * 4
         + [pl.BlockSpec(memory_space=pltpu.HBM)] * 2
-        + [anywhere] * 2,
+        + [anywhere],
         out_specs=vmem,
         scratch_shapes=[
             pltpu.VMEM((9, channels, slots * LANES), BF16),
@@ -539,27 +550,27 @@
             transcendentals=0,
         ),
         name="first_block",
-    )(place, *pieces, gains, weight_one, weight_two, *later)
+    )(place, *pieces, gains, weight_one, weight_two, later)
 
 
 def second_kernel(
     wide,
     sizes,
     place,
-    near,
+    near_ref,
     blocked,
-    far,
+    far_ref,
     tile_near,
     windows,
     tile_far,
     gains,
     wt,
     wu,
-    weight_three,
-    weight_four,
-    out_ref,
     w3,
     w4,
+    out_ref,
+    near,
+    far,
     sems,
     acc,
     mixed,
@@ -573,9 +584,10 @@
     planes_four = [buffers[15 + 2 * g : 17 + 2 * g] for g in range(3)]
     copies = [
         pltpu.make_async_copy(source, target, sems.at[i])
-        for i, (source, target) in enumerate(((weight_three, w3), (weight_four, w4)))
+        for i, (source, target) in enumerate(((near_ref, near), (far_ref, far)))
     ]
-    copies[0].start()
+    for copy in copies:
+        copy.start()
     channels = blocked.shape[-1]
     half = channels // 2
     size = 6 * wide
@@ -598,6 +610,12 @@
         return jnp.concatenate(parts, axis=0)
 
     for f in range(2):
+        store(*planes_three[0], f, cached(4, 4, 4, 2, f), 8, wide)
+        store(*planes_four[0], f, cached(8, 12, 4, 1, f), 6, wide)
+    for copy in copies:
+        copy.wait()
+
+    for f in range(2):
         mixed[f * size : (f + 1) * size, :] = cached(0, 0, 2, 2, f).astype(BF16)
     for f in range(frames):
         first, last = chosen(is_even, far, near, f), chosen(is_even, near, far, f)
@@ -628,9 +646,6 @@
     lax.fori_loop(0, frames, double, 0)
 
 
-    for f in range(2):
-        store(*planes_three[0], f, cached(4, 4, 4, 2, f), 8, wide)
-        store(*planes_four[0], f, cached(8, 12, 4, 1, f), 6, wide)
     gain3, gain4 = gains[2:3, :], gains[3:4, :]
     mask_three = line_mask(place, wide, 4 * row - 2, 8, 2 * height, width)
     mask_four = mask_three[wide : 7 * wide]
@@ -697,11 +712,6 @@
         ((fourth, 2), (finish, 1)),
         (None, (finish, 2)),
     ):
-        if product == (third, 0):
-            copies[0].wait()
-            copies[1].start()
-        if product == (fourth, 0):
-            copies[1].wait()
         for n in range(max(2 * channels // LANES, *(last - first for first, last in groups))):
             if product is not None and n < 2 * channels // LANES:
                 product[0](product[1], n)
@@ -716,16 +726,15 @@
     sizes_of = [last - first for first, last in groups]
     slots = [last - first for first, last in (group_slots(g, groups) for g in range(3))]
     vmem = pl.BlockSpec(memory_space=pltpu.VMEM)
+    anywhere = pl.BlockSpec(memory_space=pl.ANY)
     return pl.pallas_call(
         functools.partial(second_kernel, wide, sizes),
         out_shape=jax.ShapeDtypeStruct((count, 4, wide - 2 * HALO, channels), BF16),
-        in_specs=[pl.BlockSpec(memory_space=pltpu.SMEM)]
-        + [vmem] * 9
-        + [pl.BlockSpec(memory_space=pl.ANY)] * 2,
+        in_specs=[pl.BlockSpec(memory_space=pltpu.SMEM), anywhere, vmem, anywhere] + [vmem] * 8,
         out_specs=vmem,
         scratch_shapes=[
-            pltpu.VMEM(weights[2].shape, BF16),
-            pltpu.VMEM(weights[3].shape, BF16),
+            pltpu.VMEM(pieces[0].shape, BF16),
+            pltpu.VMEM(pieces[2].shape, BF16),
             pltpu.SemaphoreType.DMA((2,)),
             pltpu.VMEM((3, frames * 6 * wide, LANES), F32),
             pltpu.VMEM(((frames + 2) * 6 * wide, channels), BF16),
@@ -737,7 +746,7 @@
             *(ref for n in slots for ref in planes(n, 8, wide, channels)),
             *(ref for n in slots for ref in planes(n, 6, wide, channels)),
         ],
-        compiler_params=pltpu.CompilerParams(vmem_limit_bytes=50 * 1024 * 1024),
+        compiler_params=pltpu.CompilerParams(vmem_limit_bytes=34 * 1024 * 1024),
         name="second_block",
     )(place, *pieces, *tiles, gains, *weights)
 
@@ -796,23 +805,22 @@
     near = paired(near, "rows", 0)
     tile_far = paired(tile_far, "rows", 1)
     tile_near = paired(tile_near, "rows", 0)
-    weight_upsample, weight_four, own = lax.optimization_barrier(
-        (weight_upsample, weight_four, own)
-    )
+    weight_upsample, own = lax.optimization_barrier((weight_upsample, own))
     weight_upsample = combine_weights(weight_upsample)
-    weight_four = align_weights(weight_four)
     blocked = first_block(
         place,
         [near, own, far],
         gains,
         weight_one.reshape(9, 3, channels, channels),
         weight_two.reshape(9, 3, channels, channels),
-        (weight_upsample, weight_four),
+        weight_upsample,
         sizes,
     )
     far = paired(blocked, "rows", 1)
     near = paired(blocked, "rows", 0)
     blocks = [near, blocked, far]
+    weight_four, _ = lax.optimization_barrier((weight_four, blocked))
+    weight_four = align_weights(weight_four)
     tiles = [tile_near, windows, tile_far]
     frames = second_block(
         place,

time: 76.6 us -> 76.6 us (level)
  starting transfers between devices: 17.8 us -> 23 us
  local copies, waits for them, and re-layouts: 11.1 us -> 8 us
  waiting for transfers between devices: 8.8 us -> 7.61 us
  Pallas kernels: 37.5 us -> 36.6 us
    ppermute x3, starting transfers between devices: 5.68 us -> 11.2 us  [swapped(): return lax.ppermute(value, axis, [(0, 1), (1, 0)])]
    unnamed x30 -> x32, local copies, waits for them, and re-layouts: 9.83 us -> 6.68 us
    pallas_call x1, Pallas kernels: 19.3 us -> 17.9 us  [second_block(): pl.pallas_call(functools.partial(second_kernel, wide, sizes), out_shape=j...]
    ppermute x6, waiting for transfers between devices: 4.66 us -> 3.4 us  [paired(): lax.ppermute(value, axis, pairs + [(high, low) for low, high in pairs])]
where the time goes in v15:
time: 76.6 us; the launch traced here: 76.2 us
  Pallas kernels  36.6 us (48%)
  starting transfers between devices  23 us (30%)
  local copies, waits for them, and re-layouts  8 us (10%)
  waiting for transfers between devices  7.61 us (10%)
    pallas_call x1, Pallas kernels, second_block(): pl.pallas_call(functools.partial(second_kernel, wide, sizes), out_shape=j...  17.9 us
    ppermute x6, starting transfers between devices, paired(): lax.ppermute(value, axis, pairs + [(high, low) for low, high in pairs])  11.8 us
    ppermute x3, starting transfers between devices, swapped(): return lax.ppermute(value, axis, [(0, 1), (1, 0)])  11.2 us
    pallas_call x1, Pallas kernels, first_block(): pl.pallas_call(functools.partial(first_kernel, wide, sizes), out_shape=ja...  10.7 us
    unnamed x32, local copies, waits for them, and re-layouts  6.68 us
    ppermute x3, waiting for transfers between devices, swapped(): return lax.ppermute(value, axis, [(0, 1), (1, 0)])  4.22 us
    ppermute x6, waiting for transfers between devices, paired(): lax.ppermute(value, axis, pairs + [(high, low) for low, high in pairs])  3.4 us
    pallas_call x1, Pallas kernels, pack(): pl.pallas_call(functools.partial(pack_kernel, wide, tile, part), out_shap...  3.14 us
  transfers between devices with their start and end apart: 9, of which 5 were waited for; matrix products, arithmetic and copies ran while one was open for 1% of the time, Pallas kernels for 19%

profile of v15, /device:TPU:9, one launch (start us, length us, event | category | flops | bytes accessed | tf_op | source)
XLA Modules:
  0.0 76.2 jit_solution(15883662143284032781)
XLA Ops:
  0.0 0.7 collective-permute-start
  0.7 0.6 pad_add_fusion.place
  1.3 0.6 collective-permute-done.arrived_ref
  1.8 0.6 copy-done.11
  2.5 3.1 %pack.1 = (bf16[8,24,384]{2,1,0:T(8,128)(2,1)}, bf16[12,24,384]{2,1,0:T(8,128)(2,1)}, bf16[20,32,384]{2,1,0:T(8,128)(2,1)}) custom-call(s32[4]{0:T(128)} %pad_add_fusion.place, bf16[2,64,384]{2,1,0:T(8,128)(2,1)} %bitcast.20, bf16[2,64,384]{2,1,0:T(8,128)(2,1)} %copy-done.11, bf16[2,64,384]{2,1,0:T(8,128)(2,1)} %bitcast.21, bf16[2,64,384]{2,1,0:T(8,128)(2,1)} %bitcast.22, ...), custom_call_target="tpu_custom_call" | custom-call | tf_op jit(solution)/shard_map/pack/pallas_call | solution.py:247
  5.6 1.3 %collective-permute-start.1 = (bf16[12,24,384]{2,1,0:T(8,128)(2,1)}, bf16[12,24,384]{2,1,0:T(8,128)(2,1)S(1)}, u32[]{:S(2)}, u32[]{:S(2)}) collective-permute-start(bf16[12,24,384]{2,1,0:T(8,128)(2,1)} %get-tuple-element.21), channel_id=1, source_target_pairs={{0,1},{1,0},{2,3},{3,2},{4,5},{5,4},{6,7},{7,6},{8,9},{9,8},{10,11... | collective-permute-start | bytes 663560 | tf_op jit(solution)/shard_map/ppermute | solution.py:18
  6.9 1.6 %copy-done.2 = bf16[5184,192]{0,1:T(8,128)(2,1)S(1)} copy-done((bf16[5184,192]{0,1:T(8,128)(2,1)S(1)}, bf16[5184,192]{0,1:T(8,128)(2,1)}, u32[]{:S(2)}) %copy-start.2) | copy-done | bytes 1990680
  8.5 1.5 %align_weights.2.later.w3 = bf16[768,3456]{1,0:T(8,128)(2,1)S(1)} custom-call(bf16[192,5184]{1,0:T(8,128)(2,1)S(1)} %bitcast.14), custom_call_target="tpu_custom_call" | custom-call | tf_op jit(solution)/shard_map/align_weights/pallas_call | solution.py:381
  10.0 2.6 %collective-permute-done.1.theirs = bf16[12,24,384]{2,1,0:T(8,128)(2,1)S(1)} collective-permute-done((bf16[12,24,384]{2,1,0:T(8,128)(2,1)}, bf16[12,24,384]{2,1,0:T(8,128)(2,1)S(1)}, u32[]{:S(2)}, u32[]{:S(2)}) %collective-permute-start.1) | collective-permute-done | bytes 221216 | tf_op jit(solution)/shard_map/ppermute | solution.py:18
  12.6 0.0 copy-start.14
  12.6 1.5 %stack.33 = (bf16[2,8,24,384]{3,2,1,0:T(8,128)(2,1)S(1)}, bf16[14,24,384]{2,1,0:T(8,128)(2,1)}, bf16[14,24,384]{2,1,0:T(8,128)(2,1)}, bf16[20,24,384]{2,1,0:T(8,...) custom-call(s32[4]{0:T(128)S(1)} %copy-done.10, bf16[8,24,384]{2,1,0:T(8,128)(2,1)S(1)} %copy-done.7, ...), custom_call_target="tpu_custom_call" | custom-call | tf_op jit(solution)/shard_map/stack/pallas_call | solution.py:320
  14.1 1.2 %collective-permute-start.2 = (bf16[14,24,384]{2,1,0:T(8,128)(2,1)}, bf16[14,24,384]{2,1,0:T(8,128)(2,1)S(1)}, u32[]{:S(2)}, u32[]{:S(2)}) collective-permute-start(bf16[14,24,384]{2,1,0:T(8,128)(2,1)} %get-tuple-element.24), channel_id=1, source_target_pairs={{0,2},{4,6},{8,10},{12,14},{2,0},{6,4},{10,8},{14,12},{1,3},{5,7},... | collective-permute-start | bytes 774152 | tf_op jit(solution)/shard_map/ppermute | solution.py:23
  15.4 2.1 %collective-permute-start.3 = (bf16[14,24,384]{2,1,0:T(8,128)(2,1)}, bf16[14,24,384]{2,1,0:T(8,128)(2,1)}, u32[]{:S(2)}, u32[]{:S(2)}) collective-permute-start(bf16[14,24,384]{2,1,0:T(8,128)(2,1)} %get-tuple-element.27), channel_id=1, source_target_pairs={{2,4},{6,8},{10,12},{4,2},{8,6},{12,10},{3,5},{7,9},{11,13},{5,3},... | collective-permute-start | bytes 774152 | tf_op jit(solution)/shard_map/ppermute | solution.py:23
  17.5 0.1 stack_tile.6
  17.6 0.1 stack_tile.7
  17.7 1.3 %copy-done.5 = bf16[3456,192]{0,1:T(8,128)(2,1)S(1)} copy-done((bf16[3456,192]{0,1:T(8,128)(2,1)S(1)}, bf16[3456,192]{0,1:T(8,128)(2,1)}, u32[]{:S(2)}) %copy-start.5) | copy-done | bytes 1327128
  19.0 0.5 combine_weights.1.later.wu
  19.5 2.4 %collective-permute-start.6 = (bf16[10,24,384]{2,1,0:T(8,128)(2,1)}, bf16[10,24,384]{2,1,0:T(8,128)(2,1)}, u32[]{:S(2)}, u32[]{:S(2)}) collective-permute-start(bf16[10,24,384]{2,1,0:T(8,128)(2,1)} %get-tuple-element.29), channel_id=1, source_target_pairs={{0,2},{4,6},{8,10},{12,14},{2,0},{6,4},{10,8},{14,12},{1,3},{5,7},... | collective-permute-start | bytes 552968 | tf_op jit(solution)/shard_map/ppermute | solution.py:23
  21.8 1.9 %collective-permute-start.7 = (bf16[10,24,384]{2,1,0:T(8,128)(2,1)}, bf16[10,24,384]{2,1,0:T(8,128)(2,1)}, u32[]{:S(2)}, u32[]{:S(2)}) collective-permute-start(bf16[10,24,384]{2,1,0:T(8,128)(2,1)} %get-tuple-element.31), channel_id=1, source_target_pairs={{2,4},{6,8},{10,12},{4,2},{8,6},{12,10},{3,5},{7,9},{11,13},{5,3},... | collective-permute-start | bytes 552968 | tf_op jit(solution)/shard_map/ppermute | solution.py:23
  23.8 1.6 %collective-permute-done.2.near = bf16[14,24,384]{2,1,0:T(8,128)(2,1)S(1)} collective-permute-done((bf16[14,24,384]{2,1,0:T(8,128)(2,1)}, bf16[14,24,384]{2,1,0:T(8,128)(2,1)S(1)}, u32[]{:S(2)}, u32[]{:S(2)}) %collective-permute-start.2) | collective-permute-done | bytes 258080 | tf_op jit(solution)/shard_map/ppermute | solution.py:23
  25.4 10.7 %first_block.1.blocked = bf16[4,48,384]{2,1,0:T(8,128)(2,1)S(1)} custom-call(s32[4]{0:T(128)S(1)} %copy-done.10, bf16[14,24,384]{2,1,0:T(8,128)(2,1)S(1)} %collective-permute-done.2.near, bf16[2,8,24,384]{3,2,1,0:T(8,128)(2,1)S(1)} %get-tuple-element.26.own, bf16[14,24,384]{2,1,0:T(8,128)(2,1)} %collective-permute-done.3.far, ...), custom_call_target="tpu_custom_call" | custom-call | flops 4586471424 | bytes 15925248 | tf_op jit(solution)/shard_map/first_block/pallas_call | solution.py:529
  36.1 2.3 %collective-permute-start.4 = (bf16[4,48,384]{2,1,0:T(8,128)(2,1)S(1)}, bf16[4,48,384]{2,1,0:T(8,128)(2,1)S(1)}, u32[]{:S(2)}, u32[]{:S(2)}) collective-permute-start(bf16[4,48,384]{2,1,0:T(8,128)(2,1)S(1)} %first_block.1.blocked), channel_id=1, source_target_pairs={{0,2},{4,6},{8,10},{12,14},{2,0},{6,4},{10,8},{14,12},{1,3},{5,7},... | collective-permute-start | bytes 442376 | tf_op jit(solution)/shard_map/ppermute | solution.py:23
  38.4 1.9 %collective-permute-start.5 = (bf16[4,48,384]{2,1,0:T(8,128)(2,1)S(1)}, bf16[4,48,384]{2,1,0:T(8,128)(2,1)S(1)}, u32[]{:S(2)}, u32[]{:S(2)}) collective-permute-start(bf16[4,48,384]{2,1,0:T(8,128)(2,1)S(1)} %first_block.1.blocked), channel_id=1, source_target_pairs={{2,4},{6,8},{10,12},{4,2},{8,6},{12,10},{3,5},{7,9},{11,13},{5,3},... | collective-permute-start | bytes 442376 | tf_op jit(solution)/shard_map/ppermute | solution.py:23
  40.3 1.6 %copy-done.3 = bf16[5184,192]{0,1:T(8,128)(2,1)S(1)} copy-done((bf16[5184,192]{0,1:T(8,128)(2,1)S(1)}, bf16[5184,192]{0,1:T(8,128)(2,1)}, u32[]{:S(2)}) %copy-start.3) | copy-done | bytes 1990680
  41.9 1.5 %align_weights.3.w4 = bf16[768,3456]{1,0:T(8,128)(2,1)S(1)} custom-call(bf16[192,5184]{1,0:T(8,128)(2,1)S(1)} %bitcast.15), custom_call_target="tpu_custom_call" | custom-call | tf_op jit(solution)/shard_map/align_weights/pallas_call | solution.py:381
  43.4 1.8 %collective-permute-done.5.far_ref = bf16[4,48,384]{2,1,0:T(8,128)(2,1)S(1)} collective-permute-done((bf16[4,48,384]{2,1,0:T(8,128)(2,1)S(1)}, bf16[4,48,384]{2,1,0:T(8,128)(2,1)S(1)}, u32[]{:S(2)}, u32[]{:S(2)}) %collective-permute-start.5) | collective-permute-done | bytes 147488 | tf_op jit(solution)/shard_map/ppermute | solution.py:23
  45.2 0.7 copy-done.8
  45.8 0.9 %copy-done.9 = bf16[4,48,384]{2,1,0:T(8,128)(2,1)S(1)} copy-done((bf16[4,48,384]{2,1,0:T(8,128)(2,1)S(1)}, bf16[4,48,384]{2,1,0:T(8,128)(2,1)}, u32[]{:S(2)}) %copy-start.9) | copy-done | bytes 147480
  46.7 17.9 %second_block.1 = bf16[8,4,16,384]{3,2,1,0:T(8,128)(2,1)S(1)} custom-call(s32[4]{0:T(128)S(1)} %copy-done.10, bf16[4,48,384]{2,1,0:T(8,128)(2,1)S(1)} %collective-permute-done.4.near_ref, bf16[4,48,384]{2,1,0:T(8,128)(2,1)S(1)} %first_block.1.blocked, bf16[4,48,384]{2,1,0:T(8,128)(2,1)S(1)} %copy-done.9, ...), custom_call_target="tpu_custom_call" | custom-call | tf_op jit(solution)/shard_map/second_block/pallas_call | solution.py:730
  64.6 9.3 %collective-permute-start.8 = (bf16[4,4,16,384]{3,2,1,0:T(8,128)(2,1)S(1)}, bf16[4,4,16,384]{3,2,1,0:T(8,128)(2,1)S(1)}, u32[]{:S(2)}, u32[]{:S(2)}) collective-permute-start(bf16[4,4,16,384]{3,2,1,0:T(8,128)(2,1)S(1)} %constant_dynamic-slice_fusion), channel_id=1, source_target_pairs={{0,16},{16,0},{1,17},{17,1},{2,18},{18,2},{3,19},{19,3},{4,20},{20... | collective-permute-start | bytes 589832 | tf_op jit(solution)/shard_map/ppermute | solution.py:18
  73.9 1.1 %collective-permute-done.8 = bf16[4,4,16,384]{3,2,1,0:T(8,128)(2,1)S(1)} collective-permute-done((bf16[4,4,16,384]{3,2,1,0:T(8,128)(2,1)S(1)}, bf16[4,4,16,384]{3,2,1,0:T(8,128)(2,1)S(1)}, u32[]{:S(2)}, u32[]{:S(2)}) %collective-permute-start.8) | collective-permute-done | bytes 196640 | tf_op jit(solution)/shard_map/ppermute | solution.py:18
  75.1 1.1 %reshape.17 = bf16[4,4,64,192]{3,2,1,0:T(8,128)(2,1)} reshape(bf16[4,4,32,384]{3,2,1,0:T(8,128)(2,1)S(1)} %pad_maximum_fusion) | data formatting | bytes 786432 | tf_op jit(solution)/shard_map/reshape | solution.py:842
  (37 shorter events, 0.2 us)
Async XLA Ops:
  0.0 1.8 %collective-permute-start = (bf16[2,64,384]{2,1,0:T(8,128)(2,1)}, bf16[2,64,384]{2,1,0:T(8,128)(2,1)S(1)}, u32[]{:S(2)}, u32[]{:S(2)}) collective-permute-start(bf16[2,64,384]{2,1,0:T(8,128)(2,1)} %bitcast.19), channel_id=1, source_target_pairs={{0,16},{16,0},{1,17},{17,1},{2,18},{18,2},{3,19},{19,3},{4,20},{20... | collective-permute-start | bytes 294920 | tf_op jit(solution)/shard_map/ppermute | solution.py:18
  1.8 0.6 copy-start.11
  5.6 6.9 %collective-permute-start.1 = (bf16[12,24,384]{2,1,0:T(8,128)(2,1)}, bf16[12,24,384]{2,1,0:T(8,128)(2,1)S(1)}, u32[]{:S(2)}, u32[]{:S(2)}) collective-permute-start(bf16[12,24,384]{2,1,0:T(8,128)(2,1)} %get-tuple-element.21), channel_id=1, source_target_pairs={{0,1},{1,0},{2,3},{3,2},{4,5},{5,4},{6,7},{7,6},{8,9},{9,8},{10,11... | collective-permute-start | bytes 663560 | tf_op jit(solution)/shard_map/ppermute | solution.py:18
  6.9 1.6 %copy-start.2 = (bf16[5184,192]{0,1:T(8,128)(2,1)S(1)}, bf16[5184,192]{0,1:T(8,128)(2,1)}, u32[]{:S(2)}) copy-start(bf16[5184,192]{0,1:T(8,128)(2,1)} %param.30) | copy-start | bytes 5971972
  8.4 4.1 %copy-start.6 = (bf16[20,32,384]{2,1,0:T(8,128)(2,1)S(1)}, bf16[20,32,384]{2,1,0:T(8,128)(2,1)}, u32[]{:S(2)}) copy-start(bf16[20,32,384]{2,1,0:T(8,128)(2,1)} %get-tuple-element.22.tiles) | copy-start | bytes 1474564
  8.4 4.1 %copy-start.7 = (bf16[8,24,384]{2,1,0:T(8,128)(2,1)S(1)}, bf16[8,24,384]{2,1,0:T(8,128)(2,1)}, u32[]{:S(2)}) copy-start(bf16[8,24,384]{2,1,0:T(8,128)(2,1)} %get-tuple-element.20.mine) | copy-start | bytes 442372
  8.4 4.1 %copy-start.10 = (s32[4]{0:T(128)S(1)}, s32[4]{0:T(128)}, u32[]{:S(2)}) copy-start(s32[4]{0:T(128)} %pad_add_fusion.place) | copy-start | bytes 52
  9.9 4.2 %copy-start = (bf16[768,3456]{1,0:T(8,128)(2,1)}, bf16[768,3456]{1,0:T(8,128)(2,1)S(1)}, u32[]{:S(2)}) copy-start(bf16[768,3456]{1,0:T(8,128)(2,1)S(1)} %align_weights.2.later.w3) | copy-start | bytes 15925252
  12.6 4.9 %copy-start.14 = (f32[192]{0:T(256)S(1)}, f32[192]{0:T(256)}, u32[]{:S(2)}) copy-start(f32[192]{0:T(256)} %param.24) | copy-start | bytes 2308
  12.6 5.0 %copy-start.15 = (f32[192]{0:T(256)S(1)}, f32[192]{0:T(256)}, u32[]{:S(2)}) copy-start(f32[192]{0:T(256)} %param.25) | copy-start | bytes 2308
  12.6 5.1 %copy-start.12 = (f32[384]{0:T(512)S(1)}, f32[384]{0:T(512)}, u32[]{:S(2)}) copy-start(f32[384]{0:T(512)} %param.22) | copy-start | bytes 4612
  12.6 5.1 %copy-start.13 = (f32[384]{0:T(512)S(1)}, f32[384]{0:T(512)}, u32[]{:S(2)}) copy-start(f32[384]{0:T(512)} %param.23) | copy-start | bytes 4612
  14.1 11.3 %collective-permute-start.2 = (bf16[14,24,384]{2,1,0:T(8,128)(2,1)}, bf16[14,24,384]{2,1,0:T(8,128)(2,1)S(1)}, u32[]{:S(2)}, u32[]{:S(2)}) collective-permute-start(bf16[14,24,384]{2,1,0:T(8,128)(2,1)} %get-tuple-element.24), channel_id=1, source_target_pairs={{0,2},{4,6},{8,10},{12,14},{2,0},{6,4},{10,8},{14,12},{1,3},{5,7},... | collective-permute-start | bytes 774152 | tf_op jit(solution)/shard_map/ppermute | solution.py:23
  15.4 10.0 %collective-permute-start.3 = (bf16[14,24,384]{2,1,0:T(8,128)(2,1)}, bf16[14,24,384]{2,1,0:T(8,128)(2,1)}, u32[]{:S(2)}, u32[]{:S(2)}) collective-permute-start(bf16[14,24,384]{2,1,0:T(8,128)(2,1)} %get-tuple-element.27), channel_id=1, source_target_pairs={{2,4},{6,8},{10,12},{4,2},{8,6},{12,10},{3,5},{7,9},{11,13},{5,3},... | collective-permute-start | bytes 774152 | tf_op jit(solution)/shard_map/ppermute | solution.py:23
  17.7 1.3 %copy-start.5 = (bf16[3456,192]{0,1:T(8,128)(2,1)S(1)}, bf16[3456,192]{0,1:T(8,128)(2,1)}, u32[]{:S(2)}) copy-start(bf16[3456,192]{0,1:T(8,128)(2,1)} %param.29) | copy-start | bytes 3981316
  19.5 23.9 %collective-permute-start.6 = (bf16[10,24,384]{2,1,0:T(8,128)(2,1)}, bf16[10,24,384]{2,1,0:T(8,128)(2,1)}, u32[]{:S(2)}, u32[]{:S(2)}) collective-permute-start(bf16[10,24,384]{2,1,0:T(8,128)(2,1)} %get-tuple-element.29), channel_id=1, source_target_pairs={{0,2},{4,6},{8,10},{12,14},{2,0},{6,4},{10,8},{14,12},{1,3},{5,7},... | collective-permute-start | bytes 552968 | tf_op jit(solution)/shard_map/ppermute | solution.py:23
  21.8 21.6 %collective-permute-start.7 = (bf16[10,24,384]{2,1,0:T(8,128)(2,1)}, bf16[10,24,384]{2,1,0:T(8,128)(2,1)}, u32[]{:S(2)}, u32[]{:S(2)}) collective-permute-start(bf16[10,24,384]{2,1,0:T(8,128)(2,1)} %get-tuple-element.31), channel_id=1, source_target_pairs={{2,4},{6,8},{10,12},{4,2},{8,6},{12,10},{3,5},{7,9},{11,13},{5,3},... | collective-permute-start | bytes 552968 | tf_op jit(solution)/shard_map/ppermute | solution.py:23
  36.1 7.3 %collective-permute-start.4 = (bf16[4,48,384]{2,1,0:T(8,128)(2,1)S(1)}, bf16[4,48,384]{2,1,0:T(8,128)(2,1)S(1)}, u32[]{:S(2)}, u32[]{:S(2)}) collective-permute-start(bf16[4,48,384]{2,1,0:T(8,128)(2,1)S(1)} %first_block.1.blocked), channel_id=1, source_target_pairs={{0,2},{4,6},{8,10},{12,14},{2,0},{6,4},{10,8},{14,12},{1,3},{5,7},... | collective-permute-start | bytes 442376 | tf_op jit(solution)/shard_map/ppermute | solution.py:23
  38.4 6.8 %collective-permute-start.5 = (bf16[4,48,384]{2,1,0:T(8,128)(2,1)S(1)}, bf16[4,48,384]{2,1,0:T(8,128)(2,1)S(1)}, u32[]{:S(2)}, u32[]{:S(2)}) collective-permute-start(bf16[4,48,384]{2,1,0:T(8,128)(2,1)S(1)} %first_block.1.blocked), channel_id=1, source_target_pairs={{2,4},{6,8},{10,12},{4,2},{8,6},{12,10},{3,5},{7,9},{11,13},{5,3},... | collective-permute-start | bytes 442376 | tf_op jit(solution)/shard_map/ppermute | solution.py:23
  40.3 1.6 %copy-start.3 = (bf16[5184,192]{0,1:T(8,128)(2,1)S(1)}, bf16[5184,192]{0,1:T(8,128)(2,1)}, u32[]{:S(2)}) copy-start(bf16[5184,192]{0,1:T(8,128)(2,1)} %param.31) | copy-start | bytes 5971972
  41.9 4.0 %copy-start.1 = (bf16[768,3456]{1,0:T(8,128)(2,1)S(1)}, bf16[768,3456]{1,0:T(8,128)(2,1)}, u32[]{:S(2)}) copy-start(bf16[768,3456]{1,0:T(8,128)(2,1)} %copy-done) | copy-start | bytes 15925252
  41.9 4.0 %copy-start.4 = (bf16[1152,768]{1,0:T(8,128)(2,1)S(1)}, bf16[1152,768]{1,0:T(8,128)(2,1)}, u32[]{:S(2)}) copy-start(bf16[1152,768]{1,0:T(8,128)(2,1)} %wt.1) | copy-start | bytes 5308420
  45.2 0.7 copy-start.8
  45.8 0.9 %copy-start.9 = (bf16[4,48,384]{2,1,0:T(8,128)(2,1)S(1)}, bf16[4,48,384]{2,1,0:T(8,128)(2,1)}, u32[]{:S(2)}) copy-start(bf16[4,48,384]{2,1,0:T(8,128)(2,1)} %copy-done.8) | copy-start | bytes 442372
  64.6 10.3 %collective-permute-start.8 = (bf16[4,4,16,384]{3,2,1,0:T(8,128)(2,1)S(1)}, bf16[4,4,16,384]{3,2,1,0:T(8,128)(2,1)S(1)}, u32[]{:S(2)}, u32[]{:S(2)}) collective-permute-start(bf16[4,4,16,384]{3,2,1,0:T(8,128)(2,1)S(1)} %constant_dynamic-slice_fusion), channel_id=1, source_target_pairs={{0,16},{16,0},{1,17},{17,1},{2,18},{18,2},{3,19},{19,3},{4,20},{20... | collective-permute-start | bytes 589832 | tf_op jit(solution)/shard_map/ppermute | solution.py:18

commit v16 on v14

--- a/solution.py
+++ b/solution.py
@@ -376,7 +376,8 @@
     )(weight.T)
 
 
-def combine_kernel(weight, out):
+def combine_kernel(weight, later, out):
+    del later
     half = weight.shape[0]
     channels = weight.shape[1] // 9
     chunk = 16
@@ -401,17 +402,17 @@
     lax.fori_loop(0, half // chunk, combine, 0)
 
 
-def combine_weights(weight):
+def combine_weights(weight, later):
     channels = 2 * weight.shape[1]
     vmem = pl.BlockSpec(memory_space=pltpu.VMEM)
     return pl.pallas_call(
         combine_kernel,
         out_shape=jax.ShapeDtypeStruct((2, 2 * channels, 2 * channels), BF16),
-        in_specs=[vmem],
+        in_specs=[vmem, pl.BlockSpec(memory_space=pl.ANY)],
         out_specs=vmem,
         compiler_params=pltpu.CompilerParams(vmem_limit_bytes=8 * 1024 * 1024),
         name="combine_weights",
-    )(weight.T)
+    )(weight.T, later)
 
 
 def weight_copies(source, target, sems, base):
@@ -434,8 +435,7 @@
     gains,
     weight_one,
     weight_two,
-    later_one,
-    later_two,
+    later,
     out_ref,
     w1,
     w2,
@@ -452,7 +452,7 @@
     height, width = sizes
     col, row = place[1], place[3]
     units = frames + 2
-    del later_one, later_two
+    del later
 
     copies_one = weight_copies(weight_one, w1, sems, 0)
     copies_two = weight_copies(weight_two, w2, sems, 3)
@@ -521,7 +521,7 @@
         in_specs=[pl.BlockSpec(memory_space=pltpu.SMEM)]
         + [vmem] * 4
         + [pl.BlockSpec(memory_space=pltpu.HBM)] * 2
-        + [anywhere] * 2,
+        + [anywhere],
         out_specs=vmem,
         scratch_shapes=[
             pltpu.VMEM((9, channels, slots * LANES), BF16),
@@ -539,7 +539,7 @@
             transcendentals=0,
         ),
         name="first_block",
-    )(place, *pieces, gains, weight_one, weight_two, *later)
+    )(place, *pieces, gains, weight_one, weight_two, later)
 
 
 def second_kernel(
@@ -626,6 +626,8 @@
         return carry
 
     lax.fori_loop(0, frames, double, 0)
+    copies[0].wait()
+    copies[1].start()
 
 
     for f in range(2):
@@ -697,9 +699,6 @@
         ((fourth, 2), (finish, 1)),
         (None, (finish, 2)),
     ):
-        if product == (third, 0):
-            copies[0].wait()
-            copies[1].start()
         if product == (fourth, 0):
             copies[1].wait()
         for n in range(max(2 * channels // LANES, *(last - first for first, last in groups))):
@@ -799,15 +798,15 @@
     weight_upsample, weight_four, own = lax.optimization_barrier(
         (weight_upsample, weight_four, own)
     )
-    weight_upsample = combine_weights(weight_upsample)
     weight_four = align_weights(weight_four)
+    weight_upsample = combine_weights(weight_upsample, weight_four)
     blocked = first_block(
         place,
         [near, own, far],
         gains,
         weight_one.reshape(9, 3, channels, channels),
         weight_two.reshape(9, 3, channels, channels),
-        (weight_upsample, weight_four),
+        weight_upsample,
         sizes,
     )
     far = paired(blocked, "rows", 1)

time: 76.6 us -> 77.5 us (1.012)
  local copies, waits for them, and re-layouts: 11.1 us -> 5.05 us
  starting transfers between devices: 17.8 us -> 23.1 us
  waiting for transfers between devices: 8.8 us -> 10.2 us
    unnamed x30, local copies, waits for them, and re-layouts: 9.83 us -> 3.73 us
    ppermute x3, starting transfers between devices: 5.68 us -> 9.17 us  [swapped(): return lax.ppermute(value, axis, [(0, 1), (1, 0)])]
    ppermute x6, starting transfers between devices: 12.1 us -> 14 us  [paired(): lax.ppermute(value, axis, pairs + [(high, low) for low, high in pairs])]
    ppermute x6, waiting for transfers between devices: 4.66 us -> 6.05 us  [paired(): lax.ppermute(value, axis, pairs + [(high, low) for low, high in pairs])]
  transfers between devices with their start and end apart: 9 -> 9, of which waited for: 5 -> 6; matrix products, arithmetic and copies ran while one was open for 1% -> 1% of each run, Pallas kernels for 19% -> 18%
where the time goes in v16:
time: 77.5 us; the launch traced here: 77.1 us
  Pallas kernels  37.7 us (49%)
  starting transfers between devices  23.1 us (30%)
  waiting for transfers between devices  10.2 us (13%)
  local copies, waits for them, and re-layouts  5.05 us (7%)
    pallas_call x1, Pallas kernels, second_block(): pl.pallas_call(functools.partial(second_kernel, wide, sizes), out_shape=j...  19.6 us
    ppermute x6, starting transfers between devices, paired(): lax.ppermute(value, axis, pairs + [(high, low) for low, high in pairs])  14 us
    pallas_call x1, Pallas kernels, first_block(): pl.pallas_call(functools.partial(first_kernel, wide, sizes), out_shape=ja...  10.7 us
    ppermute x3, starting transfers between devices, swapped(): return lax.ppermute(value, axis, [(0, 1), (1, 0)])  9.17 us
    ppermute x6, waiting for transfers between devices, paired(): lax.ppermute(value, axis, pairs + [(high, low) for low, high in pairs])  6.05 us
    ppermute x3, waiting for transfers between devices, swapped(): return lax.ppermute(value, axis, [(0, 1), (1, 0)])  4.14 us
    unnamed x30, local copies, waits for them, and re-layouts  3.73 us
    pallas_call x2, Pallas kernels, align_weights(): pl.pallas_call(align_kernel, out_shape=jax.ShapeDtypeStruct((4 * half, 18...  2.98 us
  transfers between devices with their start and end apart: 9, of which 6 were waited for; matrix products, arithmetic and copies ran while one was open for 1% of the time, Pallas kernels for 18%

profile of v16, /device:TPU:9, one launch (start us, length us, event | category | flops | bytes accessed | tf_op | source)
XLA Modules:
  0.0 77.1 jit_solution(3503510335065835400)
XLA Ops:
  0.0 0.7 collective-permute-start
  0.7 0.7 pad_add_fusion.place
  1.3 0.5 collective-permute-done.arrived
  1.8 0.6 copy-done.10
  2.5 2.4 %pack.1 = (bf16[8,24,384]{2,1,0:T(8,128)(2,1)}, bf16[12,24,384]{2,1,0:T(8,128)(2,1)}, bf16[20,32,384]{2,1,0:T(8,128)(2,1)}) custom-call(s32[4]{0:T(128)} %pad_add_fusion.place, bf16[2,64,384]{2,1,0:T(8,128)(2,1)} %bitcast.20, bf16[2,64,384]{2,1,0:T(8,128)(2,1)} %copy-done.10, bf16[2,64,384]{2,1,0:T(8,128)(2,1)} %bitcast.21, bf16[2,64,384]{2,1,0:T(8,128)(2,1)} %bitcast.22, ...), custom_call_target="tpu_custom_call" | custom-call | tf_op jit(solution)/shard_map/pack/pallas_call | solution.py:242
  4.9 1.2 %collective-permute-start.1 = (bf16[12,24,384]{2,1,0:T(8,128)(2,1)}, bf16[12,24,384]{2,1,0:T(8,128)(2,1)S(1)}, u32[]{:S(2)}, u32[]{:S(2)}) collective-permute-start(bf16[12,24,384]{2,1,0:T(8,128)(2,1)} %get-tuple-element.21), channel_id=1, source_target_pairs={{0,1},{1,0},{2,3},{3,2},{4,5},{5,4},{6,7},{7,6},{8,9},{9,8},{10,11... | collective-permute-start | bytes 663560 | tf_op jit(solution)/shard_map/ppermute | solution.py:18
  6.1 1.6 %copy-done.3 = bf16[5184,192]{0,1:T(8,128)(2,1)S(1)} copy-done((bf16[5184,192]{0,1:T(8,128)(2,1)S(1)}, bf16[5184,192]{0,1:T(8,128)(2,1)}, u32[]{:S(2)}) %copy-start.3) | copy-done | bytes 1990680
  7.7 1.5 %align_weights.2.later.weight_three = bf16[768,3456]{1,0:T(8,128)(2,1)S(1)} custom-call(bf16[192,5184]{1,0:T(8,128)(2,1)S(1)} %bitcast.14), custom_call_target="tpu_custom_call" | custom-call | tf_op jit(solution)/shard_map/align_weights/pallas_call | solution.py:369
  9.2 2.6 %collective-permute-done.1.theirs = bf16[12,24,384]{2,1,0:T(8,128)(2,1)S(1)} collective-permute-done((bf16[12,24,384]{2,1,0:T(8,128)(2,1)}, bf16[12,24,384]{2,1,0:T(8,128)(2,1)S(1)}, u32[]{:S(2)}, u32[]{:S(2)}) %collective-permute-start.1) | collective-permute-done | bytes 221216 | tf_op jit(solution)/shard_map/ppermute | solution.py:18
  11.8 0.0 copy-start.13
  11.8 0.0 copy-start.12
  11.8 0.0 copy-start.4
  11.8 1.5 %stack.33 = (bf16[2,8,24,384]{3,2,1,0:T(8,128)(2,1)S(1)}, bf16[14,24,384]{2,1,0:T(8,128)(2,1)}, bf16[14,24,384]{2,1,0:T(8,128)(2,1)}, bf16[20,24,384]{2,1,0:T(8,...) custom-call(s32[4]{0:T(128)S(1)} %copy-done.9, bf16[8,24,384]{2,1,0:T(8,128)(2,1)S(1)} %copy-done.8, ...), custom_call_target="tpu_custom_call" | custom-call | tf_op jit(solution)/shard_map/stack/pallas_call | solution.py:308
  13.4 1.2 %collective-permute-start.2 = (bf16[14,24,384]{2,1,0:T(8,128)(2,1)}, bf16[14,24,384]{2,1,0:T(8,128)(2,1)S(1)}, u32[]{:S(2)}, u32[]{:S(2)}) collective-permute-start(bf16[14,24,384]{2,1,0:T(8,128)(2,1)} %get-tuple-element.24), channel_id=1, source_target_pairs={{0,2},{4,6},{8,10},{12,14},{2,0},{6,4},{10,8},{14,12},{1,3},{5,7},... | collective-permute-start | bytes 774152 | tf_op jit(solution)/shard_map/ppermute | solution.py:23
  14.6 2.1 %collective-permute-start.3 = (bf16[14,24,384]{2,1,0:T(8,128)(2,1)}, bf16[14,24,384]{2,1,0:T(8,128)(2,1)}, u32[]{:S(2)}, u32[]{:S(2)}) collective-permute-start(bf16[14,24,384]{2,1,0:T(8,128)(2,1)} %get-tuple-element.27), channel_id=1, source_target_pairs={{2,4},{6,8},{10,12},{4,2},{8,6},{12,10},{3,5},{7,9},{11,13},{5,3},... | collective-permute-start | bytes 774152 | tf_op jit(solution)/shard_map/ppermute | solution.py:23
  16.7 0.1 stack_tile.7
  16.8 0.1 stack_tile.6
  17.0 1.5 %align_weights.3.later.weight_four = bf16[768,3456]{1,0:T(8,128)(2,1)S(1)} custom-call(bf16[192,5184]{1,0:T(8,128)(2,1)S(1)} %bitcast.15), custom_call_target="tpu_custom_call" | custom-call | tf_op jit(solution)/shard_map/align_weights/pallas_call | solution.py:369
  18.5 2.4 %collective-permute-start.6 = (bf16[10,24,384]{2,1,0:T(8,128)(2,1)}, bf16[10,24,384]{2,1,0:T(8,128)(2,1)}, u32[]{:S(2)}, u32[]{:S(2)}) collective-permute-start(bf16[10,24,384]{2,1,0:T(8,128)(2,1)} %get-tuple-element.30), channel_id=1, source_target_pairs={{0,2},{4,6},{8,10},{12,14},{2,0},{6,4},{10,8},{14,12},{1,3},{5,7},... | collective-permute-start | bytes 552968 | tf_op jit(solution)/shard_map/ppermute | solution.py:23
  20.9 1.9 %collective-permute-start.7 = (bf16[10,24,384]{2,1,0:T(8,128)(2,1)}, bf16[10,24,384]{2,1,0:T(8,128)(2,1)}, u32[]{:S(2)}, u32[]{:S(2)}) collective-permute-start(bf16[10,24,384]{2,1,0:T(8,128)(2,1)} %get-tuple-element.32), channel_id=1, source_target_pairs={{2,4},{6,8},{10,12},{4,2},{8,6},{12,10},{3,5},{7,9},{11,13},{5,3},... | collective-permute-start | bytes 552968 | tf_op jit(solution)/shard_map/ppermute | solution.py:23
  22.8 0.5 combine_weights.1.later.wu
  23.3 1.4 %collective-permute-done.2.near = bf16[14,24,384]{2,1,0:T(8,128)(2,1)S(1)} collective-permute-done((bf16[14,24,384]{2,1,0:T(8,128)(2,1)}, bf16[14,24,384]{2,1,0:T(8,128)(2,1)S(1)}, u32[]{:S(2)}, u32[]{:S(2)}) %collective-permute-start.2) | collective-permute-done | bytes 258080 | tf_op jit(solution)/shard_map/ppermute | solution.py:23
  24.7 10.7 %first_block.1.blocked = bf16[4,48,384]{2,1,0:T(8,128)(2,1)S(1)} custom-call(s32[4]{0:T(128)S(1)} %copy-done.9, bf16[14,24,384]{2,1,0:T(8,128)(2,1)S(1)} %collective-permute-done.2.near, bf16[2,8,24,384]{3,2,1,0:T(8,128)(2,1)S(1)} %get-tuple-element.26.own, bf16[14,24,384]{2,1,0:T(8,128)(2,1)} %collective-permute-done.3.far, ...), custom_call_target="tpu_custom_call" | custom-call | flops 4586471424 | bytes 15925248 | tf_op jit(solution)/shard_map/first_block/pallas_call | solution.py:518
  35.4 4.3 %collective-permute-start.4 = (bf16[4,48,384]{2,1,0:T(8,128)(2,1)S(1)}, bf16[4,48,384]{2,1,0:T(8,128)(2,1)S(1)}, u32[]{:S(2)}, u32[]{:S(2)}) collective-permute-start(bf16[4,48,384]{2,1,0:T(8,128)(2,1)S(1)} %first_block.1.blocked), channel_id=1, source_target_pairs={{0,2},{4,6},{8,10},{12,14},{2,0},{6,4},{10,8},{14,12},{1,3},{5,7},... | collective-permute-start | bytes 442376 | tf_op jit(solution)/shard_map/ppermute | solution.py:23
  39.7 2.1 %collective-permute-start.5 = (bf16[4,48,384]{2,1,0:T(8,128)(2,1)S(1)}, bf16[4,48,384]{2,1,0:T(8,128)(2,1)S(1)}, u32[]{:S(2)}, u32[]{:S(2)}) collective-permute-start(bf16[4,48,384]{2,1,0:T(8,128)(2,1)S(1)} %first_block.1.blocked), channel_id=1, source_target_pairs={{2,4},{6,8},{10,12},{4,2},{8,6},{12,10},{3,5},{7,9},{11,13},{5,3},... | collective-permute-start | bytes 442376 | tf_op jit(solution)/shard_map/ppermute | solution.py:23
  41.8 0.4 collective-permute-done.4.near
  42.2 4.2 %collective-permute-done.5.far = bf16[4,48,384]{2,1,0:T(8,128)(2,1)S(1)} collective-permute-done((bf16[4,48,384]{2,1,0:T(8,128)(2,1)S(1)}, bf16[4,48,384]{2,1,0:T(8,128)(2,1)S(1)}, u32[]{:S(2)}, u32[]{:S(2)}) %collective-permute-start.5) | collective-permute-done | bytes 147488 | tf_op jit(solution)/shard_map/ppermute | solution.py:23
  46.4 1.5 %copy-done.5 = bf16[1152,768]{1,0:T(8,128)(2,1)S(1)} copy-done((bf16[1152,768]{1,0:T(8,128)(2,1)S(1)}, bf16[1152,768]{1,0:T(8,128)(2,1)}, u32[]{:S(2)}) %copy-start.5) | copy-done | bytes 1769496
  47.9 19.6 %second_block.1 = bf16[8,4,16,384]{3,2,1,0:T(8,128)(2,1)S(1)} custom-call(s32[4]{0:T(128)S(1)} %copy-done.9, bf16[4,48,384]{2,1,0:T(8,128)(2,1)S(1)} %collective-permute-done.4.near, bf16[4,48,384]{2,1,0:T(8,128)(2,1)S(1)} %first_block.1.blocked, bf16[4,48,384]{2,1,0:T(8,128)(2,1)S(1)} %collective-permute-done.5.far, ...), custom_call_target="tpu_custom_call" | custom-call | tf_op jit(solution)/shard_map/second_block/pallas_call | solution.py:718
  67.5 7.3 %collective-permute-start.8 = (bf16[4,4,16,384]{3,2,1,0:T(8,128)(2,1)S(1)}, bf16[4,4,16,384]{3,2,1,0:T(8,128)(2,1)S(1)}, u32[]{:S(2)}, u32[]{:S(2)}) collective-permute-start(bf16[4,4,16,384]{3,2,1,0:T(8,128)(2,1)S(1)} %constant_dynamic-slice_fusion), channel_id=1, source_target_pairs={{0,16},{16,0},{1,17},{17,1},{2,18},{18,2},{3,19},{19,3},{4,20},{20... | collective-permute-start | bytes 589832 | tf_op jit(solution)/shard_map/ppermute | solution.py:18
  74.8 1.1 %collective-permute-done.8 = bf16[4,4,16,384]{3,2,1,0:T(8,128)(2,1)S(1)} collective-permute-done((bf16[4,4,16,384]{3,2,1,0:T(8,128)(2,1)S(1)}, bf16[4,4,16,384]{3,2,1,0:T(8,128)(2,1)S(1)}, u32[]{:S(2)}, u32[]{:S(2)}) %collective-permute-start.8) | collective-permute-done | bytes 196640 | tf_op jit(solution)/shard_map/ppermute | solution.py:18
  76.0 1.1 %reshape.17 = bf16[4,4,64,192]{3,2,1,0:T(8,128)(2,1)} reshape(bf16[4,4,32,384]{3,2,1,0:T(8,128)(2,1)S(1)} %pad_maximum_fusion) | data formatting | bytes 786432 | tf_op jit(solution)/shard_map/reshape | solution.py:833
  (35 shorter events, 0.2 us)
Async XLA Ops:
  0.0 1.8 %collective-permute-start = (bf16[2,64,384]{2,1,0:T(8,128)(2,1)}, bf16[2,64,384]{2,1,0:T(8,128)(2,1)S(1)}, u32[]{:S(2)}, u32[]{:S(2)}) collective-permute-start(bf16[2,64,384]{2,1,0:T(8,128)(2,1)} %bitcast.19), channel_id=1, source_target_pairs={{0,16},{16,0},{1,17},{17,1},{2,18},{18,2},{3,19},{19,3},{4,20},{20... | collective-permute-start | bytes 294920 | tf_op jit(solution)/shard_map/ppermute | solution.py:18
  1.8 0.6 copy-start.10
  4.9 6.9 %collective-permute-start.1 = (bf16[12,24,384]{2,1,0:T(8,128)(2,1)}, bf16[12,24,384]{2,1,0:T(8,128)(2,1)S(1)}, u32[]{:S(2)}, u32[]{:S(2)}) collective-permute-start(bf16[12,24,384]{2,1,0:T(8,128)(2,1)} %get-tuple-element.21), channel_id=1, source_target_pairs={{0,1},{1,0},{2,3},{3,2},{4,5},{5,4},{6,7},{7,6},{8,9},{9,8},{10,11... | collective-permute-start | bytes 663560 | tf_op jit(solution)/shard_map/ppermute | solution.py:18
  6.1 1.6 %copy-start.3 = (bf16[5184,192]{0,1:T(8,128)(2,1)S(1)}, bf16[5184,192]{0,1:T(8,128)(2,1)}, u32[]{:S(2)}) copy-start(bf16[5184,192]{0,1:T(8,128)(2,1)} %param.30) | copy-start | bytes 5971972
  7.7 4.1 %copy-start.7 = (bf16[20,32,384]{2,1,0:T(8,128)(2,1)S(1)}, bf16[20,32,384]{2,1,0:T(8,128)(2,1)}, u32[]{:S(2)}) copy-start(bf16[20,32,384]{2,1,0:T(8,128)(2,1)} %get-tuple-element.22.tiles) | copy-start | bytes 1474564
  7.7 4.1 %copy-start.8 = (bf16[8,24,384]{2,1,0:T(8,128)(2,1)S(1)}, bf16[8,24,384]{2,1,0:T(8,128)(2,1)}, u32[]{:S(2)}) copy-start(bf16[8,24,384]{2,1,0:T(8,128)(2,1)} %get-tuple-element.20.mine) | copy-start | bytes 442372
  7.7 4.1 %copy-start.9 = (s32[4]{0:T(128)S(1)}, s32[4]{0:T(128)}, u32[]{:S(2)}) copy-start(s32[4]{0:T(128)} %pad_add_fusion.place) | copy-start | bytes 52
  9.2 4.2 %copy-start = (bf16[768,3456]{1,0:T(8,128)(2,1)}, bf16[768,3456]{1,0:T(8,128)(2,1)S(1)}, u32[]{:S(2)}) copy-start(bf16[768,3456]{1,0:T(8,128)(2,1)S(1)} %align_weights.2.later.weight_three) | copy-start | bytes 15925252
  11.8 4.9 %copy-start.13 = (f32[192]{0:T(256)S(1)}, f32[192]{0:T(256)}, u32[]{:S(2)}) copy-start(f32[192]{0:T(256)} %param.25) | copy-start | bytes 2308
  11.8 5.0 %copy-start.14 = (f32[192]{0:T(256)S(1)}, f32[192]{0:T(256)}, u32[]{:S(2)}) copy-start(f32[192]{0:T(256)} %param.24) | copy-start | bytes 2308
  11.8 5.1 %copy-start.11 = (f32[384]{0:T(512)S(1)}, f32[384]{0:T(512)}, u32[]{:S(2)}) copy-start(f32[384]{0:T(512)} %param.23) | copy-start | bytes 4612
  11.8 5.1 %copy-start.12 = (f32[384]{0:T(512)S(1)}, f32[384]{0:T(512)}, u32[]{:S(2)}) copy-start(f32[384]{0:T(512)} %param.22) | copy-start | bytes 4612
  11.8 5.1 %copy-start.4 = (bf16[5184,192]{0,1:T(8,128)(2,1)S(1)}, bf16[5184,192]{0,1:T(8,128)(2,1)}, u32[]{:S(2)}) copy-start(bf16[5184,192]{0,1:T(8,128)(2,1)} %param.31) | copy-start | bytes 5971972
  13.4 11.3 %collective-permute-start.2 = (bf16[14,24,384]{2,1,0:T(8,128)(2,1)}, bf16[14,24,384]{2,1,0:T(8,128)(2,1)S(1)}, u32[]{:S(2)}, u32[]{:S(2)}) collective-permute-start(bf16[14,24,384]{2,1,0:T(8,128)(2,1)} %get-tuple-element.24), channel_id=1, source_target_pairs={{0,2},{4,6},{8,10},{12,14},{2,0},{6,4},{10,8},{14,12},{1,3},{5,7},... | collective-permute-start | bytes 774152 | tf_op jit(solution)/shard_map/ppermute | solution.py:23
  14.6 10.0 %collective-permute-start.3 = (bf16[14,24,384]{2,1,0:T(8,128)(2,1)}, bf16[14,24,384]{2,1,0:T(8,128)(2,1)}, u32[]{:S(2)}, u32[]{:S(2)}) collective-permute-start(bf16[14,24,384]{2,1,0:T(8,128)(2,1)} %get-tuple-element.27), channel_id=1, source_target_pairs={{2,4},{6,8},{10,12},{4,2},{8,6},{12,10},{3,5},{7,9},{11,13},{5,3},... | collective-permute-start | bytes 774152 | tf_op jit(solution)/shard_map/ppermute | solution.py:23
  17.0 5.8 %copy-start.6 = (bf16[3456,192]{0,1:T(8,128)(2,1)S(1)}, bf16[3456,192]{0,1:T(8,128)(2,1)}, u32[]{:S(2)}) copy-start(bf16[3456,192]{0,1:T(8,128)(2,1)} %param.29) | copy-start | bytes 3981316
  18.5 4.8 %copy-start.1 = (bf16[768,3456]{1,0:T(8,128)(2,1)}, bf16[768,3456]{1,0:T(8,128)(2,1)S(1)}, u32[]{:S(2)}) copy-start(bf16[768,3456]{1,0:T(8,128)(2,1)S(1)} %align_weights.3.later.weight_four) | copy-start | bytes 15925252
  18.5 23.3 %collective-permute-start.6 = (bf16[10,24,384]{2,1,0:T(8,128)(2,1)}, bf16[10,24,384]{2,1,0:T(8,128)(2,1)}, u32[]{:S(2)}, u32[]{:S(2)}) collective-permute-start(bf16[10,24,384]{2,1,0:T(8,128)(2,1)} %get-tuple-element.30), channel_id=1, source_target_pairs={{0,2},{4,6},{8,10},{12,14},{2,0},{6,4},{10,8},{14,12},{1,3},{5,7},... | collective-permute-start | bytes 552968 | tf_op jit(solution)/shard_map/ppermute | solution.py:23
  20.9 20.9 %collective-permute-start.7 = (bf16[10,24,384]{2,1,0:T(8,128)(2,1)}, bf16[10,24,384]{2,1,0:T(8,128)(2,1)}, u32[]{:S(2)}, u32[]{:S(2)}) collective-permute-start(bf16[10,24,384]{2,1,0:T(8,128)(2,1)} %get-tuple-element.32), channel_id=1, source_target_pairs={{2,4},{6,8},{10,12},{4,2},{8,6},{12,10},{3,5},{7,9},{11,13},{5,3},... | collective-permute-start | bytes 552968 | tf_op jit(solution)/shard_map/ppermute | solution.py:23
  23.3 12.1 %copy-start.2 = (bf16[2,768,768]{2,1,0:T(8,128)(2,1)}, bf16[2,768,768]{2,1,0:T(8,128)(2,1)S(1)}, u32[]{:S(2)}) copy-start(bf16[2,768,768]{2,1,0:T(8,128)(2,1)S(1)} %combine_weights.1.later.wu) | copy-start | bytes 7077892
  35.4 6.8 %collective-permute-start.4 = (bf16[4,48,384]{2,1,0:T(8,128)(2,1)S(1)}, bf16[4,48,384]{2,1,0:T(8,128)(2,1)S(1)}, u32[]{:S(2)}, u32[]{:S(2)}) collective-permute-start(bf16[4,48,384]{2,1,0:T(8,128)(2,1)S(1)} %first_block.1.blocked), channel_id=1, source_target_pairs={{0,2},{4,6},{8,10},{12,14},{2,0},{6,4},{10,8},{14,12},{1,3},{5,7},... | collective-permute-start | bytes 442376 | tf_op jit(solution)/shard_map/ppermute | solution.py:23
  39.7 6.8 %collective-permute-start.5 = (bf16[4,48,384]{2,1,0:T(8,128)(2,1)S(1)}, bf16[4,48,384]{2,1,0:T(8,128)(2,1)S(1)}, u32[]{:S(2)}, u32[]{:S(2)}) collective-permute-start(bf16[4,48,384]{2,1,0:T(8,128)(2,1)S(1)} %first_block.1.blocked), channel_id=1, source_target_pairs={{2,4},{6,8},{10,12},{4,2},{8,6},{12,10},{3,5},{7,9},{11,13},{5,3},... | collective-permute-start | bytes 442376 | tf_op jit(solution)/shard_map/ppermute | solution.py:23
  46.4 1.5 %copy-start.5 = (bf16[1152,768]{1,0:T(8,128)(2,1)S(1)}, bf16[1152,768]{1,0:T(8,128)(2,1)}, u32[]{:S(2)}) copy-start(bf16[1152,768]{1,0:T(8,128)(2,1)} %wt.1) | copy-start | bytes 5308420
  67.5 8.4 %collective-permute-start.8 = (bf16[4,4,16,384]{3,2,1,0:T(8,128)(2,1)S(1)}, bf16[4,4,16,384]{3,2,1,0:T(8,128)(2,1)S(1)}, u32[]{:S(2)}, u32[]{:S(2)}) collective-permute-start(bf16[4,4,16,384]{3,2,1,0:T(8,128)(2,1)S(1)} %constant_dynamic-slice_fusion), channel_id=1, source_target_pairs={{0,16},{16,0},{1,17},{17,1},{2,18},{18,2},{3,19},{19,3},{4,20},{20... | collective-permute-start | bytes 589832 | tf_op jit(solution)/shard_map/ppermute | solution.py:18

commit v17 on v11

--- a/solution.py
+++ b/solution.py
@@ -259,9 +259,8 @@
 
 
 def stack_kernel(
-    wide, place, mine, theirs, tiles, later, own, near, far, windows, tile_near, tile_far
+    wide, place, mine, theirs, tiles, own, near, far, windows, tile_near, tile_far
 ):
-    del later
     section, col = place[0], place[1]
     count = mine.shape[0] - 2
     own[0], own[1] = mine[...], theirs[0 : count + 2]
@@ -300,7 +299,7 @@
                 tile_far[slot] = jnp.where(is_even, high, low)
 
 
-def stack(place, mine, theirs, tiles, later):
+def stack(place, mine, theirs, tiles):
     units, wide, channels = mine.shape
     vmem = pl.BlockSpec(memory_space=pltpu.VMEM)
     lines = 2 * units - 2
@@ -309,12 +308,11 @@
         functools.partial(stack_kernel, wide),
         out_shape=[jax.ShapeDtypeStruct(shape + (wide, channels), BF16) for shape in shapes],
         in_specs=[pl.BlockSpec(memory_space=pltpu.SMEM)]
-        + [vmem] * 3
-        + [pl.BlockSpec(memory_space=pl.ANY)],
+        + [vmem] * 3,
         out_specs=[vmem] * 6,
         compiler_params=pltpu.CompilerParams(vmem_limit_bytes=8 * 1024 * 1024),
         name="stack",
-    )(place, mine, theirs, tiles, later)
+    )(place, mine, theirs, tiles)
 
 
 def align_kernel(weight, out):
@@ -778,15 +776,19 @@
         tile,
         part,
     )
-    weight_three, mine = lax.optimization_barrier((weight_three, mine))
-    weight_three = align_weights(weight_three)
     own, near, far, windows, tile_near, tile_far = stack(
-        place, mine, swapped(theirs, "cols"), tiles, weight_three
+        place, mine, swapped(theirs, "cols"), tiles
     )
     pieces = [paired(near, "rows", 0), own, paired(far, "rows", 1)]
+    weight_upsample, weight_three, own = lax.optimization_barrier(
+        (weight_upsample, weight_three, own)
+    )
+    weight_upsample = combine_weights(weight_upsample)
+    weight_three = align_weights(weight_three)
+    tile_near, tile_far, weight_upsample, weight_three = lax.optimization_barrier(
+        (tile_near, tile_far, weight_upsample, weight_three)
+    )
     tiles = [paired(tile_near, "rows", 0), windows, paired(tile_far, "rows", 1)]
-    weight_upsample, own = lax.optimization_barrier((weight_upsample, own))
-    weight_upsample = combine_weights(weight_upsample)
     blocked = first_block(
         place,
         pieces,

time: 75.6 us -> 78.2 us (1.034)
  local copies, waits for them, and re-layouts: 8 us -> 14.3 us
  starting transfers between devices: 22.9 us -> 17.7 us
  waiting for transfers between devices: 7.61 us -> 9.01 us
    ppermute x3, starting transfers between devices: 11.1 us -> 5.67 us  [swapped(): return lax.ppermute(value, axis, [(0, 1), (1, 0)])]
    unnamed x32 -> x26, local copies, waits for them, and re-layouts: 6.68 us -> 10.3 us
    ppermute x3, waiting for transfers between devices: 4.22 us -> 7.24 us  [swapped(): return lax.ppermute(value, axis, [(0, 1), (1, 0)])]
    ppermute x6, waiting for transfers between devices: 3.4 us -> 1.77 us  [paired(): lax.ppermute(value, axis, pairs + [(high, low) for low, high in pairs])]
    another operation x4, local copies, waits for them, and re-layouts: 0.17 us -> 1.54 us  [body(): jnp.stack([gain_one, gain_two, jnp.tile(gain_three, 2), jnp.tile(gain_fou...]
  transfers between devices with their start and end apart: 9 -> 9, of which waited for: 5 -> 4; matrix products, arithmetic and copies ran while one was open for 1% -> 5% of each run, Pallas kernels for 19% -> 19%
where the time goes in v17:
time: 78.2 us; the launch traced here: 77.8 us
  Pallas kernels  35.8 us (46%)
  starting transfers between devices  17.7 us (23%)
  local copies, waits for them, and re-layouts  14.3 us (18%)
  waiting for transfers between devices  9.01 us (12%)
    pallas_call x1, Pallas kernels, second_block(): pl.pallas_call(functools.partial(second_kernel, wide, sizes), out_shape=j...  17.4 us
    ppermute x6, starting transfers between devices, paired(): lax.ppermute(value, axis, pairs + [(high, low) for low, high in pairs])  12 us
    pallas_call x1, Pallas kernels, first_block(): pl.pallas_call(functools.partial(first_kernel, wide, sizes), out_shape=ja...  11 us
    unnamed x26, local copies, waits for them, and re-layouts  10.3 us
    ppermute x3, waiting for transfers between devices, swapped(): return lax.ppermute(value, axis, [(0, 1), (1, 0)])  7.24 us
    ppermute x3, starting transfers between devices, swapped(): return lax.ppermute(value, axis, [(0, 1), (1, 0)])  5.67 us
    pallas_call x2, Pallas kernels, align_weights(): pl.pallas_call(align_kernel, out_shape=jax.ShapeDtypeStruct((4 * half, 18...  2.98 us
    pallas_call x1, Pallas kernels, pack(): pl.pallas_call(functools.partial(pack_kernel, wide, tile, part), out_shap...  2.44 us
  transfers between devices with their start and end apart: 9, of which 4 were waited for; matrix products, arithmetic and copies ran while one was open for 5% of the time, Pallas kernels for 19%

profile of v17, /device:TPU:9, one launch (start us, length us, event | category | flops | bytes accessed | tf_op | source)
XLA Modules:
  0.0 77.8 jit_solution(2704368969888113312)
XLA Ops:
  0.0 0.7 collective-permute-start
  0.7 0.6 pad_add_fusion.place
  2.5 2.4 %pack.1 = (bf16[8,24,384]{2,1,0:T(8,128)(2,1)}, bf16[12,24,384]{2,1,0:T(8,128)(2,1)}, bf16[20,32,384]{2,1,0:T(8,128)(2,1)}) custom-call(s32[4]{0:T(128)} %pad_add_fusion.place, bf16[2,64,384]{2,1,0:T(8,128)(2,1)} %bitcast.20, bf16[2,64,384]{2,1,0:T(8,128)(2,1)} %copy-done.12, bf16[2,64,384]{2,1,0:T(8,128)(2,1)} %bitcast.21, bf16[2,64,384]{2,1,0:T(8,128)(2,1)} %bitcast.22, ...), custom_call_target="tpu_custom_call" | custom-call | tf_op jit(solution)/shard_map/pack/pallas_call | solution.py:242
  4.9 1.2 %collective-permute-start.1 = (bf16[12,24,384]{2,1,0:T(8,128)(2,1)}, bf16[12,24,384]{2,1,0:T(8,128)(2,1)S(1)}, u32[]{:S(2)}, u32[]{:S(2)}) collective-permute-start(bf16[12,24,384]{2,1,0:T(8,128)(2,1)} %get-tuple-element.22), channel_id=1, source_target_pairs={{0,1},{1,0},{2,3},{3,2},{4,5},{5,4},{6,7},{7,6},{8,9},{9,8},{10,11... | collective-permute-start | bytes 663560 | tf_op jit(solution)/shard_map/ppermute | solution.py:18
  6.1 5.7 %collective-permute-done.1.theirs = bf16[12,24,384]{2,1,0:T(8,128)(2,1)S(1)} collective-permute-done((bf16[12,24,384]{2,1,0:T(8,128)(2,1)}, bf16[12,24,384]{2,1,0:T(8,128)(2,1)S(1)}, u32[]{:S(2)}, u32[]{:S(2)}) %collective-permute-start.1) | collective-permute-done | bytes 221216 | tf_op jit(solution)/shard_map/ppermute | solution.py:18
  11.8 1.0 %copy-done.6 = bf16[20,32,384]{2,1,0:T(8,128)(2,1)S(1)} copy-done((bf16[20,32,384]{2,1,0:T(8,128)(2,1)S(1)}, bf16[20,32,384]{2,1,0:T(8,128)(2,1)}, u32[]{:S(2)}) %copy-start.6) | copy-done | bytes 491544
  12.8 0.9 %copy-done.7 = bf16[8,24,384]{2,1,0:T(8,128)(2,1)S(1)} copy-done((bf16[8,24,384]{2,1,0:T(8,128)(2,1)S(1)}, bf16[8,24,384]{2,1,0:T(8,128)(2,1)}, u32[]{:S(2)}) %copy-start.7) | copy-done | bytes 147480
  13.7 0.7 copy-done.10
  14.4 1.5 %stack.33 = (bf16[2,8,24,384]{3,2,1,0:T(8,128)(2,1)S(1)}, bf16[14,24,384]{2,1,0:T(8,128)(2,1)}, bf16[14,24,384]{2,1,0:T(8,128)(2,1)}, bf16[20,24,384]{2,1,0:T(8,...) custom-call(s32[4]{0:T(128)S(1)} %copy-done.10, bf16[8,24,384]{2,1,0:T(8,128)(2,1)S(1)} %copy-done.7, ...), custom_call_target="tpu_custom_call" | custom-call | tf_op jit(solution)/shard_map/stack/pallas_call | solution.py:307
  15.9 1.2 %collective-permute-start.2 = (bf16[14,24,384]{2,1,0:T(8,128)(2,1)}, bf16[14,24,384]{2,1,0:T(8,128)(2,1)S(1)}, u32[]{:S(2)}, u32[]{:S(2)}) collective-permute-start(bf16[14,24,384]{2,1,0:T(8,128)(2,1)} %get-tuple-element.24), channel_id=1, source_target_pairs={{0,2},{4,6},{8,10},{12,14},{2,0},{6,4},{10,8},{14,12},{1,3},{5,7},... | collective-permute-start | bytes 774152 | tf_op jit(solution)/shard_map/ppermute | solution.py:23
  17.1 2.1 %collective-permute-start.3 = (bf16[14,24,384]{2,1,0:T(8,128)(2,1)}, bf16[14,24,384]{2,1,0:T(8,128)(2,1)}, u32[]{:S(2)}, u32[]{:S(2)}) collective-permute-start(bf16[14,24,384]{2,1,0:T(8,128)(2,1)} %get-tuple-element.26), channel_id=1, source_target_pairs={{2,4},{6,8},{10,12},{4,2},{8,6},{12,10},{3,5},{7,9},{11,13},{5,3},... | collective-permute-start | bytes 774152 | tf_op jit(solution)/shard_map/ppermute | solution.py:23
  19.2 0.7 tile.4
  20.0 0.7 tile.5
  20.8 0.7 stack.30
  21.5 0.7 stack.31
  22.2 1.6 %copy-done.2 = bf16[5184,192]{0,1:T(8,128)(2,1)S(1)} copy-done((bf16[5184,192]{0,1:T(8,128)(2,1)S(1)}, bf16[5184,192]{0,1:T(8,128)(2,1)}, u32[]{:S(2)}) %copy-start.2) | copy-done | bytes 1990680
  23.7 1.5 %align_weights.2.w3 = bf16[768,3456]{1,0:T(8,128)(2,1)S(1)} custom-call(bf16[192,5184]{1,0:T(8,128)(2,1)S(1)} %bitcast.14), custom_call_target="tpu_custom_call" | custom-call | tf_op jit(solution)/shard_map/align_weights/pallas_call | solution.py:367
  25.2 2.3 %copy-done = bf16[768,3456]{1,0:T(8,128)(2,1)} copy-done((bf16[768,3456]{1,0:T(8,128)(2,1)}, bf16[768,3456]{1,0:T(8,128)(2,1)S(1)}, u32[]{:S(2)}) %copy-start) | copy-done | bytes 5308440
  28.0 2.4 %collective-permute-start.6 = (bf16[10,24,384]{2,1,0:T(8,128)(2,1)}, bf16[10,24,384]{2,1,0:T(8,128)(2,1)}, u32[]{:S(2)}, u32[]{:S(2)}) collective-permute-start(bf16[10,24,384]{2,1,0:T(8,128)(2,1)} %get-tuple-element.32), channel_id=1, source_target_pairs={{0,2},{4,6},{8,10},{12,14},{2,0},{6,4},{10,8},{14,12},{1,3},{5,7},... | collective-permute-start | bytes 552968 | tf_op jit(solution)/shard_map/ppermute | solution.py:23
  30.4 1.9 %collective-permute-start.7 = (bf16[10,24,384]{2,1,0:T(8,128)(2,1)}, bf16[10,24,384]{2,1,0:T(8,128)(2,1)}, u32[]{:S(2)}, u32[]{:S(2)}) collective-permute-start(bf16[10,24,384]{2,1,0:T(8,128)(2,1)} %get-tuple-element.34), channel_id=1, source_target_pairs={{2,4},{6,8},{10,12},{4,2},{8,6},{12,10},{3,5},{7,9},{11,13},{5,3},... | collective-permute-start | bytes 552968 | tf_op jit(solution)/shard_map/ppermute | solution.py:23
  32.4 11.0 %first_block.1.blocked = bf16[4,48,384]{2,1,0:T(8,128)(2,1)S(1)} custom-call(s32[4]{0:T(128)S(1)} %copy-done.11, bf16[14,24,384]{2,1,0:T(8,128)(2,1)S(1)} %collective-permute-done.2.near, bf16[2,8,24,384]{3,2,1,0:T(8,128)(2,1)S(1)} %get-tuple-element.25.own, bf16[14,24,384]{2,1,0:T(8,128)(2,1)} %collective-permute-done.3.far, ...), custom_call_target="tpu_custom_call" | custom-call | flops 4586471424 | bytes 15925248 | tf_op jit(solution)/shard_map/first_block/pallas_call | solution.py:525
  43.3 2.5 %collective-permute-start.4 = (bf16[4,48,384]{2,1,0:T(8,128)(2,1)S(1)}, bf16[4,48,384]{2,1,0:T(8,128)(2,1)S(1)}, u32[]{:S(2)}, u32[]{:S(2)}) collective-permute-start(bf16[4,48,384]{2,1,0:T(8,128)(2,1)S(1)} %first_block.1.blocked), channel_id=1, source_target_pairs={{0,2},{4,6},{8,10},{12,14},{2,0},{6,4},{10,8},{14,12},{1,3},{5,7},... | collective-permute-start | bytes 442376 | tf_op jit(solution)/shard_map/ppermute | solution.py:23
  45.9 1.9 %collective-permute-start.5 = (bf16[4,48,384]{2,1,0:T(8,128)(2,1)S(1)}, bf16[4,48,384]{2,1,0:T(8,128)(2,1)S(1)}, u32[]{:S(2)}, u32[]{:S(2)}) collective-permute-start(bf16[4,48,384]{2,1,0:T(8,128)(2,1)S(1)} %first_block.1.blocked), channel_id=1, source_target_pairs={{2,4},{6,8},{10,12},{4,2},{8,6},{12,10},{3,5},{7,9},{11,13},{5,3},... | collective-permute-start | bytes 442376 | tf_op jit(solution)/shard_map/ppermute | solution.py:23
  47.8 1.6 %copy-done.3 = bf16[5184,192]{0,1:T(8,128)(2,1)S(1)} copy-done((bf16[5184,192]{0,1:T(8,128)(2,1)S(1)}, bf16[5184,192]{0,1:T(8,128)(2,1)}, u32[]{:S(2)}) %copy-start.3) | copy-done | bytes 1990680
  49.4 1.5 %align_weights.3.w4 = bf16[768,3456]{1,0:T(8,128)(2,1)S(1)} custom-call(bf16[192,5184]{1,0:T(8,128)(2,1)S(1)} %bitcast.15), custom_call_target="tpu_custom_call" | custom-call | tf_op jit(solution)/shard_map/align_weights/pallas_call | solution.py:367
  50.9 1.8 %collective-permute-done.5.far = bf16[4,48,384]{2,1,0:T(8,128)(2,1)S(1)} collective-permute-done((bf16[4,48,384]{2,1,0:T(8,128)(2,1)S(1)}, bf16[4,48,384]{2,1,0:T(8,128)(2,1)S(1)}, u32[]{:S(2)}, u32[]{:S(2)}) %collective-permute-start.5) | collective-permute-done | bytes 147488 | tf_op jit(solution)/shard_map/ppermute | solution.py:23
  52.6 0.7 copy-done.8
  53.3 0.9 %copy-done.9 = bf16[4,48,384]{2,1,0:T(8,128)(2,1)S(1)} copy-done((bf16[4,48,384]{2,1,0:T(8,128)(2,1)S(1)}, bf16[4,48,384]{2,1,0:T(8,128)(2,1)}, u32[]{:S(2)}) %copy-start.9) | copy-done | bytes 147480
  54.2 17.4 %second_block.1 = bf16[8,4,16,384]{3,2,1,0:T(8,128)(2,1)S(1)} custom-call(s32[4]{0:T(128)S(1)} %copy-done.11, bf16[4,48,384]{2,1,0:T(8,128)(2,1)S(1)} %collective-permute-done.4.near, bf16[4,48,384]{2,1,0:T(8,128)(2,1)S(1)} %first_block.1.blocked, bf16[4,48,384]{2,1,0:T(8,128)(2,1)S(1)} %copy-done.9, bf16[10,24,384]{2,1,0:T(8,128)(2,1)} %collective-permute-done.6.tile_near, ...), custom_call_target="tpu_custom_call" | custom-call | tf_op jit(solution)/shard_map/second_block/pallas_call | solution.py:712
  71.7 3.8 %collective-permute-start.8 = (bf16[4,4,16,384]{3,2,1,0:T(8,128)(2,1)S(1)}, bf16[4,4,16,384]{3,2,1,0:T(8,128)(2,1)S(1)}, u32[]{:S(2)}, u32[]{:S(2)}) collective-permute-start(bf16[4,4,16,384]{3,2,1,0:T(8,128)(2,1)S(1)} %constant_dynamic-slice_fusion), channel_id=1, source_target_pairs={{0,16},{16,0},{1,17},{17,1},{2,18},{18,2},{3,19},{19,3},{4,20},{20... | collective-permute-start | bytes 589832 | tf_op jit(solution)/shard_map/ppermute | solution.py:18
  75.5 1.1 %collective-permute-done.8 = bf16[4,4,16,384]{3,2,1,0:T(8,128)(2,1)S(1)} collective-permute-done((bf16[4,4,16,384]{3,2,1,0:T(8,128)(2,1)S(1)}, bf16[4,4,16,384]{3,2,1,0:T(8,128)(2,1)S(1)}, u32[]{:S(2)}, u32[]{:S(2)}) %collective-permute-start.8) | collective-permute-done | bytes 196640 | tf_op jit(solution)/shard_map/ppermute | solution.py:18
  76.6 1.1 %reshape.17 = bf16[4,4,64,192]{3,2,1,0:T(8,128)(2,1)} reshape(bf16[4,4,32,384]{3,2,1,0:T(8,128)(2,1)S(1)} %pad_maximum_fusion) | data formatting | bytes 786432 | tf_op jit(solution)/shard_map/reshape | solution.py:821
  (31 shorter events, 1.9 us)
Async XLA Ops:
  0.0 1.8 %collective-permute-start = (bf16[2,64,384]{2,1,0:T(8,128)(2,1)}, bf16[2,64,384]{2,1,0:T(8,128)(2,1)S(1)}, u32[]{:S(2)}, u32[]{:S(2)}) collective-permute-start(bf16[2,64,384]{2,1,0:T(8,128)(2,1)} %bitcast.19), channel_id=1, source_target_pairs={{0,16},{16,0},{1,17},{17,1},{2,18},{18,2},{3,19},{19,3},{4,20},{20... | collective-permute-start | bytes 294920 | tf_op jit(solution)/shard_map/ppermute | solution.py:18
  1.8 0.6 copy-start.12
  4.9 6.9 %collective-permute-start.1 = (bf16[12,24,384]{2,1,0:T(8,128)(2,1)}, bf16[12,24,384]{2,1,0:T(8,128)(2,1)S(1)}, u32[]{:S(2)}, u32[]{:S(2)}) collective-permute-start(bf16[12,24,384]{2,1,0:T(8,128)(2,1)} %get-tuple-element.22), channel_id=1, source_target_pairs={{0,1},{1,0},{2,3},{3,2},{4,5},{5,4},{6,7},{7,6},{8,9},{9,8},{10,11... | collective-permute-start | bytes 663560 | tf_op jit(solution)/shard_map/ppermute | solution.py:18
  11.8 1.0 %copy-start.6 = (bf16[20,32,384]{2,1,0:T(8,128)(2,1)S(1)}, bf16[20,32,384]{2,1,0:T(8,128)(2,1)}, u32[]{:S(2)}) copy-start(bf16[20,32,384]{2,1,0:T(8,128)(2,1)} %get-tuple-element.23.tiles) | copy-start | bytes 1474564
  12.8 0.9 %copy-start.7 = (bf16[8,24,384]{2,1,0:T(8,128)(2,1)S(1)}, bf16[8,24,384]{2,1,0:T(8,128)(2,1)}, u32[]{:S(2)}) copy-start(bf16[8,24,384]{2,1,0:T(8,128)(2,1)} %get-tuple-element.21.mine) | copy-start | bytes 442372
  13.7 0.7 copy-start.10
  15.9 16.4 %collective-permute-start.2 = (bf16[14,24,384]{2,1,0:T(8,128)(2,1)}, bf16[14,24,384]{2,1,0:T(8,128)(2,1)S(1)}, u32[]{:S(2)}, u32[]{:S(2)}) collective-permute-start(bf16[14,24,384]{2,1,0:T(8,128)(2,1)} %get-tuple-element.24), channel_id=1, source_target_pairs={{0,2},{4,6},{8,10},{12,14},{2,0},{6,4},{10,8},{14,12},{1,3},{5,7},... | collective-permute-start | bytes 774152 | tf_op jit(solution)/shard_map/ppermute | solution.py:23
  17.1 15.2 %collective-permute-start.3 = (bf16[14,24,384]{2,1,0:T(8,128)(2,1)}, bf16[14,24,384]{2,1,0:T(8,128)(2,1)}, u32[]{:S(2)}, u32[]{:S(2)}) collective-permute-start(bf16[14,24,384]{2,1,0:T(8,128)(2,1)} %get-tuple-element.26), channel_id=1, source_target_pairs={{2,4},{6,8},{10,12},{4,2},{8,6},{12,10},{3,5},{7,9},{11,13},{5,3},... | collective-permute-start | bytes 774152 | tf_op jit(solution)/shard_map/ppermute | solution.py:23
  22.1 1.6 %copy-start.2 = (bf16[5184,192]{0,1:T(8,128)(2,1)S(1)}, bf16[5184,192]{0,1:T(8,128)(2,1)}, u32[]{:S(2)}) copy-start(bf16[5184,192]{0,1:T(8,128)(2,1)} %param.30) | copy-start | bytes 5971972
  23.7 3.9 %copy-start.5 = (bf16[3456,192]{0,1:T(8,128)(2,1)S(1)}, bf16[3456,192]{0,1:T(8,128)(2,1)}, u32[]{:S(2)}) copy-start(bf16[3456,192]{0,1:T(8,128)(2,1)} %param.29) | copy-start | bytes 3981316
  25.2 2.4 %copy-start = (bf16[768,3456]{1,0:T(8,128)(2,1)}, bf16[768,3456]{1,0:T(8,128)(2,1)S(1)}, u32[]{:S(2)}) copy-start(bf16[768,3456]{1,0:T(8,128)(2,1)S(1)} %align_weights.2.w3) | copy-start | bytes 15925252
  27.6 4.8 %copy-start.11 = (s32[4]{0:T(128)S(1)}, s32[4]{0:T(128)}, u32[]{:S(2)}) copy-start(s32[4]{0:T(128)} %pad_add_fusion.place) | copy-start | bytes 52
  28.0 22.8 %collective-permute-start.6 = (bf16[10,24,384]{2,1,0:T(8,128)(2,1)}, bf16[10,24,384]{2,1,0:T(8,128)(2,1)}, u32[]{:S(2)}, u32[]{:S(2)}) collective-permute-start(bf16[10,24,384]{2,1,0:T(8,128)(2,1)} %get-tuple-element.32), channel_id=1, source_target_pairs={{0,2},{4,6},{8,10},{12,14},{2,0},{6,4},{10,8},{14,12},{1,3},{5,7},... | collective-permute-start | bytes 552968 | tf_op jit(solution)/shard_map/ppermute | solution.py:23
  30.4 20.5 %collective-permute-start.7 = (bf16[10,24,384]{2,1,0:T(8,128)(2,1)}, bf16[10,24,384]{2,1,0:T(8,128)(2,1)}, u32[]{:S(2)}, u32[]{:S(2)}) collective-permute-start(bf16[10,24,384]{2,1,0:T(8,128)(2,1)} %get-tuple-element.34), channel_id=1, source_target_pairs={{2,4},{6,8},{10,12},{4,2},{8,6},{12,10},{3,5},{7,9},{11,13},{5,3},... | collective-permute-start | bytes 552968 | tf_op jit(solution)/shard_map/ppermute | solution.py:23
  43.3 7.6 %collective-permute-start.4 = (bf16[4,48,384]{2,1,0:T(8,128)(2,1)S(1)}, bf16[4,48,384]{2,1,0:T(8,128)(2,1)S(1)}, u32[]{:S(2)}, u32[]{:S(2)}) collective-permute-start(bf16[4,48,384]{2,1,0:T(8,128)(2,1)S(1)} %first_block.1.blocked), channel_id=1, source_target_pairs={{0,2},{4,6},{8,10},{12,14},{2,0},{6,4},{10,8},{14,12},{1,3},{5,7},... | collective-permute-start | bytes 442376 | tf_op jit(solution)/shard_map/ppermute | solution.py:23
  45.9 6.8 %collective-permute-start.5 = (bf16[4,48,384]{2,1,0:T(8,128)(2,1)S(1)}, bf16[4,48,384]{2,1,0:T(8,128)(2,1)S(1)}, u32[]{:S(2)}, u32[]{:S(2)}) collective-permute-start(bf16[4,48,384]{2,1,0:T(8,128)(2,1)S(1)} %first_block.1.blocked), channel_id=1, source_target_pairs={{2,4},{6,8},{10,12},{4,2},{8,6},{12,10},{3,5},{7,9},{11,13},{5,3},... | collective-permute-start | bytes 442376 | tf_op jit(solution)/shard_map/ppermute | solution.py:23
  47.8 1.6 %copy-start.3 = (bf16[5184,192]{0,1:T(8,128)(2,1)S(1)}, bf16[5184,192]{0,1:T(8,128)(2,1)}, u32[]{:S(2)}) copy-start(bf16[5184,192]{0,1:T(8,128)(2,1)} %param.31) | copy-start | bytes 5971972
  49.4 4.0 %copy-start.1 = (bf16[768,3456]{1,0:T(8,128)(2,1)S(1)}, bf16[768,3456]{1,0:T(8,128)(2,1)}, u32[]{:S(2)}) copy-start(bf16[768,3456]{1,0:T(8,128)(2,1)} %copy-done) | copy-start | bytes 15925252
  49.4 4.0 %copy-start.4 = (bf16[1152,768]{1,0:T(8,128)(2,1)S(1)}, bf16[1152,768]{1,0:T(8,128)(2,1)}, u32[]{:S(2)}) copy-start(bf16[1152,768]{1,0:T(8,128)(2,1)} %wt.1) | copy-start | bytes 5308420
  52.6 0.7 copy-start.8
  53.3 0.9 %copy-start.9 = (bf16[4,48,384]{2,1,0:T(8,128)(2,1)S(1)}, bf16[4,48,384]{2,1,0:T(8,128)(2,1)}, u32[]{:S(2)}) copy-start(bf16[4,48,384]{2,1,0:T(8,128)(2,1)} %copy-done.8) | copy-start | bytes 442372
  71.7 4.9 %collective-permute-start.8 = (bf16[4,4,16,384]{3,2,1,0:T(8,128)(2,1)S(1)}, bf16[4,4,16,384]{3,2,1,0:T(8,128)(2,1)S(1)}, u32[]{:S(2)}, u32[]{:S(2)}) collective-permute-start(bf16[4,4,16,384]{3,2,1,0:T(8,128)(2,1)S(1)} %constant_dynamic-slice_fusion), channel_id=1, source_target_pairs={{0,16},{16,0},{1,17},{17,1},{2,18},{18,2},{3,19},{19,3},{4,20},{20... | collective-permute-start | bytes 589832 | tf_op jit(solution)/shard_map/ppermute | solution.py:18
